TPU v7x, 32 devices: a whole 2x2x4 slice. The times are simulated.
32 devices in a mesh: wide: 8 (over z, y), narrow: 4 (over x, core).
Axes of the slice: x: 2, y: 2, z: 4, core: 2. Of those that a mesh axis runs over, the one named last changes fastest.
Arguments:
- tokens: bfloat16 [8192, 768], P(('wide', 'narrow')), may hold values from -6 to 6
- image_size: int32 [8, 4], P('wide'), may hold values from 0 to 2
- cotangent: bfloat16 [8192, 768], P(('wide', 'narrow')), may hold values from -6 to 6
- ln1_gain: float32 [768], replicated, may hold values from 0.5 to 1.5
- ln1_bias: float32 [768], replicated, may hold values from -1.5 to 1.5
- qkv_weight: bfloat16 [768, 2304], replicated, may hold values from -0.3125 to 0.3125
- qv_bias: float32 [1536], replicated, may hold values from -1.5 to 1.5
- proj_weight: bfloat16 [768, 768], replicated, may hold values from -0.625 to 0.625
- proj_bias: float32 [768], replicated, may hold values from -1.5 to 1.5
- ln2_gain: float32 [768], replicated, may hold values from 0.5 to 1.5
- ln2_bias: float32 [768], replicated, may hold values from -1.5 to 1.5
- up_weight: bfloat16 [768, 3072], replicated, may hold values from -0.21875 to 0.21875
- up_bias: float32 [3072], replicated, may hold values from -1.5 to 1.5
- down_weight: bfloat16 [3072, 768], replicated, may hold values from -0.109375 to 0.109375
- down_bias: float32 [768], replicated, may hold values from -1.5 to 1.5
Outputs:
- mixed: bfloat16 [8192, 768], P(('wide', 'narrow'))
- input_grad: bfloat16 [8192, 768], P(('wide', 'narrow'))
- ln1_gain_grad: float32 [768], P('wide')
- ln1_bias_grad: float32 [768], P('wide')
- qkv_weight_grad: float32 [768, 2304], P('narrow', 'wide')
- qv_bias_grad: float32 [1536], P('wide')
- proj_weight_grad: float32 [768, 768], P('narrow', 'wide')
- proj_bias_grad: float32 [768], P('wide')
- ln2_gain_grad: float32 [768], P('wide')
- ln2_bias_grad: float32 [768], P('wide')
- up_weight_grad: float32 [768, 3072], P('narrow', 'wide')
- up_bias_grad: float32 [3072], P('wide')
- down_weight_grad: float32 [3072, 768], P('narrow', 'wide')
- down_bias_grad: float32 [768], P('wide')
Inputs may be any that keep to these rules, and one draw needn't show every extreme that they name: `image_size`: 0, 1, 2 stand for images of 100, 196, 256 patches, a quarter of them on each index of narrow.
All inputs are finite; a program needn't handle non-finite values.
Results may differ from a plain program's by a relative error of at most 0.015.
Values may be sent and summed in bfloat16 or wider, within the bound.
No kernel may reach another device: no remote copies, remote signals or barrier semaphores. Data moves between devices by JAX's collectives and lax.ppermute only.
A program may use at most 192 MiB of HBM per device.

v0:
```python
import functools

import jax
import jax.numpy as jnp
from jax import lax
from jax.experimental import pallas as pl
from jax.experimental.pallas import tpu as pltpu
from jax.sharding import PartitionSpec as P

HEADS = 12
HEAD = 64
AXES = ("wide", "narrow")
GROUPS = 8
BF = jnp.bfloat16
F32 = jnp.float32

eps = 1e-06
neg_big = -1e30

X_LINK, Y_LINK, A_LINK, B_LINK = range(4)
DOWN_ORDER = ((0, 1, 2, 3), (1, 0, 3, 2))
UP_ORDER = ((2, 3, 0, 1), (3, 2, 1, 0))
MIX_ORDERS = (((0, 1, 2, 3), (1, 2, 3, 0)), ((2, 3, 0, 1), (3, 0, 1, 2)))


def times_trans(left, right):
    return lax.dot_general(
        left, right, (((1,), (1,)), ((), ())), preferred_element_type=jnp.float32
    )


class Place:
    def __init__(self):
        self.wide_n = lax.axis_size("wide")
        self.narrow_n = lax.axis_size("narrow")
        self.rest = self.wide_n // GROUPS
        self.rest_bits = self.rest.bit_length() - 1
        self.count = self.wide_n * self.narrow_n
        wide_at = lax.axis_index("wide")
        narrow_at = lax.axis_index("narrow")
        self.wide_at = wide_at
        self.narrow_at = narrow_at
        self.core = narrow_at & 1
        self.x_at = narrow_at >> 1
        group = wide_at >> self.rest_bits
        z_at = group >> 1
        self.bits = (self.x_at, group & 1, (z_at & 1) ^ (z_at >> 1), z_at >> 1)
        shift = 2 + self.rest_bits
        self.masks = (2, 1 << shift, 2 << shift, 6 << shift)

    def swap(self, value, mask):
        pairs = [(index, index ^ mask) for index in range(self.count)]
        return lax.ppermute(value, AXES, pairs)

    def swap_by_core(self, value, links):
        pairs = [(index, index ^ self.masks[links[index & 1]]) for index in range(self.count)]
        return lax.ppermute(value, AXES, pairs)

    def positions(self, order):
        rows = []
        owner_x = jnp.arange(2, dtype=jnp.int32)[:, None]
        owner_g = jnp.arange(GROUPS, dtype=jnp.int32)[None, :]
        owner_z = owner_g >> 1
        owner = (owner_x, owner_g & 1, (owner_z & 1) ^ (owner_z >> 1), owner_z >> 1)
        differ = [jnp.broadcast_to(o ^ b, (2, GROUPS)) for o, b in zip(owner, self.bits)]
        for links in order:
            spot = jnp.zeros((2, GROUPS), jnp.int32)
            for link in links:
                spot = spot * 2 + differ[link]
            rows.append(spot)
        return jnp.where(self.core == 0, rows[0], rows[1]).reshape(2 * GROUPS)


def to_slots(place, rows):
    parts = rows.reshape(2, 2, rows.shape[0] // 4, rows.shape[1])
    near = lax.dynamic_index_in_dim(parts, place.x_at, 0, keepdims=False)
    far = lax.dynamic_index_in_dim(parts, 1 - place.x_at, 0, keepdims=False)
    far = place.swap(far, 2)
    both = jnp.stack([near, far])
    mine = lax.dynamic_index_in_dim(both, place.core, 1, keepdims=False)
    other = lax.dynamic_index_in_dim(both, 1 - place.core, 1, keepdims=False)
    other = place.swap(other, 1)
    return jnp.concatenate([mine, other], axis=0).reshape(rows.shape)


def from_slots(place, rows):
    parts = rows.reshape(2, 2, rows.shape[0] // 4, rows.shape[1])
    other = place.swap(parts[1], 1)
    near = jnp.stack([parts[0, 0], other[0]])
    far = jnp.stack([parts[0, 1], other[1]])
    far = place.swap(far, 2)
    both = jnp.stack([near, far])
    both = jnp.where(place.x_at == 1, both[::-1], both)
    both = jnp.where(place.core == 1, both[:, ::-1], both)
    return both.reshape(rows.shape)


def store_block(send_ref, keep_ref, spot, value):
    half = send_ref.shape[0]

    @pl.when(spot >= half)
    def _():
        send_ref[spot - half] = value

    @pl.when(spot < half)
    def _():
        keep_ref[spot] = value


def mat(left, right):
    return jnp.dot(left, right, preferred_element_type=jnp.float32)


def load_all(copies):
    for copy in copies:
        copy.start()


def norm_parts(source):
    average = jnp.mean(source, axis=1, keepdims=True)
    centered = source - average
    scale = lax.rsqrt(jnp.mean(centered * centered, axis=1, keepdims=True) + eps)
    return centered * scale, scale


def norm_back(grad, normed, scale, gain):
    scaled = grad * gain
    mean_one = jnp.mean(scaled, axis=1, keepdims=True)
    mean_two = jnp.mean(scaled * normed, axis=1, keepdims=True)
    return scale * (scaled - mean_one - normed * mean_two)


def live_rows(rows, chunk, live):
    spot = lax.broadcasted_iota(jnp.int32, (rows, 1), 0)
    return lax.rem(spot, chunk) < live


def gelu_pair(value):
    tail = jnp.exp(value * value * -0.5)
    step = 1.0 / (1.0 + (0.3275911 * 0.7071067811865476) * jnp.abs(value))
    series = 0.5 * 1.061405429
    for term in (-1.453152027, 1.421413741, -0.284496736, 0.254829592):
        series = series * step + 0.5 * term
    upper = series * step * tail
    share = jnp.where(value >= 0.0, 1.0 - upper, upper)
    return value * share, share + value * tail * 0.3989422804014327


def forward_kernel(
    at_ref,
    row_ref,
    gain1_ref,
    bias1_ref,
    qkv_hbm,
    qv_bias_ref,
    proj_hbm,
    proj_bias_ref,
    gain2_ref,
    bias2_ref,
    up_hbm,
    up_bias_ref,
    norm_t_ref,
    query_t_ref,
    key_t_ref,
    value_ref,
    prob_ref,
    att_t_ref,
    resid_ref,
    second_t_ref,
    act_own_ref,
    act_send_ref,
    slope_ref,
    qkv_ref,
    proj_ref,
    up_ref,
    key_ref,
    value_t_ref,
    sems,
):
    qkv_copy = pltpu.make_async_copy(qkv_hbm, qkv_ref, sems.at[0])
    proj_copy = pltpu.make_async_copy(proj_hbm, proj_ref, sems.at[1])
    up_copy = pltpu.make_async_copy(up_hbm, up_ref, sems.at[2])
    load_all([qkv_copy, proj_copy, up_copy])
    rows, width = row_ref.shape
    live = at_ref[0]
    core = at_ref[1]
    source = row_ref[...].astype(F32)
    normed, _ = norm_parts(source)
    normed = (normed * gain1_ref[...] + bias1_ref[...]).astype(BF)
    norm_t_ref[...] = normed.T
    qkv_copy.wait()
    queries = mat(normed, qkv_ref[:, :width]) + qv_bias_ref[:, :width]
    query_t_ref[...] = (queries * 0.125).astype(BF).T
    keys = mat(normed, qkv_ref[:, width : 2 * width]).astype(BF)
    key_ref[...] = keys
    key_t_ref[...] = keys.T
    values = (mat(normed, qkv_ref[:, 2 * width :]) + qv_bias_ref[:, width:]).astype(BF)
    value_ref[...] = values
    value_t_ref[...] = values.T
    key_mask = jnp.where(live_rows(rows, rows // 4, live), 0.0, neg_big)
    blank = jnp.zeros((HEAD, rows), BF)

    @pl.loop(0, HEADS // 2)
    def _(pair):
        lanes = pl.ds(pl.multiple_of(pair * 2 * HEAD, 2 * HEAD), 2 * HEAD)
        keys_pair = key_ref[:, lanes]
        for side in range(2):
            spots = pl.ds(pl.multiple_of(pair * 2 * HEAD + side * HEAD, HEAD), HEAD)
            query = query_t_ref[spots, :]
            padded = jnp.concatenate([query, blank] if side == 0 else [blank, query], axis=0)
            scores = mat(keys_pair, padded) + key_mask
            top = jnp.max(scores, axis=0, keepdims=True)
            weights = jnp.exp(scores - top)
            total = jnp.sum(weights, axis=0, keepdims=True)
            prob = (weights * (1.0 / total)).astype(BF)
            prob_ref[pair * 2 + side] = prob
            att_t_ref[spots, :] = mat(value_t_ref[spots, :], prob).astype(BF)

    proj_copy.wait()
    residual = source + mat(att_t_ref[...].T, proj_ref[...]) + proj_bias_ref[...]
    resid_ref[...] = residual
    normed, _ = norm_parts(residual)
    normed = (normed * gain2_ref[...] + bias2_ref[...]).astype(BF)
    second_t_ref[...] = normed.T
    up_copy.wait()
    for owner_x in range(2):
        for other in range(2):
            quarter = 2 * owner_x + (core if other == 0 else 1 - core)
            columns = pl.ds(pl.multiple_of(quarter * width, width), width)
            before = mat(normed, up_ref[:, columns]) + up_bias_ref[:, columns]
            act, slope = gelu_pair(before)
            target = act_own_ref if other == 0 else act_send_ref
            target[owner_x] = act.astype(BF)
            slope_ref[quarter] = slope.astype(BF)


def mixed_kernel(
    at_ref, act_own_ref, act_send_ref, resid_ref, down_hbm, down_bias_ref, mixed_ref, down_ref, sems
):
    copies = [
        pltpu.make_async_copy(down_hbm.at[pl.ds(q * 768, 768)], down_ref.at[pl.ds(q * 768, 768)], sems.at[q])
        for q in range(4)
    ]
    load_all(copies)
    rows, width = resid_ref.shape
    live = at_ref[0]
    core = at_ref[1]
    for copy in copies:
        copy.wait()
    total = resid_ref[...] + down_bias_ref[...]
    for owner_x in range(2):
        for other in range(2):
            quarter = 2 * owner_x + (core if other == 0 else 1 - core)
            act = (act_own_ref if other == 0 else act_send_ref)[owner_x]
            spots = pl.ds(pl.multiple_of(quarter * width, width), width)
            total += mat(act, down_ref[spots, :])
    valid = live_rows(rows, rows // 4, live)
    mixed_ref[...] = jnp.where(valid, total, 0.0).astype(BF)


def down_terms_kernel(
    spot_ref, at_ref, cot_own, cot_other, act_own, act_other, send_ref, keep_ref, bias_ref
):
    rows = cot_own.shape[0]
    block = cot_own.shape[1] // GROUPS
    zero = jnp.zeros((), BF)
    own = jnp.where(live_rows(rows, rows // 4, at_ref[0]), cot_own[...], zero)
    other = jnp.where(live_rows(rows, rows // 4, at_ref[2]), cot_other[...], zero)
    bias_ref[...] = jnp.sum(own.astype(F32), axis=0, keepdims=True) + jnp.sum(
        other.astype(F32), axis=0, keepdims=True
    )
    own = own.T
    other = other.T
    for owner_x in range(2):
        for half in range(2):
            span = slice(half * 4 * block, (half + 1) * 4 * block)
            total = mat(own[span], act_own[owner_x]) + mat(other[span], act_other[owner_x])
            total = total.astype(BF)
            for step in range(4):
                store_block(
                    send_ref,
                    keep_ref,
                    spot_ref[owner_x * GROUPS + half * 4 + step],
                    total[step * block : (step + 1) * block],
                )


def hidden_back_kernel(
    at_ref,
    cot_ref,
    slope_ref,
    resid_ref,
    gain2_ref,
    down_hbm,
    up_hbm,
    proj_hbm,
    hidden_ref,
    grad_ref,
    branch_t_ref,
    att_grad_t_ref,
    up_bias_ref,
    gain_ref,
    bias_ref,
    proj_bias_ref,
    down_ref,
    up_ref,
    proj_ref,
    sems,
):
    rows, width = cot_ref.shape
    copies = []
    for q in range(4):
        copies.append(
            (
                pltpu.make_async_copy(
                    down_hbm.at[pl.ds(q * width, width)], down_ref.at[pl.ds(q * width, width)], sems.at[2 * q]
                ),
                pltpu.make_async_copy(
                    up_hbm.at[:, pl.ds(q * width, width)], up_ref.at[:, pl.ds(q * width, width)], sems.at[2 * q + 1]
                ),
            )
        )
    for pair in copies:
        load_all(pair)
    proj_copy = pltpu.make_async_copy(proj_hbm, proj_ref, sems.at[8])
    proj_copy.start()
    valid = live_rows(rows, rows // 4, at_ref[0])
    out_grad = jnp.where(valid, cot_ref[...], jnp.zeros((), BF))
    second = jnp.zeros((rows, width), F32)
    for q in range(4):
        span = slice(q * width, (q + 1) * width)
        copies[q][0].wait()
        hidden = times_trans(out_grad, down_ref[span, :]) * slope_ref[q].astype(F32)
        hidden = hidden.astype(BF)
        hidden_ref[:, span] = hidden
        up_bias_ref[:, span] = jnp.sum(hidden.astype(F32), axis=0, keepdims=True)
        copies[q][1].wait()
        second += times_trans(hidden, up_ref[:, span])
    normed, scale = norm_parts(resid_ref[...])
    gain_ref[...] = jnp.sum(second * normed, axis=0, keepdims=True)
    bias_ref[...] = jnp.sum(second, axis=0, keepdims=True)
    grad = out_grad.astype(F32) + norm_back(second, normed, scale, gain2_ref[...])
    grad_ref[...] = grad
    branch = grad.astype(BF)
    proj_bias_ref[...] = jnp.sum(branch.astype(F32), axis=0, keepdims=True)
    branch_t = branch.T
    branch_t_ref[...] = branch_t
    proj_copy.wait()
    att_grad_t_ref[...] = mat(proj_ref[...], branch_t).astype(BF)


def attention_back_kernel(
    query_t_ref,
    key_t_ref,
    value_ref,
    prob_ref,
    att_grad_t_ref,
    stacked_ref,
):
    rows, width = value_ref.shape
    blank = jnp.zeros((HEAD, rows), BF)

    @pl.loop(0, HEADS // 2)
    def _(pair):
        lanes = pl.ds(pl.multiple_of(pair * 2 * HEAD, 2 * HEAD), 2 * HEAD)
        values_pair = value_ref[:, lanes]
        for side in range(2):
            start = pl.multiple_of(pair * 2 * HEAD + side * HEAD, HEAD)
            spots = pl.ds(start, HEAD)
            grad = att_grad_t_ref[spots, :]
            padded = jnp.concatenate([grad, blank] if side == 0 else [blank, grad], axis=0)
            prob_low = prob_ref[pair * 2 + side]
            prob = prob_low.astype(F32)
            prob_grad = mat(values_pair, padded)
            delta = jnp.sum(prob * prob_grad, axis=0, keepdims=True)
            score_grad = (prob * (prob_grad - delta)).astype(BF)
            query_grad = mat(key_t_ref[spots, :], score_grad).astype(BF)
            stacked_ref[spots, :] = query_grad * jnp.asarray(0.125, BF)
            stacked_ref[pl.ds(start + width, HEAD), :] = times_trans(query_t_ref[spots, :], score_grad).astype(BF)
            stacked_ref[pl.ds(start + 2 * width, HEAD), :] = times_trans(grad, prob_low).astype(BF)


def first_back_kernel(
    row_ref,
    gain1_ref,
    grad_ref,
    stacked_ref,
    qkv_hbm,
    input_ref,
    gain_ref,
    bias_ref,
    qv_bias_ref,
    qkv_ref,
    sems,
):
    qkv_copy = pltpu.make_async_copy(qkv_hbm, qkv_ref, sems.at[0])
    qkv_copy.start()
    rows, width = row_ref.shape
    stacked = stacked_ref[...]
    ones = jnp.ones((8, rows), BF)
    qv_bias_ref[:, :width] = times_trans(ones, stacked[:width])[:1]
    qv_bias_ref[:, width:] = times_trans(ones, stacked[2 * width :])[:1]
    normed, scale = norm_parts(row_ref[...].astype(F32))
    qkv_copy.wait()
    first = mat(qkv_ref[...], stacked).T
    gain_ref[...] = jnp.sum(first * normed, axis=0, keepdims=True)
    bias_ref[...] = jnp.sum(first, axis=0, keepdims=True)
    input_ref[...] = (grad_ref[...] + norm_back(first, normed, scale, gain1_ref[...])).astype(BF)


def up_terms_kernel(spot_ref, at_ref, left_own, left_other, right_own, right_other, send_ref, keep_ref):
    rows = left_own.shape[0] // 4
    width = right_own.shape[1] // GROUPS
    core = at_ref[1]

    def quarter(ref, owner_x):
        return ref[pl.ds(pl.multiple_of((2 * owner_x + core) * rows, rows), rows), :]

    own = jnp.concatenate([quarter(left_own, 0), quarter(left_own, 1)], axis=0)
    other = jnp.concatenate([quarter(left_other, 0), quarter(left_other, 1)], axis=0)
    for group in range(GROUPS):
        columns = slice(group * width, (group + 1) * width)
        total = mat(own, right_own[:, columns]) + mat(other, right_other[:, columns])
        total = total.astype(BF)
        for owner_x in range(2):
            store_block(
                send_ref,
                keep_ref,
                spot_ref[owner_x * GROUPS + group],
                total[owner_x * rows : (owner_x + 1) * rows],
            )


def mix_terms_kernel(
    spot0_ref,
    spot1_ref,
    at_ref,
    norm_own,
    norm_other,
    att_own,
    att_other,
    stacked_own,
    stacked_other,
    branch_own,
    branch_other,
    vec_ref,
    send0_ref,
    keep0_ref,
    send1_ref,
    keep1_ref,
):
    rows = norm_own.shape[0] // 4
    half = rows // 2
    core = at_ref[1]
    qkv_rows = stacked_own.shape[0] // GROUPS
    proj_rows = branch_own.shape[0] // GROUPS
    edge = qkv_rows - qkv_rows % 128

    def quarters(ref):
        return jnp.concatenate(
            [
                ref[pl.ds(pl.multiple_of((2 * owner_x + core) * rows, rows), rows), :]
                for owner_x in range(2)
            ],
            axis=0,
        )

    norm_a, norm_b = quarters(norm_own), quarters(norm_other)
    att_a, att_b = quarters(att_own), quarters(att_other)
    for group in range(GROUPS):
        at = group * qkv_rows
        first = times_trans(norm_a, stacked_own[at : at + qkv_rows])
        first += times_trans(norm_b, stacked_other[at : at + qkv_rows])
        spots = slice(group * proj_rows, (group + 1) * proj_rows)
        second = times_trans(att_a, branch_own[spots]) + times_trans(att_b, branch_other[spots])
        total = jnp.concatenate([first, second], axis=1).astype(BF)
        extra = vec_ref[group].astype(BF)
        for owner_x in range(2):
            base = owner_x * rows
            block = jnp.concatenate([total[base : base + half], extra], axis=0)
            store_block(send0_ref, keep0_ref, spot0_ref[owner_x * GROUPS + group], block)
            store_block(
                send1_ref,
                keep1_ref,
                spot1_ref[owner_x * GROUPS + group],
                total[base + half : base + rows],
            )


S_SPEC = pl.BlockSpec(memory_space=pltpu.SMEM)
V_SPEC = pl.BlockSpec(memory_space=pltpu.VMEM)
H_SPEC = pl.BlockSpec(memory_space=pl.ANY)
PARAMS = pltpu.CompilerParams(vmem_limit_bytes=56 * 1024 * 1024)


def halves(rows, columns):
    shape = jax.ShapeDtypeStruct((GROUPS, rows, columns), BF)
    return [shape, shape]


def shaped(kind, *dims):
    return jax.ShapeDtypeStruct(dims, kind)


def kernel_call(body, specs, operands, outs, flops, scratch=()):
    moved = sum(item.size * item.dtype.itemsize for item in list(operands) + list(outs))
    return pl.pallas_call(
        body,
        out_shape=outs,
        in_specs=[{"s": S_SPEC, "v": V_SPEC, "h": H_SPEC}[kind] for kind in specs],
        out_specs=[V_SPEC] * len(outs),
        scratch_shapes=list(scratch),
        compiler_params=PARAMS,
        cost_estimate=pl.CostEstimate(flops=flops, bytes_accessed=moved, transcendentals=0),
    )(*operands)


def reduce_part(place, order, send, keep):
    for step in range(4):
        got = place.swap_by_core(send, (order[0][step], order[1][step]))
        half = keep.shape[0] // 2
        if step == 3:
            return (keep.astype(F32) + got.astype(F32))[0]
        send = (keep[half:].astype(F32) + got[half:].astype(F32)).astype(BF)
        keep = (keep[:half].astype(F32) + got[:half].astype(F32)).astype(BF)


def within_group(place, block, axis):
    for bit in reversed(range(place.rest_bits)):
        here = (place.wide_at >> bit) & 1
        size = block.shape[axis] // 2
        keep = lax.dynamic_slice_in_dim(block, here * size, size, axis)
        send = lax.dynamic_slice_in_dim(block, (1 - here) * size, size, axis)
        block = keep + place.swap(send, 4 << bit)
    return block


def shards(
    tokens,
    image_size,
    cotangent,
    ln1_gain,
    ln1_bias,
    qkv_weight,
    qv_bias,
    proj_weight,
    proj_bias,
    ln2_gain,
    ln2_bias,
    up_weight,
    up_bias,
    down_weight,
    down_bias,
):
    place = Place()
    row_count, width = tokens.shape
    hidden = up_weight.shape[1]
    slot_rows = row_count // 4
    sizes = jnp.where(image_size[0] == 0, 25, jnp.where(image_size[0] == 1, 49, 64))
    live = lax.dynamic_index_in_dim(sizes.astype(jnp.int32), place.narrow_at, 0, keepdims=False)

    slot_tokens = to_slots(place, tokens)
    slot_cot = to_slots(place, cotangent)

    rows = row_count
    matmul = 2 * rows * width
    live_other = lax.dynamic_index_in_dim(
        sizes.astype(jnp.int32), place.narrow_at ^ 1, 0, keepdims=False
    )
    at = jnp.stack([live, place.core, live_other])
    ln1_gain, ln1_bias, qv_bias = ln1_gain[None], ln1_bias[None], qv_bias[None]
    ln2_gain, ln2_bias, proj_bias = ln2_gain[None], ln2_bias[None], proj_bias[None]
    up_bias, down_bias = up_bias[None], down_bias[None]

    tall = shaped(BF, width, rows)
    flat = shaped(F32, rows, width)
    (
        norm_t,
        query_t,
        key_t,
        values,
        prob,
        att_t,
        residual,
        second_t,
        act_own,
        act_send,
        slope,
    ) = kernel_call(
        forward_kernel,
        "svvvhvhvvvhv",
        [
            at,
            slot_tokens,
            ln1_gain,
            ln1_bias,
            qkv_weight,
            qv_bias,
            proj_weight,
            proj_bias,
            ln2_gain,
            ln2_bias,
            up_weight,
            up_bias,
        ],
        [
            tall,
            tall,
            tall,
            shaped(BF, rows, width),
            shaped(BF, HEADS, rows, rows),
            tall,
            flat,
            tall,
            shaped(BF, 2, rows, hidden // 4),
            shaped(BF, 2, rows, hidden // 4),
            shaped(BF, 4, rows, hidden // 4),
        ],
        matmul * (4 * width + hidden),
        [
            pltpu.VMEM(qkv_weight.shape, BF),
            pltpu.VMEM(proj_weight.shape, BF),
            pltpu.VMEM(up_weight.shape, BF),
            pltpu.VMEM((rows, width), BF),
            pltpu.VMEM((width, rows), BF),
            pltpu.SemaphoreType.DMA((3,)),
        ],
    )
    act_other = place.swap(act_send, 1)
    cot_other = place.swap(slot_cot, 1)
    (mixed,) = kernel_call(
        mixed_kernel,
        "svvvhv",
        [at, act_own, act_send, residual, down_weight, down_bias],
        [shaped(BF, rows, width)],
        matmul * hidden,
        [pltpu.VMEM(down_weight.shape, BF), pltpu.SemaphoreType.DMA((4,))],
    )
    mixed = from_slots(place, mixed)

    down_send, down_keep, down_bias_grad = kernel_call(
        down_terms_kernel,
        "ssvvvv",
        [place.positions(DOWN_ORDER), at, slot_cot, cot_other, act_own, act_other],
        halves(width // GROUPS, hidden // 4) + [shaped(F32, 1, width)],
        matmul * hidden,
    )
    down_block = reduce_part(place, DOWN_ORDER, down_send, down_keep)

    (
        hidden_grad,
        residual_grad,
        branch_t,
        att_grad_t,
        up_bias_grad,
        ln2_gain_grad,
        ln2_bias_grad,
        proj_bias_grad,
    ) = kernel_call(
        hidden_back_kernel,
        "svvvvhhh",
        [at, slot_cot, slope, residual, ln2_gain, down_weight, up_weight, proj_weight],
        [
            shaped(BF, rows, hidden),
            flat,
            tall,
            tall,
            shaped(F32, 1, hidden),
            shaped(F32, 1, width),
            shaped(F32, 1, width),
            shaped(F32, 1, width),
        ],
        matmul * (2 * hidden + width),
        [
            pltpu.VMEM(down_weight.shape, BF),
            pltpu.VMEM(up_weight.shape, BF),
            pltpu.VMEM(proj_weight.shape, BF),
            pltpu.SemaphoreType.DMA((9,)),
        ],
    )
    up_send, up_keep = kernel_call(
        up_terms_kernel,
        "ssvvvv",
        [
            place.positions(UP_ORDER),
            at,
            second_t,
            place.swap(second_t, 1),
            hidden_grad,
            place.swap(hidden_grad, 1),
        ],
        halves(width // 4, hidden // GROUPS),
        matmul * hidden,
    )
    up_block = reduce_part(place, UP_ORDER, up_send, up_keep)

    (stacked,) = kernel_call(
        attention_back_kernel,
        "vvvvv",
        [query_t, key_t, values, prob, att_grad_t],
        [shaped(BF, 3 * width, rows)],
        matmul * rows * 12,
    )
    input_grad, ln1_gain_grad, ln1_bias_grad, qv_bias_grad = kernel_call(
        first_back_kernel,
        "vvvvh",
        [slot_tokens, ln1_gain, residual_grad, stacked, qkv_weight],
        [
            shaped(BF, rows, width),
            shaped(F32, 1, width),
            shaped(F32, 1, width),
            shaped(F32, 1, 2 * width),
        ],
        matmul * 3 * width,
        [pltpu.VMEM(qkv_weight.shape, BF), pltpu.SemaphoreType.DMA((1,))],
    )
    input_grad = from_slots(place, input_grad)

    vectors = [
        up_bias_grad,
        ln1_gain_grad,
        ln1_bias_grad,
        qv_bias_grad,
        proj_bias_grad,
        ln2_gain_grad,
        ln2_bias_grad,
        down_bias_grad * 0.5,
    ]
    packed = jnp.concatenate([item.reshape(GROUPS, -1) for item in vectors], axis=1)
    packed = packed.reshape(GROUPS, -1, hidden // GROUPS)
    packed = packed + place.swap(packed, 1)
    vec_rows = packed.shape[1]
    packed = jnp.pad(packed, ((0, 0), (0, 16 - vec_rows), (0, 0)))

    part_rows = width // 8
    mix = kernel_call(
        mix_terms_kernel,
        "sssvvvvvvvvv",
        [
            place.positions(MIX_ORDERS[0]),
            place.positions(MIX_ORDERS[1]),
            at,
            norm_t,
            place.swap(norm_t, 1),
            att_t,
            place.swap(att_t, 1),
            stacked,
            place.swap(stacked, 1),
            branch_t,
            place.swap(branch_t, 1),
            packed,
        ],
        halves(part_rows + 16, hidden // GROUPS) + halves(part_rows, hidden // GROUPS),
        matmul * hidden,
    )
    first_block = reduce_part(place, MIX_ORDERS[0], mix[0], mix[1])
    last_block = reduce_part(place, MIX_ORDERS[1], mix[2], mix[3])
    mix_block = jnp.concatenate([first_block[:part_rows], last_block], axis=0)
    split = 3 * width // GROUPS
    sums = first_block[part_rows : part_rows + vec_rows].reshape(-1)
    reduced = []
    start = 0
    for item in vectors:
        size = item.size // GROUPS
        reduced.append(within_group(place, sums[start : start + size], 0))
        start += size
    return (
        mixed,
        input_grad,
        reduced[1],
        reduced[2],
        within_group(place, mix_block[:, :split], 1),
        reduced[3],
        within_group(place, mix_block[:, split:], 1),
        reduced[4],
        reduced[5],
        reduced[6],
        within_group(place, up_block, 1),
        reduced[0],
        within_group(place, down_block, 0).T,
        reduced[7],
    )


def solution(mesh):
    rows = P(AXES, None)
    whole = P()
    placed = (rows, P("wide", None), rows) + (whole,) * 12
    vector = P("wide")
    matrix = P("narrow", "wide")
    return jax.shard_map(
        shards,
        mesh=mesh,
        in_specs=placed,
        out_specs=(
            rows,
            rows,
            vector,
            vector,
            matrix,
            vector,
            matrix,
            vector,
            vector,
            vector,
            matrix,
            vector,
            matrix,
            vector,
        ),
        check_vma=False,
    )
```

profile of v0, /device:TPU:0, one launch (start us, length us, event | category | flops | bytes accessed | tf_op | source)
XLA Modules:
  0.0 193.1 jit_solution(10805025569255634406)
XLA Ops:
  0.7 1.1 dynamic-slice_bitcast_fusion.1
  1.8 3.0 %collective-permute-start = (bf16[2,64,768]{2,1,0:T(8,128)(2,1)S(1)}, bf16[2,64,768]{2,1,0:T(8,128)(2,1)S(1)}, u32[]{:S(2)}, u32[]{:S(2)}) collective-permute-start(bf16[2,64,768]{2,1,0:T(8,128)(2,1)S(1)} %get-tuple-element.104), channel_id=1, source_target_pairs={{0,2},{1,3},{2,0},{3,1},{4,6},{5,7},{6,4},{7,5},{8,10},{9,11},{10,... | collective-permute-start | bytes 589832 | tf_op jit(solution)/shard_map/ppermute | solution.py:53
  4.8 1.0 dynamic-slice_bitcast_fusion
  12.5 1.9 pad_add_fusion.at_ref
  15.0 0.8 pad_maximum_fusion
  15.7 16.2 %shard_map.254 = (bf16[768,256]{1,0:T(8,128)(2,1)}, bf16[768,256]{1,0:T(8,128)(2,1)}, bf16[768,256]{1,0:T(8,128)(2,1)}, bf16[256,768]{1,0:T(8,128)(2,1)}, bf16[1...) custom-call(s32[3]{0:T(128)} %pad_add_fusion.at_ref, ...), custom_call_target="tpu_custom_call" | custom-call | flops 2415919104 | bytes 17728524 | tf_op jit(solution)/shard_map/pallas_call | solution.py:507
  32.0 6.1 %shard_map.255 = bf16[256,768]{1,0:T(8,128)(2,1)} custom-call(s32[3]{0:T(128)} %pad_add_fusion.at_ref, bf16[2,256,768]{2,1,0:T(8,128)(2,1)} %get-tuple-element.46.act_own_ref.act_own, bf16[2,256,768]{2,1,0:T(8,128)(2,1)} %get-tuple-element.47.act_send_ref, f32[256,768]{1,0:T(8,128)} %get-tuple-element.48.resid_ref, bf16[3072,768]{1,0:T(8,128)(2,1)} %down_hbm.3, ...), custom_call_target="tpu_custom_call" | custom-call | flops 1207959552 | bytes 7474188 | tf_op jit(solution)/shard_map/pallas_call | solution.py:507
  38.2 0.9 slice.293
  39.7 1.0 slice_bitcast_fusion.4
  41.4 9.8 %shard_map.256 = (bf16[256,3072]{1,0:T(8,128)(2,1)}, f32[256,768]{1,0:T(8,128)}, bf16[768,256]{1,0:T(8,128)(2,1)}, bf16[768,256]{1,0:T(8,128)(2,1)}, f32[1,3072]...) custom-call(s32[3]{0:T(128)} %pad_add_fusion.at_ref, bf16[256,768]{1,0:T(8,128)(2,1)} %bitcast.55, ...), custom_call_target="tpu_custom_call" | custom-call | flops 2717908992 | bytes 16539660 | tf_op jit(solution)/shard_map/pallas_call | solution.py:507
  51.2 7.9 %shard_map.257.stacked_ref.stacked_own = bf16[2304,256]{1,0:T(8,128)(2,1)} custom-call(bf16[768,256]{1,0:T(8,128)(2,1)} %get-tuple-element.51.query_t_ref, bf16[768,256]{1,0:T(8,128)(2,1)} %get-tuple-element.52.key_t_ref, bf16[256,768]{1,0:T(8,128)(2,1)} %get-tuple-element.53.value_ref, bf16[12,256,256]{2,1,0:T(8,128)(2,1)} %get-tuple-element.54.prob_ref, ...), custom_call_target="tpu_custom_call" | custom-call | flops 1207959552 | bytes 4325376 | tf_op jit(solution)/shard_map/pallas_call | solution.py:507
  59.2 5.9 %shard_map.258 = (bf16[256,768]{1,0:T(8,128)(2,1)}, f32[1,768]{1,0:T(1,128)}, f32[1,768]{1,0:T(1,128)}, f32[1,1536]{1,0:T(1,128)}) custom-call(bf16[256,768]{1,0:T(8,128)(2,1)} %bitcast.53, f32[1,768]{1,0:T(1,128)} %broadcast_in_dim.135.gain1_ref, f32[256,768]{1,0:T(8,128)} %get-tuple-element.50.grad_ref, ...), custom_call_target="tpu_custom_call" | custom-call | flops 905969664 | bytes 6306816 | tf_op jit(solution)/shard_map/pallas_call | solution.py:507
  65.1 1.6 slice.226
  71.0 1.0 slice_bitcast_fusion.2
  73.4 2.0 %collective-permute-start.3 = (bf16[2,64,768]{2,1,0:T(8,128)(2,1)}, bf16[2,64,768]{2,1,0:T(8,128)(2,1)S(1)}, u32[]{:S(2)}, u32[]{:S(2)}) collective-permute-start(bf16[2,64,768]{2,1,0:T(8,128)(2,1)} %pad_maximum_fusion.4), channel_id=1, source_target_pairs={{0,2},{1,3},{2,0},{3,1},{4,6},{5,7},{6,4},{7,5},{8,10},{9,11},{10,... | collective-permute-start | bytes 589832 | tf_op jit(solution)/shard_map/ppermute | solution.py:53
  75.6 5.8 %shard_map.259 = (bf16[8,96,768]{2,1,0:T(8,128)(2,1)}, bf16[8,96,768]{2,1,0:T(8,128)(2,1)}, f32[1,768]{1,0:T(1,128)}) custom-call(s32[16]{0:T(128)} %get-tuple-element.121.spot_ref, s32[3]{0:T(128)} %pad_add_fusion.at_ref, bf16[256,768]{1,0:T(8,128)(2,1)} %bitcast.56, bf16[256,768]{1,0:T(8,128)(2,1)} %collective-permute-done.12.cot_other, ...), custom_call_target="tpu_custom_call" | custom-call | flops 1207959552 | bytes 4721740 | tf_op jit(solution)/shard_map/pallas_call | solution.py:507
  82.4 2.6 %collective-permute-done.7 = bf16[2,64,768]{2,1,0:T(8,128)(2,1)S(1)} collective-permute-done((bf16[2,64,768]{2,1,0:T(8,128)(2,1)S(1)}, bf16[2,64,768]{2,1,0:T(8,128)(2,1)S(1)}, u32[]{:S(2)}, u32[]{:S(2)}) %collective-permute-start.7) | collective-permute-done | bytes 196640 | tf_op jit(solution)/shard_map/ppermute | solution.py:53
  87.2 1.7 collective-permute-start.29
  90.1 9.3 %shard_map.260 = (bf16[8,112,384]{2,1,0:T(8,128)(2,1)}, bf16[8,112,384]{2,1,0:T(8,128)(2,1)}, bf16[8,96,384]{2,1,0:T(8,128)(2,1)}, bf16[8,96,384]{2,1,0:T(8,128)(2,1)}) custom-call(s32[16]{0:T(128)} %get-tuple-element.120.spot0_ref, s32[16]{0:T(128)} %get-tuple-element.119.spot1_ref, s32[3]{0:T(128)} %pad_add_fusion.at_ref, ...), custom_call_target="tpu_custom_call" | custom-call | flops 1207959552 | bytes 7471244 | tf_op jit(solution)/shard_map/pallas_call | solution.py:507
  99.7 1.8 collective-permute-start.19
  101.5 0.8 reverse_select_fusion.2
  102.3 0.8 reverse_select_fusion
  103.2 0.8 copy-done.24
  103.9 7.1 %shard_map.261 = (bf16[8,192,384]{2,1,0:T(8,128)(2,1)}, bf16[8,192,384]{2,1,0:T(8,128)(2,1)}) custom-call(s32[16]{0:T(128)} %get-tuple-element.118.spot_ref, s32[3]{0:T(128)} %pad_add_fusion.at_ref, bf16[768,256]{1,0:T(8,128)(2,1)} %get-tuple-element.72.left_own, bf16[768,256]{1,0:T(8,128)(2,1)} %copy-done.24, ...), custom_call_target="tpu_custom_call" | custom-call | flops 1207959552 | bytes 6291532 | tf_op jit(solution)/shard_map/pallas_call | solution.py:507
  111.3 4.9 %collective-permute-done.19 = bf16[8,96,384]{2,1,0:T(8,128)(2,1)S(1)} collective-permute-done((bf16[8,96,384]{2,1,0:T(8,128)(2,1)}, bf16[8,96,384]{2,1,0:T(8,128)(2,1)S(1)}, u32[]{:S(2)}, u32[]{:S(2)}) %collective-permute-start.19) | collective-permute-done | bytes 589856 | tf_op jit(solution)/shard_map/ppermute | solution.py:57
  116.3 3.5 %collective-permute-start.20 = (bf16[4,96,384]{2,1,0:T(8,128)(2,1)S(1)}, bf16[4,96,384]{2,1,0:T(8,128)(2,1)S(1)}, u32[]{:S(2)}, u32[]{:S(2)}) collective-permute-start(bf16[4,96,384]{2,1,0:T(8,128)(2,1)S(1)} %get-tuple-element.89), channel_id=1, source_target_pairs={{0,24},{1,3},{2,26},{3,1},{4,28},{5,7},{6,30},{7,5},{8,16},{9,11},... | collective-permute-start | bytes 884744 | tf_op jit(solution)/shard_map/ppermute | solution.py:57
  119.9 1.8 collective-permute-start.16
  121.7 1.2 add_convert_fusion.1
  123.2 25.2 %collective-permute-done.20 = bf16[4,96,384]{2,1,0:T(8,128)(2,1)S(1)} collective-permute-done((bf16[4,96,384]{2,1,0:T(8,128)(2,1)S(1)}, bf16[4,96,384]{2,1,0:T(8,128)(2,1)S(1)}, u32[]{:S(2)}, u32[]{:S(2)}) %collective-permute-start.20) | collective-permute-done | bytes 294944 | tf_op jit(solution)/shard_map/ppermute | solution.py:57
  148.5 1.5 collective-permute-start.21
  150.2 3.5 %collective-permute-done.21 = bf16[2,96,384]{2,1,0:T(8,128)(2,1)S(1)} collective-permute-done((bf16[2,96,384]{2,1,0:T(8,128)(2,1)S(1)}, bf16[2,96,384]{2,1,0:T(8,128)(2,1)S(1)}, u32[]{:S(2)}, u32[]{:S(2)}) %collective-permute-start.21) | collective-permute-done | bytes 147488 | tf_op jit(solution)/shard_map/ppermute | solution.py:57
  153.7 1.6 collective-permute-start.22
  155.3 0.7 collective-permute-done.17
  156.1 1.9 %collective-permute-start.18 = (bf16[1,112,384]{2,1,0:T(8,128)(2,1)S(1)}, bf16[1,112,384]{2,1,0:T(8,128)(2,1)S(1)}, u32[]{:S(2)}, u32[]{:S(2)}) collective-permute-start(bf16[1,112,384]{2,1,0:T(8,128)(2,1)S(1)} %add_convert_fusion.20), channel_id=1, source_target_pairs={{0,24},{1,3},{2,26},{3,1},{4,28},{5,7},{6,30},{7,5},{8,16},{9,11},... | collective-permute-start | bytes 258056 | tf_op jit(solution)/shard_map/ppermute | solution.py:57
  158.2 4.3 %collective-permute-done.18 = bf16[1,112,384]{2,1,0:T(8,128)(2,1)S(1)} collective-permute-done((bf16[1,112,384]{2,1,0:T(8,128)(2,1)S(1)}, bf16[1,112,384]{2,1,0:T(8,128)(2,1)S(1)}, u32[]{:S(2)}, u32[]{:S(2)}) %collective-permute-start.18) | collective-permute-done | bytes 86048 | tf_op jit(solution)/shard_map/ppermute | solution.py:57
  163.1 0.7 slice_maximum_fusion
  164.2 2.0 %collective-permute-start.26 = (bf16[4,192,384]{2,1,0:T(8,128)(2,1)S(1)}, bf16[4,192,384]{2,1,0:T(8,128)(2,1)S(1)}, u32[]{:S(2)}, u32[]{:S(2)}) collective-permute-start(bf16[4,192,384]{2,1,0:T(8,128)(2,1)S(1)} %get-tuple-element.81), channel_id=1, source_target_pairs={{0,24},{1,9},{2,26},{3,11},{4,28},{5,13},{6,30},{7,15},{8,16},{9,1... | collective-permute-start | bytes 1769480 | tf_op jit(solution)/shard_map/ppermute | solution.py:57
  166.2 0.7 pad_maximum_fusion.6
  167.5 1.2 add_convert_fusion.7
  168.8 10.7 %collective-permute-done.26 = bf16[4,192,384]{2,1,0:T(8,128)(2,1)S(1)} collective-permute-done((bf16[4,192,384]{2,1,0:T(8,128)(2,1)S(1)}, bf16[4,192,384]{2,1,0:T(8,128)(2,1)S(1)}, u32[]{:S(2)}, u32[]{:S(2)}) %collective-permute-start.26) | collective-permute-done | bytes 589856 | tf_op jit(solution)/shard_map/ppermute | solution.py:57
  179.6 1.6 collective-permute-start.27
  182.5 3.4 %collective-permute-start.32 = (bf16[1,96,768]{2,1,0:T(8,128)(2,1)S(1)}, bf16[1,96,768]{2,1,0:T(8,128)(2,1)S(1)}, u32[]{:S(2)}, u32[]{:S(2)}) collective-permute-start(bf16[1,96,768]{2,1,0:T(8,128)(2,1)S(1)} %add_convert_fusion.14), channel_id=1, source_target_pairs={{0,24},{1,9},{2,26},{3,11},{4,28},{5,13},{6,30},{7,15},{8,16},{9,1... | collective-permute-start | bytes 442376 | tf_op jit(solution)/shard_map/ppermute | solution.py:57
  186.0 1.1 collective-permute-done.27
  187.1 1.4 collective-permute-start.28
  188.5 1.0 collective-permute-done.32
  189.5 0.8 add_bitcast_fusion
  190.3 2.0 %collective-permute-done.28 = bf16[1,192,384]{2,1,0:T(8,128)(2,1)S(1)} collective-permute-done((bf16[1,192,384]{2,1,0:T(8,128)(2,1)S(1)}, bf16[1,192,384]{2,1,0:T(8,128)(2,1)S(1)}, u32[]{:S(2)}, u32[]{:S(2)}) %collective-permute-start.28) | collective-permute-done | bytes 147488 | tf_op jit(solution)/shard_map/ppermute | solution.py:57
  192.3 0.8 add_bitcast_fusion.1
  (181 shorter events, 23.4 us)
Async XLA Ops:
  0.7 6.0 %copy-start.14 = (f32[768]{0:T(1024)S(1)}, f32[768]{0:T(1024)}, u32[]{:S(2)}) copy-start(f32[768]{0:T(1024)} %param.19) | copy-start | bytes 9220
  0.7 6.6 %copy-start.12 = (f32[1536]{0:T(1024)S(1)}, f32[1536]{0:T(1024)}, u32[]{:S(2)}) copy-start(f32[1536]{0:T(1024)} %param.21) | copy-start | bytes 18436
  0.7 7.2 %copy-start.15 = (f32[768]{0:T(1024)S(1)}, f32[768]{0:T(1024)}, u32[]{:S(2)}) copy-start(f32[768]{0:T(1024)} %param.23) | copy-start | bytes 9220
  0.7 7.7 %copy-start.16 = (f32[768]{0:T(1024)S(1)}, f32[768]{0:T(1024)}, u32[]{:S(2)}) copy-start(f32[768]{0:T(1024)} %param.24) | copy-start | bytes 9220
  0.7 8.3 %copy-start.17 = (f32[768]{0:T(1024)S(1)}, f32[768]{0:T(1024)}, u32[]{:S(2)}) copy-start(f32[768]{0:T(1024)} %param.25) | copy-start | bytes 9220
  0.7 8.9 %copy-start.18 = (f32[768]{0:T(1024)S(1)}, f32[768]{0:T(1024)}, u32[]{:S(2)}) copy-start(f32[768]{0:T(1024)} %param.29) | copy-start | bytes 9220
  1.8 10.5 %collective-permute-start = (bf16[2,64,768]{2,1,0:T(8,128)(2,1)S(1)}, bf16[2,64,768]{2,1,0:T(8,128)(2,1)S(1)}, u32[]{:S(2)}, u32[]{:S(2)}) collective-permute-start(bf16[2,64,768]{2,1,0:T(8,128)(2,1)S(1)} %get-tuple-element.104), channel_id=1, source_target_pairs={{0,2},{1,3},{2,0},{3,1},{4,6},{5,7},{6,4},{7,5},{8,10},{9,11},{10,... | collective-permute-start | bytes 589832 | tf_op jit(solution)/shard_map/ppermute | solution.py:53
  5.9 8.5 %collective-permute-start.4 = (bf16[2,64,768]{2,1,0:T(8,128)(2,1)S(1)}, bf16[2,64,768]{2,1,0:T(8,128)(2,1)S(1)}, u32[]{:S(2)}, u32[]{:S(2)}) collective-permute-start(bf16[2,64,768]{2,1,0:T(8,128)(2,1)S(1)} %get-tuple-element.98), channel_id=1, source_target_pairs={{0,2},{1,3},{2,0},{3,1},{4,6},{5,7},{6,4},{7,5},{8,10},{9,11},{10,... | collective-permute-start | bytes 589832 | tf_op jit(solution)/shard_map/ppermute | solution.py:53
  12.4 2.6 %collective-permute-start.1 = (bf16[2,64,768]{2,1,0:T(8,128)(2,1)S(1)}, bf16[2,64,768]{2,1,0:T(8,128)(2,1)S(1)}, u32[]{:S(2)}, u32[]{:S(2)}) collective-permute-start(bf16[2,64,768]{2,1,0:T(8,128)(2,1)S(1)} %get-tuple-element.103), channel_id=1, source_target_pairs={{0,1},{1,0},{2,3},{3,2},{4,5},{5,4},{6,7},{7,6},{8,9},{9,8},{10,11... | collective-permute-start | bytes 589832 | tf_op jit(solution)/shard_map/ppermute | solution.py:53
  14.4 26.2 %collective-permute-start.5 = (bf16[2,64,768]{2,1,0:T(8,128)(2,1)S(1)}, bf16[2,64,768]{2,1,0:T(8,128)(2,1)S(1)}, u32[]{:S(2)}, u32[]{:S(2)}) collective-permute-start(bf16[2,64,768]{2,1,0:T(8,128)(2,1)S(1)} %get-tuple-element.97), channel_id=1, source_target_pairs={{0,1},{1,0},{2,3},{3,2},{4,5},{5,4},{6,7},{7,6},{8,9},{9,8},{10,11... | collective-permute-start | bytes 589832 | tf_op jit(solution)/shard_map/ppermute | solution.py:53
  31.9 43.5 %collective-permute-start.13 = (bf16[2,256,768]{2,1,0:T(8,128)(2,1)}, bf16[2,256,768]{2,1,0:T(8,128)(2,1)}, u32[]{:S(2)}, u32[]{:S(2)}) collective-permute-start(bf16[2,256,768]{2,1,0:T(8,128)(2,1)} %get-tuple-element.47.act_send_ref), channel_id=1, source_target_pairs={{0,1},{1,0},{2,3},{3,2},{4,5},{5,4},{6,7},{7,6},{8,9},{9,8},{10,11... | collective-permute-start | bytes 2359304 | tf_op jit(solution)/shard_map/ppermute | solution.py:53
  39.1 32.8 %collective-permute-start.2 = (bf16[2,64,768]{2,1,0:T(8,128)(2,1)S(1)}, bf16[2,64,768]{2,1,0:T(8,128)(2,1)S(1)}, u32[]{:S(2)}, u32[]{:S(2)}) collective-permute-start(bf16[2,64,768]{2,1,0:T(8,128)(2,1)S(1)} %bitcast.63), channel_id=1, source_target_pairs={{0,1},{1,0},{2,3},{3,2},{4,5},{5,4},{6,7},{7,6},{8,9},{9,8},{10,11... | collective-permute-start | bytes 589832 | tf_op jit(solution)/shard_map/ppermute | solution.py:53
  40.7 32.7 %collective-permute-start.12 = (bf16[256,768]{1,0:T(8,128)(2,1)S(1)}, bf16[256,768]{1,0:T(8,128)(2,1)}, u32[]{:S(2)}, u32[]{:S(2)}) collective-permute-start(bf16[256,768]{1,0:T(8,128)(2,1)S(1)} %bitcast.54), channel_id=1, source_target_pairs={{0,1},{1,0},{2,3},{3,2},{4,5},{5,4},{6,7},{7,6},{8,9},{9,8},{10,11... | collective-permute-start | bytes 1179656 | tf_op jit(solution)/shard_map/ppermute | solution.py:53
  59.1 29.8 %collective-permute-start.10 = (bf16[2304,256]{1,0:T(8,128)(2,1)}, bf16[2304,256]{1,0:T(8,128)(2,1)S(1)}, u32[]{:S(2)}, u32[]{:S(2)}) collective-permute-start(bf16[2304,256]{1,0:T(8,128)(2,1)} %shard_map.257.stacked_ref.stacked_own), channel_id=1, source_target_pairs={{0,1},{1,0},{2,3},{3,2},{4,5},{5,4},{6,7},{7,6},{8,9},{9,8},{10,11... | collective-permute-start | bytes 3538952 | tf_op jit(solution)/shard_map/ppermute | solution.py:53
  59.2 8.5 %copy-start.11 = (f32[1,3072]{1,0:T(1,128)S(1)}, f32[1,3072]{1,0:T(1,128)}, u32[]{:S(2)}) copy-start(f32[1,3072]{1,0:T(1,128)} %get-tuple-element.60) | copy-start | bytes 36868
  59.2 11.5 %copy-start.21 = (f32[1,768]{1,0:T(1,128)S(1)}, f32[1,768]{1,0:T(1,128)}, u32[]{:S(2)}) copy-start(f32[1,768]{1,0:T(1,128)} %get-tuple-element.64) | copy-start | bytes 9220
  59.2 11.6 %copy-start.20 = (f32[1,768]{1,0:T(1,128)S(1)}, f32[1,768]{1,0:T(1,128)}, u32[]{:S(2)}) copy-start(f32[1,768]{1,0:T(1,128)} %get-tuple-element.65) | copy-start | bytes 9220
  59.2 11.7 %copy-start.19 = (f32[1,768]{1,0:T(1,128)S(1)}, f32[1,768]{1,0:T(1,128)}, u32[]{:S(2)}) copy-start(f32[1,768]{1,0:T(1,128)} %get-tuple-element.66) | copy-start | bytes 9220
  59.2 12.8 %copy-start.6 = (bf16[768,256]{1,0:T(8,128)(2,1)S(1)}, bf16[768,256]{1,0:T(8,128)(2,1)}, u32[]{:S(2)}) copy-start(bf16[768,256]{1,0:T(8,128)(2,1)} %get-tuple-element.57.norm_own) | copy-start | bytes 1179652
  66.7 5.4 %collective-permute-start.6 = (bf16[2,64,768]{2,1,0:T(8,128)(2,1)}, bf16[2,64,768]{2,1,0:T(8,128)(2,1)S(1)}, u32[]{:S(2)}, u32[]{:S(2)}) collective-permute-start(bf16[2,64,768]{2,1,0:T(8,128)(2,1)} %bitcast.25), channel_id=1, source_target_pairs={{0,1},{1,0},{2,3},{3,2},{4,5},{5,4},{6,7},{7,6},{8,9},{9,8},{10,11... | collective-permute-start | bytes 589832 | tf_op jit(solution)/shard_map/ppermute | solution.py:53
  72.0 14.5 %collective-permute-start.8 = (bf16[768,256]{1,0:T(8,128)(2,1)S(1)}, bf16[768,256]{1,0:T(8,128)(2,1)S(1)}, u32[]{:S(2)}, u32[]{:S(2)}) collective-permute-start(bf16[768,256]{1,0:T(8,128)(2,1)S(1)} %copy-done.6), channel_id=1, source_target_pairs={{0,1},{1,0},{2,3},{3,2},{4,5},{5,4},{6,7},{7,6},{8,9},{9,8},{10,11... | collective-permute-start | bytes 1179656 | tf_op jit(solution)/shard_map/ppermute | solution.py:53
  72.1 31.1 %collective-permute-start.24 = (bf16[256,3072]{1,0:T(8,128)(2,1)}, bf16[256,3072]{1,0:T(8,128)(2,1)}, u32[]{:S(2)}, u32[]{:S(2)}) collective-permute-start(bf16[256,3072]{1,0:T(8,128)(2,1)} %get-tuple-element.73.right_own), channel_id=1, source_target_pairs={{0,1},{1,0},{2,3},{3,2},{4,5},{5,4},{6,7},{7,6},{8,9},{9,8},{10,11... | collective-permute-start | bytes 4718600 | tf_op jit(solution)/shard_map/ppermute | solution.py:53
  73.4 8.8 %collective-permute-start.3 = (bf16[2,64,768]{2,1,0:T(8,128)(2,1)}, bf16[2,64,768]{2,1,0:T(8,128)(2,1)S(1)}, u32[]{:S(2)}, u32[]{:S(2)}) collective-permute-start(bf16[2,64,768]{2,1,0:T(8,128)(2,1)} %pad_maximum_fusion.4), channel_id=1, source_target_pairs={{0,2},{1,3},{2,0},{3,1},{4,6},{5,7},{6,4},{7,5},{8,10},{9,11},{10,... | collective-permute-start | bytes 589832 | tf_op jit(solution)/shard_map/ppermute | solution.py:53
  75.5 9.5 %collective-permute-start.7 = (bf16[2,64,768]{2,1,0:T(8,128)(2,1)S(1)}, bf16[2,64,768]{2,1,0:T(8,128)(2,1)S(1)}, u32[]{:S(2)}, u32[]{:S(2)}) collective-permute-start(bf16[2,64,768]{2,1,0:T(8,128)(2,1)S(1)} %pad_maximum_fusion.5), channel_id=1, source_target_pairs={{0,2},{1,3},{2,0},{3,1},{4,6},{5,7},{6,4},{7,5},{8,10},{9,11},{10,... | collective-permute-start | bytes 589832 | tf_op jit(solution)/shard_map/ppermute | solution.py:53
  75.6 9.4 %copy-start.7 = (bf16[768,256]{1,0:T(8,128)(2,1)S(1)}, bf16[768,256]{1,0:T(8,128)(2,1)}, u32[]{:S(2)}) copy-start(bf16[768,256]{1,0:T(8,128)(2,1)} %get-tuple-element.58.att_own) | copy-start | bytes 1179652
  82.3 2.8 %collective-permute-start.14 = (f32[8,3,384]{2,1,0:T(4,128)S(1)}, f32[8,3,384]{2,1,0:T(4,128)S(1)}, u32[]{:S(2)}, u32[]{:S(2)}) collective-permute-start(f32[8,3,384]{2,1,0:T(4,128)S(1)} %reshape.177), channel_id=1, source_target_pairs={{0,1},{1,0},{2,3},{3,2},{4,5},{5,4},{6,7},{7,6},{8,9},{9,8},{10,11... | collective-permute-start | bytes 110600 | tf_op jit(solution)/shard_map/ppermute | solution.py:53
  85.0 1.7 collective-permute-start.9
  85.0 3.9 %collective-permute-start.11 = (bf16[768,256]{1,0:T(8,128)(2,1)}, bf16[768,256]{1,0:T(8,128)(2,1)S(1)}, u32[]{:S(2)}, u32[]{:S(2)}) collective-permute-start(bf16[768,256]{1,0:T(8,128)(2,1)} %get-tuple-element.59.branch_own), channel_id=1, source_target_pairs={{0,1},{1,0},{2,3},{3,2},{4,5},{5,4},{6,7},{7,6},{8,9},{9,8},{10,11... | collective-permute-start | bytes 1179656 | tf_op jit(solution)/shard_map/ppermute | solution.py:53
  86.6 16.6 %collective-permute-start.23 = (bf16[768,256]{1,0:T(8,128)(2,1)S(1)}, bf16[768,256]{1,0:T(8,128)(2,1)S(1)}, u32[]{:S(2)}, u32[]{:S(2)}) collective-permute-start(bf16[768,256]{1,0:T(8,128)(2,1)S(1)} %copy-done.23), channel_id=1, source_target_pairs={{0,1},{1,0},{2,3},{3,2},{4,5},{5,4},{6,7},{7,6},{8,9},{9,8},{10,11... | collective-permute-start | bytes 1179656 | tf_op jit(solution)/shard_map/ppermute | solution.py:53
  87.2 34.5 %collective-permute-start.29 = (bf16[8,96,768]{2,1,0:T(8,128)(2,1)S(1)}, bf16[8,96,768]{2,1,0:T(8,128)(2,1)S(1)}, u32[]{:S(2)}, u32[]{:S(2)}) collective-permute-start(bf16[8,96,768]{2,1,0:T(8,128)(2,1)S(1)} %copy-done.22), channel_id=1, source_target_pairs={{0,2},{1,5},{2,0},{3,7},{4,6},{5,1},{6,4},{7,3},{8,10},{9,13},{10,... | collective-permute-start | bytes 3538952 | tf_op jit(solution)/shard_map/ppermute | solution.py:57
  99.4 20.3 %collective-permute-start.15 = (bf16[8,112,384]{2,1,0:T(8,128)(2,1)}, bf16[8,112,384]{2,1,0:T(8,128)(2,1)S(1)}, u32[]{:S(2)}, u32[]{:S(2)}) collective-permute-start(bf16[8,112,384]{2,1,0:T(8,128)(2,1)} %get-tuple-element.69), channel_id=1, source_target_pairs={{0,2},{1,5},{2,0},{3,7},{4,6},{5,1},{6,4},{7,3},{8,10},{9,13},{10,... | collective-permute-start | bytes 2064392 | tf_op jit(solution)/shard_map/ppermute | solution.py:57
  99.7 16.4 %collective-permute-start.19 = (bf16[8,96,384]{2,1,0:T(8,128)(2,1)}, bf16[8,96,384]{2,1,0:T(8,128)(2,1)S(1)}, u32[]{:S(2)}, u32[]{:S(2)}) collective-permute-start(bf16[8,96,384]{2,1,0:T(8,128)(2,1)} %get-tuple-element.71), channel_id=1, source_target_pairs={{0,8},{1,25},{2,10},{3,27},{4,12},{5,29},{6,14},{7,31},{8,0},{9,17... | collective-permute-start | bytes 1769480 | tf_op jit(solution)/shard_map/ppermute | solution.py:57
  103.9 12.2 %copy-start.5 = (bf16[8,96,384]{2,1,0:T(8,128)(2,1)S(1)}, bf16[8,96,384]{2,1,0:T(8,128)(2,1)}, u32[]{:S(2)}) copy-start(bf16[8,96,384]{2,1,0:T(8,128)(2,1)} %get-tuple-element.70) | copy-start | bytes 1769476
  111.0 8.7 %copy-start.4 = (bf16[8,112,384]{2,1,0:T(8,128)(2,1)S(1)}, bf16[8,112,384]{2,1,0:T(8,128)(2,1)}, u32[]{:S(2)}) copy-start(bf16[8,112,384]{2,1,0:T(8,128)(2,1)} %get-tuple-element.68) | copy-start | bytes 2064388
  111.0 52.8 %collective-permute-start.25 = (bf16[8,192,384]{2,1,0:T(8,128)(2,1)}, bf16[8,192,384]{2,1,0:T(8,128)(2,1)S(1)}, u32[]{:S(2)}, u32[]{:S(2)}) collective-permute-start(bf16[8,192,384]{2,1,0:T(8,128)(2,1)} %get-tuple-element.75), channel_id=1, source_target_pairs={{0,8},{1,25},{2,10},{3,27},{4,12},{5,29},{6,14},{7,31},{8,0},{9,17... | collective-permute-start | bytes 3538952 | tf_op jit(solution)/shard_map/ppermute | solution.py:57
  116.3 32.1 %collective-permute-start.20 = (bf16[4,96,384]{2,1,0:T(8,128)(2,1)S(1)}, bf16[4,96,384]{2,1,0:T(8,128)(2,1)S(1)}, u32[]{:S(2)}, u32[]{:S(2)}) collective-permute-start(bf16[4,96,384]{2,1,0:T(8,128)(2,1)S(1)} %get-tuple-element.89), channel_id=1, source_target_pairs={{0,24},{1,3},{2,26},{3,1},{4,28},{5,7},{6,30},{7,5},{8,16},{9,11},... | collective-permute-start | bytes 884744 | tf_op jit(solution)/shard_map/ppermute | solution.py:57
  119.9 30.1 %collective-permute-start.16 = (bf16[4,112,384]{2,1,0:T(8,128)(2,1)S(1)}, bf16[4,112,384]{2,1,0:T(8,128)(2,1)S(1)}, u32[]{:S(2)}, u32[]{:S(2)}) collective-permute-start(bf16[4,112,384]{2,1,0:T(8,128)(2,1)S(1)} %get-tuple-element.83), channel_id=1, source_target_pairs={{0,4},{1,9},{2,6},{3,11},{4,0},{5,13},{6,2},{7,15},{8,12},{9,1},{1... | collective-permute-start | bytes 1032200 | tf_op jit(solution)/shard_map/ppermute | solution.py:57
  122.9 44.6 %collective-permute-start.30 = (bf16[4,96,768]{2,1,0:T(8,128)(2,1)}, bf16[4,96,768]{2,1,0:T(8,128)(2,1)}, u32[]{:S(2)}, u32[]{:S(2)}) collective-permute-start(bf16[4,96,768]{2,1,0:T(8,128)(2,1)} %get-tuple-element.79), channel_id=1, source_target_pairs={{0,4},{1,3},{2,6},{3,1},{4,0},{5,7},{6,2},{7,5},{8,12},{9,11},{10,... | collective-permute-start | bytes 1769480 | tf_op jit(solution)/shard_map/ppermute | solution.py:57
  148.5 5.2 %collective-permute-start.21 = (bf16[2,96,384]{2,1,0:T(8,128)(2,1)S(1)}, bf16[2,96,384]{2,1,0:T(8,128)(2,1)S(1)}, u32[]{:S(2)}, u32[]{:S(2)}) collective-permute-start(bf16[2,96,384]{2,1,0:T(8,128)(2,1)S(1)} %get-tuple-element.93), channel_id=1, source_target_pairs={{0,2},{1,5},{2,0},{3,7},{4,6},{5,1},{6,4},{7,3},{8,10},{9,13},{10,... | collective-permute-start | bytes 442376 | tf_op jit(solution)/shard_map/ppermute | solution.py:57
  150.1 13.8 %copy-start.2 = (bf16[8,192,384]{2,1,0:T(8,128)(2,1)S(1)}, bf16[8,192,384]{2,1,0:T(8,128)(2,1)}, u32[]{:S(2)}) copy-start(bf16[8,192,384]{2,1,0:T(8,128)(2,1)} %get-tuple-element.74) | copy-start | bytes 3538948
  150.1 5.9 %collective-permute-start.17 = (bf16[2,112,384]{2,1,0:T(8,128)(2,1)S(1)}, bf16[2,112,384]{2,1,0:T(8,128)(2,1)S(1)}, u32[]{:S(2)}, u32[]{:S(2)}) collective-permute-start(bf16[2,112,384]{2,1,0:T(8,128)(2,1)S(1)} %get-tuple-element.91), channel_id=1, source_target_pairs={{0,8},{1,25},{2,10},{3,27},{4,12},{5,29},{6,14},{7,31},{8,0},{9,17... | collective-permute-start | bytes 516104 | tf_op jit(solution)/shard_map/ppermute | solution.py:57
  153.7 4.4 %collective-permute-start.22 = (bf16[1,96,384]{2,1,0:T(8,128)(2,1)S(1)}, bf16[1,96,384]{2,1,0:T(8,128)(2,1)S(1)}, u32[]{:S(2)}, u32[]{:S(2)}) collective-permute-start(bf16[1,96,384]{2,1,0:T(8,128)(2,1)S(1)} %add_convert_fusion.22), channel_id=1, source_target_pairs={{0,4},{1,9},{2,6},{3,11},{4,0},{5,13},{6,2},{7,15},{8,12},{9,1},{1... | collective-permute-start | bytes 221192 | tf_op jit(solution)/shard_map/ppermute | solution.py:57
  156.1 6.3 %collective-permute-start.18 = (bf16[1,112,384]{2,1,0:T(8,128)(2,1)S(1)}, bf16[1,112,384]{2,1,0:T(8,128)(2,1)S(1)}, u32[]{:S(2)}, u32[]{:S(2)}) collective-permute-start(bf16[1,112,384]{2,1,0:T(8,128)(2,1)S(1)} %add_convert_fusion.20), channel_id=1, source_target_pairs={{0,24},{1,3},{2,26},{3,1},{4,28},{5,7},{6,30},{7,5},{8,16},{9,11},... | collective-permute-start | bytes 258056 | tf_op jit(solution)/shard_map/ppermute | solution.py:57
  164.2 15.3 %collective-permute-start.26 = (bf16[4,192,384]{2,1,0:T(8,128)(2,1)S(1)}, bf16[4,192,384]{2,1,0:T(8,128)(2,1)S(1)}, u32[]{:S(2)}, u32[]{:S(2)}) collective-permute-start(bf16[4,192,384]{2,1,0:T(8,128)(2,1)S(1)} %get-tuple-element.81), channel_id=1, source_target_pairs={{0,24},{1,9},{2,26},{3,11},{4,28},{5,13},{6,30},{7,15},{8,16},{9,1... | collective-permute-start | bytes 1769480 | tf_op jit(solution)/shard_map/ppermute | solution.py:57
  168.7 13.8 %collective-permute-start.31 = (bf16[2,96,768]{2,1,0:T(8,128)(2,1)S(1)}, bf16[2,96,768]{2,1,0:T(8,128)(2,1)S(1)}, u32[]{:S(2)}, u32[]{:S(2)}) collective-permute-start(bf16[2,96,768]{2,1,0:T(8,128)(2,1)S(1)} %get-tuple-element.85), channel_id=1, source_target_pairs={{0,8},{1,25},{2,10},{3,27},{4,12},{5,29},{6,14},{7,31},{8,0},{9,17... | collective-permute-start | bytes 884744 | tf_op jit(solution)/shard_map/ppermute | solution.py:57
  179.6 7.5 %collective-permute-start.27 = (bf16[2,192,384]{2,1,0:T(8,128)(2,1)S(1)}, bf16[2,192,384]{2,1,0:T(8,128)(2,1)S(1)}, u32[]{:S(2)}, u32[]{:S(2)}) collective-permute-start(bf16[2,192,384]{2,1,0:T(8,128)(2,1)S(1)} %get-tuple-element.87), channel_id=1, source_target_pairs={{0,2},{1,5},{2,0},{3,7},{4,6},{5,1},{6,4},{7,3},{8,10},{9,13},{10,... | collective-permute-start | bytes 884744 | tf_op jit(solution)/shard_map/ppermute | solution.py:57
  182.5 7.0 %collective-permute-start.32 = (bf16[1,96,768]{2,1,0:T(8,128)(2,1)S(1)}, bf16[1,96,768]{2,1,0:T(8,128)(2,1)S(1)}, u32[]{:S(2)}, u32[]{:S(2)}) collective-permute-start(bf16[1,96,768]{2,1,0:T(8,128)(2,1)S(1)} %add_convert_fusion.14), channel_id=1, source_target_pairs={{0,24},{1,9},{2,26},{3,11},{4,28},{5,13},{6,30},{7,15},{8,16},{9,1... | collective-permute-start | bytes 442376 | tf_op jit(solution)/shard_map/ppermute | solution.py:57
  187.1 5.2 %collective-permute-start.28 = (bf16[1,192,384]{2,1,0:T(8,128)(2,1)S(1)}, bf16[1,192,384]{2,1,0:T(8,128)(2,1)S(1)}, u32[]{:S(2)}, u32[]{:S(2)}) collective-permute-start(bf16[1,192,384]{2,1,0:T(8,128)(2,1)S(1)} %add_convert_fusion.16), channel_id=1, source_target_pairs={{0,4},{1,3},{2,6},{3,1},{4,0},{5,7},{6,2},{7,5},{8,12},{9,11},{10,... | collective-permute-start | bytes 442376 | tf_op jit(solution)/shard_map/ppermute | solution.py:57
  (11 other events, 24.8 us)
where the time goes:
time: 196 us; the launch traced here: 193 us
  Pallas kernels  68.1 us (35%)
  waiting for transfers between devices  56.9 us (29%)
  starting transfers between devices  31.6 us (16%)
  local copies, waits for them, and re-layouts  19.2 us (10%)
  other arithmetic  15.9 us (8%)
    pallas_call x8, Pallas kernels, kernel_call(): pl.pallas_call(body, out_shape=outs, in_specs=[{'s': S_SPEC, 'v': V_SPEC,...  68.1 us
    ppermute x16, waiting for transfers between devices, swap_by_core(): return lax.ppermute(value, AXES, pairs)  54.2 us
    ppermute x16, starting transfers between devices, swap_by_core(): return lax.ppermute(value, AXES, pairs)  23.2 us
    ppermute x17, starting transfers between devices, swap(): return lax.ppermute(value, AXES, pairs)  8.38 us
  transfers between devices with their start and end apart: 33, of which 13 were waited for; matrix products, arithmetic and copies ran while one was open for 16% of the time, Pallas kernels for 35%

commit v1 on v0

v1 whole, which is shorter than its diff:
```python
import functools

import jax
import jax.numpy as jnp
from jax import lax
from jax.experimental import pallas as pl
from jax.experimental.pallas import tpu as pltpu
from jax.sharding import PartitionSpec as P

HEADS = 12
HEAD = 64
AXES = ("wide", "narrow")
GROUPS = 8
BF = jnp.bfloat16
F32 = jnp.float32
MIB = 1024 * 1024

eps = 1e-06
neg_big = -1e30

ORDER = ((0, 1, 2, 3), (1, 0, 2, 3))


def mat(left, right):
    return jnp.dot(left, right, preferred_element_type=jnp.float32)


def times_trans(left, right):
    return lax.dot_general(
        left, right, (((1,), (1,)), ((), ())), preferred_element_type=jnp.float32
    )


class Place:
    def __init__(self):
        self.wide_n = lax.axis_size("wide")
        self.narrow_n = lax.axis_size("narrow")
        self.rest_bits = (self.wide_n // GROUPS).bit_length() - 1
        self.count = self.wide_n * self.narrow_n
        self.wide_at = lax.axis_index("wide")
        self.narrow_at = lax.axis_index("narrow")
        self.x_at = self.narrow_at >> 1
        self.group = self.wide_at >> self.rest_bits
        shift = 2 + self.rest_bits
        self.masks = (2, 1 << shift, 2 << shift, 4 << shift)

    def swap(self, value, mask):
        pairs = [(index, index ^ mask) for index in range(self.count)]
        return lax.ppermute(value, AXES, pairs)

    def swap_by_core(self, value, links):
        pairs = [(index, index ^ self.masks[links[index & 1]]) for index in range(self.count)]
        return lax.ppermute(value, AXES, pairs)


def core_of(at_ref):
    return at_ref[0] & 1


def live_of(at_ref, slot):
    size = at_ref[2 + slot]
    return jnp.where(size == 0, 25, jnp.where(size == 1, 49, 64))


def spot_of(at_ref, owner_x, owner_group):
    group = at_ref[1]
    here = (at_ref[0] >> 1, group & 1, (group >> 1) & 1, group >> 2)
    there = (owner_x, owner_group & 1, (owner_group >> 1) & 1, owner_group >> 2)
    spots = []
    for links in ORDER:
        spot = 0
        for link in links:
            spot = spot * 2 + (here[link] ^ there[link])
        spots.append(spot)
    return jnp.where(core_of(at_ref) == 0, spots[0], spots[1])


def live_rows(rows, chunk, live):
    spot = lax.broadcasted_iota(jnp.int32, (rows, 1), 0)
    return lax.rem(spot, chunk) < live


def norm_parts(source):
    average = jnp.mean(source, axis=1, keepdims=True)
    centered = source - average
    scale = lax.rsqrt(jnp.mean(centered * centered, axis=1, keepdims=True) + eps)
    return centered * scale, scale


def norm_back(grad, normed, scale, gain):
    scaled = grad * gain
    mean_one = jnp.mean(scaled, axis=1, keepdims=True)
    mean_two = jnp.mean(scaled * normed, axis=1, keepdims=True)
    return scale * (scaled - mean_one - normed * mean_two)


def gelu_pair(value):
    tail = jnp.exp(value * value * -0.5)
    step = 1.0 / (1.0 + (0.3275911 * 0.7071067811865476) * jnp.abs(value))
    series = 0.5 * 1.061405429
    for term in (-1.453152027, 1.421413741, -0.284496736, 0.254829592):
        series = series * step + 0.5 * term
    upper = series * step * tail
    share = jnp.where(value >= 0.0, 1.0 - upper, upper)
    return value * share, share + value * tail * 0.3989422804014327


def slot_copies(refs, core, target_ref, sems, first, partner=False):
    order = (refs[2], refs[3], refs[0], refs[1]) if partner else refs
    which = 1 - core if partner else core
    return [
        pltpu.make_async_copy(ref.at[which], target_ref.at[index], sems.at[first + index])
        for index, ref in enumerate(order)
    ]


def start_all(copies):
    for copy in copies:
        copy.start()


def wait_all(copies):
    for copy in copies:
        copy.wait()


def flat_rows(ref):
    return ref[...].reshape(ref.shape[0] * ref.shape[1], ref.shape[2])


def load_kernel(*refs):
    sems = refs[-1]
    count = (len(refs) - 1) // 2
    copies = [
        pltpu.make_async_copy(refs[index], refs[count + index], sems.at[index])
        for index in range(count)
    ]
    start_all(copies)
    wait_all(copies)


def forward_kernel(
    at_ref,
    near_ref,
    far_ref,
    near_other_ref,
    far_other_ref,
    gain1_hbm,
    bias1_hbm,
    qv_bias_hbm,
    proj_bias_hbm,
    gain2_hbm,
    bias2_hbm,
    up_bias_hbm,
    down_hbm,
    qkv_ref,
    proj_ref,
    up_ref,
    row_ref,
    left_ref,
    query_t_ref,
    key_t_ref,
    value_ref,
    prob_ref,
    resid_ref,
    act_own_ref,
    act_send_ref,
    slope_ref,
    down_ref,
    rows_ref,
    gain1_ref,
    bias1_ref,
    qv_bias_ref,
    proj_bias_ref,
    gain2_ref,
    bias2_ref,
    up_bias_ref,
    key_ref,
    value_t_ref,
    sems,
):
    core = core_of(at_ref)
    row_copies = slot_copies(
        [near_ref, far_ref, near_other_ref, far_other_ref], core, rows_ref, sems, 0
    )
    start_all(row_copies)
    vectors = [
        (gain1_hbm, gain1_ref),
        (bias1_hbm, bias1_ref),
        (qv_bias_hbm, qv_bias_ref),
        (proj_bias_hbm, proj_bias_ref),
        (gain2_hbm, gain2_ref),
        (bias2_hbm, bias2_ref),
        (up_bias_hbm, up_bias_ref),
    ]
    vector_copies = [
        pltpu.make_async_copy(source, target, sems.at[4 + index])
        for index, (source, target) in enumerate(vectors)
    ]
    start_all(vector_copies)
    down_copy = pltpu.make_async_copy(down_hbm, down_ref, sems.at[11])
    down_copy.start()
    rows, width = row_ref.shape
    live = live_of(at_ref, at_ref[0])
    wait_all(row_copies)
    tokens = flat_rows(rows_ref)
    row_ref[...] = tokens
    source = tokens.astype(F32)
    normed, _ = norm_parts(source)
    wait_all(vector_copies)
    normed = (normed * gain1_ref[...][None] + bias1_ref[...][None]).astype(BF)
    left_ref[0] = normed.T
    queries = mat(normed, qkv_ref[:, :width]) + qv_bias_ref[...][None, :width]
    query_t_ref[...] = (queries * 0.125).astype(BF).T
    keys = mat(normed, qkv_ref[:, width : 2 * width]).astype(BF)
    key_ref[...] = keys
    key_t_ref[...] = keys.T
    values = (mat(normed, qkv_ref[:, 2 * width :]) + qv_bias_ref[...][None, width:]).astype(BF)
    value_ref[...] = values
    value_t_ref[...] = values.T
    key_mask = jnp.where(live_rows(rows, rows // 4, live), 0.0, neg_big)
    blank = jnp.zeros((HEAD, rows), BF)

    @pl.loop(0, HEADS // 2)
    def _(pair):
        lanes = pl.ds(pl.multiple_of(pair * 2 * HEAD, 2 * HEAD), 2 * HEAD)
        keys_pair = key_ref[:, lanes]
        for side in range(2):
            spots = pl.ds(pl.multiple_of(pair * 2 * HEAD + side * HEAD, HEAD), HEAD)
            query = query_t_ref[spots, :]
            padded = jnp.concatenate([query, blank] if side == 0 else [blank, query], axis=0)
            scores = mat(keys_pair, padded) + key_mask
            top = jnp.max(scores, axis=0, keepdims=True)
            weights = jnp.exp(scores - top)
            total = jnp.sum(weights, axis=0, keepdims=True)
            prob = (weights * (1.0 / total)).astype(BF)
            prob_ref[pair * 2 + side] = prob
            left_ref[1, spots, :] = mat(value_t_ref[spots, :], prob).astype(BF)

    residual = source + mat(left_ref[1].T, proj_ref[...]) + proj_bias_ref[...][None]
    resid_ref[...] = residual
    normed, _ = norm_parts(residual)
    normed = (normed * gain2_ref[...][None] + bias2_ref[...][None]).astype(BF)
    left_ref[2] = normed.T
    for owner_x in range(2):
        for other in range(2):
            quarter = 2 * owner_x + (core if other == 0 else 1 - core)
            columns = pl.ds(pl.multiple_of(quarter * width, width), width)
            before = mat(normed, up_ref[:, columns]) + up_bias_ref[columns][None]
            act, slope = gelu_pair(before)
            target = act_own_ref if other == 0 else act_send_ref
            target[owner_x] = act.astype(BF)
            slope_ref[quarter] = slope.astype(BF)
    down_copy.wait()


def split_rows(value, keep_ref, send_ref):
    size = keep_ref.shape[1]
    for step in range(2):
        keep_ref[step] = value[step * size : (step + 1) * size]
        send_ref[step] = value[(step + 2) * size : (step + 3) * size]


def mixed_kernel(
    at_ref,
    act_own_ref,
    act_send_ref,
    resid_ref,
    down_ref,
    down_bias_hbm,
    keep_ref,
    send_ref,
    down_bias_ref,
    sems,
):
    bias_copy = pltpu.make_async_copy(down_bias_hbm, down_bias_ref, sems.at[0])
    bias_copy.start()
    rows, width = resid_ref.shape
    core = core_of(at_ref)
    total = resid_ref[...]
    for owner_x in range(2):
        for other in range(2):
            quarter = 2 * owner_x + (core if other == 0 else 1 - core)
            act = (act_own_ref if other == 0 else act_send_ref)[owner_x]
            spots = pl.ds(pl.multiple_of(quarter * width, width), width)
            total += mat(act, down_ref[spots, :])
    bias_copy.wait()
    total += down_bias_ref[...][None]
    valid = live_rows(rows, rows // 4, live_of(at_ref, at_ref[0]))
    split_rows(jnp.where(valid, total, 0.0).astype(BF), keep_ref, send_ref)


def place_kernel(at_ref, keep_ref, got_ref, far_ref, out_ref):
    core, x_at = core_of(at_ref), at_ref[0] >> 1
    size = keep_ref.shape[1]

    def put(slot, value):
        out_ref[pl.ds(pl.multiple_of(slot * size, size), size), :] = value

    put(2 * x_at + core, keep_ref[0])
    put(2 * x_at + 1 - core, got_ref[0])
    put(2 * (1 - x_at) + core, far_ref[0])
    put(2 * (1 - x_at) + 1 - core, far_ref[1])


def hand_over(block_ref, send_ref, keep_ref):
    half = send_ref.shape[0]
    keep_ref[...] = block_ref[:half]
    send_ref[...] = block_ref[half:]


def down_terms_kernel(
    at_ref,
    near_ref,
    far_ref,
    near_other_ref,
    far_other_ref,
    act_own,
    act_other,
    send_ref,
    keep_ref,
    bias_ref,
    block_ref,
    own_ref,
    other_ref,
    sems,
):
    core = core_of(at_ref)
    refs = [near_ref, far_ref, near_other_ref, far_other_ref]
    copies = slot_copies(refs, core, own_ref, sems, 0)
    copies += slot_copies(refs, core, other_ref, sems, 4, partner=True)
    start_all(copies)
    wait_all(copies)
    zero = jnp.zeros((), BF)
    rows = 4 * own_ref.shape[1]
    block = own_ref.shape[2] // GROUPS
    slot = at_ref[0]
    own = jnp.where(live_rows(rows, rows // 4, live_of(at_ref, slot)), flat_rows(own_ref), zero)
    other = jnp.where(
        live_rows(rows, rows // 4, live_of(at_ref, slot ^ 1)), flat_rows(other_ref), zero
    )
    bias_ref[...] = jnp.sum(own.astype(F32), axis=0, keepdims=True)
    both = jnp.concatenate([own.T, other.T], axis=1)
    for owner_x in range(2):
        right = jnp.concatenate([act_own[owner_x], act_other[owner_x]], axis=0)
        for half in range(2):
            span = slice(half * 4 * block, (half + 1) * 4 * block)
            total = mat(both[span], right).astype(BF)
            for step in range(4):
                spot = spot_of(at_ref, owner_x, half * 4 + step)
                block_ref[spot] = total[step * block : (step + 1) * block]
    hand_over(block_ref, send_ref, keep_ref)


def hidden_back_kernel(
    at_ref,
    near_ref,
    far_ref,
    near_other_ref,
    far_other_ref,
    after_ref,
    gain2_hbm,
    slope_ref,
    resid_ref,
    down_ref,
    up_ref,
    proj_ref,
    hidden_ref,
    grad_ref,
    branch_t_ref,
    att_grad_t_ref,
    up_bias_ref,
    gain_ref,
    bias_ref,
    proj_bias_ref,
    cot_ref,
    gain2_ref,
    sems,
):
    copies = slot_copies(
        [near_ref, far_ref, near_other_ref, far_other_ref], core_of(at_ref), cot_ref, sems, 0
    )
    copies.append(pltpu.make_async_copy(gain2_hbm, gain2_ref, sems.at[4]))
    start_all(copies)
    wait_all(copies)
    rows, width = resid_ref.shape
    valid = live_rows(rows, rows // 4, live_of(at_ref, at_ref[0]))
    out_grad = jnp.where(valid, flat_rows(cot_ref), jnp.zeros((), BF))
    second = jnp.zeros((rows, width), F32)
    for q in range(4):
        span = slice(q * width, (q + 1) * width)
        hidden = times_trans(out_grad, down_ref[span, :]) * slope_ref[q].astype(F32)
        hidden = hidden.astype(BF)
        hidden_ref[:, span] = hidden
        up_bias_ref[:, span] = jnp.sum(hidden.astype(F32), axis=0, keepdims=True)
        second += times_trans(hidden, up_ref[:, span])
    normed, scale = norm_parts(resid_ref[...])
    gain_ref[...] = jnp.sum(second * normed, axis=0, keepdims=True)
    bias_ref[...] = jnp.sum(second, axis=0, keepdims=True)
    grad = out_grad.astype(F32) + norm_back(second, normed, scale, gain2_ref[...][None])
    grad_ref[...] = grad
    branch = grad.astype(BF)
    proj_bias_ref[...] = jnp.sum(branch.astype(F32), axis=0, keepdims=True)
    branch_t = branch.T
    branch_t_ref[...] = branch_t
    att_grad_t_ref[...] = mat(proj_ref[...], branch_t).astype(BF)


def attention_back_kernel(
    query_t_ref,
    key_t_ref,
    value_ref,
    prob_ref,
    att_grad_t_ref,
    branch_t_ref,
    right_ref,
):
    rows, width = value_ref.shape
    blank = jnp.zeros((HEAD, rows), BF)
    qkv_rows = 3 * width // GROUPS
    proj_rows = width // GROUPS
    piece = 32
    for group in range(GROUPS):
        right_ref[group, qkv_rows:] = branch_t_ref[group * proj_rows : (group + 1) * proj_rows, :]

    def put(start, value):
        for at in range(0, HEAD, piece):
            row = start + at
            group = row // qkv_rows
            spots = pl.ds(pl.multiple_of(row - group * qkv_rows, piece), piece)
            right_ref[group, spots] = value[at : at + piece]

    @pl.loop(0, HEADS // 2)
    def _(pair):
        lanes = pl.ds(pl.multiple_of(pair * 2 * HEAD, 2 * HEAD), 2 * HEAD)
        values_pair = value_ref[:, lanes]
        for side in range(2):
            start = pl.multiple_of(pair * 2 * HEAD + side * HEAD, HEAD)
            spots = pl.ds(start, HEAD)
            grad = att_grad_t_ref[spots, :]
            padded = jnp.concatenate([grad, blank] if side == 0 else [blank, grad], axis=0)
            prob_low = prob_ref[pair * 2 + side]
            prob = prob_low.astype(F32)
            prob_grad = mat(values_pair, padded)
            delta = jnp.sum(prob * prob_grad, axis=0, keepdims=True)
            score_grad = (prob * (prob_grad - delta)).astype(BF)
            query_grad = mat(key_t_ref[spots, :], score_grad).astype(BF)
            put(start, query_grad * jnp.asarray(0.125, BF))
            put(start + width, times_trans(query_t_ref[spots, :], score_grad).astype(BF))
            put(start + 2 * width, times_trans(grad, prob_low).astype(BF))


def first_back_kernel(
    gain1_hbm,
    row_ref,
    grad_ref,
    right_ref,
    qkv_ref,
    up_bias_ref,
    proj_bias_ref,
    gain2_ref,
    bias2_ref,
    down_bias_ref,
    keep_ref,
    send_ref,
    vec_ref,
    gain1_ref,
    sems,
):
    gain_copy = pltpu.make_async_copy(gain1_hbm, gain1_ref, sems.at[0])
    gain_copy.start()
    rows, width = row_ref.shape
    qkv_rows = 3 * width // GROUPS
    stacked = jnp.concatenate([right_ref[group, :qkv_rows] for group in range(GROUPS)], axis=0)
    ones = jnp.ones((8, rows), BF)
    query_sum = times_trans(ones, stacked[:width])[:1]
    value_sum = times_trans(ones, stacked[2 * width :])[:1]
    normed, scale = norm_parts(row_ref[...].astype(F32))
    first = mat(qkv_ref[...], stacked).T
    gain = jnp.sum(first * normed, axis=0, keepdims=True)
    bias = jnp.sum(first, axis=0, keepdims=True)
    gain_copy.wait()
    total = grad_ref[...] + norm_back(first, normed, scale, gain1_ref[...][None])
    split_rows(total.astype(BF), keep_ref, send_ref)
    share = width // GROUPS
    hidden = up_bias_ref.shape[1] // GROUPS
    qv_sum = jnp.concatenate([query_sum, value_sum], axis=1)
    second = [proj_bias_ref[...], gain2_ref[...], bias2_ref[...], down_bias_ref[...]]
    pad = jnp.zeros((vec_ref.shape[1] - 3, hidden), F32)
    for group in range(GROUPS):
        at = group * share
        vec_ref[group] = jnp.concatenate(
            [
                up_bias_ref[:, group * hidden : (group + 1) * hidden],
                jnp.concatenate(
                    [gain[:, at : at + share], bias[:, at : at + share], qv_sum[:, 2 * at : 2 * (at + share)]],
                    axis=1,
                ),
                jnp.concatenate([item[:, at : at + share] for item in second], axis=1),
                pad,
            ],
            axis=0,
        )


def own_quarters(refs, which, core):
    size = refs[0].shape[1] // 4
    return jnp.concatenate(
        [
            jnp.concatenate(
                [
                    ref[which, pl.ds(pl.multiple_of((2 * owner_x + core) * size, size), size), :]
                    for ref in refs
                ],
                axis=1,
            )
            for owner_x in range(2)
        ],
        axis=0,
    )


def up_terms_kernel(
    at_ref, left_own, left_other, right_own, right_other, send_ref, keep_ref, block_ref
):
    rows = left_own.shape[1] // 4
    width = right_own.shape[1] // GROUPS
    left = own_quarters([left_own, left_other], 2, core_of(at_ref))
    for group in range(GROUPS):
        columns = slice(group * width, (group + 1) * width)
        right = jnp.concatenate([right_own[:, columns], right_other[:, columns]], axis=0)
        total = mat(left, right).astype(BF)
        for owner_x in range(2):
            block_ref[spot_of(at_ref, owner_x, group)] = total[owner_x * rows : (owner_x + 1) * rows]
    hand_over(block_ref, send_ref, keep_ref)


def mix_terms_kernel(
    at_ref,
    left_own,
    left_other,
    right_own,
    right_other,
    vec_own,
    vec_other,
    send0_ref,
    keep0_ref,
    send1_ref,
    keep1_ref,
    block0_ref,
    block1_ref,
):
    rows = left_own.shape[1] // 4
    half = rows // 2
    core = core_of(at_ref)
    columns = right_own.shape[1]
    qkv_rows = 3 * columns // 4
    edge = qkv_rows - qkv_rows % 128
    norm = own_quarters([left_own, left_other], 0, core)
    att = own_quarters([left_own, left_other], 1, core)
    lane = lax.broadcasted_iota(jnp.int32, (2 * rows, columns - edge), 1)
    pad = jnp.zeros((block0_ref.shape[1] - half - vec_own.shape[1], columns), F32)
    for group in range(GROUPS):
        right = jnp.concatenate([right_own[group], right_other[group]], axis=1)
        first = times_trans(norm, right)
        tail = jnp.where(lane < qkv_rows - edge, first[:, edge:], times_trans(att, right[edge:]))
        total = jnp.concatenate([first[:, :edge], tail], axis=1).astype(BF)
        extra = jnp.concatenate([vec_own[group] + vec_other[group], pad], axis=0).astype(BF)
        for owner_x in range(2):
            base = owner_x * rows
            spot = spot_of(at_ref, owner_x, group)
            block0_ref[spot, :half] = total[base : base + half]
            block0_ref[spot, half:] = extra
            block1_ref[spot] = total[base + half : base + rows]
    hand_over(block0_ref, send0_ref, keep0_ref)
    hand_over(block1_ref, send1_ref, keep1_ref)


SPECS = {
    "s": pl.BlockSpec(memory_space=pltpu.SMEM),
    "v": pl.BlockSpec(memory_space=pltpu.VMEM),
    "p": pl.BlockSpec(memory_space=pltpu.VMEM),
    "h": pl.BlockSpec(memory_space=pl.ANY),
}


def shaped(kind, *dims):
    return jax.ShapeDtypeStruct(dims, kind)


def kept(kind, *dims):
    return pltpu.VMEM(dims, kind)


def halves(rows, columns):
    return [kept(BF, GROUPS, rows, columns)] * 2


def sems(count):
    return pltpu.SemaphoreType.DMA((count,))


def kernel_call(body, specs, operands, outs, flops, scratch=(), room=12):
    moved = sum(item.size * item.dtype.itemsize for item in operands)
    operands = [
        pltpu.with_memory_space_constraint(item, pltpu.VMEM) if kind == "p" else item
        for kind, item in zip(specs, operands)
    ]
    return pl.pallas_call(
        body,
        out_shape=outs,
        in_specs=[SPECS[kind] for kind in specs],
        out_specs=[SPECS["v"]] * len(outs),
        scratch_shapes=list(scratch),
        compiler_params=pltpu.CompilerParams(vmem_limit_bytes=room * MIB),
        cost_estimate=pl.CostEstimate(flops=flops, bytes_accessed=moved, transcendentals=0),
    )(*operands)


def to_slots(place, rows):
    parts = rows.reshape(2, 2, rows.shape[0] // 4, rows.shape[1])
    far = lax.dynamic_index_in_dim(parts, 1 - place.x_at, 0, keepdims=False)
    far = place.swap(far, 2)
    near = lax.dynamic_index_in_dim(parts, place.x_at, 0, keepdims=False)
    return [near, far, place.swap(near, 1), place.swap(far, 1)]


def from_slots(place, at, keep, send):
    got = place.swap(send, 1)
    far = place.swap(jnp.stack([keep[1], got[1]]), 2)
    shape = shaped(keep.dtype, 4 * keep.shape[1], keep.shape[2])
    return kernel_call(place_kernel, "svvv", [at, keep, got, far], [shape], 0)[0]


def reduce_part(place, send, keep):
    for step in range(4):
        got = place.swap_by_core(send, (ORDER[0][step], ORDER[1][step]))
        half = keep.shape[0] // 2
        if step == 3:
            return (keep.astype(F32) + got.astype(F32))[0]
        send = (keep[half:].astype(F32) + got[half:].astype(F32)).astype(BF)
        keep = (keep[:half].astype(F32) + got[:half].astype(F32)).astype(BF)


def within_group(place, block, axis):
    for bit in reversed(range(place.rest_bits)):
        here = (place.wide_at >> bit) & 1
        size = block.shape[axis] // 2
        keep = lax.dynamic_slice_in_dim(block, here * size, size, axis)
        send = lax.dynamic_slice_in_dim(block, (1 - here) * size, size, axis)
        block = keep + place.swap(send, 4 << bit)
    return block


def shards(
    tokens,
    image_size,
    cotangent,
    ln1_gain,
    ln1_bias,
    qkv_weight,
    qv_bias,
    proj_weight,
    proj_bias,
    ln2_gain,
    ln2_bias,
    up_weight,
    up_bias,
    down_weight,
    down_bias,
):
    place = Place()
    rows, width = tokens.shape
    hidden = up_weight.shape[1]
    slot_rows = rows // 4
    matmul = 2 * rows * width
    at = jnp.concatenate([jnp.stack([place.narrow_at, place.group]), image_size[0]])

    token_parts = to_slots(place, tokens)
    cot_parts = to_slots(place, cotangent)
    qkv_kept, proj_kept, up_kept = kernel_call(
        load_kernel,
        "hhh",
        [qkv_weight, proj_weight, up_weight],
        [kept(BF, *item.shape) for item in (qkv_weight, proj_weight, up_weight)],
        0,
        [sems(3)],
    )

    tall = kept(BF, width, rows)
    flat = kept(F32, rows, width)
    natural = kept(BF, rows, width)
    vector = kept(F32, 1, width)
    act = kept(BF, 2, rows, hidden // 4)
    chunk = shaped(BF, 2, slot_rows, width)
    four = pltpu.VMEM((4, slot_rows, width), BF)

    def line(size):
        return pltpu.VMEM((size,), F32)

    def blocks(height, columns):
        return pltpu.VMEM((2 * GROUPS, height, columns), BF)

    (
        slot_tokens,
        lefts,
        query_t,
        key_t,
        values,
        prob,
        residual,
        act_own,
        act_send,
        slope,
        down_kept,
    ) = kernel_call(
        forward_kernel,
        "s" + "h" * 12 + "p" * 3,
        [at]
        + token_parts
        + [ln1_gain, ln1_bias, qv_bias, proj_bias, ln2_gain, ln2_bias, up_bias, down_weight]
        + [qkv_kept, proj_kept, up_kept],
        [
            natural,
            kept(BF, 3, width, rows),
            tall,
            tall,
            natural,
            kept(BF, HEADS, rows, rows),
            flat,
            act,
            act,
            kept(BF, 4, rows, hidden // 4),
            kept(BF, *down_weight.shape),
        ],
        matmul * (4 * width + hidden),
        [
            four,
            line(width),
            line(width),
            line(2 * width),
            line(width),
            line(width),
            line(width),
            line(hidden),
            pltpu.VMEM((rows, width), BF),
            pltpu.VMEM((width, rows), BF),
            sems(12),
        ],
        room=16,
    )
    act_other = place.swap(act_send, 1)
    lefts_other = place.swap(lefts, 1)

    mixed_keep, mixed_send = kernel_call(
        mixed_kernel,
        "spppph",
        [at, act_own, act_send, residual, down_kept, down_bias],
        [chunk, chunk],
        matmul * hidden,
        [line(width), sems(1)],
    )
    mixed = from_slots(place, at, mixed_keep, mixed_send)

    down_send, down_keep, down_bias_grad = kernel_call(
        down_terms_kernel,
        "shhhhpp",
        [at] + cot_parts + [act_own, act_other],
        halves(width // GROUPS, hidden // 4) + [vector],
        matmul * hidden,
        [blocks(width // GROUPS, hidden // 4), four, four, sems(8)],
    )
    down_block = reduce_part(place, down_send, down_keep)

    (
        hidden_grad,
        residual_grad,
        branch_t,
        att_grad_t,
        up_bias_grad,
        ln2_gain_grad,
        ln2_bias_grad,
        proj_bias_grad,
    ) = kernel_call(
        hidden_back_kernel,
        "shhhhhhppppp",
        [at]
        + cot_parts
        + [down_bias_grad, ln2_gain, slope, residual, down_kept, up_kept, proj_kept],
        [
            kept(BF, rows, hidden),
            flat,
            tall,
            tall,
            kept(F32, 1, hidden),
            vector,
            vector,
            vector,
        ],
        matmul * (2 * hidden + width),
        [four, line(width), sems(5)],
        room=16,
    )
    hidden_other = place.swap(hidden_grad, 1)
    up_send, up_keep = kernel_call(
        up_terms_kernel,
        "spppp",
        [at, lefts, lefts_other, hidden_grad, hidden_other],
        halves(width // 4, hidden // GROUPS),
        matmul * hidden,
        [blocks(width // 4, hidden // GROUPS)],
    )
    up_block = reduce_part(place, up_send, up_keep)

    (rights,) = kernel_call(
        attention_back_kernel,
        "pppppp",
        [query_t, key_t, values, prob, att_grad_t, branch_t],
        [kept(BF, GROUPS, hidden // GROUPS, rows)],
        matmul * rows * 12,
    )
    rights_other = place.swap(rights, 1)
    input_keep, input_send, packed = kernel_call(
        first_back_kernel,
        "hppppppppp",
        [
            ln1_gain,
            slot_tokens,
            residual_grad,
            rights,
            qkv_kept,
            up_bias_grad,
            proj_bias_grad,
            ln2_gain_grad,
            ln2_bias_grad,
            down_bias_grad,
        ],
        [chunk, chunk, kept(F32, GROUPS, 8, hidden // GROUPS)],
        matmul * 3 * width,
        [line(width), sems(1)],
    )
    packed_other = place.swap(packed, 1)
    input_grad = from_slots(place, at, input_keep, input_send)

    part_rows = width // 8
    columns = hidden // GROUPS
    send0, keep0, send1, keep1 = kernel_call(
        mix_terms_kernel,
        "spppppp",
        [at, lefts, lefts_other, rights, rights_other, packed, packed_other],
        halves(part_rows + 16, columns) + halves(part_rows, columns),
        matmul * hidden,
        [blocks(part_rows + 16, columns), blocks(part_rows, columns)],
    )
    first_block = reduce_part(place, send0, keep0)
    last_block = reduce_part(place, send1, keep1)
    mix_block = jnp.concatenate([first_block[:part_rows], last_block], axis=0)
    split = 3 * width // GROUPS
    sums = first_block[part_rows : part_rows + 3].reshape(-1)
    reduced = []
    start = 0
    share = width // GROUPS
    for size in (columns, share, share, 2 * share, share, share, share, share):
        reduced.append(within_group(place, sums[start : start + size], 0))
        start += size
    return (
        mixed,
        input_grad,
        reduced[1],
        reduced[2],
        within_group(place, mix_block[:, :split], 1),
        reduced[3],
        within_group(place, mix_block[:, split:], 1),
        reduced[4],
        reduced[5],
        reduced[6],
        within_group(place, up_block, 1),
        reduced[0],
        within_group(place, down_block, 0).T,
        reduced[7],
    )


def solution(mesh):
    rows = P(AXES, None)
    whole = P()
    placed = (rows, P("wide", None), rows) + (whole,) * 12
    vector = P("wide")
    matrix = P("narrow", "wide")
    return jax.shard_map(
        shards,
        mesh=mesh,
        in_specs=placed,
        out_specs=(
            rows,
            rows,
            vector,
            vector,
            matrix,
            vector,
            matrix,
            vector,
            vector,
            vector,
            matrix,
            vector,
            matrix,
            vector,
        ),
        check_vma=False,
    )
```

time: 196 us -> 146 us (0.74); the launches traced: 193 us -> 145 us
  Pallas kernels: 68.1 us -> 39.1 us
  other arithmetic: 15.9 us -> 4.71 us
  local copies, waits for them, and re-layouts: 19.2 us -> 9.81 us
  starting transfers between devices: 31.6 us -> 37.8 us
  waiting for transfers between devices: 56.9 us -> 53.1 us
    ppermute x16, waiting for transfers between devices: 54.2 us -> 24.8 us  [swap_by_core(): return lax.ppermute(value, AXES, pairs)]
    pallas_call x8 -> x11, Pallas kernels: 68.1 us -> 39.1 us  [kernel_call(): pl.pallas_call(body, out_shape=outs, in_specs=[SPECS[kind] for kind in sp...]
    ppermute x17 -> x15, waiting for transfers between devices: 2.74 us -> 28.3 us  [swap(): return lax.ppermute(value, AXES, pairs)]
    ppermute x16, starting transfers between devices: 23.2 us -> 29.9 us  [swap_by_core(): return lax.ppermute(value, AXES, pairs)]
    broadcast_in_dim x27 -> x0, local copies, waits for them, and re-layouts: 5.11 us -> none  [the longest x20 0.99 us: positions(): jnp.broadcast_to(o ^ b, (2, GROUPS))]
    unnamed x52 -> x28, local copies, waits for them, and re-layouts: 3.22 us -> 6.85 us
    pallas_call x7 -> x0, other arithmetic: 2.82 us -> none  [kernel_call(): pl.pallas_call(body, out_shape=outs, in_specs=[{'s': S_SPEC, 'v': V_SPEC,...]
    another operation x7 -> x2, other arithmetic: 2.72 us -> 0.04 us  [from_slots(): far = place.swap(jnp.stack([keep[1], got[1]]), 2)]
  transfers between devices with their start and end apart: 33 -> 31, of which waited for: 13 -> 15; matrix products, arithmetic and copies ran while one was open for 16% -> 4% of each run, Pallas kernels for 35% -> 16%
where the time goes in v1:
time: 146 us; the launch traced here: 145 us
  waiting for transfers between devices  53.1 us (36%)
  Pallas kernels  39.1 us (27%)
  starting transfers between devices  37.8 us (26%)
  local copies, waits for them, and re-layouts  9.81 us (7%)
  other arithmetic  4.71 us (3%)
    pallas_call x11, Pallas kernels, kernel_call(): pl.pallas_call(body, out_shape=outs, in_specs=[SPECS[kind] for kind in sp...  39.1 us
    ppermute x16, starting transfers between devices, swap_by_core(): return lax.ppermute(value, AXES, pairs)  29.9 us
    ppermute x15, waiting for transfers between devices, swap(): return lax.ppermute(value, AXES, pairs)  28.3 us
    ppermute x16, waiting for transfers between devices, swap_by_core(): return lax.ppermute(value, AXES, pairs)  24.8 us
    ppermute x15, starting transfers between devices, swap(): return lax.ppermute(value, AXES, pairs)  7.88 us
    unnamed x28, local copies, waits for them, and re-layouts  6.85 us
  transfers between devices with their start and end apart: 31, of which 15 were waited for; matrix products, arithmetic and copies ran while one was open for 4% of the time, Pallas kernels for 16%

profile of v1, /device:TPU:0, one launch (start us, length us, event | category | flops | bytes accessed | tf_op | source)
XLA Modules:
  0.0 145.5 jit_solution(13763378822123610853)
XLA Ops:
  0.6 1.1 dynamic-slice_bitcast_fusion.2
  1.7 3.0 %collective-permute-start = (bf16[2,64,768]{2,1,0:T(8,128)(2,1)S(1)}, bf16[2,64,768]{2,1,0:T(8,128)(2,1)S(1)}, u32[]{:S(2)}, u32[]{:S(2)}) collective-permute-start(bf16[2,64,768]{2,1,0:T(8,128)(2,1)S(1)} %get-tuple-element.104), channel_id=1, source_target_pairs={{0,2},{1,3},{2,0},{3,1},{4,6},{5,7},{6,4},{7,5},{8,10},{9,11},{10,... | collective-permute-start | bytes 589832 | tf_op jit(solution)/shard_map/ppermute | solution.py:49
  4.7 4.9 %collective-permute-done.far_ref = bf16[2,64,768]{2,1,0:T(8,128)(2,1)S(1)} collective-permute-done((bf16[2,64,768]{2,1,0:T(8,128)(2,1)S(1)}, bf16[2,64,768]{2,1,0:T(8,128)(2,1)S(1)}, u32[]{:S(2)}, u32[]{:S(2)}) %collective-permute-start) | collective-permute-done | bytes 196640 | tf_op jit(solution)/shard_map/ppermute | solution.py:49
  9.6 2.3 %copy-done = bf16[768,3072]{1,0:T(8,128)(2,1)S(1)} copy-done((bf16[768,3072]{1,0:T(8,128)(2,1)S(1)}, bf16[768,3072]{1,0:T(8,128)(2,1)}, u32[]{:S(2)}) %copy-start) | copy-done | bytes 4718616
  12.0 2.0 %copy-done.2 = bf16[768,2304]{1,0:T(8,128)(2,1)S(1)} copy-done((bf16[768,2304]{1,0:T(8,128)(2,1)S(1)}, bf16[768,2304]{1,0:T(8,128)(2,1)}, u32[]{:S(2)}) %copy-start.2) | copy-done | bytes 3538968
  14.0 1.3 copy-done.3
  15.3 1.0 shard_map.254
  16.4 1.2 copy-done.1
  17.6 12.2 %shard_map.255 = (bf16[256,768]{1,0:T(8,128)(2,1)S(1)}, bf16[3,768,256]{2,1,0:T(8,128)(2,1)S(1)}, bf16[768,256]{1,0:T(8,128)(2,1)S(1)}, bf16[768,256]{1,0:T(8,12...) custom-call(s32[6]{0:T(128)S(1)} %pad_add_fusion.at_ref, ...), custom_call_target="tpu_custom_call" | custom-call | flops 2415919104 | bytes 14976024 | tf_op jit(solution)/shard_map/pallas_call | solution.py:609
  30.5 1.8 %collective-permute-start.5 = (bf16[2,64,768]{2,1,0:T(8,128)(2,1)S(1)}, bf16[2,64,768]{2,1,0:T(8,128)(2,1)S(1)}, u32[]{:S(2)}, u32[]{:S(2)}) collective-permute-start(bf16[2,64,768]{2,1,0:T(8,128)(2,1)S(1)} %get-tuple-element.102), channel_id=1, source_target_pairs={{0,2},{1,3},{2,0},{3,1},{4,6},{5,7},{6,4},{7,5},{8,10},{9,11},{10,... | collective-permute-start | bytes 589832 | tf_op jit(solution)/shard_map/ppermute | solution.py:49
  32.3 5.1 %collective-permute-done.5.far_ref = bf16[2,64,768]{2,1,0:T(8,128)(2,1)S(1)} collective-permute-done((bf16[2,64,768]{2,1,0:T(8,128)(2,1)S(1)}, bf16[2,64,768]{2,1,0:T(8,128)(2,1)S(1)}, u32[]{:S(2)}, u32[]{:S(2)}) %collective-permute-start.5) | collective-permute-done | bytes 196640 | tf_op jit(solution)/shard_map/ppermute | solution.py:49
  37.4 1.4 collective-permute-done.7.far_other_ref
  38.8 3.3 %shard_map.258 = (bf16[8,96,768]{2,1,0:T(8,128)(2,1)S(1)}, bf16[8,96,768]{2,1,0:T(8,128)(2,1)S(1)}, f32[1,768]{1,0:T(1,128)S(1)}) custom-call(s32[6]{0:T(128)S(1)} %pad_add_fusion.at_ref, bf16[2,64,768]{2,1,0:T(8,128)(2,1)S(1)} %get-tuple-element.103.near_ref, bf16[2,64,768]{2,1,0:T(8,128)(2,1)S(1)} %collective-permute-done.5.far_ref, ...), custom_call_target="tpu_custom_call" | custom-call | flops 1207959552 | bytes 2359320 | tf_op jit(solution)/shard_map/pallas_call | solution.py:609
  42.1 1.8 %collective-permute-start.27 = (bf16[8,96,768]{2,1,0:T(8,128)(2,1)S(1)}, bf16[8,96,768]{2,1,0:T(8,128)(2,1)S(1)}, u32[]{:S(2)}, u32[]{:S(2)}) collective-permute-start(bf16[8,96,768]{2,1,0:T(8,128)(2,1)S(1)} %get-tuple-element.85), channel_id=1, source_target_pairs={{0,2},{1,5},{2,0},{3,7},{4,6},{5,1},{6,4},{7,3},{8,10},{9,13},{10,... | collective-permute-start | bytes 3538952 | tf_op jit(solution)/shard_map/ppermute | solution.py:53
  44.0 5.1 %shard_map.259 = (bf16[256,3072]{1,0:T(8,128)(2,1)S(1)}, f32[256,768]{1,0:T(8,128)S(1)}, bf16[768,256]{1,0:T(8,128)(2,1)S(1)}, bf16[768,256]{1,0:T(8,128)(2,1)S(...) custom-call(s32[6]{0:T(128)S(1)} %pad_add_fusion.at_ref, ...), custom_call_target="tpu_custom_call" | custom-call | flops 2717908992 | bytes 13768728 | tf_op jit(solution)/shard_map/pallas_call | solution.py:609
  49.0 5.1 %shard_map.260.right_ref.right_own = bf16[8,384,256]{2,1,0:T(8,128)(2,1)S(1)} custom-call(bf16[768,256]{1,0:T(8,128)(2,1)S(1)} %get-tuple-element.63.query_t_ref, bf16[768,256]{1,0:T(8,128)(2,1)S(1)} %get-tuple-element.64.key_t_ref, bf16[256,768]{1,0:T(8,128)(2,1)S(1)} %get-tuple-element.65.value_ref, bf16[12,256,256]{2,1,0:T(8,128)(2,1)S(1)} %get-tuple-element.66.prob_ref, ...), custom_call_target="tpu_custom_call" | custom-call | flops 1207959552 | bytes 3538944 | tf_op jit(solution)/shard_map/pallas_call | solution.py:609
  54.8 2.1 %shard_map.256 = (bf16[2,64,768]{2,1,0:T(8,128)(2,1)S(1)}, bf16[2,64,768]{2,1,0:T(8,128)(2,1)S(1)}) custom-call(s32[6]{0:T(128)S(1)} %pad_add_fusion.at_ref, bf16[2,256,768]{2,1,0:T(8,128)(2,1)S(1)} %get-tuple-element.53.act_own_ref.act_own, bf16[2,256,768]{2,1,0:T(8,128)(2,1)S(1)} %get-tuple-element.54.act_send_ref, ...), custom_call_target="tpu_custom_call" | custom-call | flops 1207959552 | bytes 7080984 | tf_op jit(solution)/shard_map/pallas_call | solution.py:609
  57.3 1.8 %shard_map.261 = (bf16[2,64,768]{2,1,0:T(8,128)(2,1)S(1)}, bf16[2,64,768]{2,1,0:T(8,128)(2,1)S(1)}, f32[8,8,384]{2,1,0:T(8,128)S(1)}) custom-call(f32[768]{0:T(1024)S(1)} %copy-done.5, bf16[256,768]{1,0:T(8,128)(2,1)S(1)} %get-tuple-element.59.row_ref, f32[256,768]{1,0:T(8,128)S(1)} %get-tuple-element.62.grad_ref, ...), custom_call_target="tpu_custom_call" | custom-call | flops 905969664 | bytes 6319104 | tf_op jit(solution)/shard_map/pallas_call | solution.py:609
  59.6 2.2 %collective-permute-done.3.got_ref = bf16[2,64,768]{2,1,0:T(8,128)(2,1)S(1)} collective-permute-done((bf16[2,64,768]{2,1,0:T(8,128)(2,1)S(1)}, bf16[2,64,768]{2,1,0:T(8,128)(2,1)S(1)}, u32[]{:S(2)}, u32[]{:S(2)}) %collective-permute-start.3) | collective-permute-done | bytes 196640 | tf_op jit(solution)/shard_map/ppermute | solution.py:49
  61.8 1.5 %collective-permute-start.28 = (bf16[4,96,768]{2,1,0:T(8,128)(2,1)S(1)}, bf16[4,96,768]{2,1,0:T(8,128)(2,1)S(1)}, u32[]{:S(2)}, u32[]{:S(2)}) collective-permute-start(bf16[4,96,768]{2,1,0:T(8,128)(2,1)S(1)} %get-tuple-element.87), channel_id=1, source_target_pairs={{0,4},{1,3},{2,6},{3,1},{4,0},{5,7},{6,2},{7,5},{8,12},{9,11},{10,... | collective-permute-start | bytes 1769480 | tf_op jit(solution)/shard_map/ppermute | solution.py:53
  63.5 1.2 collective-permute-done.13.vec_other
  65.3 3.4 %shard_map.263 = (bf16[8,112,384]{2,1,0:T(8,128)(2,1)S(1)}, bf16[8,112,384]{2,1,0:T(8,128)(2,1)S(1)}, bf16[8,96,384]{2,1,0:T(8,128)(2,1)S(1)}, bf16[8,96,384]{2,1,0:T(8,128)(2,1)S(1)}) custom-call(s32[6]{0:T(128)S(1)} %pad_add_fusion.at_ref, bf16[3,768,256]{2,1,0:T(8,128)(2,1)S(1)} %get-tuple-element.75.left_own, ...), custom_call_target="tpu_custom_call" | custom-call | flops 1207959552 | bytes 5701656 | tf_op jit(solution)/shard_map/pallas_call | solution.py:609
  68.7 1.6 %collective-permute-start.18 = (bf16[8,96,384]{2,1,0:T(8,128)(2,1)S(1)}, bf16[8,96,384]{2,1,0:T(8,128)(2,1)S(1)}, u32[]{:S(2)}, u32[]{:S(2)}) collective-permute-start(bf16[8,96,384]{2,1,0:T(8,128)(2,1)S(1)} %get-tuple-element.80), channel_id=1, source_target_pairs={{0,2},{1,5},{2,0},{3,7},{4,6},{5,1},{6,4},{7,3},{8,10},{9,13},{10,... | collective-permute-start | bytes 1769480 | tf_op jit(solution)/shard_map/ppermute | solution.py:53
  70.8 1.7 %collective-permute-done.4.far_ref = bf16[2,64,768]{2,1,0:T(8,128)(2,1)S(1)} collective-permute-done((bf16[2,64,768]{2,1,0:T(8,128)(2,1)S(1)}, bf16[2,64,768]{2,1,0:T(8,128)(2,1)S(1)}, u32[]{:S(2)}, u32[]{:S(2)}) %collective-permute-start.4) | collective-permute-done | bytes 196640 | tf_op jit(solution)/shard_map/ppermute | solution.py:49
  72.6 1.3 shard_map.257
  73.9 11.7 %collective-permute-done.10.far_ref = bf16[2,64,768]{2,1,0:T(8,128)(2,1)S(1)} collective-permute-done((bf16[2,64,768]{2,1,0:T(8,128)(2,1)S(1)}, bf16[2,64,768]{2,1,0:T(8,128)(2,1)S(1)}, u32[]{:S(2)}, u32[]{:S(2)}) %collective-permute-start.10) | collective-permute-done | bytes 196640 | tf_op jit(solution)/shard_map/ppermute | solution.py:49
  85.6 1.3 shard_map.262
  86.9 1.2 collective-permute-start.14
  88.3 1.6 %collective-permute-start.29 = (bf16[2,96,768]{2,1,0:T(8,128)(2,1)S(1)}, bf16[2,96,768]{2,1,0:T(8,128)(2,1)S(1)}, u32[]{:S(2)}, u32[]{:S(2)}) collective-permute-start(bf16[2,96,768]{2,1,0:T(8,128)(2,1)S(1)} %get-tuple-element.93), channel_id=1, source_target_pairs={{0,8},{1,9},{2,10},{3,11},{4,12},{5,13},{6,14},{7,15},{8,0},{9,1},... | collective-permute-start | bytes 884744 | tf_op jit(solution)/shard_map/ppermute | solution.py:53
  90.0 2.5 %shard_map.264 = (bf16[8,192,384]{2,1,0:T(8,128)(2,1)S(1)}, bf16[8,192,384]{2,1,0:T(8,128)(2,1)S(1)}) custom-call(s32[6]{0:T(128)S(1)} %pad_add_fusion.at_ref, bf16[3,768,256]{2,1,0:T(8,128)(2,1)S(1)} %get-tuple-element.75.left_own, bf16[3,768,256]{2,1,0:T(8,128)(2,1)S(1)} %collective-permute-done.11.left_other, ...), custom_call_target="tpu_custom_call" | custom-call | flops 1207959552 | bytes 5505048 | tf_op jit(solution)/shard_map/pallas_call | solution.py:609
  93.5 1.6 %collective-permute-start.19 = (bf16[4,96,384]{2,1,0:T(8,128)(2,1)S(1)}, bf16[4,96,384]{2,1,0:T(8,128)(2,1)S(1)}, u32[]{:S(2)}, u32[]{:S(2)}) collective-permute-start(bf16[4,96,384]{2,1,0:T(8,128)(2,1)S(1)} %get-tuple-element.97), channel_id=1, source_target_pairs={{0,4},{1,3},{2,6},{3,1},{4,0},{5,7},{6,2},{7,5},{8,12},{9,11},{10,... | collective-permute-start | bytes 884744 | tf_op jit(solution)/shard_map/ppermute | solution.py:53
  95.1 1.2 collective-permute-done.29
  96.4 2.6 %collective-permute-start.30 = (bf16[1,96,768]{2,1,0:T(8,128)(2,1)S(1)}, bf16[1,96,768]{2,1,0:T(8,128)(2,1)S(1)}, u32[]{:S(2)}, u32[]{:S(2)}) collective-permute-start(bf16[1,96,768]{2,1,0:T(8,128)(2,1)S(1)} %add_convert_fusion.14), channel_id=1, source_target_pairs={{0,16},{1,17},{2,18},{3,19},{4,20},{5,21},{6,22},{7,23},{8,24},{9,... | collective-permute-start | bytes 442376 | tf_op jit(solution)/shard_map/ppermute | solution.py:53
  99.0 4.5 %collective-permute-done.14 = bf16[8,112,384]{2,1,0:T(8,128)(2,1)S(1)} collective-permute-done((bf16[8,112,384]{2,1,0:T(8,128)(2,1)S(1)}, bf16[8,112,384]{2,1,0:T(8,128)(2,1)S(1)}, u32[]{:S(2)}, u32[]{:S(2)}) %collective-permute-start.14) | collective-permute-done | bytes 688160 | tf_op jit(solution)/shard_map/ppermute | solution.py:53
  103.7 1.4 collective-permute-start.15
  105.1 2.9 %collective-permute-start.20 = (bf16[2,96,384]{2,1,0:T(8,128)(2,1)S(1)}, bf16[2,96,384]{2,1,0:T(8,128)(2,1)S(1)}, u32[]{:S(2)}, u32[]{:S(2)}) collective-permute-start(bf16[2,96,384]{2,1,0:T(8,128)(2,1)S(1)} %get-tuple-element.101), channel_id=1, source_target_pairs={{0,8},{1,9},{2,10},{3,11},{4,12},{5,13},{6,14},{7,15},{8,0},{9,1},... | collective-permute-start | bytes 442376 | tf_op jit(solution)/shard_map/ppermute | solution.py:53
  108.8 3.9 %collective-permute-done.20 = bf16[2,96,384]{2,1,0:T(8,128)(2,1)S(1)} collective-permute-done((bf16[2,96,384]{2,1,0:T(8,128)(2,1)S(1)}, bf16[2,96,384]{2,1,0:T(8,128)(2,1)S(1)}, u32[]{:S(2)}, u32[]{:S(2)}) %collective-permute-start.20) | collective-permute-done | bytes 147488 | tf_op jit(solution)/shard_map/ppermute | solution.py:53
  112.6 2.2 %collective-permute-start.21 = (bf16[1,96,384]{2,1,0:T(8,128)(2,1)S(1)}, bf16[1,96,384]{2,1,0:T(8,128)(2,1)S(1)}, u32[]{:S(2)}, u32[]{:S(2)}) collective-permute-start(bf16[1,96,384]{2,1,0:T(8,128)(2,1)S(1)} %add_convert_fusion.22), channel_id=1, source_target_pairs={{0,16},{1,17},{2,18},{3,19},{4,20},{5,21},{6,22},{7,23},{8,24},{9,... | collective-permute-start | bytes 221192 | tf_op jit(solution)/shard_map/ppermute | solution.py:53
  115.0 1.0 collective-permute-start.16
  116.0 3.9 %collective-permute-done.23 = bf16[8,192,384]{2,1,0:T(8,128)(2,1)S(1)} collective-permute-done((bf16[8,192,384]{2,1,0:T(8,128)(2,1)S(1)}, bf16[8,192,384]{2,1,0:T(8,128)(2,1)S(1)}, u32[]{:S(2)}, u32[]{:S(2)}) %collective-permute-start.23) | collective-permute-done | bytes 1179680 | tf_op jit(solution)/shard_map/ppermute | solution.py:53
  120.2 0.9 collective-permute-start.24
  121.2 2.7 %collective-permute-start.17 = (bf16[1,112,384]{2,1,0:T(8,128)(2,1)S(1)}, bf16[1,112,384]{2,1,0:T(8,128)(2,1)S(1)}, u32[]{:S(2)}, u32[]{:S(2)}) collective-permute-start(bf16[1,112,384]{2,1,0:T(8,128)(2,1)S(1)} %add_convert_fusion.20), channel_id=1, source_target_pairs={{0,16},{1,17},{2,18},{3,19},{4,20},{5,21},{6,22},{7,23},{8,24},{9,... | collective-permute-start | bytes 258056 | tf_op jit(solution)/shard_map/ppermute | solution.py:53
  123.9 2.8 %collective-permute-done.17 = bf16[1,112,384]{2,1,0:T(8,128)(2,1)S(1)} collective-permute-done((bf16[1,112,384]{2,1,0:T(8,128)(2,1)S(1)}, bf16[1,112,384]{2,1,0:T(8,128)(2,1)S(1)}, u32[]{:S(2)}, u32[]{:S(2)}) %collective-permute-start.17) | collective-permute-done | bytes 86048 | tf_op jit(solution)/shard_map/ppermute | solution.py:53
  126.7 3.4 %collective-permute-done.24 = bf16[4,192,384]{2,1,0:T(8,128)(2,1)S(1)} collective-permute-done((bf16[4,192,384]{2,1,0:T(8,128)(2,1)S(1)}, bf16[4,192,384]{2,1,0:T(8,128)(2,1)S(1)}, u32[]{:S(2)}, u32[]{:S(2)}) %collective-permute-start.24) | collective-permute-done | bytes 589856 | tf_op jit(solution)/shard_map/ppermute | solution.py:53
  130.3 2.9 %collective-permute-start.25 = (bf16[2,192,384]{2,1,0:T(8,128)(2,1)S(1)}, bf16[2,192,384]{2,1,0:T(8,128)(2,1)S(1)}, u32[]{:S(2)}, u32[]{:S(2)}) collective-permute-start(bf16[2,192,384]{2,1,0:T(8,128)(2,1)S(1)} %get-tuple-element.95), channel_id=1, source_target_pairs={{0,8},{1,9},{2,10},{3,11},{4,12},{5,13},{6,14},{7,15},{8,0},{9,1},... | collective-permute-start | bytes 884744 | tf_op jit(solution)/shard_map/ppermute | solution.py:53
  134.5 3.9 %collective-permute-done.25 = bf16[2,192,384]{2,1,0:T(8,128)(2,1)S(1)} collective-permute-done((bf16[2,192,384]{2,1,0:T(8,128)(2,1)S(1)}, bf16[2,192,384]{2,1,0:T(8,128)(2,1)S(1)}, u32[]{:S(2)}, u32[]{:S(2)}) %collective-permute-start.25) | collective-permute-done | bytes 294944 | tf_op jit(solution)/shard_map/ppermute | solution.py:53
  138.5 3.1 %collective-permute-start.26 = (bf16[1,192,384]{2,1,0:T(8,128)(2,1)S(1)}, bf16[1,192,384]{2,1,0:T(8,128)(2,1)S(1)}, u32[]{:S(2)}, u32[]{:S(2)}) collective-permute-start(bf16[1,192,384]{2,1,0:T(8,128)(2,1)S(1)} %add_convert_fusion.16), channel_id=1, source_target_pairs={{0,16},{1,17},{2,18},{3,19},{4,20},{5,21},{6,22},{7,23},{8,24},{9,... | collective-permute-start | bytes 442376 | tf_op jit(solution)/shard_map/ppermute | solution.py:53
  143.5 1.2 collective-permute-done.26
  (86 shorter events, 10.6 us)
Async XLA Ops:
  1.7 7.9 %collective-permute-start = (bf16[2,64,768]{2,1,0:T(8,128)(2,1)S(1)}, bf16[2,64,768]{2,1,0:T(8,128)(2,1)S(1)}, u32[]{:S(2)}, u32[]{:S(2)}) collective-permute-start(bf16[2,64,768]{2,1,0:T(8,128)(2,1)S(1)} %get-tuple-element.104), channel_id=1, source_target_pairs={{0,2},{1,3},{2,0},{3,1},{4,6},{5,7},{6,4},{7,5},{8,10},{9,11},{10,... | collective-permute-start | bytes 589832 | tf_op jit(solution)/shard_map/ppermute | solution.py:49
  4.7 11.7 %collective-permute-start.1 = (bf16[2,64,768]{2,1,0:T(8,128)(2,1)S(1)}, bf16[2,64,768]{2,1,0:T(8,128)(2,1)S(1)}, u32[]{:S(2)}, u32[]{:S(2)}) collective-permute-start(bf16[2,64,768]{2,1,0:T(8,128)(2,1)S(1)} %get-tuple-element.105.near_ref), channel_id=1, source_target_pairs={{0,1},{1,0},{2,3},{3,2},{4,5},{5,4},{6,7},{7,6},{8,9},{9,8},{10,11... | collective-permute-start | bytes 589832 | tf_op jit(solution)/shard_map/ppermute | solution.py:49
  9.6 6.8 %collective-permute-start.2 = (bf16[2,64,768]{2,1,0:T(8,128)(2,1)S(1)}, bf16[2,64,768]{2,1,0:T(8,128)(2,1)S(1)}, u32[]{:S(2)}, u32[]{:S(2)}) collective-permute-start(bf16[2,64,768]{2,1,0:T(8,128)(2,1)S(1)} %collective-permute-done.far_ref), channel_id=1, source_target_pairs={{0,1},{1,0},{2,3},{3,2},{4,5},{5,4},{6,7},{7,6},{8,9},{9,8},{10,11... | collective-permute-start | bytes 589832 | tf_op jit(solution)/shard_map/ppermute | solution.py:49
  9.6 2.3 %copy-start = (bf16[768,3072]{1,0:T(8,128)(2,1)S(1)}, bf16[768,3072]{1,0:T(8,128)(2,1)}, u32[]{:S(2)}) copy-start(bf16[768,3072]{1,0:T(8,128)(2,1)} %refs_2_.1) | copy-start | bytes 14155780
  12.0 2.0 %copy-start.2 = (bf16[768,2304]{1,0:T(8,128)(2,1)S(1)}, bf16[768,2304]{1,0:T(8,128)(2,1)}, u32[]{:S(2)}) copy-start(bf16[768,2304]{1,0:T(8,128)(2,1)} %refs_0_.1) | copy-start | bytes 10616836
  14.0 1.3 copy-start.3
  15.2 1.1 copy-start.13
  15.2 2.4 %copy-start.1 = (bf16[3072,768]{1,0:T(8,128)(2,1)S(1)}, bf16[3072,768]{1,0:T(8,128)(2,1)}, u32[]{:S(2)}) copy-start(bf16[3072,768]{1,0:T(8,128)(2,1)} %down_hbm.1) | copy-start | bytes 14155780
  15.2 2.4 %copy-start.4 = (f32[768]{0:T(1024)S(1)}, f32[768]{0:T(1024)}, u32[]{:S(2)}) copy-start(f32[768]{0:T(1024)} %gain2_hbm.3) | copy-start | bytes 9220
  15.2 2.4 %copy-start.5 = (f32[768]{0:T(1024)S(1)}, f32[768]{0:T(1024)}, u32[]{:S(2)}) copy-start(f32[768]{0:T(1024)} %gain1_hbm.3) | copy-start | bytes 9220
  15.2 2.3 %copy-start.6 = (f32[3072]{0:T(1024)S(1)}, f32[3072]{0:T(1024)}, u32[]{:S(2)}) copy-start(f32[3072]{0:T(1024)} %up_bias_hbm.1) | copy-start | bytes 36868
  15.3 2.3 %copy-start.7 = (f32[1536]{0:T(1024)S(1)}, f32[1536]{0:T(1024)}, u32[]{:S(2)}) copy-start(f32[1536]{0:T(1024)} %qv_bias_hbm.1) | copy-start | bytes 18436
  15.3 2.3 %copy-start.9 = (f32[768]{0:T(1024)S(1)}, f32[768]{0:T(1024)}, u32[]{:S(2)}) copy-start(f32[768]{0:T(1024)} %bias1_hbm.1) | copy-start | bytes 9220
  15.3 2.3 %copy-start.10 = (f32[768]{0:T(1024)S(1)}, f32[768]{0:T(1024)}, u32[]{:S(2)}) copy-start(f32[768]{0:T(1024)} %proj_bias_hbm.1) | copy-start | bytes 9220
  15.3 2.3 %copy-start.11 = (f32[768]{0:T(1024)S(1)}, f32[768]{0:T(1024)}, u32[]{:S(2)}) copy-start(f32[768]{0:T(1024)} %bias2_hbm.1) | copy-start | bytes 9220
  17.6 12.8 %copy-start.12 = (bf16[256,768]{1,0:T(8,128)(2,1)S(1)}, bf16[256,768]{1,0:T(8,128)(2,1)}, u32[]{:S(2)}) copy-start(bf16[256,768]{1,0:T(8,128)(2,1)} %param.17) | copy-start | bytes 1179652
  29.9 9.0 %collective-permute-start.8 = (bf16[2,256,768]{2,1,0:T(8,128)(2,1)S(1)}, bf16[2,256,768]{2,1,0:T(8,128)(2,1)S(1)}, u32[]{:S(2)}, u32[]{:S(2)}) collective-permute-start(bf16[2,256,768]{2,1,0:T(8,128)(2,1)S(1)} %get-tuple-element.54.act_send_ref), channel_id=1, source_target_pairs={{0,1},{1,0},{2,3},{3,2},{4,5},{5,4},{6,7},{7,6},{8,9},{9,8},{10,11... | collective-permute-start | bytes 2359304 | tf_op jit(solution)/shard_map/ppermute | solution.py:49
  30.5 6.9 %collective-permute-start.5 = (bf16[2,64,768]{2,1,0:T(8,128)(2,1)S(1)}, bf16[2,64,768]{2,1,0:T(8,128)(2,1)S(1)}, u32[]{:S(2)}, u32[]{:S(2)}) collective-permute-start(bf16[2,64,768]{2,1,0:T(8,128)(2,1)S(1)} %get-tuple-element.102), channel_id=1, source_target_pairs={{0,2},{1,3},{2,0},{3,1},{4,6},{5,7},{6,4},{7,5},{8,10},{9,11},{10,... | collective-permute-start | bytes 589832 | tf_op jit(solution)/shard_map/ppermute | solution.py:49
  32.3 5.1 %collective-permute-start.6 = (bf16[2,64,768]{2,1,0:T(8,128)(2,1)S(1)}, bf16[2,64,768]{2,1,0:T(8,128)(2,1)S(1)}, u32[]{:S(2)}, u32[]{:S(2)}) collective-permute-start(bf16[2,64,768]{2,1,0:T(8,128)(2,1)S(1)} %get-tuple-element.103.near_ref), channel_id=1, source_target_pairs={{0,1},{1,0},{2,3},{3,2},{4,5},{5,4},{6,7},{7,6},{8,9},{9,8},{10,11... | collective-permute-start | bytes 589832 | tf_op jit(solution)/shard_map/ppermute | solution.py:49
  37.4 1.4 collective-permute-start.7
  42.1 17.0 %collective-permute-start.27 = (bf16[8,96,768]{2,1,0:T(8,128)(2,1)S(1)}, bf16[8,96,768]{2,1,0:T(8,128)(2,1)S(1)}, u32[]{:S(2)}, u32[]{:S(2)}) collective-permute-start(bf16[8,96,768]{2,1,0:T(8,128)(2,1)S(1)} %get-tuple-element.85), channel_id=1, source_target_pairs={{0,2},{1,5},{2,0},{3,7},{4,6},{5,1},{6,4},{7,3},{8,10},{9,13},{10,... | collective-permute-start | bytes 3538952 | tf_op jit(solution)/shard_map/ppermute | solution.py:53
  49.0 5.7 %copy-start.8 = (f32[768]{0:T(1024)S(1)}, f32[768]{0:T(1024)}, u32[]{:S(2)}) copy-start(f32[768]{0:T(1024)} %down_bias_hbm.1) | copy-start | bytes 9220
  54.1 11.2 %collective-permute-start.12 = (bf16[8,384,256]{2,1,0:T(8,128)(2,1)S(1)}, bf16[8,384,256]{2,1,0:T(8,128)(2,1)S(1)}, u32[]{:S(2)}, u32[]{:S(2)}) collective-permute-start(bf16[8,384,256]{2,1,0:T(8,128)(2,1)S(1)} %shard_map.260.right_ref.right_own), channel_id=1, source_target_pairs={{0,1},{1,0},{2,3},{3,2},{4,5},{5,4},{6,7},{7,6},{8,9},{9,8},{10,11... | collective-permute-start | bytes 4718600 | tf_op jit(solution)/shard_map/ppermute | solution.py:49
  54.2 11.1 %collective-permute-start.11 = (bf16[3,768,256]{2,1,0:T(8,128)(2,1)S(1)}, bf16[3,768,256]{2,1,0:T(8,128)(2,1)S(1)}, u32[]{:S(2)}, u32[]{:S(2)}) collective-permute-start(bf16[3,768,256]{2,1,0:T(8,128)(2,1)S(1)} %get-tuple-element.75.left_own), channel_id=1, source_target_pairs={{0,1},{1,0},{2,3},{3,2},{4,5},{5,4},{6,7},{7,6},{8,9},{9,8},{10,11... | collective-permute-start | bytes 3538952 | tf_op jit(solution)/shard_map/ppermute | solution.py:49
  54.7 35.3 %collective-permute-start.22 = (bf16[256,3072]{1,0:T(8,128)(2,1)S(1)}, bf16[256,3072]{1,0:T(8,128)(2,1)S(1)}, u32[]{:S(2)}, u32[]{:S(2)}) collective-permute-start(bf16[256,3072]{1,0:T(8,128)(2,1)S(1)} %get-tuple-element.81.right_own), channel_id=1, source_target_pairs={{0,1},{1,0},{2,3},{3,2},{4,5},{5,4},{6,7},{7,6},{8,9},{9,8},{10,11... | collective-permute-start | bytes 4718600 | tf_op jit(solution)/shard_map/ppermute | solution.py:49
  56.8 5.0 %collective-permute-start.3 = (bf16[2,64,768]{2,1,0:T(8,128)(2,1)S(1)}, bf16[2,64,768]{2,1,0:T(8,128)(2,1)S(1)}, u32[]{:S(2)}, u32[]{:S(2)}) collective-permute-start(bf16[2,64,768]{2,1,0:T(8,128)(2,1)S(1)} %get-tuple-element.58), channel_id=1, source_target_pairs={{0,1},{1,0},{2,3},{3,2},{4,5},{5,4},{6,7},{7,6},{8,9},{9,8},{10,11... | collective-permute-start | bytes 589832 | tf_op jit(solution)/shard_map/ppermute | solution.py:49
  59.2 4.2 %collective-permute-start.9 = (bf16[2,64,768]{2,1,0:T(8,128)(2,1)S(1)}, bf16[2,64,768]{2,1,0:T(8,128)(2,1)S(1)}, u32[]{:S(2)}, u32[]{:S(2)}) collective-permute-start(bf16[2,64,768]{2,1,0:T(8,128)(2,1)S(1)} %get-tuple-element.74), channel_id=1, source_target_pairs={{0,1},{1,0},{2,3},{3,2},{4,5},{5,4},{6,7},{7,6},{8,9},{9,8},{10,11... | collective-permute-start | bytes 589832 | tf_op jit(solution)/shard_map/ppermute | solution.py:49
  61.8 26.4 %collective-permute-start.28 = (bf16[4,96,768]{2,1,0:T(8,128)(2,1)S(1)}, bf16[4,96,768]{2,1,0:T(8,128)(2,1)S(1)}, u32[]{:S(2)}, u32[]{:S(2)}) collective-permute-start(bf16[4,96,768]{2,1,0:T(8,128)(2,1)S(1)} %get-tuple-element.87), channel_id=1, source_target_pairs={{0,4},{1,3},{2,6},{3,1},{4,0},{5,7},{6,2},{7,5},{8,12},{9,11},{10,... | collective-permute-start | bytes 1769480 | tf_op jit(solution)/shard_map/ppermute | solution.py:53
  63.4 1.4 collective-permute-start.13
  64.7 7.8 %collective-permute-start.4 = (bf16[2,64,768]{2,1,0:T(8,128)(2,1)S(1)}, bf16[2,64,768]{2,1,0:T(8,128)(2,1)S(1)}, u32[]{:S(2)}, u32[]{:S(2)}) collective-permute-start(bf16[2,64,768]{2,1,0:T(8,128)(2,1)S(1)} %pad_maximum_fusion), channel_id=1, source_target_pairs={{0,2},{1,3},{2,0},{3,1},{4,6},{5,7},{6,4},{7,5},{8,10},{9,11},{10,... | collective-permute-start | bytes 589832 | tf_op jit(solution)/shard_map/ppermute | solution.py:49
  68.7 24.7 %collective-permute-start.18 = (bf16[8,96,384]{2,1,0:T(8,128)(2,1)S(1)}, bf16[8,96,384]{2,1,0:T(8,128)(2,1)S(1)}, u32[]{:S(2)}, u32[]{:S(2)}) collective-permute-start(bf16[8,96,384]{2,1,0:T(8,128)(2,1)S(1)} %get-tuple-element.80), channel_id=1, source_target_pairs={{0,2},{1,5},{2,0},{3,7},{4,6},{5,1},{6,4},{7,3},{8,10},{9,13},{10,... | collective-permute-start | bytes 1769480 | tf_op jit(solution)/shard_map/ppermute | solution.py:53
  70.2 15.4 %collective-permute-start.10 = (bf16[2,64,768]{2,1,0:T(8,128)(2,1)S(1)}, bf16[2,64,768]{2,1,0:T(8,128)(2,1)S(1)}, u32[]{:S(2)}, u32[]{:S(2)}) collective-permute-start(bf16[2,64,768]{2,1,0:T(8,128)(2,1)S(1)} %pad_maximum_fusion.1), channel_id=1, source_target_pairs={{0,2},{1,3},{2,0},{3,1},{4,6},{5,7},{6,4},{7,5},{8,10},{9,11},{10,... | collective-permute-start | bytes 589832 | tf_op jit(solution)/shard_map/ppermute | solution.py:49
  86.9 16.6 %collective-permute-start.14 = (bf16[8,112,384]{2,1,0:T(8,128)(2,1)S(1)}, bf16[8,112,384]{2,1,0:T(8,128)(2,1)S(1)}, u32[]{:S(2)}, u32[]{:S(2)}) collective-permute-start(bf16[8,112,384]{2,1,0:T(8,128)(2,1)S(1)} %get-tuple-element.78), channel_id=1, source_target_pairs={{0,2},{1,5},{2,0},{3,7},{4,6},{5,1},{6,4},{7,3},{8,10},{9,13},{10,... | collective-permute-start | bytes 2064392 | tf_op jit(solution)/shard_map/ppermute | solution.py:53
  88.3 8.0 %collective-permute-start.29 = (bf16[2,96,768]{2,1,0:T(8,128)(2,1)S(1)}, bf16[2,96,768]{2,1,0:T(8,128)(2,1)S(1)}, u32[]{:S(2)}, u32[]{:S(2)}) collective-permute-start(bf16[2,96,768]{2,1,0:T(8,128)(2,1)S(1)} %get-tuple-element.93), channel_id=1, source_target_pairs={{0,8},{1,9},{2,10},{3,11},{4,12},{5,13},{6,14},{7,15},{8,0},{9,1},... | collective-permute-start | bytes 884744 | tf_op jit(solution)/shard_map/ppermute | solution.py:53
  92.5 27.4 %collective-permute-start.23 = (bf16[8,192,384]{2,1,0:T(8,128)(2,1)S(1)}, bf16[8,192,384]{2,1,0:T(8,128)(2,1)S(1)}, u32[]{:S(2)}, u32[]{:S(2)}) collective-permute-start(bf16[8,192,384]{2,1,0:T(8,128)(2,1)S(1)} %get-tuple-element.83), channel_id=1, source_target_pairs={{0,2},{1,5},{2,0},{3,7},{4,6},{5,1},{6,4},{7,3},{8,10},{9,13},{10,... | collective-permute-start | bytes 3538952 | tf_op jit(solution)/shard_map/ppermute | solution.py:53
  93.5 11.5 %collective-permute-start.19 = (bf16[4,96,384]{2,1,0:T(8,128)(2,1)S(1)}, bf16[4,96,384]{2,1,0:T(8,128)(2,1)S(1)}, u32[]{:S(2)}, u32[]{:S(2)}) collective-permute-start(bf16[4,96,384]{2,1,0:T(8,128)(2,1)S(1)} %get-tuple-element.97), channel_id=1, source_target_pairs={{0,4},{1,3},{2,6},{3,1},{4,0},{5,7},{6,2},{7,5},{8,12},{9,11},{10,... | collective-permute-start | bytes 884744 | tf_op jit(solution)/shard_map/ppermute | solution.py:53
  96.4 11.6 %collective-permute-start.30 = (bf16[1,96,768]{2,1,0:T(8,128)(2,1)S(1)}, bf16[1,96,768]{2,1,0:T(8,128)(2,1)S(1)}, u32[]{:S(2)}, u32[]{:S(2)}) collective-permute-start(bf16[1,96,768]{2,1,0:T(8,128)(2,1)S(1)} %add_convert_fusion.14), channel_id=1, source_target_pairs={{0,16},{1,17},{2,18},{3,19},{4,20},{5,21},{6,22},{7,23},{8,24},{9,... | collective-permute-start | bytes 442376 | tf_op jit(solution)/shard_map/ppermute | solution.py:53
  103.7 11.2 %collective-permute-start.15 = (bf16[4,112,384]{2,1,0:T(8,128)(2,1)S(1)}, bf16[4,112,384]{2,1,0:T(8,128)(2,1)S(1)}, u32[]{:S(2)}, u32[]{:S(2)}) collective-permute-start(bf16[4,112,384]{2,1,0:T(8,128)(2,1)S(1)} %get-tuple-element.91), channel_id=1, source_target_pairs={{0,4},{1,3},{2,6},{3,1},{4,0},{5,7},{6,2},{7,5},{8,12},{9,11},{10,... | collective-permute-start | bytes 1032200 | tf_op jit(solution)/shard_map/ppermute | solution.py:53
  105.1 7.5 %collective-permute-start.20 = (bf16[2,96,384]{2,1,0:T(8,128)(2,1)S(1)}, bf16[2,96,384]{2,1,0:T(8,128)(2,1)S(1)}, u32[]{:S(2)}, u32[]{:S(2)}) collective-permute-start(bf16[2,96,384]{2,1,0:T(8,128)(2,1)S(1)} %get-tuple-element.101), channel_id=1, source_target_pairs={{0,8},{1,9},{2,10},{3,11},{4,12},{5,13},{6,14},{7,15},{8,0},{9,1},... | collective-permute-start | bytes 442376 | tf_op jit(solution)/shard_map/ppermute | solution.py:53
  112.6 11.2 %collective-permute-start.21 = (bf16[1,96,384]{2,1,0:T(8,128)(2,1)S(1)}, bf16[1,96,384]{2,1,0:T(8,128)(2,1)S(1)}, u32[]{:S(2)}, u32[]{:S(2)}) collective-permute-start(bf16[1,96,384]{2,1,0:T(8,128)(2,1)S(1)} %add_convert_fusion.22), channel_id=1, source_target_pairs={{0,16},{1,17},{2,18},{3,19},{4,20},{5,21},{6,22},{7,23},{8,24},{9,... | collective-permute-start | bytes 221192 | tf_op jit(solution)/shard_map/ppermute | solution.py:53
  115.0 6.2 %collective-permute-start.16 = (bf16[2,112,384]{2,1,0:T(8,128)(2,1)S(1)}, bf16[2,112,384]{2,1,0:T(8,128)(2,1)S(1)}, u32[]{:S(2)}, u32[]{:S(2)}) collective-permute-start(bf16[2,112,384]{2,1,0:T(8,128)(2,1)S(1)} %get-tuple-element.99), channel_id=1, source_target_pairs={{0,8},{1,9},{2,10},{3,11},{4,12},{5,13},{6,14},{7,15},{8,0},{9,1},... | collective-permute-start | bytes 516104 | tf_op jit(solution)/shard_map/ppermute | solution.py:53
  120.2 9.9 %collective-permute-start.24 = (bf16[4,192,384]{2,1,0:T(8,128)(2,1)S(1)}, bf16[4,192,384]{2,1,0:T(8,128)(2,1)S(1)}, u32[]{:S(2)}, u32[]{:S(2)}) collective-permute-start(bf16[4,192,384]{2,1,0:T(8,128)(2,1)S(1)} %get-tuple-element.89), channel_id=1, source_target_pairs={{0,4},{1,3},{2,6},{3,1},{4,0},{5,7},{6,2},{7,5},{8,12},{9,11},{10,... | collective-permute-start | bytes 1769480 | tf_op jit(solution)/shard_map/ppermute | solution.py:53
  121.2 5.5 %collective-permute-start.17 = (bf16[1,112,384]{2,1,0:T(8,128)(2,1)S(1)}, bf16[1,112,384]{2,1,0:T(8,128)(2,1)S(1)}, u32[]{:S(2)}, u32[]{:S(2)}) collective-permute-start(bf16[1,112,384]{2,1,0:T(8,128)(2,1)S(1)} %add_convert_fusion.20), channel_id=1, source_target_pairs={{0,16},{1,17},{2,18},{3,19},{4,20},{5,21},{6,22},{7,23},{8,24},{9,... | collective-permute-start | bytes 258056 | tf_op jit(solution)/shard_map/ppermute | solution.py:53
  130.3 8.1 %collective-permute-start.25 = (bf16[2,192,384]{2,1,0:T(8,128)(2,1)S(1)}, bf16[2,192,384]{2,1,0:T(8,128)(2,1)S(1)}, u32[]{:S(2)}, u32[]{:S(2)}) collective-permute-start(bf16[2,192,384]{2,1,0:T(8,128)(2,1)S(1)} %get-tuple-element.95), channel_id=1, source_target_pairs={{0,8},{1,9},{2,10},{3,11},{4,12},{5,13},{6,14},{7,15},{8,0},{9,1},... | collective-permute-start | bytes 884744 | tf_op jit(solution)/shard_map/ppermute | solution.py:53
  138.5 6.3 %collective-permute-start.26 = (bf16[1,192,384]{2,1,0:T(8,128)(2,1)S(1)}, bf16[1,192,384]{2,1,0:T(8,128)(2,1)S(1)}, u32[]{:S(2)}, u32[]{:S(2)}) collective-permute-start(bf16[1,192,384]{2,1,0:T(8,128)(2,1)S(1)} %add_convert_fusion.16), channel_id=1, source_target_pairs={{0,16},{1,17},{2,18},{3,19},{4,20},{5,21},{6,22},{7,23},{8,24},{9,... | collective-permute-start | bytes 442376 | tf_op jit(solution)/shard_map/ppermute | solution.py:53

commit v2 on v1

v2 whole, which is shorter than its diff:
```python
import functools

import jax
import jax.numpy as jnp
from jax import lax
from jax.experimental import pallas as pl
from jax.experimental.pallas import tpu as pltpu
from jax.sharding import PartitionSpec as P

HEADS = 12
HEAD = 64
AXES = ("wide", "narrow")
GROUPS = 8
BF = jnp.bfloat16
F32 = jnp.float32
MIB = 1024 * 1024

eps = 1e-06
neg_big = -1e30

ORDER = ((0, 1, 2, 3), (1, 0, 2, 3))
MIX_ORDER = ((0, 1, 3), (1, 0, 3))


def mat(left, right):
    return jnp.dot(left, right, preferred_element_type=jnp.float32)


def times_trans(left, right):
    return lax.dot_general(
        left, right, (((1,), (1,)), ((), ())), preferred_element_type=jnp.float32
    )


class Place:
    def __init__(self):
        self.wide_n = lax.axis_size("wide")
        self.narrow_n = lax.axis_size("narrow")
        self.rest_bits = (self.wide_n // GROUPS).bit_length() - 1
        self.count = self.wide_n * self.narrow_n
        self.wide_at = lax.axis_index("wide")
        self.narrow_at = lax.axis_index("narrow")
        self.x_at = self.narrow_at >> 1
        self.group = self.wide_at >> self.rest_bits
        shift = 2 + self.rest_bits
        self.masks = (2, 1 << shift, 2 << shift, 4 << shift)

    def swap(self, value, mask):
        pairs = [(index, index ^ mask) for index in range(self.count)]
        return lax.ppermute(value, AXES, pairs)

    def swap_by_core(self, value, links):
        pairs = [(index, index ^ self.masks[links[index & 1]]) for index in range(self.count)]
        return lax.ppermute(value, AXES, pairs)


def core_of(at_ref):
    return at_ref[0] & 1


def live_of(at_ref, slot):
    size = at_ref[2 + slot]
    return jnp.where(size == 0, 25, jnp.where(size == 1, 49, 64))


def spot_of(at_ref, owner_x, owner_group, order=ORDER):
    group = at_ref[1]
    here = (at_ref[0] >> 1, group & 1, (group >> 1) & 1, group >> 2)
    there = (owner_x, owner_group & 1, (owner_group >> 1) & 1, owner_group >> 2)
    spots = []
    for links in order:
        spot = 0
        for link in links:
            spot = spot * 2 + (here[link] ^ there[link])
        spots.append(spot)
    return jnp.where(core_of(at_ref) == 0, spots[0], spots[1])


def near_first(at_ref, group):
    differ = ((at_ref[1] ^ group) >> 1) & 1
    return differ * 4 + (group & 1) + 2 * (group >> 2)


def live_rows(rows, chunk, live):
    spot = lax.broadcasted_iota(jnp.int32, (rows, 1), 0)
    return lax.rem(spot, chunk) < live


def norm_parts(source):
    average = jnp.mean(source, axis=1, keepdims=True)
    centered = source - average
    scale = lax.rsqrt(jnp.mean(centered * centered, axis=1, keepdims=True) + eps)
    return centered * scale, scale


def norm_back(grad, normed, scale, gain):
    scaled = grad * gain
    mean_one = jnp.mean(scaled, axis=1, keepdims=True)
    mean_two = jnp.mean(scaled * normed, axis=1, keepdims=True)
    return scale * (scaled - mean_one - normed * mean_two)


def reciprocal(value):
    first = pl.reciprocal(value, approx=True)
    return first * (2.0 - value * first)


def gelu_pair(value):
    tail = jnp.exp(value * value * -0.5)
    step = reciprocal(1.0 + (0.3275911 * 0.7071067811865476) * jnp.abs(value))
    series = 0.5 * 1.061405429
    for term in (-1.453152027, 1.421413741, -0.284496736, 0.254829592):
        series = series * step + 0.5 * term
    upper = series * step * tail
    share = jnp.where(value >= 0.0, 1.0 - upper, upper)
    return value * share, share + value * tail * 0.3989422804014327


def slot_copies(refs, core, target_ref, sems, first, partner=False):
    order = (refs[2], refs[3], refs[0], refs[1]) if partner else refs
    which = 1 - core if partner else core
    return [
        pltpu.make_async_copy(ref.at[which], target_ref.at[index], sems.at[first + index])
        for index, ref in enumerate(order)
    ]


def copy_all(sources, targets, sems):
    copies = [
        pltpu.make_async_copy(source, target, sems.at[index])
        for index, (source, target) in enumerate(zip(sources, targets))
    ]
    start_all(copies)
    wait_all(copies)


def token_slice_kernel(at_ref, token_hbm, near_ref, near_core_ref, far_ref, sems):
    core, x_at = core_of(at_ref), at_ref[0] >> 1
    sources = [token_hbm.at[x_at, core], token_hbm.at[x_at, 1 - core], token_hbm.at[1 - x_at]]
    copy_all(sources, [near_ref, near_core_ref, far_ref], sems)


def far_slice_kernel(at_ref, far_ref, mine_ref, other_ref):
    core = core_of(at_ref)
    mine_ref[...] = far_ref[core]
    other_ref[...] = far_ref[1 - core]


def cot_slice_kernel(at_ref, cot_hbm, near_ref, far_ref, sems):
    x_at = at_ref[0] >> 1
    copy_all([cot_hbm.at[x_at], cot_hbm.at[1 - x_at]], [near_ref, far_ref], sems)


def start_all(copies):
    for copy in copies:
        copy.start()


def wait_all(copies):
    for copy in copies:
        copy.wait()


def flat_rows(ref):
    return ref[...].reshape(ref.shape[0] * ref.shape[1], ref.shape[2])


def load_kernel(*refs):
    sems = refs[-1]
    count = (len(refs) - 1) // 2
    copies = [
        pltpu.make_async_copy(refs[index], refs[count + index], sems.at[index])
        for index in range(count)
    ]
    start_all(copies)
    wait_all(copies)


def attention_kernel(
    at_ref,
    near_ref,
    far_ref,
    near_other_ref,
    far_other_ref,
    gain1_hbm,
    bias1_hbm,
    qv_bias_hbm,
    proj_bias_hbm,
    up_hbm,
    qkv_ref,
    proj_ref,
    row_ref,
    left_ref,
    query_t_ref,
    key_t_ref,
    value_ref,
    prob_ref,
    scale_ref,
    resid_ref,
    up_ref,
    rows_ref,
    gain1_ref,
    bias1_ref,
    qv_bias_ref,
    proj_bias_ref,
    sems,
):
    row_copies = [
        pltpu.make_async_copy(source, rows_ref.at[index], sems.at[index])
        for index, source in enumerate([near_ref, far_ref, near_other_ref, far_other_ref])
    ]
    start_all(row_copies)
    vectors = [
        (gain1_hbm, gain1_ref),
        (bias1_hbm, bias1_ref),
        (qv_bias_hbm, qv_bias_ref),
        (proj_bias_hbm, proj_bias_ref),
        (up_hbm, up_ref),
    ]
    vector_copies = [
        pltpu.make_async_copy(source, target, sems.at[4 + index])
        for index, (source, target) in enumerate(vectors)
    ]
    start_all(vector_copies)
    rows, width = row_ref.shape
    live = live_of(at_ref, at_ref[0])
    wait_all(row_copies)
    tokens = flat_rows(rows_ref)
    row_ref[...] = tokens
    source = tokens.astype(F32)
    normed, _ = norm_parts(source)
    wait_all(vector_copies[:4])
    normed = (normed * gain1_ref[...][None] + bias1_ref[...][None]).astype(BF)
    left_ref[0] = normed.T
    queries = mat(normed, qkv_ref[:, :width]) + qv_bias_ref[...][None, :width]
    query_t = (queries * 0.125).astype(BF).T
    query_t_ref[...] = query_t
    keys = mat(normed, qkv_ref[:, width : 2 * width]).astype(BF)
    key_t_ref[...] = keys.T
    values = (mat(normed, qkv_ref[:, 2 * width :]) + qv_bias_ref[...][None, width:]).astype(BF)
    value_ref[...] = values
    value_t = values.T
    lane = lax.broadcasted_iota(jnp.int32, (rows, 2 * HEAD), 1)
    masked = jnp.where(live_rows(rows, rows // 4, live), 0.0, neg_big)
    row = lax.broadcasted_iota(jnp.int32, (HEAD, rows), 0)
    mark = jnp.where(row == 0, 1.0, 0.0).astype(BF)
    ones = jnp.ones((16, rows), BF)
    halves_of = [
        (lane < HEAD, jnp.where(lane == HEAD, masked, 0.0).astype(BF)),
        (lane >= HEAD, jnp.where(lane == 0, masked, 0.0).astype(BF)),
    ]
    for head in range(HEADS):
        pair, side = head // 2, head % 2
        spots = slice(head * HEAD, (head + 1) * HEAD)
        inside, mask = halves_of[side]
        keys_head = jnp.where(inside, keys[:, pair * 2 * HEAD : (pair + 1) * 2 * HEAD], mask)
        query = query_t[spots]
        padded = jnp.concatenate([query, mark] if side == 0 else [mark, query], axis=0)
        scores = mat(keys_head, padded)
        top = jnp.max(scores, axis=0, keepdims=True)
        weights = jnp.exp(scores - top).astype(BF)
        prob_ref[head] = weights
        total = mat(jnp.concatenate([value_t[spots], ones], axis=0), weights)
        scale = 1.0 / total[HEAD : HEAD + 1]
        scale_ref[head : head + 1] = scale
        left_ref[1, spots, :] = (total[:HEAD] * scale).astype(BF)

    resid_ref[...] = source + mat(left_ref[1].T, proj_ref[...]) + proj_bias_ref[...][None]
    vector_copies[4].wait()


def hidden_terms(at_ref, other, normed, up_ref, up_bias_ref, act_ref, slope_ref):
    width = normed.shape[1]
    for owner_x in range(2):
        quarter = 2 * owner_x + (core_of(at_ref) ^ other)
        columns = pl.ds(pl.multiple_of(quarter * width, width), width)
        before = mat(normed, up_ref[:, columns]) + up_bias_ref[columns][None]
        act, slope = gelu_pair(before)
        act_ref[owner_x] = act.astype(BF)
        slope_ref[owner_x] = slope.astype(BF)


def hidden_send_kernel(
    at_ref,
    gain2_hbm,
    bias2_hbm,
    up_bias_hbm,
    resid_ref,
    up_ref,
    left_ref,
    normed_ref,
    act_ref,
    slope_ref,
    gain2_ref,
    bias2_ref,
    up_bias_ref,
    sems,
):
    vectors = [(gain2_hbm, gain2_ref), (bias2_hbm, bias2_ref), (up_bias_hbm, up_bias_ref)]
    copies = [
        pltpu.make_async_copy(source, target, sems.at[index])
        for index, (source, target) in enumerate(vectors)
    ]
    start_all(copies)
    normed, _ = norm_parts(resid_ref[...])
    wait_all(copies)
    normed = (normed * gain2_ref[...][None] + bias2_ref[...][None]).astype(BF)
    normed_ref[...] = normed
    left_ref[...] = normed.T
    hidden_terms(at_ref, 1, normed, up_ref, up_bias_ref, act_ref, slope_ref)


def hidden_own_kernel(
    at_ref,
    up_bias_hbm,
    down_hbm,
    normed_ref,
    up_ref,
    act_ref,
    slope_ref,
    down_ref,
    up_bias_ref,
    sems,
):
    bias_copy = pltpu.make_async_copy(up_bias_hbm, up_bias_ref, sems.at[0])
    down_copy = pltpu.make_async_copy(down_hbm, down_ref, sems.at[1])
    start_all([bias_copy, down_copy])
    bias_copy.wait()
    hidden_terms(at_ref, 0, normed_ref[...], up_ref, up_bias_ref, act_ref, slope_ref)
    down_copy.wait()


def split_rows(value, keep_ref, send_ref):
    size = keep_ref.shape[1]
    for step in range(2):
        keep_ref[step] = value[step * size : (step + 1) * size]
        send_ref[step] = value[(step + 2) * size : (step + 3) * size]


def mixed_kernel(
    at_ref,
    act_own_ref,
    act_send_ref,
    resid_ref,
    down_ref,
    down_bias_hbm,
    keep_ref,
    send_ref,
    down_bias_ref,
    sems,
):
    bias_copy = pltpu.make_async_copy(down_bias_hbm, down_bias_ref, sems.at[0])
    bias_copy.start()
    rows, width = resid_ref.shape
    core = core_of(at_ref)
    total = resid_ref[...]
    for owner_x in range(2):
        for other in range(2):
            quarter = 2 * owner_x + (core if other == 0 else 1 - core)
            act = (act_own_ref if other == 0 else act_send_ref)[owner_x]
            spots = pl.ds(pl.multiple_of(quarter * width, width), width)
            total += mat(act, down_ref[spots, :])
    bias_copy.wait()
    total += down_bias_ref[...][None]
    valid = live_rows(rows, rows // 4, live_of(at_ref, at_ref[0]))
    split_rows(jnp.where(valid, total, 0.0).astype(BF), keep_ref, send_ref)


def gather_kernel(mixed_keep, mixed_got, input_keep, input_got, far_ref):
    for index, ref in enumerate([mixed_keep, mixed_got, input_keep, input_got]):
        far_ref[index] = ref[1]


def place_kernel(at_ref, mixed_keep, mixed_got, input_keep, input_got, far_ref, mixed_ref, input_ref):
    core, x_at = core_of(at_ref), at_ref[0] >> 1
    size = far_ref.shape[1]

    def put(ref, slot, value):
        ref[pl.ds(pl.multiple_of(slot * size, size), size), :] = value

    for index, (keep, got, out) in enumerate(
        [(mixed_keep, mixed_got, mixed_ref), (input_keep, input_got, input_ref)]
    ):
        put(out, 2 * x_at + core, keep[0])
        put(out, 2 * x_at + 1 - core, got[0])
        put(out, 2 * (1 - x_at) + core, far_ref[2 * index])
        put(out, 2 * (1 - x_at) + 1 - core, far_ref[2 * index + 1])


def hand_over(block_ref, send_ref, keep_ref):
    half = send_ref.shape[0]
    keep_ref[...] = block_ref[:half]
    send_ref[...] = block_ref[half:]


def down_terms_kernel(
    at_ref,
    near_ref,
    far_ref,
    near_other_ref,
    far_other_ref,
    act_own,
    act0_other,
    act1_other,
    send_ref,
    keep_ref,
    bias_ref,
    block_ref,
    own_ref,
    other_ref,
    sems,
):
    core = core_of(at_ref)
    refs = [near_ref, far_ref, near_other_ref, far_other_ref]
    copies = slot_copies(refs, core, own_ref, sems, 0)
    copies += slot_copies(refs, core, other_ref, sems, 4, partner=True)
    start_all(copies)
    wait_all(copies)
    zero = jnp.zeros((), BF)
    rows = 4 * own_ref.shape[1]
    block = own_ref.shape[2] // GROUPS
    slot = at_ref[0]
    own = jnp.where(live_rows(rows, rows // 4, live_of(at_ref, slot)), flat_rows(own_ref), zero)
    other = jnp.where(
        live_rows(rows, rows // 4, live_of(at_ref, slot ^ 1)), flat_rows(other_ref), zero
    )
    bias_ref[...] = jnp.sum(own.astype(F32), axis=0, keepdims=True)
    both = jnp.concatenate([own.T, other.T], axis=1)
    for owner_x in range(2):
        act_other = act1_other if owner_x else act0_other
        right = jnp.concatenate([act_own[owner_x], act_other[...]], axis=0)
        for half in range(2):
            span = slice(half * 4 * block, (half + 1) * 4 * block)
            total = mat(both[span], right).astype(BF)
            for step in range(4):
                spot = spot_of(at_ref, owner_x, half * 4 + step)
                block_ref[spot] = total[step * block : (step + 1) * block]
    hand_over(block_ref, send_ref, keep_ref)


def hidden_back_kernel(
    at_ref,
    near_ref,
    far_ref,
    near_other_ref,
    far_other_ref,
    gain2_hbm,
    proj_hbm,
    up_ref,
    slope_own_ref,
    slope_send_ref,
    resid_ref,
    down_ref,
    hidden0_ref,
    hidden1_ref,
    grad_ref,
    branch_ref,
    att_grad_t_ref,
    up_bias_ref,
    gain_ref,
    bias_ref,
    proj_bias_ref,
    cot_ref,
    gain2_ref,
    proj_ref,
    sems,
):
    copies = slot_copies(
        [near_ref, far_ref, near_other_ref, far_other_ref], core_of(at_ref), cot_ref, sems, 0
    )
    copies.append(pltpu.make_async_copy(gain2_hbm, gain2_ref, sems.at[4]))
    start_all(copies)
    proj_copy = pltpu.make_async_copy(proj_hbm, proj_ref, sems.at[5])
    proj_copy.start()
    rows, width = resid_ref.shape
    core = core_of(at_ref)
    order = [(owner_x, other) for owner_x in range(2) for other in range(2)]
    spans = []
    hidden_refs = [hidden0_ref, hidden1_ref]
    for owner_x, other in order:
        quarter = 2 * owner_x + (core ^ other)
        spans.append(pl.ds(pl.multiple_of(quarter * width, width), width))
    wait_all(copies)
    valid = live_rows(rows, rows // 4, live_of(at_ref, at_ref[0]))
    out_grad = jnp.where(valid, flat_rows(cot_ref), jnp.zeros((), BF))
    second = jnp.zeros((rows, width), F32)
    for index, (owner_x, other) in enumerate(order):
        slope = (slope_send_ref if other else slope_own_ref)[owner_x]
        hidden = times_trans(out_grad, down_ref[spans[index], :]) * slope.astype(F32)
        hidden = hidden.astype(BF)
        hidden_refs[owner_x][other] = hidden
        up_bias_ref[:, spans[index]] = jnp.sum(hidden.astype(F32), axis=0, keepdims=True)
        second += times_trans(hidden, up_ref[:, spans[index]])
    normed, scale = norm_parts(resid_ref[...])
    gain_ref[...] = jnp.sum(second * normed, axis=0, keepdims=True)
    bias_ref[...] = jnp.sum(second, axis=0, keepdims=True)
    grad = out_grad.astype(F32) + norm_back(second, normed, scale, gain2_ref[...][None])
    grad_ref[...] = grad
    branch = grad.astype(BF)
    proj_bias_ref[...] = jnp.sum(branch.astype(F32), axis=0, keepdims=True)
    branch_t = branch.T
    share = width // GROUPS
    for group in range(GROUPS):
        branch_ref[near_first(at_ref, group)] = branch_t[group * share : (group + 1) * share]
    proj_copy.wait()
    att_grad_t_ref[...] = mat(proj_ref[...], branch_t).astype(BF)


def attention_back_kernel(
    at_ref,
    qkv_hbm,
    left_ref,
    query_t_ref,
    key_t_ref,
    value_ref,
    prob_ref,
    scale_ref,
    att_grad_t_ref,
    branch_ref,
    right_ref,
    qkv_ref,
    sems,
):
    qkv_copy = pltpu.make_async_copy(qkv_hbm, qkv_ref, sems.at[0])
    qkv_copy.start()
    rows, width = value_ref.shape
    blank = jnp.zeros((HEAD, rows), BF)
    qkv_rows = 3 * width // GROUPS
    places = [near_first(at_ref, group) for group in range(GROUPS)]
    right_ref[:, qkv_rows:] = branch_ref[...]

    def put(start, value):
        while value.shape[0]:
            group = start // qkv_rows
            at = start - group * qkv_rows
            count = min(value.shape[0], qkv_rows - at)
            right_ref[places[group], at : at + count] = value[:count]
            value, start = value[count:], start + count

    for head in range(HEADS):
        pair, side = head // 2, head % 2
        spots = slice(head * HEAD, (head + 1) * HEAD)
        values_pair = value_ref[:, pair * 2 * HEAD : (pair + 1) * 2 * HEAD]
        grad = att_grad_t_ref[spots, :].astype(F32)
        scale = scale_ref[head : head + 1]
        delta = jnp.sum(grad * left_ref[1, spots, :].astype(F32), axis=0, keepdims=True) * scale
        grad = (grad * scale).astype(BF)
        padded = jnp.concatenate([grad, blank] if side == 0 else [blank, grad], axis=0)
        weights = prob_ref[head]
        prob_grad = mat(values_pair, padded)
        score_grad = (weights.astype(F32) * (prob_grad - delta)).astype(BF)
        query_grad = mat(key_t_ref[spots, :], score_grad).astype(BF)
        start = head * HEAD
        put(start, query_grad * jnp.asarray(0.125, BF))
        put(start + width, times_trans(query_t_ref[spots, :], score_grad).astype(BF))
        put(start + 2 * width, times_trans(grad, weights).astype(BF))
    qkv_copy.wait()


def first_back_kernel(
    at_ref,
    gain1_hbm,
    row_ref,
    grad_ref,
    right_ref,
    qkv_ref,
    up_bias_ref,
    proj_bias_ref,
    gain2_ref,
    bias2_ref,
    down_bias_ref,
    keep_ref,
    send_ref,
    vec_ref,
    gain1_ref,
    sems,
):
    gain_copy = pltpu.make_async_copy(gain1_hbm, gain1_ref, sems.at[0])
    gain_copy.start()
    rows, width = row_ref.shape
    qkv_rows = 3 * width // GROUPS
    places = [near_first(at_ref, group) for group in range(GROUPS)]
    stacked = jnp.concatenate([right_ref[place, :qkv_rows] for place in places], axis=0)
    ones = jnp.ones((8, rows), BF)
    query_sum = times_trans(ones, stacked[:width])[:1]
    value_sum = times_trans(ones, stacked[2 * width :])[:1]
    normed, scale = norm_parts(row_ref[...].astype(F32))
    first = mat(qkv_ref[...], stacked).T
    gain = jnp.sum(first * normed, axis=0, keepdims=True)
    bias = jnp.sum(first, axis=0, keepdims=True)
    gain_copy.wait()
    total = grad_ref[...] + norm_back(first, normed, scale, gain1_ref[...][None])
    split_rows(total.astype(BF), keep_ref, send_ref)
    share = width // GROUPS
    hidden = up_bias_ref.shape[1] // GROUPS
    qv_sum = jnp.concatenate([query_sum, value_sum], axis=1)
    second = [proj_bias_ref[...], gain2_ref[...], bias2_ref[...], down_bias_ref[...]]
    pad = jnp.zeros((vec_ref.shape[1] - 3, hidden), F32)
    for group in range(GROUPS):
        at = group * share
        vec_ref[places[group]] = jnp.concatenate(
            [
                up_bias_ref[:, group * hidden : (group + 1) * hidden],
                jnp.concatenate(
                    [gain[:, at : at + share], bias[:, at : at + share], qv_sum[:, 2 * at : 2 * (at + share)]],
                    axis=1,
                ),
                jnp.concatenate([item[:, at : at + share] for item in second], axis=1),
                pad,
            ],
            axis=0,
        )


def own_quarters(refs, core):
    size = refs[0].shape[0] // 4
    return jnp.concatenate(
        [
            jnp.concatenate(
                [
                    ref[pl.ds(pl.multiple_of((2 * owner_x + core) * size, size), size), :]
                    for ref in refs
                ],
                axis=1,
            )
            for owner_x in range(2)
        ],
        axis=0,
    )


def up_terms_kernel(at_ref, left_own, left_other, *refs):
    own, other = refs[:2], refs[2:4]
    send_ref, keep_ref, block_ref = refs[4:]
    core = core_of(at_ref)
    rows = left_own.shape[0] // 4
    width = own[0].shape[2] // 2
    left = own_quarters([left_own, left_other], core)
    for owner_x in range(2):
        for side in range(2):
            quarter = 2 * owner_x + (core ^ side)
            for half in range(2):
                span = slice(half * width, (half + 1) * width)
                right = jnp.concatenate(
                    [own[owner_x][side, :, span], other[owner_x][1 - side, :, span]], axis=0
                )
                total = mat(left, right).astype(BF)
                for index in range(2):
                    spot = spot_of(at_ref, index, 2 * quarter + half)
                    block_ref[spot] = total[index * rows : (index + 1) * rows]
    hand_over(block_ref, send_ref, keep_ref)


def mix_terms_kernel(at_ref, *refs):
    lefts, rights = refs[:4], refs[4:8]
    vec_ref, send_ref, keep_ref, block_ref = refs[8:]
    core = core_of(at_ref)
    rows = lefts[0].shape[1] // 4
    count, columns = rights[0].shape[0], rights[0].shape[1]
    qkv_rows = 3 * columns // 4
    edge = qkv_rows - qkv_rows % 128
    norm = own_quarters([ref.at[0] for ref in lefts], core)
    att = own_quarters([ref.at[1] for ref in lefts], core)
    lane = lax.broadcasted_iota(jnp.int32, (2 * rows, columns - edge), 1)
    pad = jnp.zeros((block_ref.shape[1] - rows - vec_ref.shape[1], columns), F32)
    here = (at_ref[1] >> 1) & 1
    for index in range(count):
        right = jnp.concatenate([ref[index] for ref in rights], axis=1)
        first = times_trans(norm, right)
        tail = jnp.where(lane < qkv_rows - edge, first[:, edge:], times_trans(att, right[edge:]))
        total = jnp.concatenate([first[:, :edge], tail], axis=1).astype(BF)
        extra = jnp.concatenate([vec_ref[index], pad], axis=0).astype(BF)
        group = (index & 1) + 2 * here + 4 * (index >> 1)
        for owner_x in range(2):
            spot = spot_of(at_ref, owner_x, group, MIX_ORDER)
            block_ref[spot, :rows] = total[owner_x * rows : (owner_x + 1) * rows]
            block_ref[spot, rows:] = extra
    hand_over(block_ref, send_ref, keep_ref)


def add_kernel(keep_ref, got_ref, next_send_ref, next_keep_ref):
    half = next_keep_ref.shape[0]
    next_send_ref[...] = (keep_ref[half:].astype(F32) + got_ref[half:].astype(F32)).astype(BF)
    next_keep_ref[...] = (keep_ref[:half].astype(F32) + got_ref[:half].astype(F32)).astype(BF)


def mix_end_kernel(keep_ref, got_ref, qkv_ref, proj_ref, *vec_refs):
    total = keep_ref[0].astype(F32) + got_ref[0].astype(F32)
    rows, split = qkv_ref.shape
    qkv_ref[...] = total[:rows, :split]
    proj_ref[...] = total[:rows, split:]
    at, row = 0, rows
    for ref in vec_refs:
        size = ref.shape[1]
        ref[...] = total[row : row + 1, at : at + size]
        at += size
        if at == total.shape[1]:
            at, row = 0, row + 1


SPECS = {
    "s": pl.BlockSpec(memory_space=pltpu.SMEM),
    "v": pl.BlockSpec(memory_space=pltpu.VMEM),
    "p": pl.BlockSpec(memory_space=pltpu.VMEM),
    "a": pl.BlockSpec(memory_space=pl.ANY),
    "h": pl.BlockSpec(memory_space=pltpu.HBM),
}
SPACES = {"p": pltpu.VMEM, "h": pltpu.HBM}


def shaped(kind, *dims):
    return jax.ShapeDtypeStruct(dims, kind)


def kept(kind, *dims):
    return pltpu.VMEM(dims, kind)


def sems(count):
    return pltpu.SemaphoreType.DMA((count,))


def kernel_call(body, specs, operands, outs, scratch=(), room=12, after=()):
    count = len(operands)
    specs = specs + "p" * len(after)
    operands = [
        pltpu.with_memory_space_constraint(item, SPACES[kind]) if kind in SPACES else item
        for kind, item in zip(specs, list(operands) + list(after))
    ]

    def run(*refs):
        body(*refs[:count], *refs[len(operands) :])

    return pl.pallas_call(
        run,
        out_shape=outs,
        in_specs=[SPECS[kind] for kind in specs],
        out_specs=[SPECS["v"]] * len(outs),
        scratch_shapes=list(scratch),
        compiler_params=pltpu.CompilerParams(vmem_limit_bytes=room * MIB),
        cost_estimate=pl.CostEstimate(flops=1000, bytes_accessed=1000, transcendentals=0),
        name=body.__name__.replace("_kernel", ""),
    )(*operands)


class Sum:
    def __init__(self, place, order, send, keep):
        self.place, self.order, self.step = place, order, 0
        self.send, self.keep = send, keep

    def pass_on(self):
        step = self.step
        self.step += 1
        return self.place.swap_by_core(self.send, (self.order[0][step], self.order[1][step]))

    def go(self, after):
        got = self.pass_on()
        half = kept(BF, self.keep.shape[0] // 2, *self.keep.shape[1:])
        self.send, self.keep = kernel_call(
            add_kernel, "pp", [self.keep, got], [half, half], after=after
        )
        return self.keep

    def end(self):
        got = self.pass_on()
        return (self.keep.astype(F32) + got.astype(F32))[0]

    def end_mix(self, qkv_columns):
        got = self.pass_on()
        _, rows, columns = self.keep.shape
        rows -= 16
        share = columns - qkv_columns
        sizes = (columns, share, share, 2 * share, share, share, share, share)
        return kernel_call(
            mix_end_kernel,
            "pp",
            [self.keep, got],
            [shaped(F32, rows, qkv_columns), shaped(F32, rows, share)]
            + [shaped(F32, 1, size) for size in sizes],
        )


def within_group(place, block, axis):
    for bit in reversed(range(place.rest_bits)):
        here = (place.wide_at >> bit) & 1
        size = block.shape[axis] // 2
        keep = lax.dynamic_slice_in_dim(block, here * size, size, axis)
        send = lax.dynamic_slice_in_dim(block, (1 - here) * size, size, axis)
        block = keep + place.swap(send, 4 << bit)
    return block


def shards(
    tokens,
    image_size,
    cotangent,
    ln1_gain,
    ln1_bias,
    qkv_weight,
    qv_bias,
    proj_weight,
    proj_bias,
    ln2_gain,
    ln2_bias,
    up_weight,
    up_bias,
    down_weight,
    down_bias,
):
    place = Place()
    rows, width = tokens.shape
    hidden = up_weight.shape[1]
    slot_rows = rows // 4
    at = jnp.concatenate([jnp.stack([place.narrow_at, place.group]), image_size[0]])

    tall = kept(BF, width, rows)
    flat = kept(F32, rows, width)
    natural = kept(BF, rows, width)
    vector = kept(F32, 1, width)
    act = kept(BF, 2, rows, hidden // 4)
    chunk = kept(BF, slot_rows, width)
    chunks = kept(BF, 2, slot_rows, width)
    four = pltpu.VMEM((4, slot_rows, width), BF)
    columns = hidden // GROUPS
    share = width // GROUPS

    def line(size):
        return pltpu.VMEM((size,), F32)

    def blocks(count, height, lanes):
        return pltpu.VMEM((count, height, lanes), BF)

    def halves(count, height, lanes):
        return [kept(BF, count // 2, height, lanes)] * 2

    parted = (2, 2, slot_rows, width)
    near, near_core, far = kernel_call(
        token_slice_kernel,
        "sh",
        [at, tokens.reshape(parted)],
        [chunk, chunk, chunks],
        [sems(3)],
    )
    far = place.swap(far, 2)
    qkv_kept, proj_kept = kernel_call(
        load_kernel,
        "hh",
        [qkv_weight, proj_weight],
        [kept(BF, *item.shape) for item in (qkv_weight, proj_weight)],
        [sems(2)],
        after=[near],
    )
    cot_near, cot_far = kernel_call(
        cot_slice_kernel,
        "sh",
        [at, cotangent.reshape(parted)],
        [chunks, chunks],
        [sems(2)],
        after=[proj_kept],
    )
    cot_far = place.swap(cot_far, 2)
    cot_parts = [cot_near, cot_far, place.swap(cot_near, 1), place.swap(cot_far, 1)]
    far_mine, far_other = kernel_call(
        far_slice_kernel, "sp", [at, far], [chunk, chunk], after=[cot_near]
    )
    token_parts = [near, far_mine, place.swap(near_core, 1), place.swap(far_other, 1)]
    slot_tokens, lefts, query_t, key_t, values, prob, scale, residual, up_kept = kernel_call(
        attention_kernel,
        "s" + "a" * 4 + "h" * 5 + "pp",
        [at]
        + token_parts
        + [ln1_gain, ln1_bias, qv_bias, proj_bias, up_weight]
        + [qkv_kept, proj_kept],
        [
            natural,
            kept(BF, 2, width, rows),
            tall,
            tall,
            natural,
            kept(BF, HEADS, rows, rows),
            kept(F32, 16, rows),
            flat,
            kept(BF, *up_weight.shape),
        ],
        [four, line(width), line(width), line(2 * width), line(width), sems(9)],
    )
    z_mask = place.masks[2]

    lefts_beyond = place.swap(lefts, z_mask)
    left_sets = [lefts, place.swap(lefts, 1), lefts_beyond, place.swap(lefts_beyond, 1)]
    second_left, second_normed, act_send, slope_send = kernel_call(
        hidden_send_kernel,
        "shhhpp",
        [at, ln2_gain, ln2_bias, up_bias, residual, up_kept],
        [tall, natural, act, act],
        [line(width), line(width), line(hidden), sems(3)],
        after=[cot_far],
    )
    act_own, slope_own, down_kept = kernel_call(
        hidden_own_kernel,
        "shhpp",
        [at, up_bias, down_weight, second_normed, up_kept],
        [act, act, kept(BF, *down_weight.shape)],
        [line(hidden), sems(2)],
    )
    act_other = [place.swap(act_send[index], 1) for index in range(2)]
    down_send, down_keep, down_bias_grad = kernel_call(
        down_terms_kernel,
        "s" + "a" * 4 + "p" * 3,
        [at] + cot_parts + [act_own] + act_other,
        halves(2 * GROUPS, share, hidden // 4) + [vector],
        [blocks(2 * GROUPS, share, hidden // 4), four, four, sems(8)],
    )
    down_sum = Sum(place, ORDER, down_send, down_keep)
    (
        hidden0,
        hidden1,
        residual_grad,
        branches,
        att_grad_t,
        up_bias_grad,
        ln2_gain_grad,
        ln2_bias_grad,
        proj_bias_grad,
    ) = kernel_call(
        hidden_back_kernel,
        "s" + "a" * 4 + "hhppppp",
        [at]
        + cot_parts
        + [ln2_gain, proj_weight, up_kept, slope_own, slope_send, residual, down_kept],
        [
            act,
            act,
            flat,
            kept(BF, GROUPS, share, rows),
            tall,
            kept(F32, 1, hidden),
            vector,
            vector,
            vector,
        ],
        [
            four,
            line(width),
            pltpu.VMEM(proj_weight.shape, BF),
            sems(6),
        ],
        after=[down_bias_grad],
    )
    hidden_own = [hidden0, hidden1]
    hidden_other = [place.swap(item, 1) for item in hidden_own]
    rights, qkv_again = kernel_call(
        attention_back_kernel,
        "sh" + "p" * 8,
        [at, qkv_weight, lefts, query_t, key_t, values, prob, scale, att_grad_t, branches],
        [kept(BF, GROUPS, columns, rows), kept(BF, *qkv_weight.shape)],
        [sems(1)],
        after=[lefts_beyond],
    )
    half = GROUPS // 2
    def near_and_far(item):
        near, far = item[:half], place.swap(item[half:], z_mask)
        return [near, place.swap(near, 1), far, place.swap(far, 1)]

    right_sets = near_and_far(rights)
    last = down_sum.go([rights])
    up_send, up_keep = kernel_call(
        up_terms_kernel,
        "s" + "p" * 6,
        [at, second_left, place.swap(second_left, 1)] + hidden_own + hidden_other,
        halves(2 * GROUPS, width // 4, columns),
        [blocks(2 * GROUPS, width // 4, columns)],
        after=[last],
    )
    up_sum = Sum(place, ORDER, up_send, up_keep)
    mixed_keep, mixed_send = kernel_call(
        mixed_kernel,
        "spppph",
        [at, act_own, act_send, residual, down_kept, down_bias],
        [chunks, chunks],
        [line(width), sems(1)],
        after=[up_keep],
    )
    input_keep, input_send, packed = kernel_call(
        first_back_kernel,
        "shppppppppp",
        [
            at,
            ln1_gain,
            slot_tokens,
            residual_grad,
            rights,
            qkv_again,
            up_bias_grad,
            proj_bias_grad,
            ln2_gain_grad,
            ln2_bias_grad,
            down_bias_grad,
        ],
        [chunks, chunks, kept(F32, GROUPS, 8, columns)],
        [line(width), sems(1)],
        after=[mixed_keep],
    )
    packed = packed + place.swap(packed, 1)
    packed = packed[:half] + place.swap(packed[half:], z_mask)
    last = down_sum.go([input_keep])
    mix_send, mix_keep = kernel_call(
        mix_terms_kernel,
        "s" + "p" * 9,
        [at] + left_sets + right_sets + [packed],
        halves(GROUPS, width // 4 + 16, columns),
        [blocks(GROUPS, width // 4 + 16, columns)],
        after=[last],
    )
    mix_sum = Sum(place, MIX_ORDER, mix_send, mix_keep)
    last = up_sum.go([mix_keep])
    last = down_sum.go([last])
    last = mix_sum.go([last])
    last = up_sum.go([last])
    last = mix_sum.go([last])
    returns = [mixed_keep, place.swap(mixed_send, 1), input_keep, place.swap(input_send, 1)]
    (far_rows,) = kernel_call(
        gather_kernel, "pppp", returns, [kept(BF, 4, slot_rows, width)], after=[last]
    )
    far_rows = place.swap(far_rows, 2)
    down_block = down_sum.end()
    last = up_sum.go([last])
    mixed, input_grad = kernel_call(
        place_kernel, "spppp" + "p", [at] + returns + [far_rows], [shaped(BF, rows, width)] * 2, after=[last]
    )
    up_block = up_sum.end()
    mix_block = mix_sum.end_mix(3 * share)

    qkv_block, proj_block = mix_block[:2]
    reduced = [within_group(place, item.reshape(-1), 0) for item in mix_block[2:]]
    return (
        mixed,
        input_grad,
        reduced[1],
        reduced[2],
        within_group(place, qkv_block, 1),
        reduced[3],
        within_group(place, proj_block, 1),
        reduced[4],
        reduced[5],
        reduced[6],
        within_group(place, up_block, 1),
        reduced[0],
        within_group(place, down_block, 0).T,
        reduced[7],
    )


def solution(mesh):
    rows = P(AXES, None)
    whole = P()
    placed = (rows, P("wide", None), rows) + (whole,) * 12
    vector = P("wide")
    matrix = P("narrow", "wide")
    return jax.shard_map(
        shards,
        mesh=mesh,
        in_specs=placed,
        out_specs=(
            rows,
            rows,
            vector,
            vector,
            matrix,
            vector,
            matrix,
            vector,
            vector,
            vector,
            matrix,
            vector,
            matrix,
            vector,
        ),
        check_vma=False,
    )
```

time: 146 us -> 125 us (0.86)
  waiting for transfers between devices: 53.1 us -> 42.7 us
  local copies, waits for them, and re-layouts: 9.81 us -> 0.16 us
  Pallas kernels: 39.1 us -> 47.5 us
  starting transfers between devices: 37.8 us -> 30 us
  other arithmetic: 4.71 us -> 2.84 us
    ppermute x15 -> x22, waiting for transfers between devices: 28.3 us -> 14.8 us  [swap(): return lax.ppermute(value, AXES, pairs)]
    ppermute x16 -> x11, starting transfers between devices: 29.9 us -> 17.4 us  [swap_by_core(): return lax.ppermute(value, AXES, pairs)]
    pallas_call x11 -> x25, Pallas kernels: 39.1 us -> 47.5 us  [kernel_call(): pl.pallas_call(run, out_shape=outs, in_specs=[SPECS[kind] for kind in spe...]
    unnamed x28 -> x0, local copies, waits for them, and re-layouts: 6.85 us -> none
    ppermute x15 -> x22, starting transfers between devices: 7.88 us -> 12.6 us  [swap(): return lax.ppermute(value, AXES, pairs)]
    ppermute x16 -> x11, waiting for transfers between devices: 24.8 us -> 27.9 us  [swap_by_core(): return lax.ppermute(value, AXES, pairs)]
    slice x9 -> x2, local copies, waits for them, and re-layouts: 1.87 us -> 0.11 us  [the longest x1 0.1 us: near_and_far(): near, far = (item[:half], place.swap(item[half:], z_mask))]
    convert_element_type x12 -> x0, other arithmetic: 1.52 us -> none  [the longest x8 1.4 us: reduce_part(): keep = (keep[:half].astype(F32) + got[:half].astype(F32)).astype(BF)]
  transfers between devices with their start and end apart: 31 -> 33, of which waited for: 15 -> 16; matrix products, arithmetic and copies ran while one was open for 4% -> 1% of each run, Pallas kernels for 16% -> 34%
where the time goes in v2:
time: 125 us; the launch traced here: 124 us
  Pallas kernels  47.5 us (38%)
  waiting for transfers between devices  42.7 us (34%)
  starting transfers between devices  30 us (24%)
  other arithmetic  2.84 us (2%)
    pallas_call x25, Pallas kernels, kernel_call(): pl.pallas_call(run, out_shape=outs, in_specs=[SPECS[kind] for kind in spe...  47.5 us
    ppermute x11, waiting for transfers between devices, swap_by_core(): return lax.ppermute(value, AXES, pairs)  27.9 us
    ppermute x11, starting transfers between devices, swap_by_core(): return lax.ppermute(value, AXES, pairs)  17.4 us
    ppermute x22, waiting for transfers between devices, swap(): return lax.ppermute(value, AXES, pairs)  14.8 us
    ppermute x22, starting transfers between devices, swap(): return lax.ppermute(value, AXES, pairs)  12.6 us
  transfers between devices with their start and end apart: 33, of which 16 were waited for; matrix products, arithmetic and copies ran while one was open for 1% of the time, Pallas kernels for 34%

profile of v2, /device:TPU:0, one launch (start us, length us, event | category | flops | bytes accessed | tf_op | source)
XLA Modules:
  0.0 124.1 jit_solution(11555122700898026110)
XLA Ops:
  0.6 0.7 pad_add_fusion.refs_0_
  1.4 1.6 %token_slice.1 = (bf16[64,768]{1,0:T(8,128)(2,1)S(1)}, bf16[64,768]{1,0:T(8,128)(2,1)S(1)}, bf16[2,64,768]{2,1,0:T(8,128)(2,1)S(1)}) custom-call(s32[6]{0:T(128)S(1)} %pad_add_fusion.refs_0_, bf16[2,2,64,768]{3,2,1,0:T(8,128)(2,1)} %bitcast.22), custom_call_target="tpu_custom_call" | custom-call | flops 1000 | bytes 1000 | tf_op jit(solution)/shard_map/token_slice/pallas_call | solution.py:734
  3.0 3.0 %collective-permute-start = (bf16[2,64,768]{2,1,0:T(8,128)(2,1)S(1)}, bf16[2,64,768]{2,1,0:T(8,128)(2,1)S(1)}, u32[]{:S(2)}, u32[]{:S(2)}) collective-permute-start(bf16[2,64,768]{2,1,0:T(8,128)(2,1)S(1)} %get-tuple-element.91), channel_id=1, source_target_pairs={{0,2},{1,3},{2,0},{3,1},{4,6},{5,7},{6,4},{7,5},{8,10},{9,11},{10,... | collective-permute-start | bytes 589832 | tf_op jit(solution)/shard_map/ppermute | solution.py:50
  6.0 2.4 %load.1 = (bf16[768,2304]{1,0:T(8,128)(2,1)S(1)}, bf16[768,768]{1,0:T(8,128)(2,1)S(1)}) custom-call(bf16[768,2304]{1,0:T(8,128)(2,1)} %refs_1_.8, bf16[768,768]{1,0:T(8,128)(2,1)} %refs_6_.3, bf16[64,768]{1,0:T(8,128)(2,1)S(1)} %get-tuple-element.90.refs_2_.refs_1_), custom_call_target="tpu_custom_call" | custom-call | flops 1000 | bytes 1000 | tf_op jit(solution)/shard_map/load/pallas_call | solution.py:734
  8.3 1.6 %cot_slice.1 = (bf16[2,64,768]{2,1,0:T(8,128)(2,1)S(1)}, bf16[2,64,768]{2,1,0:T(8,128)(2,1)S(1)}) custom-call(s32[6]{0:T(128)S(1)} %pad_add_fusion.refs_0_, bf16[2,2,64,768]{3,2,1,0:T(8,128)(2,1)} %bitcast.23, bf16[768,768]{1,0:T(8,128)(2,1)S(1)} %get-tuple-element.92.refs_2_.refs_11_), custom_call_target="tpu_custom_call" | custom-call | flops 1000 | bytes 1000 | tf_op jit(solution)/shard_map/cot_slice/pallas_call | solution.py:734
  10.1 0.8 collective-permute-done.refs_1_
  11.5 1.3 %collective-permute-done.2.refs_4_ = bf16[64,768]{1,0:T(8,128)(2,1)S(1)} collective-permute-done((bf16[64,768]{1,0:T(8,128)(2,1)S(1)}, bf16[64,768]{1,0:T(8,128)(2,1)S(1)}, u32[]{:S(2)}, u32[]{:S(2)}) %collective-permute-start.2) | collective-permute-done | bytes 98336 | tf_op jit(solution)/shard_map/ppermute | solution.py:50
  12.8 6.6 %attention.1 = (bf16[256,768]{1,0:T(8,128)(2,1)S(1)}, bf16[2,768,256]{2,1,0:T(8,128)(2,1)S(1)}, bf16[768,256]{1,0:T(8,128)(2,1)S(1)}, bf16[768,256]{1,0:T(8,128)...) custom-call(s32[6]{0:T(128)S(1)} %pad_add_fusion.refs_0_, ...), custom_call_target="tpu_custom_call" | custom-call | flops 1000 | bytes 1000 | tf_op jit(solution)/shard_map/attention/pallas_call | solution.py:734
  19.4 3.7 %hidden_send.1 = (bf16[768,256]{1,0:T(8,128)(2,1)S(1)}, bf16[256,768]{1,0:T(8,128)(2,1)S(1)}, bf16[2,256,768]{2,1,0:T(8,128)(2,1)S(1)}, bf16[2,256,768]{2,1,0:T(8,128)(2,1)S(1)}) custom-call(s32[6]{0:T(128)S(1)} %pad_add_fusion.refs_0_, f32[768]{0:T(1024)} %refs_5_.4, f32[768]{0:T(1024)} %refs_2_.2, f32[3072]{0:T(1024)} %refs_1_.7, ...), custom_call_target="tpu_custom_call" | custom-call | flops 1000 | bytes 1000 | tf_op jit(solution)/shard_map/hidden_send/pallas_call | solution.py:734
  24.3 1.8 %collective-permute-start.12 = (bf16[2,768,256]{2,1,0:T(8,128)(2,1)S(1)}, bf16[2,768,256]{2,1,0:T(8,128)(2,1)S(1)}, u32[]{:S(2)}, u32[]{:S(2)}) collective-permute-start(bf16[2,768,256]{2,1,0:T(8,128)(2,1)S(1)} %get-tuple-element.113.refs_2_.refs_1_), channel_id=1, source_target_pairs={{0,8},{1,9},{2,10},{3,11},{4,12},{5,13},{6,14},{7,15},{8,0},{9,1},... | collective-permute-start | bytes 2359304 | tf_op jit(solution)/shard_map/ppermute | solution.py:50
  26.1 3.4 %hidden_own.1 = (bf16[2,256,768]{2,1,0:T(8,128)(2,1)S(1)}, bf16[2,256,768]{2,1,0:T(8,128)(2,1)S(1)}, bf16[3072,768]{1,0:T(8,128)(2,1)S(1)}) custom-call(s32[6]{0:T(128)S(1)} %pad_add_fusion.refs_0_, f32[3072]{0:T(1024)} %refs_1_.7, bf16[3072,768]{1,0:T(8,128)(2,1)} %refs_2_.3, bf16[256,768]{1,0:T(8,128)(2,1)S(1)} %get-tuple-element.101.refs_3_, ...), custom_call_target="tpu_custom_call" | custom-call | flops 1000 | bytes 1000 | tf_op jit(solution)/shard_map/hidden_own/pallas_call | solution.py:734
  29.6 3.3 %down_terms.1 = (bf16[8,96,768]{2,1,0:T(8,128)(2,1)S(1)}, bf16[8,96,768]{2,1,0:T(8,128)(2,1)S(1)}, f32[1,768]{1,0:T(1,128)S(1)}) custom-call(s32[6]{0:T(128)S(1)} %pad_add_fusion.refs_0_, bf16[2,64,768]{2,1,0:T(8,128)(2,1)S(1)} %get-tuple-element.93.refs_2_.refs_1_, bf16[2,64,768]{2,1,0:T(8,128)(2,1)S(1)} %collective-permute-done.3.refs_6_.refs_2_, ...), custom_call_target="tpu_custom_call" | custom-call | flops 1000 | bytes 1000 | tf_op jit(solution)/shard_map/down_terms/pallas_call | solution.py:734
  32.9 1.6 %collective-permute-start.11 = (bf16[8,96,768]{2,1,0:T(8,128)(2,1)S(1)}, bf16[8,96,768]{2,1,0:T(8,128)(2,1)S(1)}, u32[]{:S(2)}, u32[]{:S(2)}) collective-permute-start(bf16[8,96,768]{2,1,0:T(8,128)(2,1)S(1)} %get-tuple-element.112), channel_id=1, source_target_pairs={{0,2},{1,5},{2,0},{3,7},{4,6},{5,1},{6,4},{7,3},{8,10},{9,13},{10,... | collective-permute-start | bytes 3538952 | tf_op jit(solution)/shard_map/ppermute | solution.py:54
  34.4 6.0 %hidden_back.1 = (bf16[2,256,768]{2,1,0:T(8,128)(2,1)S(1)}, bf16[2,256,768]{2,1,0:T(8,128)(2,1)S(1)}, f32[256,768]{1,0:T(8,128)S(1)}, bf16[8,96,256]{2,1,0:T(8,1...) custom-call(s32[6]{0:T(128)S(1)} %pad_add_fusion.refs_0_, ...), custom_call_target="tpu_custom_call" | custom-call | flops 1000 | bytes 1000 | tf_op jit(solution)/shard_map/hidden_back/pallas_call | solution.py:734
  41.1 2.9 %collective-permute-done.12.refs_10_.refs_3_ = bf16[2,768,256]{2,1,0:T(8,128)(2,1)S(1)} collective-permute-done((bf16[2,768,256]{2,1,0:T(8,128)(2,1)S(1)}, bf16[2,768,256]{2,1,0:T(8,128)(2,1)S(1)}, u32[]{:S(2)}, u32[]{:S(2)}) %collective-permute-start.12) | collective-permute-done | bytes 786464 | tf_op jit(solution)/shard_map/ppermute | solution.py:50
  44.0 3.9 %attention_back.1 = (bf16[8,384,256]{2,1,0:T(8,128)(2,1)S(1)}, bf16[768,2304]{1,0:T(8,128)(2,1)S(1)}) custom-call(s32[6]{0:T(128)S(1)} %pad_add_fusion.refs_0_, bf16[768,2304]{1,0:T(8,128)(2,1)} %refs_1_.8, bf16[2,768,256]{2,1,0:T(8,128)(2,1)S(1)} %get-tuple-element.113.refs_2_.refs_1_, bf16[768,256]{1,0:T(8,128)(2,1)S(1)} %get-tuple-element.114.refs_3_, ...), custom_call_target="tpu_custom_call" | custom-call | flops 1000 | bytes 1000 | tf_op jit(solution)/shard_map/attention_back/pallas_call | solution.py:734
  48.0 1.8 %collective-permute-start.18 = (bf16[4,384,256]{2,1,0:T(8,128)(2,1)S(1)}, bf16[4,384,256]{2,1,0:T(8,128)(2,1)S(1)}, u32[]{:S(2)}, u32[]{:S(2)}) collective-permute-start(bf16[4,384,256]{2,1,0:T(8,128)(2,1)S(1)} %get-tuple-element.166), channel_id=1, source_target_pairs={{0,8},{1,9},{2,10},{3,11},{4,12},{5,13},{6,14},{7,15},{8,0},{9,1},... | collective-permute-start | bytes 2359304 | tf_op jit(solution)/shard_map/ppermute | solution.py:50
  50.1 1.6 %collective-permute-start.22 = (bf16[4,96,768]{2,1,0:T(8,128)(2,1)S(1)}, bf16[4,96,768]{2,1,0:T(8,128)(2,1)S(1)}, u32[]{:S(2)}, u32[]{:S(2)}) collective-permute-start(bf16[4,96,768]{2,1,0:T(8,128)(2,1)S(1)} %get-tuple-element.136), channel_id=1, source_target_pairs={{0,4},{1,3},{2,6},{3,1},{4,0},{5,7},{6,2},{7,5},{8,12},{9,11},{10,... | collective-permute-start | bytes 1769480 | tf_op jit(solution)/shard_map/ppermute | solution.py:54
  51.6 1.7 %collective-permute-done.4.refs_2_ = bf16[768,256]{1,0:T(8,128)(2,1)S(1)} collective-permute-done((bf16[768,256]{1,0:T(8,128)(2,1)S(1)}, bf16[768,256]{1,0:T(8,128)(2,1)S(1)}, u32[]{:S(2)}, u32[]{:S(2)}) %collective-permute-start.4) | collective-permute-done | bytes 393248 | tf_op jit(solution)/shard_map/ppermute | solution.py:50
  53.4 2.5 %up_terms.1 = (bf16[8,192,384]{2,1,0:T(8,128)(2,1)S(1)}, bf16[8,192,384]{2,1,0:T(8,128)(2,1)S(1)}) custom-call(s32[6]{0:T(128)S(1)} %pad_add_fusion.refs_0_, bf16[768,256]{1,0:T(8,128)(2,1)S(1)} %get-tuple-element.105.refs_1_, bf16[768,256]{1,0:T(8,128)(2,1)S(1)} %collective-permute-done.4.refs_2_, bf16[2,256,768]{2,1,0:T(8,128)(2,1)S(1)} %get-tuple-element.109.refs_3_, ...), custom_call_target="tpu_custom_call" | custom-call | flops 1000 | bytes 1000 | tf_op jit(solution)/shard_map/up_terms/pallas_call | solution.py:734
  55.9 1.6 %collective-permute-start.25 = (bf16[8,192,384]{2,1,0:T(8,128)(2,1)S(1)}, bf16[8,192,384]{2,1,0:T(8,128)(2,1)S(1)}, u32[]{:S(2)}, u32[]{:S(2)}) collective-permute-start(bf16[8,192,384]{2,1,0:T(8,128)(2,1)S(1)} %get-tuple-element.141), channel_id=1, source_target_pairs={{0,2},{1,5},{2,0},{3,7},{4,6},{5,1},{6,4},{7,3},{8,10},{9,13},{10,... | collective-permute-start | bytes 3538952 | tf_op jit(solution)/shard_map/ppermute | solution.py:54
  57.5 2.0 %mixed.1 = (bf16[2,64,768]{2,1,0:T(8,128)(2,1)S(1)}, bf16[2,64,768]{2,1,0:T(8,128)(2,1)S(1)}) custom-call(s32[6]{0:T(128)S(1)} %pad_add_fusion.refs_0_, bf16[2,256,768]{2,1,0:T(8,128)(2,1)S(1)} %get-tuple-element.102.refs_5_.refs_1_, bf16[2,256,768]{2,1,0:T(8,128)(2,1)S(1)} %get-tuple-element.103.refs_2_, ...), custom_call_target="tpu_custom_call" | custom-call | flops 1000 | bytes 1000 | tf_op jit(solution)/shard_map/mixed/pallas_call | solution.py:734
  59.5 2.8 %first_back.1 = (bf16[2,64,768]{2,1,0:T(8,128)(2,1)S(1)}, bf16[2,64,768]{2,1,0:T(8,128)(2,1)S(1)}, f32[8,8,384]{2,1,0:T(8,128)S(1)}) custom-call(s32[6]{0:T(128)S(1)} %pad_add_fusion.refs_0_, f32[768]{0:T(1024)} %refs_1_.9, bf16[256,768]{1,0:T(8,128)(2,1)S(1)} %get-tuple-element.126.refs_2_, f32[256,768]{1,0:T(8,128)S(1)} %get-tuple-element.127.refs_3_, ...), custom_call_target="tpu_custom_call" | custom-call | flops 1000 | bytes 1000 | tf_op jit(solution)/shard_map/first_back/pallas_call | solution.py:734
  62.4 1.3 %collective-permute-done.20 = f32[8,8,384]{2,1,0:T(8,128)S(1)} collective-permute-done((f32[8,8,384]{2,1,0:T(8,128)S(1)}, f32[8,8,384]{2,1,0:T(8,128)S(1)}, u32[]{:S(2)}, u32[]{:S(2)}) %collective-permute-start.20) | collective-permute-done | bytes 98336 | tf_op jit(solution)/shard_map/ppermute | solution.py:50
  64.2 3.0 %collective-permute-done.18.refs_7_ = bf16[4,384,256]{2,1,0:T(8,128)(2,1)S(1)} collective-permute-done((bf16[4,384,256]{2,1,0:T(8,128)(2,1)S(1)}, bf16[4,384,256]{2,1,0:T(8,128)(2,1)S(1)}, u32[]{:S(2)}, u32[]{:S(2)}) %collective-permute-start.18) | collective-permute-done | bytes 786464 | tf_op jit(solution)/shard_map/ppermute | solution.py:50
  67.2 0.7 collective-permute-done.21
  68.6 0.9 collective-permute-done.17.refs_6_
  69.5 1.1 collective-permute-done.16.refs_4_
  70.6 1.1 collective-permute-done.19.refs_8_
  71.7 3.5 %mix_terms.1 = (bf16[4,208,384]{2,1,0:T(8,128)(2,1)S(1)}, bf16[4,208,384]{2,1,0:T(8,128)(2,1)S(1)}) custom-call(s32[6]{0:T(128)S(1)} %pad_add_fusion.refs_0_, bf16[2,768,256]{2,1,0:T(8,128)(2,1)S(1)} %get-tuple-element.113.refs_2_.refs_1_, bf16[2,768,256]{2,1,0:T(8,128)(2,1)S(1)} %collective-permute-done.15.refs_2_, ...), custom_call_target="tpu_custom_call" | custom-call | flops 1000 | bytes 1000 | tf_op jit(solution)/shard_map/mix_terms/pallas_call | solution.py:734
  75.3 2.0 %collective-permute-start.23 = (bf16[4,208,384]{2,1,0:T(8,128)(2,1)S(1)}, bf16[4,208,384]{2,1,0:T(8,128)(2,1)S(1)}, u32[]{:S(2)}, u32[]{:S(2)}) collective-permute-start(bf16[4,208,384]{2,1,0:T(8,128)(2,1)S(1)} %get-tuple-element.139), channel_id=1, source_target_pairs={{0,2},{1,5},{2,0},{3,7},{4,6},{5,1},{6,4},{7,3},{8,10},{9,13},{10,... | collective-permute-start | bytes 1916936 | tf_op jit(solution)/shard_map/ppermute | solution.py:54
  77.5 1.5 %collective-permute-start.27 = (bf16[4,192,384]{2,1,0:T(8,128)(2,1)S(1)}, bf16[4,192,384]{2,1,0:T(8,128)(2,1)S(1)}, u32[]{:S(2)}, u32[]{:S(2)}) collective-permute-start(bf16[4,192,384]{2,1,0:T(8,128)(2,1)S(1)} %get-tuple-element.146), channel_id=1, source_target_pairs={{0,4},{1,3},{2,6},{3,1},{4,0},{5,7},{6,2},{7,5},{8,12},{9,11},{10,... | collective-permute-start | bytes 1769480 | tf_op jit(solution)/shard_map/ppermute | solution.py:54
  79.0 1.6 %collective-permute-start.24 = (bf16[2,96,768]{2,1,0:T(8,128)(2,1)S(1)}, bf16[2,96,768]{2,1,0:T(8,128)(2,1)S(1)}, u32[]{:S(2)}, u32[]{:S(2)}) collective-permute-start(bf16[2,96,768]{2,1,0:T(8,128)(2,1)S(1)} %get-tuple-element.140), channel_id=1, source_target_pairs={{0,8},{1,9},{2,10},{3,11},{4,12},{5,13},{6,14},{7,15},{8,0},{9,1},... | collective-permute-start | bytes 884744 | tf_op jit(solution)/shard_map/ppermute | solution.py:54
  80.6 6.9 %collective-permute-done.24.refs_1_ = bf16[2,96,768]{2,1,0:T(8,128)(2,1)S(1)} collective-permute-done((bf16[2,96,768]{2,1,0:T(8,128)(2,1)S(1)}, bf16[2,96,768]{2,1,0:T(8,128)(2,1)S(1)}, u32[]{:S(2)}, u32[]{:S(2)}) %collective-permute-start.24) | collective-permute-done | bytes 294944 | tf_op jit(solution)/shard_map/ppermute | solution.py:54
  87.5 4.0 %collective-permute-done.23.refs_1_ = bf16[4,208,384]{2,1,0:T(8,128)(2,1)S(1)} collective-permute-done((bf16[4,208,384]{2,1,0:T(8,128)(2,1)S(1)}, bf16[4,208,384]{2,1,0:T(8,128)(2,1)S(1)}, u32[]{:S(2)}, u32[]{:S(2)}) %collective-permute-start.23) | collective-permute-done | bytes 639008 | tf_op jit(solution)/shard_map/ppermute | solution.py:54
  91.7 2.0 %collective-permute-start.26 = (bf16[2,208,384]{2,1,0:T(8,128)(2,1)S(1)}, bf16[2,208,384]{2,1,0:T(8,128)(2,1)S(1)}, u32[]{:S(2)}, u32[]{:S(2)}) collective-permute-start(bf16[2,208,384]{2,1,0:T(8,128)(2,1)S(1)} %get-tuple-element.145), channel_id=1, source_target_pairs={{0,4},{1,3},{2,6},{3,1},{4,0},{5,7},{6,2},{7,5},{8,12},{9,11},{10,... | collective-permute-start | bytes 958472 | tf_op jit(solution)/shard_map/ppermute | solution.py:54
  94.4 1.8 %collective-permute-start.29 = (bf16[2,192,384]{2,1,0:T(8,128)(2,1)S(1)}, bf16[2,192,384]{2,1,0:T(8,128)(2,1)S(1)}, u32[]{:S(2)}, u32[]{:S(2)}) collective-permute-start(bf16[2,192,384]{2,1,0:T(8,128)(2,1)S(1)} %get-tuple-element.149), channel_id=1, source_target_pairs={{0,8},{1,9},{2,10},{3,11},{4,12},{5,13},{6,14},{7,15},{8,0},{9,1},... | collective-permute-start | bytes 884744 | tf_op jit(solution)/shard_map/ppermute | solution.py:54
  96.2 2.6 %collective-permute-done.26.refs_1_ = bf16[2,208,384]{2,1,0:T(8,128)(2,1)S(1)} collective-permute-done((bf16[2,208,384]{2,1,0:T(8,128)(2,1)S(1)}, bf16[2,208,384]{2,1,0:T(8,128)(2,1)S(1)}, u32[]{:S(2)}, u32[]{:S(2)}) %collective-permute-start.26) | collective-permute-done | bytes 319520 | tf_op jit(solution)/shard_map/ppermute | solution.py:54
  98.9 2.5 %collective-permute-start.28 = (bf16[4,64,768]{2,1,0:T(8,128)(2,1)S(1)}, bf16[4,64,768]{2,1,0:T(8,128)(2,1)S(1)}, u32[]{:S(2)}, u32[]{:S(2)}) collective-permute-start(bf16[4,64,768]{2,1,0:T(8,128)(2,1)S(1)} %gather.1), channel_id=1, source_target_pairs={{0,2},{1,3},{2,0},{3,1},{4,6},{5,7},{6,4},{7,5},{8,10},{9,11},{10,... | collective-permute-start | bytes 1179656 | tf_op jit(solution)/shard_map/ppermute | solution.py:50
  101.3 2.3 %collective-permute-start.32 = (bf16[1,96,768]{2,1,0:T(8,128)(2,1)S(1)}, bf16[1,96,768]{2,1,0:T(8,128)(2,1)S(1)}, u32[]{:S(2)}, u32[]{:S(2)}) collective-permute-start(bf16[1,96,768]{2,1,0:T(8,128)(2,1)S(1)} %get-tuple-element.164), channel_id=1, source_target_pairs={{0,16},{1,17},{2,18},{3,19},{4,20},{5,21},{6,22},{7,23},{8,24},{9,... | collective-permute-start | bytes 442376 | tf_op jit(solution)/shard_map/ppermute | solution.py:54
  104.3 1.8 %collective-permute-done.29.refs_1_ = bf16[2,192,384]{2,1,0:T(8,128)(2,1)S(1)} collective-permute-done((bf16[2,192,384]{2,1,0:T(8,128)(2,1)S(1)}, bf16[2,192,384]{2,1,0:T(8,128)(2,1)S(1)}, u32[]{:S(2)}, u32[]{:S(2)}) %collective-permute-start.29) | collective-permute-done | bytes 294944 | tf_op jit(solution)/shard_map/ppermute | solution.py:54
  106.1 1.0 collective-permute-start.31
  107.1 11.0 %collective-permute-done.32 = bf16[1,96,768]{2,1,0:T(8,128)(2,1)S(1)} collective-permute-done((bf16[1,96,768]{2,1,0:T(8,128)(2,1)S(1)}, bf16[1,96,768]{2,1,0:T(8,128)(2,1)S(1)}, u32[]{:S(2)}, u32[]{:S(2)}) %collective-permute-start.32) | collective-permute-done | bytes 147488 | tf_op jit(solution)/shard_map/ppermute | solution.py:54
  118.1 0.7 add_bitcast_fusion
  118.8 1.6 %collective-permute-done.30.refs_1_ = bf16[1,208,384]{2,1,0:T(8,128)(2,1)S(1)} collective-permute-done((bf16[1,208,384]{2,1,0:T(8,128)(2,1)S(1)}, bf16[1,208,384]{2,1,0:T(8,128)(2,1)S(1)}, u32[]{:S(2)}, u32[]{:S(2)}) %collective-permute-start.30) | collective-permute-done | bytes 159776 | tf_op jit(solution)/shard_map/ppermute | solution.py:54
  120.5 0.8 mix_end.1
  121.9 1.5 %place.1 = (bf16[256,768]{1,0:T(8,128)(2,1)}, bf16[256,768]{1,0:T(8,128)(2,1)}) custom-call(s32[6]{0:T(128)S(1)} %pad_add_fusion.refs_0_, bf16[2,64,768]{2,1,0:T(8,128)(2,1)S(1)} %get-tuple-element.124.refs_11_.refs_0_.refs_1_, bf16[2,64,768]{2,1,0:T(8,128)(2,1)S(1)} %collective-permute-done.13.refs_1_.refs_2_, ...), custom_call_target="tpu_custom_call" | custom-call | flops 1000 | bytes 1000 | tf_op jit(solution)/shard_map/place/pallas_call | solution.py:734
  123.4 0.7 add_bitcast_fusion.1
  (52 shorter events, 6.7 us)
Async XLA Ops:
  3.0 7.9 %collective-permute-start = (bf16[2,64,768]{2,1,0:T(8,128)(2,1)S(1)}, bf16[2,64,768]{2,1,0:T(8,128)(2,1)S(1)}, u32[]{:S(2)}, u32[]{:S(2)}) collective-permute-start(bf16[2,64,768]{2,1,0:T(8,128)(2,1)S(1)} %get-tuple-element.91), channel_id=1, source_target_pairs={{0,2},{1,3},{2,0},{3,1},{4,6},{5,7},{6,4},{7,5},{8,10},{9,11},{10,... | collective-permute-start | bytes 589832 | tf_op jit(solution)/shard_map/ppermute | solution.py:50
  9.9 9.4 %collective-permute-start.3 = (bf16[2,64,768]{2,1,0:T(8,128)(2,1)S(1)}, bf16[2,64,768]{2,1,0:T(8,128)(2,1)S(1)}, u32[]{:S(2)}, u32[]{:S(2)}) collective-permute-start(bf16[2,64,768]{2,1,0:T(8,128)(2,1)S(1)} %get-tuple-element.100), channel_id=1, source_target_pairs={{0,2},{1,3},{2,0},{3,1},{4,6},{5,7},{6,4},{7,5},{8,10},{9,11},{10,... | collective-permute-start | bytes 589832 | tf_op jit(solution)/shard_map/ppermute | solution.py:50
  10.0 1.5 %collective-permute-start.1 = (bf16[64,768]{1,0:T(8,128)(2,1)S(1)}, bf16[64,768]{1,0:T(8,128)(2,1)S(1)}, u32[]{:S(2)}, u32[]{:S(2)}) collective-permute-start(bf16[64,768]{1,0:T(8,128)(2,1)S(1)} %get-tuple-element.95), channel_id=1, source_target_pairs={{0,1},{1,0},{2,3},{3,2},{4,5},{5,4},{6,7},{7,6},{8,9},{9,8},{10,11... | collective-permute-start | bytes 294920 | tf_op jit(solution)/shard_map/ppermute | solution.py:50
  11.5 1.4 %collective-permute-start.2 = (bf16[64,768]{1,0:T(8,128)(2,1)S(1)}, bf16[64,768]{1,0:T(8,128)(2,1)S(1)}, u32[]{:S(2)}, u32[]{:S(2)}) collective-permute-start(bf16[64,768]{1,0:T(8,128)(2,1)S(1)} %get-tuple-element.96), channel_id=1, source_target_pairs={{0,1},{1,0},{2,3},{3,2},{4,5},{5,4},{6,7},{7,6},{8,9},{9,8},{10,11... | collective-permute-start | bytes 294920 | tf_op jit(solution)/shard_map/ppermute | solution.py:50
  23.2 6.4 %collective-permute-start.7 = (bf16[256,768]{1,0:T(8,128)(2,1)S(1)}, bf16[256,768]{1,0:T(8,128)(2,1)S(1)}, u32[]{:S(2)}, u32[]{:S(2)}) collective-permute-start(bf16[256,768]{1,0:T(8,128)(2,1)S(1)} %get-tuple-element.169), channel_id=1, source_target_pairs={{0,1},{1,0},{2,3},{3,2},{4,5},{5,4},{6,7},{7,6},{8,9},{9,8},{10,11... | collective-permute-start | bytes 1179656 | tf_op jit(solution)/shard_map/ppermute | solution.py:50
  23.4 6.2 %collective-permute-start.8 = (bf16[256,768]{1,0:T(8,128)(2,1)S(1)}, bf16[256,768]{1,0:T(8,128)(2,1)S(1)}, u32[]{:S(2)}, u32[]{:S(2)}) collective-permute-start(bf16[256,768]{1,0:T(8,128)(2,1)S(1)} %get-tuple-element.168), channel_id=1, source_target_pairs={{0,1},{1,0},{2,3},{3,2},{4,5},{5,4},{6,7},{7,6},{8,9},{9,8},{10,11... | collective-permute-start | bytes 1179656 | tf_op jit(solution)/shard_map/ppermute | solution.py:50
  23.8 5.8 %collective-permute-start.5 = (bf16[2,64,768]{2,1,0:T(8,128)(2,1)S(1)}, bf16[2,64,768]{2,1,0:T(8,128)(2,1)S(1)}, u32[]{:S(2)}, u32[]{:S(2)}) collective-permute-start(bf16[2,64,768]{2,1,0:T(8,128)(2,1)S(1)} %get-tuple-element.93.refs_2_.refs_1_), channel_id=1, source_target_pairs={{0,1},{1,0},{2,3},{3,2},{4,5},{5,4},{6,7},{7,6},{8,9},{9,8},{10,11... | collective-permute-start | bytes 589832 | tf_op jit(solution)/shard_map/ppermute | solution.py:50
  23.9 5.6 %collective-permute-start.6 = (bf16[2,64,768]{2,1,0:T(8,128)(2,1)S(1)}, bf16[2,64,768]{2,1,0:T(8,128)(2,1)S(1)}, u32[]{:S(2)}, u32[]{:S(2)}) collective-permute-start(bf16[2,64,768]{2,1,0:T(8,128)(2,1)S(1)} %collective-permute-done.3.refs_6_.refs_2_), channel_id=1, source_target_pairs={{0,1},{1,0},{2,3},{3,2},{4,5},{5,4},{6,7},{7,6},{8,9},{9,8},{10,11... | collective-permute-start | bytes 589832 | tf_op jit(solution)/shard_map/ppermute | solution.py:50
  24.3 19.7 %collective-permute-start.12 = (bf16[2,768,256]{2,1,0:T(8,128)(2,1)S(1)}, bf16[2,768,256]{2,1,0:T(8,128)(2,1)S(1)}, u32[]{:S(2)}, u32[]{:S(2)}) collective-permute-start(bf16[2,768,256]{2,1,0:T(8,128)(2,1)S(1)} %get-tuple-element.113.refs_2_.refs_1_), channel_id=1, source_target_pairs={{0,8},{1,9},{2,10},{3,11},{4,12},{5,13},{6,14},{7,15},{8,0},{9,1},... | collective-permute-start | bytes 2359304 | tf_op jit(solution)/shard_map/ppermute | solution.py:50
  32.9 16.9 %collective-permute-start.11 = (bf16[8,96,768]{2,1,0:T(8,128)(2,1)S(1)}, bf16[8,96,768]{2,1,0:T(8,128)(2,1)S(1)}, u32[]{:S(2)}, u32[]{:S(2)}) collective-permute-start(bf16[8,96,768]{2,1,0:T(8,128)(2,1)S(1)} %get-tuple-element.112), channel_id=1, source_target_pairs={{0,2},{1,5},{2,0},{3,7},{4,6},{5,1},{6,4},{7,3},{8,10},{9,13},{10,... | collective-permute-start | bytes 3538952 | tf_op jit(solution)/shard_map/ppermute | solution.py:54
  40.5 12.9 %collective-permute-start.10 = (bf16[2,256,768]{2,1,0:T(8,128)(2,1)S(1)}, bf16[2,256,768]{2,1,0:T(8,128)(2,1)S(1)}, u32[]{:S(2)}, u32[]{:S(2)}) collective-permute-start(bf16[2,256,768]{2,1,0:T(8,128)(2,1)S(1)} %get-tuple-element.110.refs_4_), channel_id=1, source_target_pairs={{0,1},{1,0},{2,3},{3,2},{4,5},{5,4},{6,7},{7,6},{8,9},{9,8},{10,11... | collective-permute-start | bytes 2359304 | tf_op jit(solution)/shard_map/ppermute | solution.py:50
  40.6 12.8 %collective-permute-start.9 = (bf16[2,256,768]{2,1,0:T(8,128)(2,1)S(1)}, bf16[2,256,768]{2,1,0:T(8,128)(2,1)S(1)}, u32[]{:S(2)}, u32[]{:S(2)}) collective-permute-start(bf16[2,256,768]{2,1,0:T(8,128)(2,1)S(1)} %get-tuple-element.109.refs_3_), channel_id=1, source_target_pairs={{0,1},{1,0},{2,3},{3,2},{4,5},{5,4},{6,7},{7,6},{8,9},{9,8},{10,11... | collective-permute-start | bytes 2359304 | tf_op jit(solution)/shard_map/ppermute | solution.py:50
  48.0 19.2 %collective-permute-start.18 = (bf16[4,384,256]{2,1,0:T(8,128)(2,1)S(1)}, bf16[4,384,256]{2,1,0:T(8,128)(2,1)S(1)}, u32[]{:S(2)}, u32[]{:S(2)}) collective-permute-start(bf16[4,384,256]{2,1,0:T(8,128)(2,1)S(1)} %get-tuple-element.166), channel_id=1, source_target_pairs={{0,8},{1,9},{2,10},{3,11},{4,12},{5,13},{6,14},{7,15},{8,0},{9,1},... | collective-permute-start | bytes 2359304 | tf_op jit(solution)/shard_map/ppermute | solution.py:50
  50.1 17.9 %collective-permute-start.22 = (bf16[4,96,768]{2,1,0:T(8,128)(2,1)S(1)}, bf16[4,96,768]{2,1,0:T(8,128)(2,1)S(1)}, u32[]{:S(2)}, u32[]{:S(2)}) collective-permute-start(bf16[4,96,768]{2,1,0:T(8,128)(2,1)S(1)} %get-tuple-element.136), channel_id=1, source_target_pairs={{0,4},{1,3},{2,6},{3,1},{4,0},{5,7},{6,2},{7,5},{8,12},{9,11},{10,... | collective-permute-start | bytes 1769480 | tf_op jit(solution)/shard_map/ppermute | solution.py:54
  51.6 1.7 %collective-permute-start.4 = (bf16[768,256]{1,0:T(8,128)(2,1)S(1)}, bf16[768,256]{1,0:T(8,128)(2,1)S(1)}, u32[]{:S(2)}, u32[]{:S(2)}) collective-permute-start(bf16[768,256]{1,0:T(8,128)(2,1)S(1)} %get-tuple-element.105.refs_1_), channel_id=1, source_target_pairs={{0,1},{1,0},{2,3},{3,2},{4,5},{5,4},{6,7},{7,6},{8,9},{9,8},{10,11... | collective-permute-start | bytes 1179656 | tf_op jit(solution)/shard_map/ppermute | solution.py:50
  55.9 21.3 %collective-permute-start.25 = (bf16[8,192,384]{2,1,0:T(8,128)(2,1)S(1)}, bf16[8,192,384]{2,1,0:T(8,128)(2,1)S(1)}, u32[]{:S(2)}, u32[]{:S(2)}) collective-permute-start(bf16[8,192,384]{2,1,0:T(8,128)(2,1)S(1)} %get-tuple-element.141), channel_id=1, source_target_pairs={{0,2},{1,5},{2,0},{3,7},{4,6},{5,1},{6,4},{7,3},{8,10},{9,13},{10,... | collective-permute-start | bytes 3538952 | tf_op jit(solution)/shard_map/ppermute | solution.py:54
  62.3 1.4 %collective-permute-start.20 = (f32[8,8,384]{2,1,0:T(8,128)S(1)}, f32[8,8,384]{2,1,0:T(8,128)S(1)}, u32[]{:S(2)}, u32[]{:S(2)}) collective-permute-start(f32[8,8,384]{2,1,0:T(8,128)S(1)} %get-tuple-element.135), channel_id=1, source_target_pairs={{0,1},{1,0},{2,3},{3,2},{4,5},{5,4},{6,7},{7,6},{8,9},{9,8},{10,11... | collective-permute-start | bytes 294920 | tf_op jit(solution)/shard_map/ppermute | solution.py:50
  63.7 4.2 %collective-permute-start.21 = (f32[4,8,384]{2,1,0:T(8,128)S(1)}, f32[4,8,384]{2,1,0:T(8,128)S(1)}, u32[]{:S(2)}, u32[]{:S(2)}) collective-permute-start(f32[4,8,384]{2,1,0:T(8,128)S(1)} %slice.25), channel_id=1, source_target_pairs={{0,8},{1,9},{2,10},{3,11},{4,12},{5,13},{6,14},{7,15},{8,0},{9,1},... | collective-permute-start | bytes 147464 | tf_op jit(solution)/shard_map/ppermute | solution.py:50
  64.2 4.4 %collective-permute-start.15 = (bf16[2,768,256]{2,1,0:T(8,128)(2,1)S(1)}, bf16[2,768,256]{2,1,0:T(8,128)(2,1)S(1)}, u32[]{:S(2)}, u32[]{:S(2)}) collective-permute-start(bf16[2,768,256]{2,1,0:T(8,128)(2,1)S(1)} %get-tuple-element.113.refs_2_.refs_1_), channel_id=1, source_target_pairs={{0,1},{1,0},{2,3},{3,2},{4,5},{5,4},{6,7},{7,6},{8,9},{9,8},{10,11... | collective-permute-start | bytes 2359304 | tf_op jit(solution)/shard_map/ppermute | solution.py:50
  67.2 2.3 %collective-permute-start.17 = (bf16[4,384,256]{2,1,0:T(8,128)(2,1)S(1)}, bf16[4,384,256]{2,1,0:T(8,128)(2,1)S(1)}, u32[]{:S(2)}, u32[]{:S(2)}) collective-permute-start(bf16[4,384,256]{2,1,0:T(8,128)(2,1)S(1)} %get-tuple-element.167.refs_5_), channel_id=1, source_target_pairs={{0,1},{1,0},{2,3},{3,2},{4,5},{5,4},{6,7},{7,6},{8,9},{9,8},{10,11... | collective-permute-start | bytes 2359304 | tf_op jit(solution)/shard_map/ppermute | solution.py:50
  68.0 2.7 %collective-permute-start.16 = (bf16[2,768,256]{2,1,0:T(8,128)(2,1)S(1)}, bf16[2,768,256]{2,1,0:T(8,128)(2,1)S(1)}, u32[]{:S(2)}, u32[]{:S(2)}) collective-permute-start(bf16[2,768,256]{2,1,0:T(8,128)(2,1)S(1)} %collective-permute-done.12.refs_10_.refs_3_), channel_id=1, source_target_pairs={{0,1},{1,0},{2,3},{3,2},{4,5},{5,4},{6,7},{7,6},{8,9},{9,8},{10,11... | collective-permute-start | bytes 2359304 | tf_op jit(solution)/shard_map/ppermute | solution.py:50
  68.0 3.8 %collective-permute-start.19 = (bf16[4,384,256]{2,1,0:T(8,128)(2,1)S(1)}, bf16[4,384,256]{2,1,0:T(8,128)(2,1)S(1)}, u32[]{:S(2)}, u32[]{:S(2)}) collective-permute-start(bf16[4,384,256]{2,1,0:T(8,128)(2,1)S(1)} %collective-permute-done.18.refs_7_), channel_id=1, source_target_pairs={{0,1},{1,0},{2,3},{3,2},{4,5},{5,4},{6,7},{7,6},{8,9},{9,8},{10,11... | collective-permute-start | bytes 2359304 | tf_op jit(solution)/shard_map/ppermute | solution.py:50
  75.3 16.3 %collective-permute-start.23 = (bf16[4,208,384]{2,1,0:T(8,128)(2,1)S(1)}, bf16[4,208,384]{2,1,0:T(8,128)(2,1)S(1)}, u32[]{:S(2)}, u32[]{:S(2)}) collective-permute-start(bf16[4,208,384]{2,1,0:T(8,128)(2,1)S(1)} %get-tuple-element.139), channel_id=1, source_target_pairs={{0,2},{1,5},{2,0},{3,7},{4,6},{5,1},{6,4},{7,3},{8,10},{9,13},{10,... | collective-permute-start | bytes 1916936 | tf_op jit(solution)/shard_map/ppermute | solution.py:54
  77.5 16.7 %collective-permute-start.27 = (bf16[4,192,384]{2,1,0:T(8,128)(2,1)S(1)}, bf16[4,192,384]{2,1,0:T(8,128)(2,1)S(1)}, u32[]{:S(2)}, u32[]{:S(2)}) collective-permute-start(bf16[4,192,384]{2,1,0:T(8,128)(2,1)S(1)} %get-tuple-element.146), channel_id=1, source_target_pairs={{0,4},{1,3},{2,6},{3,1},{4,0},{5,7},{6,2},{7,5},{8,12},{9,11},{10,... | collective-permute-start | bytes 1769480 | tf_op jit(solution)/shard_map/ppermute | solution.py:54
  79.0 8.5 %collective-permute-start.24 = (bf16[2,96,768]{2,1,0:T(8,128)(2,1)S(1)}, bf16[2,96,768]{2,1,0:T(8,128)(2,1)S(1)}, u32[]{:S(2)}, u32[]{:S(2)}) collective-permute-start(bf16[2,96,768]{2,1,0:T(8,128)(2,1)S(1)} %get-tuple-element.140), channel_id=1, source_target_pairs={{0,8},{1,9},{2,10},{3,11},{4,12},{5,13},{6,14},{7,15},{8,0},{9,1},... | collective-permute-start | bytes 884744 | tf_op jit(solution)/shard_map/ppermute | solution.py:54
  91.7 7.1 %collective-permute-start.26 = (bf16[2,208,384]{2,1,0:T(8,128)(2,1)S(1)}, bf16[2,208,384]{2,1,0:T(8,128)(2,1)S(1)}, u32[]{:S(2)}, u32[]{:S(2)}) collective-permute-start(bf16[2,208,384]{2,1,0:T(8,128)(2,1)S(1)} %get-tuple-element.145), channel_id=1, source_target_pairs={{0,4},{1,3},{2,6},{3,1},{4,0},{5,7},{6,2},{7,5},{8,12},{9,11},{10,... | collective-permute-start | bytes 958472 | tf_op jit(solution)/shard_map/ppermute | solution.py:54
  93.7 5.1 %collective-permute-start.14 = (bf16[2,64,768]{2,1,0:T(8,128)(2,1)S(1)}, bf16[2,64,768]{2,1,0:T(8,128)(2,1)S(1)}, u32[]{:S(2)}, u32[]{:S(2)}) collective-permute-start(bf16[2,64,768]{2,1,0:T(8,128)(2,1)S(1)} %get-tuple-element.134), channel_id=1, source_target_pairs={{0,1},{1,0},{2,3},{3,2},{4,5},{5,4},{6,7},{7,6},{8,9},{9,8},{10,11... | collective-permute-start | bytes 589832 | tf_op jit(solution)/shard_map/ppermute | solution.py:50
  93.7 5.1 %collective-permute-start.13 = (bf16[2,64,768]{2,1,0:T(8,128)(2,1)S(1)}, bf16[2,64,768]{2,1,0:T(8,128)(2,1)S(1)}, u32[]{:S(2)}, u32[]{:S(2)}) collective-permute-start(bf16[2,64,768]{2,1,0:T(8,128)(2,1)S(1)} %get-tuple-element.125), channel_id=1, source_target_pairs={{0,1},{1,0},{2,3},{3,2},{4,5},{5,4},{6,7},{7,6},{8,9},{9,8},{10,11... | collective-permute-start | bytes 589832 | tf_op jit(solution)/shard_map/ppermute | solution.py:50
  94.4 11.7 %collective-permute-start.29 = (bf16[2,192,384]{2,1,0:T(8,128)(2,1)S(1)}, bf16[2,192,384]{2,1,0:T(8,128)(2,1)S(1)}, u32[]{:S(2)}, u32[]{:S(2)}) collective-permute-start(bf16[2,192,384]{2,1,0:T(8,128)(2,1)S(1)} %get-tuple-element.149), channel_id=1, source_target_pairs={{0,8},{1,9},{2,10},{3,11},{4,12},{5,13},{6,14},{7,15},{8,0},{9,1},... | collective-permute-start | bytes 884744 | tf_op jit(solution)/shard_map/ppermute | solution.py:54
  98.9 23.0 %collective-permute-start.28 = (bf16[4,64,768]{2,1,0:T(8,128)(2,1)S(1)}, bf16[4,64,768]{2,1,0:T(8,128)(2,1)S(1)}, u32[]{:S(2)}, u32[]{:S(2)}) collective-permute-start(bf16[4,64,768]{2,1,0:T(8,128)(2,1)S(1)} %gather.1), channel_id=1, source_target_pairs={{0,2},{1,3},{2,0},{3,1},{4,6},{5,7},{6,4},{7,5},{8,10},{9,11},{10,... | collective-permute-start | bytes 1179656 | tf_op jit(solution)/shard_map/ppermute | solution.py:50
  101.3 16.8 %collective-permute-start.32 = (bf16[1,96,768]{2,1,0:T(8,128)(2,1)S(1)}, bf16[1,96,768]{2,1,0:T(8,128)(2,1)S(1)}, u32[]{:S(2)}, u32[]{:S(2)}) collective-permute-start(bf16[1,96,768]{2,1,0:T(8,128)(2,1)S(1)} %get-tuple-element.164), channel_id=1, source_target_pairs={{0,16},{1,17},{2,18},{3,19},{4,20},{5,21},{6,22},{7,23},{8,24},{9,... | collective-permute-start | bytes 442376 | tf_op jit(solution)/shard_map/ppermute | solution.py:54
  103.7 16.8 %collective-permute-start.30 = (bf16[1,208,384]{2,1,0:T(8,128)(2,1)S(1)}, bf16[1,208,384]{2,1,0:T(8,128)(2,1)S(1)}, u32[]{:S(2)}, u32[]{:S(2)}) collective-permute-start(bf16[1,208,384]{2,1,0:T(8,128)(2,1)S(1)} %get-tuple-element.153), channel_id=1, source_target_pairs={{0,16},{1,17},{2,18},{3,19},{4,20},{5,21},{6,22},{7,23},{8,24},{9,... | collective-permute-start | bytes 479240 | tf_op jit(solution)/shard_map/ppermute | solution.py:54
  106.1 17.2 %collective-permute-start.31 = (bf16[1,192,384]{2,1,0:T(8,128)(2,1)S(1)}, bf16[1,192,384]{2,1,0:T(8,128)(2,1)S(1)}, u32[]{:S(2)}, u32[]{:S(2)}) collective-permute-start(bf16[1,192,384]{2,1,0:T(8,128)(2,1)S(1)} %get-tuple-element.162), channel_id=1, source_target_pairs={{0,16},{1,17},{2,18},{3,19},{4,20},{5,21},{6,22},{7,23},{8,24},{9,... | collective-permute-start | bytes 442376 | tf_op jit(solution)/shard_map/ppermute | solution.py:54

commit v3 on v2

--- a/solution.py
+++ b/solution.py
@@ -18,8 +18,9 @@
 eps = 1e-06
 neg_big = -1e30
 
-ORDER = ((0, 1, 2, 3), (1, 0, 2, 3))
-MIX_ORDER = ((0, 1, 3), (1, 0, 3))
+DOWN_ORDER = ((1, 2, 3), (1, 2, 3))
+UP_ORDER = ((0, 2, 3), (0, 2, 3))
+MIX_ORDER = ((0, 1), (1, 0))
 
 
 def mat(left, right):
@@ -63,7 +64,7 @@
     return jnp.where(size == 0, 25, jnp.where(size == 1, 49, 64))
 
 
-def spot_of(at_ref, owner_x, owner_group, order=ORDER):
+def spot_of(at_ref, owner_x, owner_group, order):
     group = at_ref[1]
     here = (at_ref[0] >> 1, group & 1, (group >> 1) & 1, group >> 2)
     there = (owner_x, owner_group & 1, (owner_group >> 1) & 1, owner_group >> 2)
@@ -77,8 +78,8 @@
 
 
 def near_first(at_ref, group):
-    differ = ((at_ref[1] ^ group) >> 1) & 1
-    return differ * 4 + (group & 1) + 2 * (group >> 2)
+    differ = at_ref[1] ^ group
+    return ((differ >> 1) & 1) * 4 + (differ >> 2) * 2 + (group & 1)
 
 
 def live_rows(rows, chunk, live):
@@ -116,13 +117,20 @@
     return value * share, share + value * tail * 0.3989422804014327
 
 
-def slot_copies(refs, core, target_ref, sems, first, partner=False):
-    order = (refs[2], refs[3], refs[0], refs[1]) if partner else refs
-    which = 1 - core if partner else core
-    return [
-        pltpu.make_async_copy(ref.at[which], target_ref.at[index], sems.at[first + index])
-        for index, ref in enumerate(order)
+RELATIVE = ((0, 0), (1, 0), (0, 1), (1, 1))
+
+
+def slot_cots(at_ref, refs, device):
+    size = refs[0].shape[0] // 4
+    far, other = RELATIVE[device]
+    slot = at_ref[0] ^ (2 * far + other)
+    spots = pl.ds(pl.multiple_of(slot * size, size), size)
+    sources = [
+        refs[RELATIVE.index((far ^ from_far, other ^ from_other))] for from_far, from_other in RELATIVE
     ]
+    rows = jnp.concatenate([ref[spots, :] for ref in sources], axis=0)
+    live = live_rows(rows.shape[0], size, live_of(at_ref, slot))
+    return jnp.where(live, rows, jnp.zeros((), BF))
 
 
 def copy_all(sources, targets, sems):
@@ -146,11 +154,6 @@
     other_ref[...] = far_ref[1 - core]
 
 
-def cot_slice_kernel(at_ref, cot_hbm, near_ref, far_ref, sems):
-    x_at = at_ref[0] >> 1
-    copy_all([cot_hbm.at[x_at], cot_hbm.at[1 - x_at]], [near_ref, far_ref], sems)
-
-
 def start_all(copies):
     for copy in copies:
         copy.start()
@@ -159,10 +162,6 @@
 def wait_all(copies):
     for copy in copies:
         copy.wait()
-
-
-def flat_rows(ref):
-    return ref[...].reshape(ref.shape[0] * ref.shape[1], ref.shape[2])
 
 
 def load_kernel(*refs):
@@ -182,11 +181,11 @@
     far_ref,
     near_other_ref,
     far_other_ref,
-    gain1_hbm,
-    bias1_hbm,
-    qv_bias_hbm,
-    proj_bias_hbm,
     up_hbm,
+    gain1_ref,
+    bias1_ref,
+    qv_bias_ref,
+    proj_bias_ref,
     qkv_ref,
     proj_ref,
     row_ref,
@@ -198,38 +197,18 @@
     scale_ref,
     resid_ref,
     up_ref,
-    rows_ref,
-    gain1_ref,
-    bias1_ref,
-    qv_bias_ref,
-    proj_bias_ref,
     sems,
 ):
-    row_copies = [
-        pltpu.make_async_copy(source, rows_ref.at[index], sems.at[index])
-        for index, source in enumerate([near_ref, far_ref, near_other_ref, far_other_ref])
-    ]
-    start_all(row_copies)
-    vectors = [
-        (gain1_hbm, gain1_ref),
-        (bias1_hbm, bias1_ref),
-        (qv_bias_hbm, qv_bias_ref),
-        (proj_bias_hbm, proj_bias_ref),
-        (up_hbm, up_ref),
-    ]
-    vector_copies = [
-        pltpu.make_async_copy(source, target, sems.at[4 + index])
-        for index, (source, target) in enumerate(vectors)
-    ]
-    start_all(vector_copies)
+    up_copy = pltpu.make_async_copy(up_hbm, up_ref, sems.at[0])
+    up_copy.start()
     rows, width = row_ref.shape
     live = live_of(at_ref, at_ref[0])
-    wait_all(row_copies)
-    tokens = flat_rows(rows_ref)
+    tokens = jnp.concatenate(
+        [ref[...] for ref in (near_ref, far_ref, near_other_ref, far_other_ref)], axis=0
+    )
     row_ref[...] = tokens
     source = tokens.astype(F32)
     normed, _ = norm_parts(source)
-    wait_all(vector_copies[:4])
     normed = (normed * gain1_ref[...][None] + bias1_ref[...][None]).astype(BF)
     left_ref[0] = normed.T
     queries = mat(normed, qkv_ref[:, :width]) + qv_bias_ref[...][None, :width]
@@ -266,67 +245,52 @@
         left_ref[1, spots, :] = (total[:HEAD] * scale).astype(BF)
 
     resid_ref[...] = source + mat(left_ref[1].T, proj_ref[...]) + proj_bias_ref[...][None]
-    vector_copies[4].wait()
-
-
-def hidden_terms(at_ref, other, normed, up_ref, up_bias_ref, act_ref, slope_ref):
+    up_copy.wait()
+
+
+def hidden_terms(at_ref, far, other, normed, up_ref, up_bias_ref):
     width = normed.shape[1]
-    for owner_x in range(2):
-        quarter = 2 * owner_x + (core_of(at_ref) ^ other)
-        columns = pl.ds(pl.multiple_of(quarter * width, width), width)
-        before = mat(normed, up_ref[:, columns]) + up_bias_ref[columns][None]
-        act, slope = gelu_pair(before)
-        act_ref[owner_x] = act.astype(BF)
-        slope_ref[owner_x] = slope.astype(BF)
-
-
-def hidden_send_kernel(
+    quarter = at_ref[0] ^ (2 * far + other)
+    columns = pl.ds(pl.multiple_of(quarter * width, width), width)
+    act, slope = gelu_pair(mat(normed, up_ref[:, columns]) + up_bias_ref[columns][None])
+    return act.astype(BF), slope.astype(BF)
+
+
+def hidden_far_kernel(
     at_ref,
-    gain2_hbm,
-    bias2_hbm,
-    up_bias_hbm,
+    gain2_ref,
+    bias2_ref,
+    up_bias_ref,
     resid_ref,
     up_ref,
-    left_ref,
     normed_ref,
     act_ref,
     slope_ref,
-    gain2_ref,
-    bias2_ref,
+):
+    normed, _ = norm_parts(resid_ref[...])
+    normed = (normed * gain2_ref[...][None] + bias2_ref[...][None]).astype(BF)
+    normed_ref[...] = normed
+    for other in range(2):
+        act_ref[other], slope_ref[other] = hidden_terms(at_ref, 1, other, normed, up_ref, up_bias_ref)
+
+
+def hidden_near_kernel(
+    at_ref,
+    down_hbm,
     up_bias_ref,
+    normed_ref,
+    up_ref,
+    act_own_ref,
+    act_other_ref,
+    slope_ref,
+    down_ref,
     sems,
 ):
-    vectors = [(gain2_hbm, gain2_ref), (bias2_hbm, bias2_ref), (up_bias_hbm, up_bias_ref)]
-    copies = [
-        pltpu.make_async_copy(source, target, sems.at[index])
-        for index, (source, target) in enumerate(vectors)
-    ]
-    start_all(copies)
-    normed, _ = norm_parts(resid_ref[...])
-    wait_all(copies)
-    normed = (normed * gain2_ref[...][None] + bias2_ref[...][None]).astype(BF)
-    normed_ref[...] = normed
-    left_ref[...] = normed.T
-    hidden_terms(at_ref, 1, normed, up_ref, up_bias_ref, act_ref, slope_ref)
-
-
-def hidden_own_kernel(
-    at_ref,
-    up_bias_hbm,
-    down_hbm,
-    normed_ref,
-    up_ref,
-    act_ref,
-    slope_ref,
-    down_ref,
-    up_bias_ref,
-    sems,
-):
-    bias_copy = pltpu.make_async_copy(up_bias_hbm, up_bias_ref, sems.at[0])
-    down_copy = pltpu.make_async_copy(down_hbm, down_ref, sems.at[1])
-    start_all([bias_copy, down_copy])
-    bias_copy.wait()
-    hidden_terms(at_ref, 0, normed_ref[...], up_ref, up_bias_ref, act_ref, slope_ref)
+    down_copy = pltpu.make_async_copy(down_hbm, down_ref, sems.at[0])
+    down_copy.start()
+    normed = normed_ref[...]
+    act_other_ref[...], slope_ref[1] = hidden_terms(at_ref, 0, 1, normed, up_ref, up_bias_ref)
+    act_own_ref[...], slope_ref[0] = hidden_terms(at_ref, 0, 0, normed, up_ref, up_bias_ref)
     down_copy.wait()
 
 
@@ -340,27 +304,20 @@
 def mixed_kernel(
     at_ref,
     act_own_ref,
-    act_send_ref,
+    act_other_ref,
+    act_far_ref,
     resid_ref,
     down_ref,
-    down_bias_hbm,
+    down_bias_ref,
     keep_ref,
     send_ref,
-    down_bias_ref,
-    sems,
 ):
-    bias_copy = pltpu.make_async_copy(down_bias_hbm, down_bias_ref, sems.at[0])
-    bias_copy.start()
     rows, width = resid_ref.shape
-    core = core_of(at_ref)
     total = resid_ref[...]
-    for owner_x in range(2):
-        for other in range(2):
-            quarter = 2 * owner_x + (core if other == 0 else 1 - core)
-            act = (act_own_ref if other == 0 else act_send_ref)[owner_x]
-            spots = pl.ds(pl.multiple_of(quarter * width, width), width)
-            total += mat(act, down_ref[spots, :])
-    bias_copy.wait()
+    for step, act in enumerate([act_own_ref, act_other_ref, act_far_ref.at[0], act_far_ref.at[1]]):
+        quarter = at_ref[0] ^ step
+        spots = pl.ds(pl.multiple_of(quarter * width, width), width)
+        total += mat(act[...], down_ref[spots, :])
     total += down_bias_ref[...][None]
     valid = live_rows(rows, rows // 4, live_of(at_ref, at_ref[0]))
     split_rows(jnp.where(valid, total, 0.0).astype(BF), keep_ref, send_ref)
@@ -393,66 +350,45 @@
     send_ref[...] = block_ref[half:]
 
 
+def out_grad_kernel(at_ref, cot0, cot1, cot2, cot3, grad_t_ref, bias_ref):
+    rows = cot0.shape[0]
+    for device in range(4):
+        grad = slot_cots(at_ref, [cot0, cot1, cot2, cot3], device)
+        if device == 0:
+            bias_ref[...] = jnp.sum(grad.astype(F32), axis=0, keepdims=True)
+        grad_t_ref[:, device * rows : (device + 1) * rows] = grad.T
+
+
 def down_terms_kernel(
-    at_ref,
-    near_ref,
-    far_ref,
-    near_other_ref,
-    far_other_ref,
-    act_own,
-    act0_other,
-    act1_other,
-    send_ref,
-    keep_ref,
-    bias_ref,
-    block_ref,
-    own_ref,
-    other_ref,
-    sems,
+    at_ref, grad_t_ref, act_own, act_far, act_other, act_far_other, send_ref, keep_ref, block_ref
 ):
-    core = core_of(at_ref)
-    refs = [near_ref, far_ref, near_other_ref, far_other_ref]
-    copies = slot_copies(refs, core, own_ref, sems, 0)
-    copies += slot_copies(refs, core, other_ref, sems, 4, partner=True)
-    start_all(copies)
-    wait_all(copies)
-    zero = jnp.zeros((), BF)
-    rows = 4 * own_ref.shape[1]
-    block = own_ref.shape[2] // GROUPS
-    slot = at_ref[0]
-    own = jnp.where(live_rows(rows, rows // 4, live_of(at_ref, slot)), flat_rows(own_ref), zero)
-    other = jnp.where(
-        live_rows(rows, rows // 4, live_of(at_ref, slot ^ 1)), flat_rows(other_ref), zero
-    )
-    bias_ref[...] = jnp.sum(own.astype(F32), axis=0, keepdims=True)
-    both = jnp.concatenate([own.T, other.T], axis=1)
-    for owner_x in range(2):
-        act_other = act1_other if owner_x else act0_other
-        right = jnp.concatenate([act_own[owner_x], act_other[...]], axis=0)
-        for half in range(2):
-            span = slice(half * 4 * block, (half + 1) * 4 * block)
-            total = mat(both[span], right).astype(BF)
-            for step in range(4):
-                spot = spot_of(at_ref, owner_x, half * 4 + step)
-                block_ref[spot] = total[step * block : (step + 1) * block]
+    block = grad_t_ref.shape[0] // GROUPS
+    right = jnp.concatenate(
+        [act_own[...], act_far[...], act_other[...], act_far_other[...]], axis=0
+    )
+    for half in range(2):
+        span = slice(half * 4 * block, (half + 1) * 4 * block)
+        total = mat(grad_t_ref[span, :], right).astype(BF)
+        for step in range(4):
+            spot = spot_of(at_ref, at_ref[0] >> 1, half * 4 + step, DOWN_ORDER)
+            block_ref[spot] = total[step * block : (step + 1) * block]
     hand_over(block_ref, send_ref, keep_ref)
 
 
 def hidden_back_kernel(
     at_ref,
-    near_ref,
-    far_ref,
-    near_other_ref,
-    far_other_ref,
-    gain2_hbm,
+    cot0,
+    cot1,
+    cot2,
+    cot3,
     proj_hbm,
+    gain2_ref,
     up_ref,
-    slope_own_ref,
-    slope_send_ref,
+    slope_near_ref,
+    slope_far_ref,
     resid_ref,
     down_ref,
-    hidden0_ref,
-    hidden1_ref,
+    hidden_ref,
     grad_ref,
     branch_ref,
     att_grad_t_ref,
@@ -460,37 +396,25 @@
     gain_ref,
     bias_ref,
     proj_bias_ref,
-    cot_ref,
-    gain2_ref,
     proj_ref,
     sems,
 ):
-    copies = slot_copies(
-        [near_ref, far_ref, near_other_ref, far_other_ref], core_of(at_ref), cot_ref, sems, 0
-    )
-    copies.append(pltpu.make_async_copy(gain2_hbm, gain2_ref, sems.at[4]))
-    start_all(copies)
-    proj_copy = pltpu.make_async_copy(proj_hbm, proj_ref, sems.at[5])
+    proj_copy = pltpu.make_async_copy(proj_hbm, proj_ref, sems.at[0])
     proj_copy.start()
     rows, width = resid_ref.shape
-    core = core_of(at_ref)
-    order = [(owner_x, other) for owner_x in range(2) for other in range(2)]
-    spans = []
-    hidden_refs = [hidden0_ref, hidden1_ref]
-    for owner_x, other in order:
-        quarter = 2 * owner_x + (core ^ other)
-        spans.append(pl.ds(pl.multiple_of(quarter * width, width), width))
-    wait_all(copies)
-    valid = live_rows(rows, rows // 4, live_of(at_ref, at_ref[0]))
-    out_grad = jnp.where(valid, flat_rows(cot_ref), jnp.zeros((), BF))
+    out_grad = slot_cots(at_ref, [cot0, cot1, cot2, cot3], 0)
     second = jnp.zeros((rows, width), F32)
-    for index, (owner_x, other) in enumerate(order):
-        slope = (slope_send_ref if other else slope_own_ref)[owner_x]
-        hidden = times_trans(out_grad, down_ref[spans[index], :]) * slope.astype(F32)
+    half = width // 2
+    for step in range(4):
+        quarter = at_ref[0] ^ step
+        span = pl.ds(pl.multiple_of(quarter * width, width), width)
+        slope = (slope_far_ref if step // 2 else slope_near_ref)[step % 2]
+        hidden = times_trans(out_grad, down_ref[span, :]) * slope.astype(F32)
         hidden = hidden.astype(BF)
-        hidden_refs[owner_x][other] = hidden
-        up_bias_ref[:, spans[index]] = jnp.sum(hidden.astype(F32), axis=0, keepdims=True)
-        second += times_trans(hidden, up_ref[:, spans[index]])
+        for side in range(2):
+            hidden_ref[(at_ref[1] & 1) ^ side, quarter] = hidden[:, side * half : (side + 1) * half]
+        up_bias_ref[:, span] = jnp.sum(hidden.astype(F32), axis=0, keepdims=True)
+        second += times_trans(hidden, up_ref[:, span])
     normed, scale = norm_parts(resid_ref[...])
     gain_ref[...] = jnp.sum(second * normed, axis=0, keepdims=True)
     bias_ref[...] = jnp.sum(second, axis=0, keepdims=True)
@@ -559,7 +483,7 @@
 
 def first_back_kernel(
     at_ref,
-    gain1_hbm,
+    gain1_ref,
     row_ref,
     grad_ref,
     right_ref,
@@ -572,11 +496,7 @@
     keep_ref,
     send_ref,
     vec_ref,
-    gain1_ref,
-    sems,
 ):
-    gain_copy = pltpu.make_async_copy(gain1_hbm, gain1_ref, sems.at[0])
-    gain_copy.start()
     rows, width = row_ref.shape
     qkv_rows = 3 * width // GROUPS
     places = [near_first(at_ref, group) for group in range(GROUPS)]
@@ -588,7 +508,6 @@
     first = mat(qkv_ref[...], stacked).T
     gain = jnp.sum(first * normed, axis=0, keepdims=True)
     bias = jnp.sum(first, axis=0, keepdims=True)
-    gain_copy.wait()
     total = grad_ref[...] + norm_back(first, normed, scale, gain1_ref[...][None])
     split_rows(total.astype(BF), keep_ref, send_ref)
     share = width // GROUPS
@@ -629,48 +548,44 @@
     )
 
 
-def up_terms_kernel(at_ref, left_own, left_other, *refs):
-    own, other = refs[:2], refs[2:4]
-    send_ref, keep_ref, block_ref = refs[4:]
-    core = core_of(at_ref)
-    rows = left_own.shape[0] // 4
-    width = own[0].shape[2] // 2
-    left = own_quarters([left_own, left_other], core)
-    for owner_x in range(2):
-        for side in range(2):
-            quarter = 2 * owner_x + (core ^ side)
-            for half in range(2):
-                span = slice(half * width, (half + 1) * width)
-                right = jnp.concatenate(
-                    [own[owner_x][side, :, span], other[owner_x][1 - side, :, span]], axis=0
-                )
-                total = mat(left, right).astype(BF)
-                for index in range(2):
-                    spot = spot_of(at_ref, index, 2 * quarter + half)
-                    block_ref[spot] = total[index * rows : (index + 1) * rows]
+def up_terms_kernel(at_ref, *refs):
+    normeds, hiddens, last_hiddens = refs[:4], refs[4:7], refs[7:11]
+    send_ref, keep_ref, block_ref, left_ref = refs[11:]
+    rows = left_ref.shape[1] // 4
+    for index, ref in enumerate(normeds):
+        left_ref[index] = ref[...].T
+    left = own_quarters([left_ref.at[index] for index in range(4)], core_of(at_ref))
+    for index in range(hiddens[0].shape[0]):
+        right = [ref[index] for ref in hiddens] + [last_hiddens[index][0]]
+        right = jnp.concatenate(right, axis=0)
+        total = mat(left, right).astype(BF)
+        group = (at_ref[1] & 1) + 2 * index
+        for owner_x in range(2):
+            spot = spot_of(at_ref, owner_x, group, UP_ORDER)
+            block_ref[spot] = total[owner_x * rows : (owner_x + 1) * rows]
     hand_over(block_ref, send_ref, keep_ref)
 
 
-def mix_terms_kernel(at_ref, *refs):
+def mix_terms_kernel(far_side, at_ref, *refs):
     lefts, rights = refs[:4], refs[4:8]
     vec_ref, send_ref, keep_ref, block_ref = refs[8:]
     core = core_of(at_ref)
     rows = lefts[0].shape[1] // 4
-    count, columns = rights[0].shape[0], rights[0].shape[1]
+    count, columns = rights[0].shape[0] // 2, rights[0].shape[1]
     qkv_rows = 3 * columns // 4
     edge = qkv_rows - qkv_rows % 128
     norm = own_quarters([ref.at[0] for ref in lefts], core)
     att = own_quarters([ref.at[1] for ref in lefts], core)
     lane = lax.broadcasted_iota(jnp.int32, (2 * rows, columns - edge), 1)
     pad = jnp.zeros((block_ref.shape[1] - rows - vec_ref.shape[1], columns), F32)
-    here = (at_ref[1] >> 1) & 1
+    group_bits = at_ref[1] ^ (4 * far_side)
     for index in range(count):
-        right = jnp.concatenate([ref[index] for ref in rights], axis=1)
+        right = jnp.concatenate([ref[2 * far_side + index] for ref in rights], axis=1)
         first = times_trans(norm, right)
         tail = jnp.where(lane < qkv_rows - edge, first[:, edge:], times_trans(att, right[edge:]))
         total = jnp.concatenate([first[:, :edge], tail], axis=1).astype(BF)
-        extra = jnp.concatenate([vec_ref[index], pad], axis=0).astype(BF)
-        group = (index & 1) + 2 * here + 4 * (index >> 1)
+        extra = jnp.concatenate([vec_ref[2 * far_side + index], pad], axis=0).astype(BF)
+        group = (group_bits & 6) + index
         for owner_x in range(2):
             spot = spot_of(at_ref, owner_x, group, MIX_ORDER)
             block_ref[spot, :rows] = total[owner_x * rows : (owner_x + 1) * rows]
@@ -678,14 +593,31 @@
     hand_over(block_ref, send_ref, keep_ref)
 
 
+def relay_kernel(source_ref, target_ref):
+    target_ref[...] = source_ref[...]
+
+
+def step_kernel(token_ref):
+    token_ref[...] = jnp.zeros_like(token_ref)
+
+
+def down_end_kernel(keep_ref, got_ref, out_ref, token_ref):
+    out_ref[...] = keep_ref[0].astype(F32) + got_ref[0].astype(F32)
+    token_ref[...] = jnp.zeros_like(token_ref)
+
+
+def add_last_kernel(keep_ref, got_ref, out_ref):
+    out_ref[...] = (keep_ref[...].astype(F32) + got_ref[...].astype(F32)).astype(BF)
+
+
 def add_kernel(keep_ref, got_ref, next_send_ref, next_keep_ref):
     half = next_keep_ref.shape[0]
     next_send_ref[...] = (keep_ref[half:].astype(F32) + got_ref[half:].astype(F32)).astype(BF)
     next_keep_ref[...] = (keep_ref[:half].astype(F32) + got_ref[:half].astype(F32)).astype(BF)
 
 
-def mix_end_kernel(keep_ref, got_ref, qkv_ref, proj_ref, *vec_refs):
-    total = keep_ref[0].astype(F32) + got_ref[0].astype(F32)
+def mix_end_kernel(keep_ref, got_ref, across_ref, qkv_ref, proj_ref, *vec_refs):
+    total = keep_ref[0].astype(F32) + got_ref[0].astype(F32) + across_ref[0].astype(F32)
     rows, split = qkv_ref.shape
     qkv_ref[...] = total[:rows, :split]
     proj_ref[...] = total[:rows, split:]
@@ -739,7 +671,7 @@
         scratch_shapes=list(scratch),
         compiler_params=pltpu.CompilerParams(vmem_limit_bytes=room * MIB),
         cost_estimate=pl.CostEstimate(flops=1000, bytes_accessed=1000, transcendentals=0),
-        name=body.__name__.replace("_kernel", ""),
+        name=getattr(body, "func", body).__name__.replace("_kernel", ""),
     )(*operands)
 
 
@@ -765,7 +697,21 @@
         got = self.pass_on()
         return (self.keep.astype(F32) + got.astype(F32))[0]
 
-    def end_mix(self, qkv_columns):
+    def end_down(self, after):
+        _, rows, columns = self.keep.shape
+        return kernel_call(
+            down_end_kernel,
+            "pp",
+            [self.keep, self.pass_on()],
+            [shaped(F32, rows, columns), kept(F32, 8, 128)],
+            after=after,
+        )
+
+    def last(self, after):
+        out = kept(BF, *self.keep.shape)
+        return kernel_call(add_last_kernel, "pp", [self.keep, self.pass_on()], [out], after=after)[0]
+
+    def end_mix(self, qkv_columns, across):
         got = self.pass_on()
         _, rows, columns = self.keep.shape
         rows -= 16
@@ -773,8 +719,8 @@
         sizes = (columns, share, share, 2 * share, share, share, share, share)
         return kernel_call(
             mix_end_kernel,
-            "pp",
-            [self.keep, got],
+            "ppp",
+            [self.keep, got, across],
             [shaped(F32, rows, qkv_columns), shaped(F32, rows, share)]
             + [shaped(F32, 1, size) for size in sizes],
         )
@@ -820,12 +766,8 @@
     act = kept(BF, 2, rows, hidden // 4)
     chunk = kept(BF, slot_rows, width)
     chunks = kept(BF, 2, slot_rows, width)
-    four = pltpu.VMEM((4, slot_rows, width), BF)
     columns = hidden // GROUPS
     share = width // GROUPS
-
-    def line(size):
-        return pltpu.VMEM((size,), F32)
 
     def blocks(count, height, lanes):
         return pltpu.VMEM((count, height, lanes), BF)
@@ -842,34 +784,38 @@
         [sems(3)],
     )
     far = place.swap(far, 2)
-    qkv_kept, proj_kept = kernel_call(
+    loads = [qkv_weight, proj_weight, cotangent, ln1_gain, ln1_bias, qv_bias, proj_bias]
+    loads += [ln2_gain, ln2_bias, up_bias, down_bias]
+    (
+        qkv_kept,
+        proj_kept,
+        cot,
+        ln1_gain,
+        ln1_bias,
+        qv_bias,
+        proj_bias,
+        ln2_gain,
+        ln2_bias,
+        up_bias,
+        down_bias,
+    ) = kernel_call(
         load_kernel,
-        "hh",
-        [qkv_weight, proj_weight],
-        [kept(BF, *item.shape) for item in (qkv_weight, proj_weight)],
-        [sems(2)],
+        "h" * len(loads),
+        loads,
+        [kept(item.dtype, *item.shape) for item in loads],
+        [sems(len(loads))],
         after=[near],
     )
-    cot_near, cot_far = kernel_call(
-        cot_slice_kernel,
-        "sh",
-        [at, cotangent.reshape(parted)],
-        [chunks, chunks],
-        [sems(2)],
-        after=[proj_kept],
-    )
-    cot_far = place.swap(cot_far, 2)
-    cot_parts = [cot_near, cot_far, place.swap(cot_near, 1), place.swap(cot_far, 1)]
     far_mine, far_other = kernel_call(
-        far_slice_kernel, "sp", [at, far], [chunk, chunk], after=[cot_near]
+        far_slice_kernel, "sp", [at, far], [chunk, chunk], after=[cot]
     )
     token_parts = [near, far_mine, place.swap(near_core, 1), place.swap(far_other, 1)]
     slot_tokens, lefts, query_t, key_t, values, prob, scale, residual, up_kept = kernel_call(
         attention_kernel,
-        "s" + "a" * 4 + "h" * 5 + "pp",
+        "s" + "p" * 4 + "h" + "p" * 6,
         [at]
         + token_parts
-        + [ln1_gain, ln1_bias, qv_bias, proj_bias, up_weight]
+        + [up_weight, ln1_gain, ln1_bias, qv_bias, proj_bias]
         + [qkv_kept, proj_kept],
         [
             natural,
@@ -882,39 +828,42 @@
             flat,
             kept(BF, *up_weight.shape),
         ],
-        [four, line(width), line(width), line(2 * width), line(width), sems(9)],
-    )
-    z_mask = place.masks[2]
-
+        [sems(1)],
+    )
+    def relay(item, after):
+        return kernel_call(relay_kernel, "p", [item], [kept(item.dtype, *item.shape)], after=after)[0]
+
+    def step(after):
+        (token,) = kernel_call(step_kernel, "", [], [kept(F32, 8, 128)], after=after)
+        return place.swap(token, 1)
+
+    x_mask, y_mask, z_mask, last_mask = place.masks
+
+    def four_sets(item, beyond):
+        return [item, place.swap(item, 1), beyond, place.swap(beyond, 1)]
+
+    cot_far = place.swap(relay(cot, [far_mine]), x_mask)
+    cots = [cot, cot_far, place.swap(cot, 1), place.swap(cot_far, 1)]
     lefts_beyond = place.swap(lefts, z_mask)
-    left_sets = [lefts, place.swap(lefts, 1), lefts_beyond, place.swap(lefts_beyond, 1)]
-    second_left, second_normed, act_send, slope_send = kernel_call(
-        hidden_send_kernel,
-        "shhhpp",
+    left_sets = four_sets(lefts, lefts_beyond)
+
+    normed, act_far, slope_far = kernel_call(
+        hidden_far_kernel,
+        "sppppp",
         [at, ln2_gain, ln2_bias, up_bias, residual, up_kept],
-        [tall, natural, act, act],
-        [line(width), line(width), line(hidden), sems(3)],
-        after=[cot_far],
-    )
-    act_own, slope_own, down_kept = kernel_call(
-        hidden_own_kernel,
-        "shhpp",
-        [at, up_bias, down_weight, second_normed, up_kept],
-        [act, act, kept(BF, *down_weight.shape)],
-        [line(hidden), sems(2)],
-    )
-    act_other = [place.swap(act_send[index], 1) for index in range(2)]
-    down_send, down_keep, down_bias_grad = kernel_call(
-        down_terms_kernel,
-        "s" + "a" * 4 + "p" * 3,
-        [at] + cot_parts + [act_own] + act_other,
-        halves(2 * GROUPS, share, hidden // 4) + [vector],
-        [blocks(2 * GROUPS, share, hidden // 4), four, four, sems(8)],
-    )
-    down_sum = Sum(place, ORDER, down_send, down_keep)
+        [natural, act, act],
+    )
+    act_own, act_other, slope_near, down_kept = kernel_call(
+        hidden_near_kernel,
+        "shppp",
+        [at, down_weight, up_bias, normed, up_kept],
+        [natural, natural, act, kept(BF, *down_weight.shape)],
+        [sems(1)],
+    )
+    act_got = place.swap(act_far, x_mask)
+    normed_sets = four_sets(normed, place.swap(normed, y_mask))
     (
-        hidden0,
-        hidden1,
+        hidden_grad,
         residual_grad,
         branches,
         att_grad_t,
@@ -924,13 +873,12 @@
         proj_bias_grad,
     ) = kernel_call(
         hidden_back_kernel,
-        "s" + "a" * 4 + "hhppppp",
+        "s" + "p" * 4 + "h" + "p" * 6,
         [at]
-        + cot_parts
-        + [ln2_gain, proj_weight, up_kept, slope_own, slope_send, residual, down_kept],
+        + cots
+        + [proj_weight, ln2_gain, up_kept, slope_near, slope_far, residual, down_kept],
         [
-            act,
-            act,
+            kept(BF, 2, 4, rows, columns),
             flat,
             kept(BF, GROUPS, share, rows),
             tall,
@@ -939,51 +887,46 @@
             vector,
             vector,
         ],
-        [
-            four,
-            line(width),
-            pltpu.VMEM(proj_weight.shape, BF),
-            sems(6),
-        ],
-        after=[down_bias_grad],
-    )
-    hidden_own = [hidden0, hidden1]
-    hidden_other = [place.swap(item, 1) for item in hidden_own]
+        [pltpu.VMEM(proj_weight.shape, BF), sems(1)],
+    )
+    hidden_beyond = place.swap(hidden_grad[1], y_mask)
     rights, qkv_again = kernel_call(
         attention_back_kernel,
         "sh" + "p" * 8,
         [at, qkv_weight, lefts, query_t, key_t, values, prob, scale, att_grad_t, branches],
         [kept(BF, GROUPS, columns, rows), kept(BF, *qkv_weight.shape)],
         [sems(1)],
-        after=[lefts_beyond],
+        after=[normed_sets[2]],
     )
     half = GROUPS // 2
-    def near_and_far(item):
-        near, far = item[:half], place.swap(item[half:], z_mask)
-        return [near, place.swap(near, 1), far, place.swap(far, 1)]
-
-    right_sets = near_and_far(rights)
-    last = down_sum.go([rights])
-    up_send, up_keep = kernel_call(
-        up_terms_kernel,
-        "s" + "p" * 6,
-        [at, second_left, place.swap(second_left, 1)] + hidden_own + hidden_other,
-        halves(2 * GROUPS, width // 4, columns),
-        [blocks(2 * GROUPS, width // 4, columns)],
-        after=[last],
-    )
-    up_sum = Sum(place, ORDER, up_send, up_keep)
+    rights_beyond = place.swap(rights[half:], z_mask)
+    grad_t, down_bias_grad = kernel_call(
+        out_grad_kernel,
+        "spppp",
+        [at] + cots,
+        [kept(BF, width, 4 * rows), vector],
+        after=[rights],
+    )
+    token = step([lefts_beyond])
+    act_far_other = place.swap(relay(act_got[1], [token]), 1)
+    down_send, down_keep = kernel_call(
+        down_terms_kernel,
+        "s" + "p" * 5,
+        [at, grad_t, act_own, act_got[0], place.swap(act_other, 1), act_far_other],
+        halves(GROUPS, share, hidden // 4),
+        [blocks(GROUPS, share, hidden // 4)],
+    )
+    down_sum = Sum(place, DOWN_ORDER, down_send, down_keep)
     mixed_keep, mixed_send = kernel_call(
         mixed_kernel,
-        "spppph",
-        [at, act_own, act_send, residual, down_kept, down_bias],
+        "s" + "p" * 6,
+        [at, act_own, act_other, act_far, residual, down_kept, down_bias],
         [chunks, chunks],
-        [line(width), sems(1)],
-        after=[up_keep],
+        after=[down_keep],
     )
     input_keep, input_send, packed = kernel_call(
         first_back_kernel,
-        "shppppppppp",
+        "s" + "p" * 10,
         [
             at,
             ln1_gain,
@@ -998,38 +941,59 @@
             down_bias_grad,
         ],
         [chunks, chunks, kept(F32, GROUPS, 8, columns)],
-        [line(width), sems(1)],
         after=[mixed_keep],
     )
     packed = packed + place.swap(packed, 1)
-    packed = packed[:half] + place.swap(packed[half:], z_mask)
-    last = down_sum.go([input_keep])
-    mix_send, mix_keep = kernel_call(
-        mix_terms_kernel,
-        "s" + "p" * 9,
-        [at] + left_sets + right_sets + [packed],
-        halves(GROUPS, width // 4 + 16, columns),
-        [blocks(GROUPS, width // 4 + 16, columns)],
-        after=[last],
-    )
-    mix_sum = Sum(place, MIX_ORDER, mix_send, mix_keep)
-    last = up_sum.go([mix_keep])
+    hidden_beyond = relay(hidden_beyond, [input_keep])
+    packed = packed[:half] + place.swap(relay(packed[half:], [hidden_beyond]), z_mask)
+    hidden_sets = [hidden_grad[0], place.swap(hidden_grad[0], 1), hidden_beyond]
+    hidden_sets += [place.swap(hidden_beyond[index : index + 1], 1) for index in range(4)]
+    up_send, up_keep = kernel_call(
+        up_terms_kernel,
+        "s" + "p" * 11,
+        [at] + normed_sets + hidden_sets,
+        halves(GROUPS, width // 4, columns),
+        [blocks(GROUPS, width // 4, columns), pltpu.VMEM((4, width, rows), BF)],
+    )
+    up_sum = Sum(place, UP_ORDER, up_send, up_keep)
+    right_sets = four_sets(rights[:half], relay(rights_beyond, [up_keep]))
+
+    def mix_terms(far_side, after):
+        send, keep = kernel_call(
+            functools.partial(mix_terms_kernel, far_side),
+            "s" + "p" * 9,
+            [at] + left_sets + right_sets + [packed],
+            halves(half, width // 4 + 16, columns),
+            [blocks(half, width // 4 + 16, columns)],
+            after=after,
+        )
+        return Sum(place, MIX_ORDER, send, keep)
+
+    first_sum = mix_terms(1, [up_keep])
+    second_sum = mix_terms(0, [first_sum.keep])
+    last = down_sum.go([second_sum.keep])
+    last = first_sum.go([last])
     last = down_sum.go([last])
-    last = mix_sum.go([last])
     last = up_sum.go([last])
-    last = mix_sum.go([last])
+    last = second_sum.go([last])
+    across = first_sum.last([last])
     returns = [mixed_keep, place.swap(mixed_send, 1), input_keep, place.swap(input_send, 1)]
     (far_rows,) = kernel_call(
-        gather_kernel, "pppp", returns, [kept(BF, 4, slot_rows, width)], after=[last]
-    )
-    far_rows = place.swap(far_rows, 2)
-    down_block = down_sum.end()
+        gather_kernel, "pppp", returns, [kept(BF, 4, slot_rows, width)], after=[across]
+    )
+    far_rows = place.swap(far_rows, x_mask)
+    down_block, last = down_sum.end_down([across])
     last = up_sum.go([last])
     mixed, input_grad = kernel_call(
-        place_kernel, "spppp" + "p", [at] + returns + [far_rows], [shaped(BF, rows, width)] * 2, after=[last]
-    )
+        place_kernel,
+        "s" + "p" * 5,
+        [at] + returns + [far_rows],
+        [shaped(BF, rows, width)] * 2,
+        after=[last],
+    )
+    across = place.swap(across, last_mask)
+    mix_block = second_sum.end_mix(3 * share, across)
     up_block = up_sum.end()
-    mix_block = mix_sum.end_mix(3 * share)
 
     qkv_block, proj_block = mix_block[:2]
     reduced = [within_group(place, item.reshape(-1), 0) for item in mix_block[2:]]

time: 125 us -> 118 us (0.944)
  the two profiles are of different devices: /device:TPU:0 before, /device:TPU:24 now
where the time goes in v3:
time: 118 us; the launch traced here: 117 us
  Pallas kernels  43.6 us (37%)
  waiting for transfers between devices  43.6 us (37%)
  starting transfers between devices  26.5 us (22%)
  other arithmetic  2.1 us (2%)
    pallas_call x32, Pallas kernels, kernel_call(): pl.pallas_call(run, out_shape=outs, in_specs=[SPECS[kind] for kind in spe...  43.6 us
    ppermute x10, waiting for transfers between devices, swap_by_core(): return lax.ppermute(value, AXES, pairs)  25.4 us
    ppermute x31, waiting for transfers between devices, swap(): return lax.ppermute(value, AXES, pairs)  18.2 us
    ppermute x31, starting transfers between devices, swap(): return lax.ppermute(value, AXES, pairs)  15.6 us
    ppermute x10, starting transfers between devices, swap_by_core(): return lax.ppermute(value, AXES, pairs)  10.9 us
  transfers between devices with their start and end apart: 41, of which 17 were waited for; matrix products, arithmetic and copies ran while one was open for 2% of the time, Pallas kernels for 34%

profile of v3, /device:TPU:24, one launch (start us, length us, event | category | flops | bytes accessed | tf_op | source)
XLA Modules:
  0.0 117.4 jit_solution(4249976979987331245)
XLA Ops:
  0.6 0.7 pad_add_fusion.refs_0_
  1.4 1.6 %token_slice.1 = (bf16[64,768]{1,0:T(8,128)(2,1)S(1)}, bf16[64,768]{1,0:T(8,128)(2,1)S(1)}, bf16[2,64,768]{2,1,0:T(8,128)(2,1)S(1)}) custom-call(s32[6]{0:T(128)S(1)} %pad_add_fusion.refs_0_, bf16[2,2,64,768]{3,2,1,0:T(8,128)(2,1)} %bitcast.22), custom_call_target="tpu_custom_call" | custom-call | flops 1000 | bytes 1000 | tf_op jit(solution)/shard_map/token_slice/pallas_call | solution.py:666
  3.0 1.6 %collective-permute-start = (bf16[2,64,768]{2,1,0:T(8,128)(2,1)S(1)}, bf16[2,64,768]{2,1,0:T(8,128)(2,1)S(1)}, u32[]{:S(2)}, u32[]{:S(2)}) collective-permute-start(bf16[2,64,768]{2,1,0:T(8,128)(2,1)S(1)} %get-tuple-element.101), channel_id=1, source_target_pairs={{0,2},{1,3},{2,0},{3,1},{4,6},{5,7},{6,4},{7,5},{8,10},{9,11},{10,... | collective-permute-start | bytes 589832 | tf_op jit(solution)/shard_map/ppermute | solution.py:51
  4.5 2.5 %load.1 = (bf16[768,2304]{1,0:T(8,128)(2,1)S(1)}, bf16[768,768]{1,0:T(8,128)(2,1)S(1)}, bf16[256,768]{1,0:T(8,128)(2,1)S(1)}, f32[768]{0:T(1024)S(1)}, f32[768]{...) custom-call(bf16[768,2304]{1,0:T(8,128)(2,1)} %refs_1_.5, ...), custom_call_target="tpu_custom_call" | custom-call | flops 1000 | bytes 1000 | tf_op jit(solution)/shard_map/load/pallas_call | solution.py:666
  7.1 2.6 %collective-permute-done.refs_1_ = bf16[2,64,768]{2,1,0:T(8,128)(2,1)S(1)} collective-permute-done((bf16[2,64,768]{2,1,0:T(8,128)(2,1)S(1)}, bf16[2,64,768]{2,1,0:T(8,128)(2,1)S(1)}, u32[]{:S(2)}, u32[]{:S(2)}) %collective-permute-start) | collective-permute-done | bytes 196640 | tf_op jit(solution)/shard_map/ppermute | solution.py:51
  10.3 1.6 %collective-permute-start.3 = (bf16[256,768]{1,0:T(8,128)(2,1)S(1)}, bf16[256,768]{1,0:T(8,128)(2,1)S(1)}, u32[]{:S(2)}, u32[]{:S(2)}) collective-permute-start(bf16[256,768]{1,0:T(8,128)(2,1)S(1)} %relay.5), channel_id=1, source_target_pairs={{0,2},{1,3},{2,0},{3,1},{4,6},{5,7},{6,4},{7,5},{8,10},{9,11},{10,... | collective-permute-start | bytes 1179656 | tf_op jit(solution)/shard_map/ppermute | solution.py:51
  12.4 0.8 collective-permute-done.1.refs_3_
  13.3 5.3 %attention.1 = (bf16[256,768]{1,0:T(8,128)(2,1)S(1)}, bf16[2,768,256]{2,1,0:T(8,128)(2,1)S(1)}, bf16[768,256]{1,0:T(8,128)(2,1)S(1)}, bf16[768,256]{1,0:T(8,128)...) custom-call(s32[6]{0:T(128)S(1)} %pad_add_fusion.refs_0_, ...), custom_call_target="tpu_custom_call" | custom-call | flops 1000 | bytes 1000 | tf_op jit(solution)/shard_map/attention/pallas_call | solution.py:666
  19.2 3.0 %hidden_far.1 = (bf16[256,768]{1,0:T(8,128)(2,1)S(1)}, bf16[2,256,768]{2,1,0:T(8,128)(2,1)S(1)}, bf16[2,256,768]{2,1,0:T(8,128)(2,1)S(1)}) custom-call(s32[6]{0:T(128)S(1)} %pad_add_fusion.refs_0_, f32[768]{0:T(1024)S(1)} %get-tuple-element.99.refs_1_.refs_6_, f32[768]{0:T(1024)S(1)} %get-tuple-element.100.refs_2_, ...), custom_call_target="tpu_custom_call" | custom-call | flops 1000 | bytes 1000 | tf_op jit(solution)/shard_map/hidden_far/pallas_call | solution.py:666
  22.1 0.6 collective-permute-start.7
  23.3 1.5 %collective-permute-start.6 = (bf16[256,768]{1,0:T(8,128)(2,1)S(1)}, bf16[256,768]{1,0:T(8,128)(2,1)S(1)}, u32[]{:S(2)}, u32[]{:S(2)}) collective-permute-start(bf16[256,768]{1,0:T(8,128)(2,1)S(1)} %get-tuple-element.114.refs_3_.refs_1_), channel_id=1, source_target_pairs={{0,4},{1,5},{2,6},{3,7},{4,0},{5,1},{6,2},{7,3},{8,12},{9,13},{10,... | collective-permute-start | bytes 1179656 | tf_op jit(solution)/shard_map/ppermute | solution.py:51
  24.8 2.9 %hidden_near.1 = (bf16[256,768]{1,0:T(8,128)(2,1)S(1)}, bf16[256,768]{1,0:T(8,128)(2,1)S(1)}, bf16[2,256,768]{2,1,0:T(8,128)(2,1)S(1)}, bf16[3072,768]{1,0:T(8,128)(2,1)S(1)}) custom-call(s32[6]{0:T(128)S(1)} %pad_add_fusion.refs_0_, bf16[3072,768]{1,0:T(8,128)(2,1)} %refs_1_.4, f32[3072]{0:T(1024)S(1)} %get-tuple-element.98.refs_3_.refs_2_, ...), custom_call_target="tpu_custom_call" | custom-call | flops 1000 | bytes 1000 | tf_op jit(solution)/shard_map/hidden_near/pallas_call | solution.py:666
  27.7 5.8 %hidden_back.1 = (bf16[2,4,256,384]{3,2,1,0:T(8,128)(2,1)S(1)}, f32[256,768]{1,0:T(8,128)S(1)}, bf16[8,96,256]{2,1,0:T(8,128)(2,1)S(1)}, bf16[768,256]{1,0:T(8,1...) custom-call(s32[6]{0:T(128)S(1)} %pad_add_fusion.refs_0_, ...), custom_call_target="tpu_custom_call" | custom-call | flops 1000 | bytes 1000 | tf_op jit(solution)/shard_map/hidden_back/pallas_call | solution.py:666
  33.9 0.6 collective-permute-start.21
  35.0 4.0 %attention_back.1 = (bf16[8,384,256]{2,1,0:T(8,128)(2,1)S(1)}, bf16[768,2304]{1,0:T(8,128)(2,1)S(1)}) custom-call(s32[6]{0:T(128)S(1)} %pad_add_fusion.refs_0_, bf16[768,2304]{1,0:T(8,128)(2,1)} %refs_1_.5, bf16[2,768,256]{2,1,0:T(8,128)(2,1)S(1)} %get-tuple-element.120.refs_2_.refs_1_, bf16[768,256]{1,0:T(8,128)(2,1)S(1)} %get-tuple-element.121.refs_3_, ...), custom_call_target="tpu_custom_call" | custom-call | flops 1000 | bytes 1000 | tf_op jit(solution)/shard_map/attention_back/pallas_call | solution.py:666
  39.1 2.6 %collective-permute-done.7 = bf16[2,256,768]{2,1,0:T(8,128)(2,1)S(1)} collective-permute-done((bf16[2,256,768]{2,1,0:T(8,128)(2,1)S(1)}, bf16[2,256,768]{2,1,0:T(8,128)(2,1)S(1)}, u32[]{:S(2)}, u32[]{:S(2)}) %collective-permute-start.7) | collective-permute-done | bytes 786464 | tf_op jit(solution)/shard_map/ppermute | solution.py:51
  42.0 1.6 %collective-permute-start.17 = (bf16[4,384,256]{2,1,0:T(8,128)(2,1)S(1)}, bf16[4,384,256]{2,1,0:T(8,128)(2,1)S(1)}, u32[]{:S(2)}, u32[]{:S(2)}) collective-permute-start(bf16[4,384,256]{2,1,0:T(8,128)(2,1)S(1)} %get-tuple-element.182), channel_id=1, source_target_pairs={{0,8},{1,9},{2,10},{3,11},{4,12},{5,13},{6,14},{7,15},{8,0},{9,1},... | collective-permute-start | bytes 2359304 | tf_op jit(solution)/shard_map/ppermute | solution.py:51
  43.9 1.0 out_grad.1
  45.3 2.0 %down_terms.1 = (bf16[4,96,768]{2,1,0:T(8,128)(2,1)S(1)}, bf16[4,96,768]{2,1,0:T(8,128)(2,1)S(1)}) custom-call(s32[6]{0:T(128)S(1)} %pad_add_fusion.refs_0_, bf16[768,1024]{1,0:T(8,128)(2,1)S(1)} %get-tuple-element.131.refs_1_, bf16[256,768]{1,0:T(8,128)(2,1)S(1)} %get-tuple-element.115.refs_2_.refs_1_, bf16[256,768]{1,0:T(8,128)(2,1)S(1)} %get-tuple-element.189.refs_3_, ...), custom_call_target="tpu_custom_call" | custom-call | flops 1000 | bytes 1000 | tf_op jit(solution)/shard_map/down_terms/pallas_call | solution.py:666
  47.3 1.9 %mixed.1 = (bf16[2,64,768]{2,1,0:T(8,128)(2,1)S(1)}, bf16[2,64,768]{2,1,0:T(8,128)(2,1)S(1)}) custom-call(s32[6]{0:T(128)S(1)} %pad_add_fusion.refs_0_, bf16[256,768]{1,0:T(8,128)(2,1)S(1)} %get-tuple-element.115.refs_2_.refs_1_, bf16[256,768]{1,0:T(8,128)(2,1)S(1)} %get-tuple-element.116.refs_2_, bf16[2,256,768]{2,1,0:T(8,128)(2,1)S(1)} %get-tuple-element.117.refs_3_, ...), custom_call_target="tpu_custom_call" | custom-call | flops 1000 | bytes 1000 | tf_op jit(solution)/shard_map/mixed/pallas_call | solution.py:666
  49.3 2.3 %first_back.1 = (bf16[2,64,768]{2,1,0:T(8,128)(2,1)S(1)}, bf16[2,64,768]{2,1,0:T(8,128)(2,1)S(1)}, f32[8,8,384]{2,1,0:T(8,128)S(1)}) custom-call(s32[6]{0:T(128)S(1)} %pad_add_fusion.refs_0_, f32[768]{0:T(1024)S(1)} %get-tuple-element.106.refs_6_.refs_1_, bf16[256,768]{1,0:T(8,128)(2,1)S(1)} %get-tuple-element.135.refs_2_, ...), custom_call_target="tpu_custom_call" | custom-call | flops 1000 | bytes 1000 | tf_op jit(solution)/shard_map/first_back/pallas_call | solution.py:666
  51.6 1.5 %collective-permute-done.21.refs_0_ = bf16[4,256,384]{2,1,0:T(8,128)(2,1)S(1)} collective-permute-done((bf16[4,256,384]{2,1,0:T(8,128)(2,1)S(1)}, bf16[4,256,384]{2,1,0:T(8,128)(2,1)S(1)}, u32[]{:S(2)}, u32[]{:S(2)}) %collective-permute-start.21) | collective-permute-done | bytes 786464 | tf_op jit(solution)/shard_map/ppermute | solution.py:51
  54.9 1.3 %collective-permute-done.23.refs_9_ = bf16[1,256,384]{2,1,0:T(8,128)(2,1)S(1)} collective-permute-done((bf16[1,256,384]{2,1,0:T(8,128)(2,1)S(1)}, bf16[1,256,384]{2,1,0:T(8,128)(2,1)S(1)}, u32[]{:S(2)}, u32[]{:S(2)}) %collective-permute-start.23) | collective-permute-done | bytes 196640 | tf_op jit(solution)/shard_map/ppermute | solution.py:51
  56.8 2.7 %up_terms.1 = (bf16[4,192,384]{2,1,0:T(8,128)(2,1)S(1)}, bf16[4,192,384]{2,1,0:T(8,128)(2,1)S(1)}) custom-call(s32[6]{0:T(128)S(1)} %pad_add_fusion.refs_0_, bf16[256,768]{1,0:T(8,128)(2,1)S(1)} %get-tuple-element.114.refs_3_.refs_1_, bf16[256,768]{1,0:T(8,128)(2,1)S(1)} %collective-permute-done.18.refs_2_, ...), custom_call_target="tpu_custom_call" | custom-call | flops 1000 | bytes 1000 | tf_op jit(solution)/shard_map/up_terms/pallas_call | solution.py:666
  59.4 2.6 %collective-permute-done.17.refs_0_ = bf16[4,384,256]{2,1,0:T(8,128)(2,1)S(1)} collective-permute-done((bf16[4,384,256]{2,1,0:T(8,128)(2,1)S(1)}, bf16[4,384,256]{2,1,0:T(8,128)(2,1)S(1)}, u32[]{:S(2)}, u32[]{:S(2)}) %collective-permute-start.17) | collective-permute-done | bytes 786464 | tf_op jit(solution)/shard_map/ppermute | solution.py:51
  62.7 1.9 %collective-permute-done.27 = f32[8,8,384]{2,1,0:T(8,128)S(1)} collective-permute-done((f32[8,8,384]{2,1,0:T(8,128)S(1)}, f32[8,8,384]{2,1,0:T(8,128)S(1)}, u32[]{:S(2)}, u32[]{:S(2)}) %collective-permute-start.27) | collective-permute-done | bytes 98336 | tf_op jit(solution)/shard_map/ppermute | solution.py:51
  64.6 1.5 %collective-permute-start.30 = (bf16[4,96,768]{2,1,0:T(8,128)(2,1)S(1)}, bf16[4,96,768]{2,1,0:T(8,128)(2,1)S(1)}, u32[]{:S(2)}, u32[]{:S(2)}) collective-permute-start(bf16[4,96,768]{2,1,0:T(8,128)(2,1)S(1)} %get-tuple-element.150), channel_id=1, source_target_pairs={{0,4},{1,5},{2,6},{3,7},{4,0},{5,1},{6,2},{7,3},{8,12},{9,13},{10,... | collective-permute-start | bytes 1769480 | tf_op jit(solution)/shard_map/ppermute | solution.py:55
  66.1 1.6 %collective-permute-start.28 = (f32[4,8,384]{2,1,0:T(8,128)S(1)}, f32[4,8,384]{2,1,0:T(8,128)S(1)}, u32[]{:S(2)}, u32[]{:S(2)}) collective-permute-start(f32[4,8,384]{2,1,0:T(8,128)S(1)} %relay.9), channel_id=1, source_target_pairs={{0,8},{1,9},{2,10},{3,11},{4,12},{5,13},{6,14},{7,15},{8,0},{9,1},... | collective-permute-start | bytes 147464 | tf_op jit(solution)/shard_map/ppermute | solution.py:51
  67.8 2.5 %collective-permute-done.28 = f32[4,8,384]{2,1,0:T(8,128)S(1)} collective-permute-done((f32[4,8,384]{2,1,0:T(8,128)S(1)}, f32[4,8,384]{2,1,0:T(8,128)S(1)}, u32[]{:S(2)}, u32[]{:S(2)}) %collective-permute-start.28) | collective-permute-done | bytes 49184 | tf_op jit(solution)/shard_map/ppermute | solution.py:51
  70.9 2.0 %mix_terms.2 = (bf16[2,208,384]{2,1,0:T(8,128)(2,1)S(1)}, bf16[2,208,384]{2,1,0:T(8,128)(2,1)S(1)}) custom-call(s32[6]{0:T(128)S(1)} %pad_add_fusion.refs_0_, bf16[2,768,256]{2,1,0:T(8,128)(2,1)S(1)} %get-tuple-element.120.refs_2_.refs_1_, bf16[2,768,256]{2,1,0:T(8,128)(2,1)S(1)} %collective-permute-done.14.refs_2_, ...), custom_call_target="tpu_custom_call" | custom-call | flops 1000 | bytes 1000 | tf_op jit(solution)/shard_map/mix_terms/pallas_call | solution.py:666
  72.9 1.6 %collective-permute-start.29 = (bf16[2,208,384]{2,1,0:T(8,128)(2,1)S(1)}, bf16[2,208,384]{2,1,0:T(8,128)(2,1)S(1)}, u32[]{:S(2)}, u32[]{:S(2)}) collective-permute-start(bf16[2,208,384]{2,1,0:T(8,128)(2,1)S(1)} %get-tuple-element.149), channel_id=1, source_target_pairs={{0,2},{1,5},{2,0},{3,7},{4,6},{5,1},{6,4},{7,3},{8,10},{9,13},{10,... | collective-permute-start | bytes 958472 | tf_op jit(solution)/shard_map/ppermute | solution.py:55
  74.4 2.0 %mix_terms.3 = (bf16[2,208,384]{2,1,0:T(8,128)(2,1)S(1)}, bf16[2,208,384]{2,1,0:T(8,128)(2,1)S(1)}) custom-call(s32[6]{0:T(128)S(1)} %pad_add_fusion.refs_0_, bf16[2,768,256]{2,1,0:T(8,128)(2,1)S(1)} %get-tuple-element.120.refs_2_.refs_1_, bf16[2,768,256]{2,1,0:T(8,128)(2,1)S(1)} %collective-permute-done.14.refs_2_, ...), custom_call_target="tpu_custom_call" | custom-call | flops 1000 | bytes 1000 | tf_op jit(solution)/shard_map/mix_terms/pallas_call | solution.py:666
  76.4 4.3 %collective-permute-done.30.refs_1_ = bf16[4,96,768]{2,1,0:T(8,128)(2,1)S(1)} collective-permute-done((bf16[4,96,768]{2,1,0:T(8,128)(2,1)S(1)}, bf16[4,96,768]{2,1,0:T(8,128)(2,1)S(1)}, u32[]{:S(2)}, u32[]{:S(2)}) %collective-permute-start.30) | collective-permute-done | bytes 589856 | tf_op jit(solution)/shard_map/ppermute | solution.py:55
  80.9 1.6 %collective-permute-start.34 = (bf16[2,96,768]{2,1,0:T(8,128)(2,1)S(1)}, bf16[2,96,768]{2,1,0:T(8,128)(2,1)S(1)}, u32[]{:S(2)}, u32[]{:S(2)}) collective-permute-start(bf16[2,96,768]{2,1,0:T(8,128)(2,1)S(1)} %get-tuple-element.157), channel_id=1, source_target_pairs={{0,8},{1,9},{2,10},{3,11},{4,12},{5,13},{6,14},{7,15},{8,0},{9,1},... | collective-permute-start | bytes 884744 | tf_op jit(solution)/shard_map/ppermute | solution.py:55
  83.0 4.9 %collective-permute-done.29.refs_1_ = bf16[2,208,384]{2,1,0:T(8,128)(2,1)S(1)} collective-permute-done((bf16[2,208,384]{2,1,0:T(8,128)(2,1)S(1)}, bf16[2,208,384]{2,1,0:T(8,128)(2,1)S(1)}, u32[]{:S(2)}, u32[]{:S(2)}) %collective-permute-start.29) | collective-permute-done | bytes 319520 | tf_op jit(solution)/shard_map/ppermute | solution.py:55
  88.6 1.6 %collective-permute-start.36 = (bf16[2,192,384]{2,1,0:T(8,128)(2,1)S(1)}, bf16[2,192,384]{2,1,0:T(8,128)(2,1)S(1)}, u32[]{:S(2)}, u32[]{:S(2)}) collective-permute-start(bf16[2,192,384]{2,1,0:T(8,128)(2,1)S(1)} %get-tuple-element.161), channel_id=1, source_target_pairs={{0,8},{1,9},{2,10},{3,11},{4,12},{5,13},{6,14},{7,15},{8,0},{9,1},... | collective-permute-start | bytes 884744 | tf_op jit(solution)/shard_map/ppermute | solution.py:55
  90.8 1.5 %collective-permute-start.31 = (bf16[1,208,384]{2,1,0:T(8,128)(2,1)S(1)}, bf16[1,208,384]{2,1,0:T(8,128)(2,1)S(1)}, u32[]{:S(2)}, u32[]{:S(2)}) collective-permute-start(bf16[1,208,384]{2,1,0:T(8,128)(2,1)S(1)} %get-tuple-element.154), channel_id=1, source_target_pairs={{0,4},{1,3},{2,6},{3,1},{4,0},{5,7},{6,2},{7,5},{8,12},{9,11},{10,... | collective-permute-start | bytes 479240 | tf_op jit(solution)/shard_map/ppermute | solution.py:55
  92.7 3.3 %collective-permute-done.31.refs_1_ = bf16[1,208,384]{2,1,0:T(8,128)(2,1)S(1)} collective-permute-done((bf16[1,208,384]{2,1,0:T(8,128)(2,1)S(1)}, bf16[1,208,384]{2,1,0:T(8,128)(2,1)S(1)}, u32[]{:S(2)}, u32[]{:S(2)}) %collective-permute-start.31) | collective-permute-done | bytes 159776 | tf_op jit(solution)/shard_map/ppermute | solution.py:55
  96.0 1.5 %collective-permute-start.38 = (bf16[1,208,384]{2,1,0:T(8,128)(2,1)S(1)}, bf16[1,208,384]{2,1,0:T(8,128)(2,1)S(1)}, u32[]{:S(2)}, u32[]{:S(2)}) collective-permute-start(bf16[1,208,384]{2,1,0:T(8,128)(2,1)S(1)} %get-tuple-element.167), channel_id=1, source_target_pairs={{0,4},{1,3},{2,6},{3,1},{4,0},{5,7},{6,2},{7,5},{8,12},{9,11},{10,... | collective-permute-start | bytes 479240 | tf_op jit(solution)/shard_map/ppermute | solution.py:55
  98.1 0.6 collective-permute-start.35
  98.6 9.6 %collective-permute-done.37.refs_1_ = bf16[1,96,768]{2,1,0:T(8,128)(2,1)S(1)} collective-permute-done((bf16[1,96,768]{2,1,0:T(8,128)(2,1)S(1)}, bf16[1,96,768]{2,1,0:T(8,128)(2,1)S(1)}, u32[]{:S(2)}, u32[]{:S(2)}) %collective-permute-start.37) | collective-permute-done | bytes 147488 | tf_op jit(solution)/shard_map/ppermute | solution.py:55
  108.2 0.7 down_end.1
  109.2 1.7 %collective-permute-done.39.refs_2_ = bf16[1,208,384]{2,1,0:T(8,128)(2,1)S(1)} collective-permute-done((bf16[1,208,384]{2,1,0:T(8,128)(2,1)S(1)}, bf16[1,208,384]{2,1,0:T(8,128)(2,1)S(1)}, u32[]{:S(2)}, u32[]{:S(2)}) %collective-permute-start.39) | collective-permute-done | bytes 159776 | tf_op jit(solution)/shard_map/ppermute | solution.py:51
  110.8 0.8 mix_end.1
  111.6 0.6 reduce
  112.2 2.9 %collective-permute-done.40 = bf16[1,192,384]{2,1,0:T(8,128)(2,1)S(1)} collective-permute-done((bf16[1,192,384]{2,1,0:T(8,128)(2,1)S(1)}, bf16[1,192,384]{2,1,0:T(8,128)(2,1)S(1)}, u32[]{:S(2)}, u32[]{:S(2)}) %collective-permute-start.40) | collective-permute-done | bytes 147488 | tf_op jit(solution)/shard_map/ppermute | solution.py:55
  115.2 0.7 add_bitcast_fusion
  115.9 1.5 %place.1 = (bf16[256,768]{1,0:T(8,128)(2,1)}, bf16[256,768]{1,0:T(8,128)(2,1)}) custom-call(s32[6]{0:T(128)S(1)} %pad_add_fusion.refs_0_, bf16[2,64,768]{2,1,0:T(8,128)(2,1)S(1)} %get-tuple-element.133.refs_11_.refs_0_.refs_1_, bf16[2,64,768]{2,1,0:T(8,128)(2,1)S(1)} %collective-permute-done.12.refs_1_.refs_2_, ...), custom_call_target="tpu_custom_call" | custom-call | flops 1000 | bytes 1000 | tf_op jit(solution)/shard_map/place/pallas_call | solution.py:666
  (76 shorter events, 10.4 us)
Async XLA Ops:
  3.0 6.7 %collective-permute-start = (bf16[2,64,768]{2,1,0:T(8,128)(2,1)S(1)}, bf16[2,64,768]{2,1,0:T(8,128)(2,1)S(1)}, u32[]{:S(2)}, u32[]{:S(2)}) collective-permute-start(bf16[2,64,768]{2,1,0:T(8,128)(2,1)S(1)} %get-tuple-element.101), channel_id=1, source_target_pairs={{0,2},{1,3},{2,0},{3,1},{4,6},{5,7},{6,4},{7,5},{8,10},{9,11},{10,... | collective-permute-start | bytes 589832 | tf_op jit(solution)/shard_map/ppermute | solution.py:51
  10.3 12.5 %collective-permute-start.3 = (bf16[256,768]{1,0:T(8,128)(2,1)S(1)}, bf16[256,768]{1,0:T(8,128)(2,1)S(1)}, u32[]{:S(2)}, u32[]{:S(2)}) collective-permute-start(bf16[256,768]{1,0:T(8,128)(2,1)S(1)} %relay.5), channel_id=1, source_target_pairs={{0,2},{1,3},{2,0},{3,1},{4,6},{5,7},{6,4},{7,5},{8,10},{9,11},{10,... | collective-permute-start | bytes 1179656 | tf_op jit(solution)/shard_map/ppermute | solution.py:51
  11.8 1.3 %collective-permute-start.1 = (bf16[64,768]{1,0:T(8,128)(2,1)S(1)}, bf16[64,768]{1,0:T(8,128)(2,1)S(1)}, u32[]{:S(2)}, u32[]{:S(2)}) collective-permute-start(bf16[64,768]{1,0:T(8,128)(2,1)S(1)} %get-tuple-element.104), channel_id=1, source_target_pairs={{0,1},{1,0},{2,3},{3,2},{4,5},{5,4},{6,7},{7,6},{8,9},{9,8},{10,11... | collective-permute-start | bytes 294920 | tf_op jit(solution)/shard_map/ppermute | solution.py:51
  11.9 1.5 %collective-permute-start.2 = (bf16[64,768]{1,0:T(8,128)(2,1)S(1)}, bf16[64,768]{1,0:T(8,128)(2,1)S(1)}, u32[]{:S(2)}, u32[]{:S(2)}) collective-permute-start(bf16[64,768]{1,0:T(8,128)(2,1)S(1)} %get-tuple-element.105), channel_id=1, source_target_pairs={{0,1},{1,0},{2,3},{3,2},{4,5},{5,4},{6,7},{7,6},{8,9},{9,8},{10,11... | collective-permute-start | bytes 294920 | tf_op jit(solution)/shard_map/ppermute | solution.py:51
  18.6 20.4 %collective-permute-start.9 = (bf16[2,768,256]{2,1,0:T(8,128)(2,1)S(1)}, bf16[2,768,256]{2,1,0:T(8,128)(2,1)S(1)}, u32[]{:S(2)}, u32[]{:S(2)}) collective-permute-start(bf16[2,768,256]{2,1,0:T(8,128)(2,1)S(1)} %get-tuple-element.120.refs_2_.refs_1_), channel_id=1, source_target_pairs={{0,8},{1,9},{2,10},{3,11},{4,12},{5,13},{6,14},{7,15},{8,0},{9,1},... | collective-permute-start | bytes 2359304 | tf_op jit(solution)/shard_map/ppermute | solution.py:51
  22.1 19.6 %collective-permute-start.7 = (bf16[2,256,768]{2,1,0:T(8,128)(2,1)S(1)}, bf16[2,256,768]{2,1,0:T(8,128)(2,1)S(1)}, u32[]{:S(2)}, u32[]{:S(2)}) collective-permute-start(bf16[2,256,768]{2,1,0:T(8,128)(2,1)S(1)} %get-tuple-element.117.refs_3_), channel_id=1, source_target_pairs={{0,2},{1,3},{2,0},{3,1},{4,6},{5,7},{6,4},{7,5},{8,10},{9,11},{10,... | collective-permute-start | bytes 2359304 | tf_op jit(solution)/shard_map/ppermute | solution.py:51
  22.8 4.9 %collective-permute-start.4 = (bf16[256,768]{1,0:T(8,128)(2,1)S(1)}, bf16[256,768]{1,0:T(8,128)(2,1)S(1)}, u32[]{:S(2)}, u32[]{:S(2)}) collective-permute-start(bf16[256,768]{1,0:T(8,128)(2,1)S(1)} %get-tuple-element.102.refs_2_.refs_0_.refs_1_), channel_id=1, source_target_pairs={{0,1},{1,0},{2,3},{3,2},{4,5},{5,4},{6,7},{7,6},{8,9},{9,8},{10,11... | collective-permute-start | bytes 1179656 | tf_op jit(solution)/shard_map/ppermute | solution.py:51
  22.8 4.9 %collective-permute-start.5 = (bf16[256,768]{1,0:T(8,128)(2,1)S(1)}, bf16[256,768]{1,0:T(8,128)(2,1)S(1)}, u32[]{:S(2)}, u32[]{:S(2)}) collective-permute-start(bf16[256,768]{1,0:T(8,128)(2,1)S(1)} %collective-permute-done.3.refs_2_), channel_id=1, source_target_pairs={{0,1},{1,0},{2,3},{3,2},{4,5},{5,4},{6,7},{7,6},{8,9},{9,8},{10,11... | collective-permute-start | bytes 1179656 | tf_op jit(solution)/shard_map/ppermute | solution.py:51
  23.3 11.2 %collective-permute-start.6 = (bf16[256,768]{1,0:T(8,128)(2,1)S(1)}, bf16[256,768]{1,0:T(8,128)(2,1)S(1)}, u32[]{:S(2)}, u32[]{:S(2)}) collective-permute-start(bf16[256,768]{1,0:T(8,128)(2,1)S(1)} %get-tuple-element.114.refs_3_.refs_1_), channel_id=1, source_target_pairs={{0,4},{1,5},{2,6},{3,7},{4,0},{5,1},{6,2},{7,3},{8,12},{9,13},{10,... | collective-permute-start | bytes 1179656 | tf_op jit(solution)/shard_map/ppermute | solution.py:51
  33.9 19.2 %collective-permute-start.21 = (bf16[4,256,384]{2,1,0:T(8,128)(2,1)S(1)}, bf16[4,256,384]{2,1,0:T(8,128)(2,1)S(1)}, u32[]{:S(2)}, u32[]{:S(2)}) collective-permute-start(bf16[4,256,384]{2,1,0:T(8,128)(2,1)S(1)} %get-tuple-element.180), channel_id=1, source_target_pairs={{0,4},{1,5},{2,6},{3,7},{4,0},{5,1},{6,2},{7,3},{8,12},{9,13},{10,... | collective-permute-start | bytes 2359304 | tf_op jit(solution)/shard_map/ppermute | solution.py:51
  34.5 9.2 %collective-permute-start.8 = (bf16[256,768]{1,0:T(8,128)(2,1)S(1)}, bf16[256,768]{1,0:T(8,128)(2,1)S(1)}, u32[]{:S(2)}, u32[]{:S(2)}) collective-permute-start(bf16[256,768]{1,0:T(8,128)(2,1)S(1)} %get-tuple-element.116.refs_2_), channel_id=1, source_target_pairs={{0,1},{1,0},{2,3},{3,2},{4,5},{5,4},{6,7},{7,6},{8,9},{9,8},{10,11... | collective-permute-start | bytes 1179656 | tf_op jit(solution)/shard_map/ppermute | solution.py:51
  34.5 19.5 %collective-permute-start.20 = (bf16[4,256,384]{2,1,0:T(8,128)(2,1)S(1)}, bf16[4,256,384]{2,1,0:T(8,128)(2,1)S(1)}, u32[]{:S(2)}, u32[]{:S(2)}) collective-permute-start(bf16[4,256,384]{2,1,0:T(8,128)(2,1)S(1)} %get-tuple-element.181.refs_5_), channel_id=1, source_target_pairs={{0,1},{1,0},{2,3},{3,2},{4,5},{5,4},{6,7},{7,6},{8,9},{9,8},{10,11... | collective-permute-start | bytes 2359304 | tf_op jit(solution)/shard_map/ppermute | solution.py:51
  39.1 2.7 %collective-permute-start.10 = (f32[8,128]{1,0:T(8,128)S(1)}, f32[8,128]{1,0:T(8,128)S(1)}, u32[]{:S(2)}, u32[]{:S(2)}) collective-permute-start(f32[8,128]{1,0:T(8,128)S(1)} %step.1), channel_id=1, source_target_pairs={{0,1},{1,0},{2,3},{3,2},{4,5},{5,4},{6,7},{7,6},{8,9},{9,8},{10,11... | collective-permute-start | bytes 12296 | tf_op jit(solution)/shard_map/ppermute | solution.py:51
  41.8 3.1 %collective-permute-start.11 = (bf16[256,768]{1,0:T(8,128)(2,1)S(1)}, bf16[256,768]{1,0:T(8,128)(2,1)S(1)}, u32[]{:S(2)}, u32[]{:S(2)}) collective-permute-start(bf16[256,768]{1,0:T(8,128)(2,1)S(1)} %relay.6), channel_id=1, source_target_pairs={{0,1},{1,0},{2,3},{3,2},{4,5},{5,4},{6,7},{7,6},{8,9},{9,8},{10,11... | collective-permute-start | bytes 1179656 | tf_op jit(solution)/shard_map/ppermute | solution.py:51
  42.0 20.0 %collective-permute-start.17 = (bf16[4,384,256]{2,1,0:T(8,128)(2,1)S(1)}, bf16[4,384,256]{2,1,0:T(8,128)(2,1)S(1)}, u32[]{:S(2)}, u32[]{:S(2)}) collective-permute-start(bf16[4,384,256]{2,1,0:T(8,128)(2,1)S(1)} %get-tuple-element.182), channel_id=1, source_target_pairs={{0,8},{1,9},{2,10},{3,11},{4,12},{5,13},{6,14},{7,15},{8,0},{9,1},... | collective-permute-start | bytes 2359304 | tf_op jit(solution)/shard_map/ppermute | solution.py:51
  43.7 9.7 %collective-permute-start.18 = (bf16[256,768]{1,0:T(8,128)(2,1)S(1)}, bf16[256,768]{1,0:T(8,128)(2,1)S(1)}, u32[]{:S(2)}, u32[]{:S(2)}) collective-permute-start(bf16[256,768]{1,0:T(8,128)(2,1)S(1)} %get-tuple-element.114.refs_3_.refs_1_), channel_id=1, source_target_pairs={{0,1},{1,0},{2,3},{3,2},{4,5},{5,4},{6,7},{7,6},{8,9},{9,8},{10,11... | collective-permute-start | bytes 1179656 | tf_op jit(solution)/shard_map/ppermute | solution.py:51
  44.9 8.9 %collective-permute-start.19 = (bf16[256,768]{1,0:T(8,128)(2,1)S(1)}, bf16[256,768]{1,0:T(8,128)(2,1)S(1)}, u32[]{:S(2)}, u32[]{:S(2)}) collective-permute-start(bf16[256,768]{1,0:T(8,128)(2,1)S(1)} %collective-permute-done.6.refs_10_.refs_3_), channel_id=1, source_target_pairs={{0,1},{1,0},{2,3},{3,2},{4,5},{5,4},{6,7},{7,6},{8,9},{9,8},{10,11... | collective-permute-start | bytes 1179656 | tf_op jit(solution)/shard_map/ppermute | solution.py:51
  53.3 1.5 %collective-permute-start.22 = (bf16[1,256,384]{2,1,0:T(8,128)(2,1)S(1)}, bf16[1,256,384]{2,1,0:T(8,128)(2,1)S(1)}, u32[]{:S(2)}, u32[]{:S(2)}) collective-permute-start(bf16[1,256,384]{2,1,0:T(8,128)(2,1)S(1)} %get-tuple-element.187), channel_id=1, source_target_pairs={{0,1},{1,0},{2,3},{3,2},{4,5},{5,4},{6,7},{7,6},{8,9},{9,8},{10,11... | collective-permute-start | bytes 589832 | tf_op jit(solution)/shard_map/ppermute | solution.py:51
  53.4 12.8 %collective-permute-start.14 = (bf16[2,768,256]{2,1,0:T(8,128)(2,1)S(1)}, bf16[2,768,256]{2,1,0:T(8,128)(2,1)S(1)}, u32[]{:S(2)}, u32[]{:S(2)}) collective-permute-start(bf16[2,768,256]{2,1,0:T(8,128)(2,1)S(1)} %get-tuple-element.120.refs_2_.refs_1_), channel_id=1, source_target_pairs={{0,1},{1,0},{2,3},{3,2},{4,5},{5,4},{6,7},{7,6},{8,9},{9,8},{10,11... | collective-permute-start | bytes 2359304 | tf_op jit(solution)/shard_map/ppermute | solution.py:51
  53.9 2.3 %collective-permute-start.23 = (bf16[1,256,384]{2,1,0:T(8,128)(2,1)S(1)}, bf16[1,256,384]{2,1,0:T(8,128)(2,1)S(1)}, u32[]{:S(2)}, u32[]{:S(2)}) collective-permute-start(bf16[1,256,384]{2,1,0:T(8,128)(2,1)S(1)} %get-tuple-element.186), channel_id=1, source_target_pairs={{0,1},{1,0},{2,3},{3,2},{4,5},{5,4},{6,7},{7,6},{8,9},{9,8},{10,11... | collective-permute-start | bytes 589832 | tf_op jit(solution)/shard_map/ppermute | solution.py:51
  54.0 2.5 %collective-permute-start.24 = (bf16[1,256,384]{2,1,0:T(8,128)(2,1)S(1)}, bf16[1,256,384]{2,1,0:T(8,128)(2,1)S(1)}, u32[]{:S(2)}, u32[]{:S(2)}) collective-permute-start(bf16[1,256,384]{2,1,0:T(8,128)(2,1)S(1)} %get-tuple-element.185), channel_id=1, source_target_pairs={{0,1},{1,0},{2,3},{3,2},{4,5},{5,4},{6,7},{7,6},{8,9},{9,8},{10,11... | collective-permute-start | bytes 589832 | tf_op jit(solution)/shard_map/ppermute | solution.py:51
  54.8 2.0 %collective-permute-start.25 = (bf16[1,256,384]{2,1,0:T(8,128)(2,1)S(1)}, bf16[1,256,384]{2,1,0:T(8,128)(2,1)S(1)}, u32[]{:S(2)}, u32[]{:S(2)}) collective-permute-start(bf16[1,256,384]{2,1,0:T(8,128)(2,1)S(1)} %get-tuple-element.184), channel_id=1, source_target_pairs={{0,1},{1,0},{2,3},{3,2},{4,5},{5,4},{6,7},{7,6},{8,9},{9,8},{10,11... | collective-permute-start | bytes 589832 | tf_op jit(solution)/shard_map/ppermute | solution.py:51
  56.2 14.6 %collective-permute-start.16 = (bf16[4,384,256]{2,1,0:T(8,128)(2,1)S(1)}, bf16[4,384,256]{2,1,0:T(8,128)(2,1)S(1)}, u32[]{:S(2)}, u32[]{:S(2)}) collective-permute-start(bf16[4,384,256]{2,1,0:T(8,128)(2,1)S(1)} %get-tuple-element.183.refs_5_), channel_id=1, source_target_pairs={{0,1},{1,0},{2,3},{3,2},{4,5},{5,4},{6,7},{7,6},{8,9},{9,8},{10,11... | collective-permute-start | bytes 2359304 | tf_op jit(solution)/shard_map/ppermute | solution.py:51
  56.5 14.4 %collective-permute-start.15 = (bf16[2,768,256]{2,1,0:T(8,128)(2,1)S(1)}, bf16[2,768,256]{2,1,0:T(8,128)(2,1)S(1)}, u32[]{:S(2)}, u32[]{:S(2)}) collective-permute-start(bf16[2,768,256]{2,1,0:T(8,128)(2,1)S(1)} %collective-permute-done.9.refs_0_.refs_3_), channel_id=1, source_target_pairs={{0,1},{1,0},{2,3},{3,2},{4,5},{5,4},{6,7},{7,6},{8,9},{9,8},{10,11... | collective-permute-start | bytes 2359304 | tf_op jit(solution)/shard_map/ppermute | solution.py:51
  62.1 8.8 %collective-permute-start.26 = (bf16[4,384,256]{2,1,0:T(8,128)(2,1)S(1)}, bf16[4,384,256]{2,1,0:T(8,128)(2,1)S(1)}, u32[]{:S(2)}, u32[]{:S(2)}) collective-permute-start(bf16[4,384,256]{2,1,0:T(8,128)(2,1)S(1)} %relay.8.refs_7_), channel_id=1, source_target_pairs={{0,1},{1,0},{2,3},{3,2},{4,5},{5,4},{6,7},{7,6},{8,9},{9,8},{10,11... | collective-permute-start | bytes 2359304 | tf_op jit(solution)/shard_map/ppermute | solution.py:51
  62.2 2.4 %collective-permute-start.27 = (f32[8,8,384]{2,1,0:T(8,128)S(1)}, f32[8,8,384]{2,1,0:T(8,128)S(1)}, u32[]{:S(2)}, u32[]{:S(2)}) collective-permute-start(f32[8,8,384]{2,1,0:T(8,128)S(1)} %get-tuple-element.147), channel_id=1, source_target_pairs={{0,1},{1,0},{2,3},{3,2},{4,5},{5,4},{6,7},{7,6},{8,9},{9,8},{10,11... | collective-permute-start | bytes 294920 | tf_op jit(solution)/shard_map/ppermute | solution.py:51
  64.6 16.2 %collective-permute-start.30 = (bf16[4,96,768]{2,1,0:T(8,128)(2,1)S(1)}, bf16[4,96,768]{2,1,0:T(8,128)(2,1)S(1)}, u32[]{:S(2)}, u32[]{:S(2)}) collective-permute-start(bf16[4,96,768]{2,1,0:T(8,128)(2,1)S(1)} %get-tuple-element.150), channel_id=1, source_target_pairs={{0,4},{1,5},{2,6},{3,7},{4,0},{5,1},{6,2},{7,3},{8,12},{9,13},{10,... | collective-permute-start | bytes 1769480 | tf_op jit(solution)/shard_map/ppermute | solution.py:55
  66.1 4.2 %collective-permute-start.28 = (f32[4,8,384]{2,1,0:T(8,128)S(1)}, f32[4,8,384]{2,1,0:T(8,128)S(1)}, u32[]{:S(2)}, u32[]{:S(2)}) collective-permute-start(f32[4,8,384]{2,1,0:T(8,128)S(1)} %relay.9), channel_id=1, source_target_pairs={{0,8},{1,9},{2,10},{3,11},{4,12},{5,13},{6,14},{7,15},{8,0},{9,1},... | collective-permute-start | bytes 147464 | tf_op jit(solution)/shard_map/ppermute | solution.py:51
  70.3 18.1 %collective-permute-start.33 = (bf16[4,192,384]{2,1,0:T(8,128)(2,1)S(1)}, bf16[4,192,384]{2,1,0:T(8,128)(2,1)S(1)}, u32[]{:S(2)}, u32[]{:S(2)}) collective-permute-start(bf16[4,192,384]{2,1,0:T(8,128)(2,1)S(1)} %get-tuple-element.156), channel_id=1, source_target_pairs={{0,2},{1,3},{2,0},{3,1},{4,6},{5,7},{6,4},{7,5},{8,10},{9,11},{10,... | collective-permute-start | bytes 1769480 | tf_op jit(solution)/shard_map/ppermute | solution.py:55
  72.9 15.1 %collective-permute-start.29 = (bf16[2,208,384]{2,1,0:T(8,128)(2,1)S(1)}, bf16[2,208,384]{2,1,0:T(8,128)(2,1)S(1)}, u32[]{:S(2)}, u32[]{:S(2)}) collective-permute-start(bf16[2,208,384]{2,1,0:T(8,128)(2,1)S(1)} %get-tuple-element.149), channel_id=1, source_target_pairs={{0,2},{1,5},{2,0},{3,7},{4,6},{5,1},{6,4},{7,3},{8,10},{9,13},{10,... | collective-permute-start | bytes 958472 | tf_op jit(solution)/shard_map/ppermute | solution.py:55
  80.9 7.5 %collective-permute-start.34 = (bf16[2,96,768]{2,1,0:T(8,128)(2,1)S(1)}, bf16[2,96,768]{2,1,0:T(8,128)(2,1)S(1)}, u32[]{:S(2)}, u32[]{:S(2)}) collective-permute-start(bf16[2,96,768]{2,1,0:T(8,128)(2,1)S(1)} %get-tuple-element.157), channel_id=1, source_target_pairs={{0,8},{1,9},{2,10},{3,11},{4,12},{5,13},{6,14},{7,15},{8,0},{9,1},... | collective-permute-start | bytes 884744 | tf_op jit(solution)/shard_map/ppermute | solution.py:55
  82.5 9.8 %collective-permute-start.32 = (bf16[2,208,384]{2,1,0:T(8,128)(2,1)S(1)}, bf16[2,208,384]{2,1,0:T(8,128)(2,1)S(1)}, u32[]{:S(2)}, u32[]{:S(2)}) collective-permute-start(bf16[2,208,384]{2,1,0:T(8,128)(2,1)S(1)} %get-tuple-element.155), channel_id=1, source_target_pairs={{0,2},{1,5},{2,0},{3,7},{4,6},{5,1},{6,4},{7,3},{8,10},{9,13},{10,... | collective-permute-start | bytes 958472 | tf_op jit(solution)/shard_map/ppermute | solution.py:55
  88.6 20.4 %collective-permute-start.36 = (bf16[2,192,384]{2,1,0:T(8,128)(2,1)S(1)}, bf16[2,192,384]{2,1,0:T(8,128)(2,1)S(1)}, u32[]{:S(2)}, u32[]{:S(2)}) collective-permute-start(bf16[2,192,384]{2,1,0:T(8,128)(2,1)S(1)} %get-tuple-element.161), channel_id=1, source_target_pairs={{0,8},{1,9},{2,10},{3,11},{4,12},{5,13},{6,14},{7,15},{8,0},{9,1},... | collective-permute-start | bytes 884744 | tf_op jit(solution)/shard_map/ppermute | solution.py:55
  90.3 7.4 %collective-permute-start.12 = (bf16[2,64,768]{2,1,0:T(8,128)(2,1)S(1)}, bf16[2,64,768]{2,1,0:T(8,128)(2,1)S(1)}, u32[]{:S(2)}, u32[]{:S(2)}) collective-permute-start(bf16[2,64,768]{2,1,0:T(8,128)(2,1)S(1)} %get-tuple-element.134), channel_id=1, source_target_pairs={{0,1},{1,0},{2,3},{3,2},{4,5},{5,4},{6,7},{7,6},{8,9},{9,8},{10,11... | collective-permute-start | bytes 589832 | tf_op jit(solution)/shard_map/ppermute | solution.py:51
  90.3 7.8 %collective-permute-start.13 = (bf16[2,64,768]{2,1,0:T(8,128)(2,1)S(1)}, bf16[2,64,768]{2,1,0:T(8,128)(2,1)S(1)}, u32[]{:S(2)}, u32[]{:S(2)}) collective-permute-start(bf16[2,64,768]{2,1,0:T(8,128)(2,1)S(1)} %get-tuple-element.144), channel_id=1, source_target_pairs={{0,1},{1,0},{2,3},{3,2},{4,5},{5,4},{6,7},{7,6},{8,9},{9,8},{10,11... | collective-permute-start | bytes 589832 | tf_op jit(solution)/shard_map/ppermute | solution.py:51
  90.8 5.3 %collective-permute-start.31 = (bf16[1,208,384]{2,1,0:T(8,128)(2,1)S(1)}, bf16[1,208,384]{2,1,0:T(8,128)(2,1)S(1)}, u32[]{:S(2)}, u32[]{:S(2)}) collective-permute-start(bf16[1,208,384]{2,1,0:T(8,128)(2,1)S(1)} %get-tuple-element.154), channel_id=1, source_target_pairs={{0,4},{1,3},{2,6},{3,1},{4,0},{5,7},{6,2},{7,5},{8,12},{9,11},{10,... | collective-permute-start | bytes 479240 | tf_op jit(solution)/shard_map/ppermute | solution.py:55
  92.3 15.9 %collective-permute-start.37 = (bf16[1,96,768]{2,1,0:T(8,128)(2,1)S(1)}, bf16[1,96,768]{2,1,0:T(8,128)(2,1)S(1)}, u32[]{:S(2)}, u32[]{:S(2)}) collective-permute-start(bf16[1,96,768]{2,1,0:T(8,128)(2,1)S(1)} %get-tuple-element.162), channel_id=1, source_target_pairs={{0,16},{1,17},{2,18},{3,19},{4,20},{5,21},{6,22},{7,23},{8,24},{9,... | collective-permute-start | bytes 442376 | tf_op jit(solution)/shard_map/ppermute | solution.py:55
  96.0 13.1 %collective-permute-start.38 = (bf16[1,208,384]{2,1,0:T(8,128)(2,1)S(1)}, bf16[1,208,384]{2,1,0:T(8,128)(2,1)S(1)}, u32[]{:S(2)}, u32[]{:S(2)}) collective-permute-start(bf16[1,208,384]{2,1,0:T(8,128)(2,1)S(1)} %get-tuple-element.167), channel_id=1, source_target_pairs={{0,4},{1,3},{2,6},{3,1},{4,0},{5,7},{6,2},{7,5},{8,12},{9,11},{10,... | collective-permute-start | bytes 479240 | tf_op jit(solution)/shard_map/ppermute | solution.py:55
  97.6 13.2 %collective-permute-start.39 = (bf16[1,208,384]{2,1,0:T(8,128)(2,1)S(1)}, bf16[1,208,384]{2,1,0:T(8,128)(2,1)S(1)}, u32[]{:S(2)}, u32[]{:S(2)}) collective-permute-start(bf16[1,208,384]{2,1,0:T(8,128)(2,1)S(1)} %add_last.1.refs_4_.refs_2_), channel_id=1, source_target_pairs={{0,16},{1,17},{2,18},{3,19},{4,20},{5,21},{6,22},{7,23},{8,24},{9,... | collective-permute-start | bytes 479240 | tf_op jit(solution)/shard_map/ppermute | solution.py:51
  98.1 17.9 %collective-permute-start.35 = (bf16[4,64,768]{2,1,0:T(8,128)(2,1)S(1)}, bf16[4,64,768]{2,1,0:T(8,128)(2,1)S(1)}, u32[]{:S(2)}, u32[]{:S(2)}) collective-permute-start(bf16[4,64,768]{2,1,0:T(8,128)(2,1)S(1)} %gather.1), channel_id=1, source_target_pairs={{0,2},{1,3},{2,0},{3,1},{4,6},{5,7},{6,4},{7,5},{8,10},{9,11},{10,... | collective-permute-start | bytes 1179656 | tf_op jit(solution)/shard_map/ppermute | solution.py:51
  109.1 6.1 %collective-permute-start.40 = (bf16[1,192,384]{2,1,0:T(8,128)(2,1)S(1)}, bf16[1,192,384]{2,1,0:T(8,128)(2,1)S(1)}, u32[]{:S(2)}, u32[]{:S(2)}) collective-permute-start(bf16[1,192,384]{2,1,0:T(8,128)(2,1)S(1)} %get-tuple-element.176), channel_id=1, source_target_pairs={{0,16},{1,17},{2,18},{3,19},{4,20},{5,21},{6,22},{7,23},{8,24},{9,... | collective-permute-start | bytes 442376 | tf_op jit(solution)/shard_map/ppermute | solution.py:55

commit v4 on v3

--- a/solution.py
+++ b/solution.py
@@ -18,7 +18,7 @@
 eps = 1e-06
 neg_big = -1e30
 
-DOWN_ORDER = ((1, 2, 3), (1, 2, 3))
+DOWN_ORDER = ((1, 3, 2), (1, 3, 2))
 UP_ORDER = ((0, 2, 3), (0, 2, 3))
 MIX_ORDER = ((0, 1), (1, 0))
 
@@ -403,6 +403,7 @@
     proj_copy.start()
     rows, width = resid_ref.shape
     out_grad = slot_cots(at_ref, [cot0, cot1, cot2, cot3], 0)
+    normed, scale = norm_parts(resid_ref[...])
     second = jnp.zeros((rows, width), F32)
     half = width // 2
     for step in range(4):
@@ -410,12 +411,11 @@
         span = pl.ds(pl.multiple_of(quarter * width, width), width)
         slope = (slope_far_ref if step // 2 else slope_near_ref)[step % 2]
         hidden = times_trans(out_grad, down_ref[span, :]) * slope.astype(F32)
+        up_bias_ref[:, span] = jnp.sum(hidden, axis=0, keepdims=True)
         hidden = hidden.astype(BF)
         for side in range(2):
             hidden_ref[(at_ref[1] & 1) ^ side, quarter] = hidden[:, side * half : (side + 1) * half]
-        up_bias_ref[:, span] = jnp.sum(hidden.astype(F32), axis=0, keepdims=True)
         second += times_trans(hidden, up_ref[:, span])
-    normed, scale = norm_parts(resid_ref[...])
     gain_ref[...] = jnp.sum(second * normed, axis=0, keepdims=True)
     bias_ref[...] = jnp.sum(second, axis=0, keepdims=True)
     grad = out_grad.astype(F32) + norm_back(second, normed, scale, gain2_ref[...][None])
@@ -623,8 +623,8 @@
     proj_ref[...] = total[:rows, split:]
     at, row = 0, rows
     for ref in vec_refs:
-        size = ref.shape[1]
-        ref[...] = total[row : row + 1, at : at + size]
+        size = ref.shape[0]
+        ref[...] = total[row, at : at + size]
         at += size
         if at == total.shape[1]:
             at, row = 0, row + 1
@@ -722,7 +722,7 @@
             "ppp",
             [self.keep, got, across],
             [shaped(F32, rows, qkv_columns), shaped(F32, rows, share)]
-            + [shaped(F32, 1, size) for size in sizes],
+            + [shaped(F32, size) for size in sizes],
         )
 
 
@@ -945,7 +945,7 @@
     )
     packed = packed + place.swap(packed, 1)
     hidden_beyond = relay(hidden_beyond, [input_keep])
-    packed = packed[:half] + place.swap(relay(packed[half:], [hidden_beyond]), z_mask)
+    packed = packed[:half] + place.swap(packed[half:], z_mask)
     hidden_sets = [hidden_grad[0], place.swap(hidden_grad[0], 1), hidden_beyond]
     hidden_sets += [place.swap(hidden_beyond[index : index + 1], 1) for index in range(4)]
     up_send, up_keep = kernel_call(
@@ -969,21 +969,25 @@
         )
         return Sum(place, MIX_ORDER, send, keep)
 
-    first_sum = mix_terms(1, [up_keep])
-    second_sum = mix_terms(0, [first_sum.keep])
-    last = down_sum.go([second_sum.keep])
+    last = up_keep
+    first_sum = mix_terms(1, [last])
+    last = first_sum.keep
+    second_sum = mix_terms(0, [last])
+    last = second_sum.keep
+    last = down_sum.go([last])
     last = first_sum.go([last])
-    last = down_sum.go([last])
     last = up_sum.go([last])
     last = second_sum.go([last])
     across = first_sum.last([last])
+    last = across
     returns = [mixed_keep, place.swap(mixed_send, 1), input_keep, place.swap(input_send, 1)]
     (far_rows,) = kernel_call(
-        gather_kernel, "pppp", returns, [kept(BF, 4, slot_rows, width)], after=[across]
+        gather_kernel, "pppp", returns, [kept(BF, 4, slot_rows, width)], after=[last]
     )
     far_rows = place.swap(far_rows, x_mask)
-    down_block, last = down_sum.end_down([across])
+    last = down_sum.go([last])
     last = up_sum.go([last])
+    down_block, last = down_sum.end_down([last])
     mixed, input_grad = kernel_call(
         place_kernel,
         "s" + "p" * 5,
@@ -996,7 +1000,7 @@
     up_block = up_sum.end()
 
     qkv_block, proj_block = mix_block[:2]
-    reduced = [within_group(place, item.reshape(-1), 0) for item in mix_block[2:]]
+    reduced = [within_group(place, item, 0) for item in mix_block[2:]]
     return (
         mixed,
         input_grad,

time: 118 us -> 116 us (0.983)
  the two profiles are of different devices: /device:TPU:24 before, /device:TPU:0 now
where the time goes in v4:
time: 116 us
  Pallas kernels  43.6 us (38%)
  waiting for transfers between devices  35.6 us (31%)
  starting transfers between devices  33.4 us (29%)
  other arithmetic  1.5 us (1%)
    pallas_call x31, Pallas kernels, kernel_call(): pl.pallas_call(run, out_shape=outs, in_specs=[SPECS[kind] for kind in spe...  43.6 us
    ppermute x31, starting transfers between devices, swap(): return lax.ppermute(value, AXES, pairs)  18.5 us
    ppermute x10, waiting for transfers between devices, swap_by_core(): return lax.ppermute(value, AXES, pairs)  18.3 us
    ppermute x31, waiting for transfers between devices, swap(): return lax.ppermute(value, AXES, pairs)  17.4 us
    ppermute x10, starting transfers between devices, swap_by_core(): return lax.ppermute(value, AXES, pairs)  14.9 us
  transfers between devices with their start and end apart: 41, of which 17 were waited for; matrix products, arithmetic and copies ran while one was open for 1% of the time, Pallas kernels for 35%

profile of v4, /device:TPU:0, one launch (start us, length us, event | category | flops | bytes accessed | tf_op | source)
XLA Modules:
  0.0 115.7 jit_solution(5674939050571919190)
XLA Ops:
  0.6 0.7 pad_add_fusion.refs_0_
  1.4 1.6 %token_slice.1 = (bf16[64,768]{1,0:T(8,128)(2,1)S(1)}, bf16[64,768]{1,0:T(8,128)(2,1)S(1)}, bf16[2,64,768]{2,1,0:T(8,128)(2,1)S(1)}) custom-call(s32[6]{0:T(128)S(1)} %pad_add_fusion.refs_0_, bf16[2,2,64,768]{3,2,1,0:T(8,128)(2,1)} %bitcast.15), custom_call_target="tpu_custom_call" | custom-call | flops 1000 | bytes 1000 | tf_op jit(solution)/shard_map/token_slice/pallas_call | solution.py:666
  3.0 3.0 %collective-permute-start = (bf16[2,64,768]{2,1,0:T(8,128)(2,1)S(1)}, bf16[2,64,768]{2,1,0:T(8,128)(2,1)S(1)}, u32[]{:S(2)}, u32[]{:S(2)}) collective-permute-start(bf16[2,64,768]{2,1,0:T(8,128)(2,1)S(1)} %get-tuple-element.101), channel_id=1, source_target_pairs={{0,2},{1,3},{2,0},{3,1},{4,6},{5,7},{6,4},{7,5},{8,10},{9,11},{10,... | collective-permute-start | bytes 589832 | tf_op jit(solution)/shard_map/ppermute | solution.py:51
  6.0 2.5 %load.1 = (bf16[768,2304]{1,0:T(8,128)(2,1)S(1)}, bf16[768,768]{1,0:T(8,128)(2,1)S(1)}, bf16[256,768]{1,0:T(8,128)(2,1)S(1)}, f32[768]{0:T(1024)S(1)}, f32[768]{...) custom-call(bf16[768,2304]{1,0:T(8,128)(2,1)} %refs_1_.5, ...), custom_call_target="tpu_custom_call" | custom-call | flops 1000 | bytes 1000 | tf_op jit(solution)/shard_map/load/pallas_call | solution.py:666
  8.5 2.4 %collective-permute-done.refs_1_ = bf16[2,64,768]{2,1,0:T(8,128)(2,1)S(1)} collective-permute-done((bf16[2,64,768]{2,1,0:T(8,128)(2,1)S(1)}, bf16[2,64,768]{2,1,0:T(8,128)(2,1)S(1)}, u32[]{:S(2)}, u32[]{:S(2)}) %collective-permute-start) | collective-permute-done | bytes 196640 | tf_op jit(solution)/shard_map/ppermute | solution.py:51
  11.5 1.8 %collective-permute-start.3 = (bf16[256,768]{1,0:T(8,128)(2,1)S(1)}, bf16[256,768]{1,0:T(8,128)(2,1)S(1)}, u32[]{:S(2)}, u32[]{:S(2)}) collective-permute-start(bf16[256,768]{1,0:T(8,128)(2,1)S(1)} %relay.4), channel_id=1, source_target_pairs={{0,2},{1,3},{2,0},{3,1},{4,6},{5,7},{6,4},{7,5},{8,10},{9,11},{10,... | collective-permute-start | bytes 1179656 | tf_op jit(solution)/shard_map/ppermute | solution.py:51
  13.8 0.8 collective-permute-done.1.refs_3_
  14.8 5.4 %attention.1 = (bf16[256,768]{1,0:T(8,128)(2,1)S(1)}, bf16[2,768,256]{2,1,0:T(8,128)(2,1)S(1)}, bf16[768,256]{1,0:T(8,128)(2,1)S(1)}, bf16[768,256]{1,0:T(8,128)...) custom-call(s32[6]{0:T(128)S(1)} %pad_add_fusion.refs_0_, ...), custom_call_target="tpu_custom_call" | custom-call | flops 1000 | bytes 1000 | tf_op jit(solution)/shard_map/attention/pallas_call | solution.py:666
  20.1 1.7 %collective-permute-start.9 = (bf16[2,768,256]{2,1,0:T(8,128)(2,1)S(1)}, bf16[2,768,256]{2,1,0:T(8,128)(2,1)S(1)}, u32[]{:S(2)}, u32[]{:S(2)}) collective-permute-start(bf16[2,768,256]{2,1,0:T(8,128)(2,1)S(1)} %get-tuple-element.120.refs_2_.refs_1_), channel_id=1, source_target_pairs={{0,8},{1,9},{2,10},{3,11},{4,12},{5,13},{6,14},{7,15},{8,0},{9,1},... | collective-permute-start | bytes 2359304 | tf_op jit(solution)/shard_map/ppermute | solution.py:51
  21.8 3.0 %hidden_far.1 = (bf16[256,768]{1,0:T(8,128)(2,1)S(1)}, bf16[2,256,768]{2,1,0:T(8,128)(2,1)S(1)}, bf16[2,256,768]{2,1,0:T(8,128)(2,1)S(1)}) custom-call(s32[6]{0:T(128)S(1)} %pad_add_fusion.refs_0_, f32[768]{0:T(1024)S(1)} %get-tuple-element.99.refs_1_.refs_6_, f32[768]{0:T(1024)S(1)} %get-tuple-element.100.refs_2_, ...), custom_call_target="tpu_custom_call" | custom-call | flops 1000 | bytes 1000 | tf_op jit(solution)/shard_map/hidden_far/pallas_call | solution.py:666
  24.7 0.6 collective-permute-start.7
  25.9 1.5 %collective-permute-start.6 = (bf16[256,768]{1,0:T(8,128)(2,1)S(1)}, bf16[256,768]{1,0:T(8,128)(2,1)S(1)}, u32[]{:S(2)}, u32[]{:S(2)}) collective-permute-start(bf16[256,768]{1,0:T(8,128)(2,1)S(1)} %get-tuple-element.114.refs_3_.refs_1_), channel_id=1, source_target_pairs={{0,4},{1,5},{2,6},{3,7},{4,0},{5,1},{6,2},{7,3},{8,12},{9,13},{10,... | collective-permute-start | bytes 1179656 | tf_op jit(solution)/shard_map/ppermute | solution.py:51
  27.4 2.9 %hidden_near.1 = (bf16[256,768]{1,0:T(8,128)(2,1)S(1)}, bf16[256,768]{1,0:T(8,128)(2,1)S(1)}, bf16[2,256,768]{2,1,0:T(8,128)(2,1)S(1)}, bf16[3072,768]{1,0:T(8,128)(2,1)S(1)}) custom-call(s32[6]{0:T(128)S(1)} %pad_add_fusion.refs_0_, bf16[3072,768]{1,0:T(8,128)(2,1)} %refs_1_.4, f32[3072]{0:T(1024)S(1)} %get-tuple-element.98.refs_3_.refs_2_, ...), custom_call_target="tpu_custom_call" | custom-call | flops 1000 | bytes 1000 | tf_op jit(solution)/shard_map/hidden_near/pallas_call | solution.py:666
  30.3 5.8 %hidden_back.1 = (bf16[2,4,256,384]{3,2,1,0:T(8,128)(2,1)S(1)}, f32[256,768]{1,0:T(8,128)S(1)}, bf16[8,96,256]{2,1,0:T(8,128)(2,1)S(1)}, bf16[768,256]{1,0:T(8,1...) custom-call(s32[6]{0:T(128)S(1)} %pad_add_fusion.refs_0_, ...), custom_call_target="tpu_custom_call" | custom-call | flops 1000 | bytes 1000 | tf_op jit(solution)/shard_map/hidden_back/pallas_call | solution.py:666
  36.5 0.6 collective-permute-start.21
  37.6 4.0 %attention_back.1 = (bf16[8,384,256]{2,1,0:T(8,128)(2,1)S(1)}, bf16[768,2304]{1,0:T(8,128)(2,1)S(1)}) custom-call(s32[6]{0:T(128)S(1)} %pad_add_fusion.refs_0_, bf16[768,2304]{1,0:T(8,128)(2,1)} %refs_1_.5, bf16[2,768,256]{2,1,0:T(8,128)(2,1)S(1)} %get-tuple-element.120.refs_2_.refs_1_, bf16[768,256]{1,0:T(8,128)(2,1)S(1)} %get-tuple-element.121.refs_3_, ...), custom_call_target="tpu_custom_call" | custom-call | flops 1000 | bytes 1000 | tf_op jit(solution)/shard_map/attention_back/pallas_call | solution.py:666
  41.7 2.6 %collective-permute-done.7 = bf16[2,256,768]{2,1,0:T(8,128)(2,1)S(1)} collective-permute-done((bf16[2,256,768]{2,1,0:T(8,128)(2,1)S(1)}, bf16[2,256,768]{2,1,0:T(8,128)(2,1)S(1)}, u32[]{:S(2)}, u32[]{:S(2)}) %collective-permute-start.7) | collective-permute-done | bytes 786464 | tf_op jit(solution)/shard_map/ppermute | solution.py:51
  45.4 1.0 out_grad.1
  46.8 2.0 %down_terms.1 = (bf16[4,96,768]{2,1,0:T(8,128)(2,1)S(1)}, bf16[4,96,768]{2,1,0:T(8,128)(2,1)S(1)}) custom-call(s32[6]{0:T(128)S(1)} %pad_add_fusion.refs_0_, bf16[768,1024]{1,0:T(8,128)(2,1)S(1)} %get-tuple-element.131.refs_1_, bf16[256,768]{1,0:T(8,128)(2,1)S(1)} %get-tuple-element.115.refs_2_.refs_1_, bf16[256,768]{1,0:T(8,128)(2,1)S(1)} %get-tuple-element.189.refs_3_, ...), custom_call_target="tpu_custom_call" | custom-call | flops 1000 | bytes 1000 | tf_op jit(solution)/shard_map/down_terms/pallas_call | solution.py:666
  48.8 1.9 %mixed.1 = (bf16[2,64,768]{2,1,0:T(8,128)(2,1)S(1)}, bf16[2,64,768]{2,1,0:T(8,128)(2,1)S(1)}) custom-call(s32[6]{0:T(128)S(1)} %pad_add_fusion.refs_0_, bf16[256,768]{1,0:T(8,128)(2,1)S(1)} %get-tuple-element.115.refs_2_.refs_1_, bf16[256,768]{1,0:T(8,128)(2,1)S(1)} %get-tuple-element.116.refs_2_, bf16[2,256,768]{2,1,0:T(8,128)(2,1)S(1)} %get-tuple-element.117.refs_3_, ...), custom_call_target="tpu_custom_call" | custom-call | flops 1000 | bytes 1000 | tf_op jit(solution)/shard_map/mixed/pallas_call | solution.py:666
  50.8 2.3 %first_back.1 = (bf16[2,64,768]{2,1,0:T(8,128)(2,1)S(1)}, bf16[2,64,768]{2,1,0:T(8,128)(2,1)S(1)}, f32[8,8,384]{2,1,0:T(8,128)S(1)}) custom-call(s32[6]{0:T(128)S(1)} %pad_add_fusion.refs_0_, f32[768]{0:T(1024)S(1)} %get-tuple-element.106.refs_6_.refs_1_, bf16[256,768]{1,0:T(8,128)(2,1)S(1)} %get-tuple-element.135.refs_2_, ...), custom_call_target="tpu_custom_call" | custom-call | flops 1000 | bytes 1000 | tf_op jit(solution)/shard_map/first_back/pallas_call | solution.py:666
  53.1 2.7 %collective-permute-done.21.refs_0_ = bf16[4,256,384]{2,1,0:T(8,128)(2,1)S(1)} collective-permute-done((bf16[4,256,384]{2,1,0:T(8,128)(2,1)S(1)}, bf16[4,256,384]{2,1,0:T(8,128)(2,1)S(1)}, u32[]{:S(2)}, u32[]{:S(2)}) %collective-permute-start.21) | collective-permute-done | bytes 786464 | tf_op jit(solution)/shard_map/ppermute | solution.py:51
  57.5 1.3 %collective-permute-done.23.refs_9_ = bf16[1,256,384]{2,1,0:T(8,128)(2,1)S(1)} collective-permute-done((bf16[1,256,384]{2,1,0:T(8,128)(2,1)S(1)}, bf16[1,256,384]{2,1,0:T(8,128)(2,1)S(1)}, u32[]{:S(2)}, u32[]{:S(2)}) %collective-permute-start.23) | collective-permute-done | bytes 196640 | tf_op jit(solution)/shard_map/ppermute | solution.py:51
  59.4 2.7 %up_terms.1 = (bf16[4,192,384]{2,1,0:T(8,128)(2,1)S(1)}, bf16[4,192,384]{2,1,0:T(8,128)(2,1)S(1)}) custom-call(s32[6]{0:T(128)S(1)} %pad_add_fusion.refs_0_, bf16[256,768]{1,0:T(8,128)(2,1)S(1)} %get-tuple-element.114.refs_3_.refs_1_, bf16[256,768]{1,0:T(8,128)(2,1)S(1)} %collective-permute-done.18.refs_2_, ...), custom_call_target="tpu_custom_call" | custom-call | flops 1000 | bytes 1000 | tf_op jit(solution)/shard_map/up_terms/pallas_call | solution.py:666
  62.0 2.6 %collective-permute-done.17.refs_0_ = bf16[4,384,256]{2,1,0:T(8,128)(2,1)S(1)} collective-permute-done((bf16[4,384,256]{2,1,0:T(8,128)(2,1)S(1)}, bf16[4,384,256]{2,1,0:T(8,128)(2,1)S(1)}, u32[]{:S(2)}, u32[]{:S(2)}) %collective-permute-start.17) | collective-permute-done | bytes 786464 | tf_op jit(solution)/shard_map/ppermute | solution.py:51
  65.2 1.9 %collective-permute-done.27 = f32[8,8,384]{2,1,0:T(8,128)S(1)} collective-permute-done((f32[8,8,384]{2,1,0:T(8,128)S(1)}, f32[8,8,384]{2,1,0:T(8,128)S(1)}, u32[]{:S(2)}, u32[]{:S(2)}) %collective-permute-start.27) | collective-permute-done | bytes 98336 | tf_op jit(solution)/shard_map/ppermute | solution.py:51
  67.7 1.5 %collective-permute-start.30 = (bf16[4,96,768]{2,1,0:T(8,128)(2,1)S(1)}, bf16[4,96,768]{2,1,0:T(8,128)(2,1)S(1)}, u32[]{:S(2)}, u32[]{:S(2)}) collective-permute-start(bf16[4,96,768]{2,1,0:T(8,128)(2,1)S(1)} %get-tuple-element.150), channel_id=1, source_target_pairs={{0,4},{1,5},{2,6},{3,7},{4,0},{5,1},{6,2},{7,3},{8,12},{9,13},{10,... | collective-permute-start | bytes 1769480 | tf_op jit(solution)/shard_map/ppermute | solution.py:55
  69.2 2.1 %collective-permute-done.28 = f32[4,8,384]{2,1,0:T(8,128)S(1)} collective-permute-done((f32[4,8,384]{2,1,0:T(8,128)S(1)}, f32[4,8,384]{2,1,0:T(8,128)S(1)}, u32[]{:S(2)}, u32[]{:S(2)}) %collective-permute-start.28) | collective-permute-done | bytes 49184 | tf_op jit(solution)/shard_map/ppermute | solution.py:51
  71.9 2.0 %mix_terms.2 = (bf16[2,208,384]{2,1,0:T(8,128)(2,1)S(1)}, bf16[2,208,384]{2,1,0:T(8,128)(2,1)S(1)}) custom-call(s32[6]{0:T(128)S(1)} %pad_add_fusion.refs_0_, bf16[2,768,256]{2,1,0:T(8,128)(2,1)S(1)} %get-tuple-element.120.refs_2_.refs_1_, bf16[2,768,256]{2,1,0:T(8,128)(2,1)S(1)} %collective-permute-done.14.refs_2_, ...), custom_call_target="tpu_custom_call" | custom-call | flops 1000 | bytes 1000 | tf_op jit(solution)/shard_map/mix_terms/pallas_call | solution.py:666
  73.9 1.6 %collective-permute-start.29 = (bf16[2,208,384]{2,1,0:T(8,128)(2,1)S(1)}, bf16[2,208,384]{2,1,0:T(8,128)(2,1)S(1)}, u32[]{:S(2)}, u32[]{:S(2)}) collective-permute-start(bf16[2,208,384]{2,1,0:T(8,128)(2,1)S(1)} %get-tuple-element.149), channel_id=1, source_target_pairs={{0,2},{1,5},{2,0},{3,7},{4,6},{5,1},{6,4},{7,3},{8,10},{9,13},{10,... | collective-permute-start | bytes 958472 | tf_op jit(solution)/shard_map/ppermute | solution.py:55
  75.5 2.0 %mix_terms.3 = (bf16[2,208,384]{2,1,0:T(8,128)(2,1)S(1)}, bf16[2,208,384]{2,1,0:T(8,128)(2,1)S(1)}) custom-call(s32[6]{0:T(128)S(1)} %pad_add_fusion.refs_0_, bf16[2,768,256]{2,1,0:T(8,128)(2,1)S(1)} %get-tuple-element.120.refs_2_.refs_1_, bf16[2,768,256]{2,1,0:T(8,128)(2,1)S(1)} %collective-permute-done.14.refs_2_, ...), custom_call_target="tpu_custom_call" | custom-call | flops 1000 | bytes 1000 | tf_op jit(solution)/shard_map/mix_terms/pallas_call | solution.py:666
  77.5 0.6 collective-permute-start.32
  78.1 5.9 %collective-permute-done.30.refs_1_ = bf16[4,96,768]{2,1,0:T(8,128)(2,1)S(1)} collective-permute-done((bf16[4,96,768]{2,1,0:T(8,128)(2,1)S(1)}, bf16[4,96,768]{2,1,0:T(8,128)(2,1)S(1)}, u32[]{:S(2)}, u32[]{:S(2)}) %collective-permute-start.30) | collective-permute-done | bytes 589856 | tf_op jit(solution)/shard_map/ppermute | solution.py:55
  84.1 2.7 %collective-permute-start.35 = (bf16[2,96,768]{2,1,0:T(8,128)(2,1)S(1)}, bf16[2,96,768]{2,1,0:T(8,128)(2,1)S(1)}, u32[]{:S(2)}, u32[]{:S(2)}) collective-permute-start(bf16[2,96,768]{2,1,0:T(8,128)(2,1)S(1)} %get-tuple-element.159), channel_id=1, source_target_pairs={{0,16},{1,17},{2,18},{3,19},{4,20},{5,21},{6,22},{7,23},{8,24},{9,... | collective-permute-start | bytes 884744 | tf_op jit(solution)/shard_map/ppermute | solution.py:55
  86.7 2.3 %collective-permute-done.29.refs_1_ = bf16[2,208,384]{2,1,0:T(8,128)(2,1)S(1)} collective-permute-done((bf16[2,208,384]{2,1,0:T(8,128)(2,1)S(1)}, bf16[2,208,384]{2,1,0:T(8,128)(2,1)S(1)}, u32[]{:S(2)}, u32[]{:S(2)}) %collective-permute-start.29) | collective-permute-done | bytes 319520 | tf_op jit(solution)/shard_map/ppermute | solution.py:55
  90.3 2.1 %collective-permute-done.32.refs_1_ = bf16[2,208,384]{2,1,0:T(8,128)(2,1)S(1)} collective-permute-done((bf16[2,208,384]{2,1,0:T(8,128)(2,1)S(1)}, bf16[2,208,384]{2,1,0:T(8,128)(2,1)S(1)}, u32[]{:S(2)}, u32[]{:S(2)}) %collective-permute-start.32) | collective-permute-done | bytes 319520 | tf_op jit(solution)/shard_map/ppermute | solution.py:55
  92.4 1.5 %collective-permute-start.31 = (bf16[1,208,384]{2,1,0:T(8,128)(2,1)S(1)}, bf16[1,208,384]{2,1,0:T(8,128)(2,1)S(1)}, u32[]{:S(2)}, u32[]{:S(2)}) collective-permute-start(bf16[1,208,384]{2,1,0:T(8,128)(2,1)S(1)} %get-tuple-element.154), channel_id=1, source_target_pairs={{0,4},{1,3},{2,6},{3,1},{4,0},{5,7},{6,2},{7,5},{8,12},{9,11},{10,... | collective-permute-start | bytes 479240 | tf_op jit(solution)/shard_map/ppermute | solution.py:55
  94.0 3.7 %collective-permute-done.31.refs_1_ = bf16[1,208,384]{2,1,0:T(8,128)(2,1)S(1)} collective-permute-done((bf16[1,208,384]{2,1,0:T(8,128)(2,1)S(1)}, bf16[1,208,384]{2,1,0:T(8,128)(2,1)S(1)}, u32[]{:S(2)}, u32[]{:S(2)}) %collective-permute-start.31) | collective-permute-done | bytes 159776 | tf_op jit(solution)/shard_map/ppermute | solution.py:55
  97.7 1.5 %collective-permute-start.38 = (bf16[1,208,384]{2,1,0:T(8,128)(2,1)S(1)}, bf16[1,208,384]{2,1,0:T(8,128)(2,1)S(1)}, u32[]{:S(2)}, u32[]{:S(2)}) collective-permute-start(bf16[1,208,384]{2,1,0:T(8,128)(2,1)S(1)} %get-tuple-element.167), channel_id=1, source_target_pairs={{0,4},{1,3},{2,6},{3,1},{4,0},{5,7},{6,2},{7,5},{8,12},{9,11},{10,... | collective-permute-start | bytes 479240 | tf_op jit(solution)/shard_map/ppermute | solution.py:55
  99.3 2.7 %collective-permute-start.39 = (bf16[1,208,384]{2,1,0:T(8,128)(2,1)S(1)}, bf16[1,208,384]{2,1,0:T(8,128)(2,1)S(1)}, u32[]{:S(2)}, u32[]{:S(2)}) collective-permute-start(bf16[1,208,384]{2,1,0:T(8,128)(2,1)S(1)} %add_last.1.refs_4_.refs_2_), channel_id=1, source_target_pairs={{0,16},{1,17},{2,18},{3,19},{4,20},{5,21},{6,22},{7,23},{8,24},{9,... | collective-permute-start | bytes 479240 | tf_op jit(solution)/shard_map/ppermute | solution.py:51
  102.0 0.6 collective-permute-start.34
  103.2 4.0 %collective-permute-start.40 = (bf16[1,192,384]{2,1,0:T(8,128)(2,1)S(1)}, bf16[1,192,384]{2,1,0:T(8,128)(2,1)S(1)}, u32[]{:S(2)}, u32[]{:S(2)}) collective-permute-start(bf16[1,192,384]{2,1,0:T(8,128)(2,1)S(1)} %get-tuple-element.176), channel_id=1, source_target_pairs={{0,16},{1,17},{2,18},{3,19},{4,20},{5,21},{6,22},{7,23},{8,24},{9,... | collective-permute-start | bytes 442376 | tf_op jit(solution)/shard_map/ppermute | solution.py:55
  107.2 2.0 %collective-permute-done.36.refs_1_ = bf16[1,96,768]{2,1,0:T(8,128)(2,1)S(1)} collective-permute-done((bf16[1,96,768]{2,1,0:T(8,128)(2,1)S(1)}, bf16[1,96,768]{2,1,0:T(8,128)(2,1)S(1)}, u32[]{:S(2)}, u32[]{:S(2)}) %collective-permute-start.36) | collective-permute-done | bytes 147488 | tf_op jit(solution)/shard_map/ppermute | solution.py:55
  109.2 0.7 down_end.1
  110.3 0.8 mix_end.1
  111.2 2.3 %collective-permute-done.40 = bf16[1,192,384]{2,1,0:T(8,128)(2,1)S(1)} collective-permute-done((bf16[1,192,384]{2,1,0:T(8,128)(2,1)S(1)}, bf16[1,192,384]{2,1,0:T(8,128)(2,1)S(1)}, u32[]{:S(2)}, u32[]{:S(2)}) %collective-permute-start.40) | collective-permute-done | bytes 147488 | tf_op jit(solution)/shard_map/ppermute | solution.py:55
  113.5 0.7 add_bitcast_fusion
  114.2 1.5 %place.1 = (bf16[256,768]{1,0:T(8,128)(2,1)}, bf16[256,768]{1,0:T(8,128)(2,1)}) custom-call(s32[6]{0:T(128)S(1)} %pad_add_fusion.refs_0_, bf16[2,64,768]{2,1,0:T(8,128)(2,1)S(1)} %get-tuple-element.133.refs_11_.refs_0_.refs_1_, bf16[2,64,768]{2,1,0:T(8,128)(2,1)S(1)} %collective-permute-done.12.refs_1_.refs_2_, ...), custom_call_target="tpu_custom_call" | custom-call | flops 1000 | bytes 1000 | tf_op jit(solution)/shard_map/place/pallas_call | solution.py:666
  (74 shorter events, 10.7 us)
Async XLA Ops:
  3.0 7.9 %collective-permute-start = (bf16[2,64,768]{2,1,0:T(8,128)(2,1)S(1)}, bf16[2,64,768]{2,1,0:T(8,128)(2,1)S(1)}, u32[]{:S(2)}, u32[]{:S(2)}) collective-permute-start(bf16[2,64,768]{2,1,0:T(8,128)(2,1)S(1)} %get-tuple-element.101), channel_id=1, source_target_pairs={{0,2},{1,3},{2,0},{3,1},{4,6},{5,7},{6,4},{7,5},{8,10},{9,11},{10,... | collective-permute-start | bytes 589832 | tf_op jit(solution)/shard_map/ppermute | solution.py:51
  11.5 13.9 %collective-permute-start.3 = (bf16[256,768]{1,0:T(8,128)(2,1)S(1)}, bf16[256,768]{1,0:T(8,128)(2,1)S(1)}, u32[]{:S(2)}, u32[]{:S(2)}) collective-permute-start(bf16[256,768]{1,0:T(8,128)(2,1)S(1)} %relay.4), channel_id=1, source_target_pairs={{0,2},{1,3},{2,0},{3,1},{4,6},{5,7},{6,4},{7,5},{8,10},{9,11},{10,... | collective-permute-start | bytes 1179656 | tf_op jit(solution)/shard_map/ppermute | solution.py:51
  13.3 1.3 %collective-permute-start.1 = (bf16[64,768]{1,0:T(8,128)(2,1)S(1)}, bf16[64,768]{1,0:T(8,128)(2,1)S(1)}, u32[]{:S(2)}, u32[]{:S(2)}) collective-permute-start(bf16[64,768]{1,0:T(8,128)(2,1)S(1)} %get-tuple-element.104), channel_id=1, source_target_pairs={{0,1},{1,0},{2,3},{3,2},{4,5},{5,4},{6,7},{7,6},{8,9},{9,8},{10,11... | collective-permute-start | bytes 294920 | tf_op jit(solution)/shard_map/ppermute | solution.py:51
  13.3 1.5 %collective-permute-start.2 = (bf16[64,768]{1,0:T(8,128)(2,1)S(1)}, bf16[64,768]{1,0:T(8,128)(2,1)S(1)}, u32[]{:S(2)}, u32[]{:S(2)}) collective-permute-start(bf16[64,768]{1,0:T(8,128)(2,1)S(1)} %get-tuple-element.105), channel_id=1, source_target_pairs={{0,1},{1,0},{2,3},{3,2},{4,5},{5,4},{6,7},{7,6},{8,9},{9,8},{10,11... | collective-permute-start | bytes 294920 | tf_op jit(solution)/shard_map/ppermute | solution.py:51
  20.1 21.5 %collective-permute-start.9 = (bf16[2,768,256]{2,1,0:T(8,128)(2,1)S(1)}, bf16[2,768,256]{2,1,0:T(8,128)(2,1)S(1)}, u32[]{:S(2)}, u32[]{:S(2)}) collective-permute-start(bf16[2,768,256]{2,1,0:T(8,128)(2,1)S(1)} %get-tuple-element.120.refs_2_.refs_1_), channel_id=1, source_target_pairs={{0,8},{1,9},{2,10},{3,11},{4,12},{5,13},{6,14},{7,15},{8,0},{9,1},... | collective-permute-start | bytes 2359304 | tf_op jit(solution)/shard_map/ppermute | solution.py:51
  24.7 19.6 %collective-permute-start.7 = (bf16[2,256,768]{2,1,0:T(8,128)(2,1)S(1)}, bf16[2,256,768]{2,1,0:T(8,128)(2,1)S(1)}, u32[]{:S(2)}, u32[]{:S(2)}) collective-permute-start(bf16[2,256,768]{2,1,0:T(8,128)(2,1)S(1)} %get-tuple-element.117.refs_3_), channel_id=1, source_target_pairs={{0,2},{1,3},{2,0},{3,1},{4,6},{5,7},{6,4},{7,5},{8,10},{9,11},{10,... | collective-permute-start | bytes 2359304 | tf_op jit(solution)/shard_map/ppermute | solution.py:51
  25.3 4.9 %collective-permute-start.4 = (bf16[256,768]{1,0:T(8,128)(2,1)S(1)}, bf16[256,768]{1,0:T(8,128)(2,1)S(1)}, u32[]{:S(2)}, u32[]{:S(2)}) collective-permute-start(bf16[256,768]{1,0:T(8,128)(2,1)S(1)} %get-tuple-element.102.refs_2_.refs_0_.refs_1_), channel_id=1, source_target_pairs={{0,1},{1,0},{2,3},{3,2},{4,5},{5,4},{6,7},{7,6},{8,9},{9,8},{10,11... | collective-permute-start | bytes 1179656 | tf_op jit(solution)/shard_map/ppermute | solution.py:51
  25.4 4.9 %collective-permute-start.5 = (bf16[256,768]{1,0:T(8,128)(2,1)S(1)}, bf16[256,768]{1,0:T(8,128)(2,1)S(1)}, u32[]{:S(2)}, u32[]{:S(2)}) collective-permute-start(bf16[256,768]{1,0:T(8,128)(2,1)S(1)} %collective-permute-done.3.refs_2_), channel_id=1, source_target_pairs={{0,1},{1,0},{2,3},{3,2},{4,5},{5,4},{6,7},{7,6},{8,9},{9,8},{10,11... | collective-permute-start | bytes 1179656 | tf_op jit(solution)/shard_map/ppermute | solution.py:51
  25.9 11.2 %collective-permute-start.6 = (bf16[256,768]{1,0:T(8,128)(2,1)S(1)}, bf16[256,768]{1,0:T(8,128)(2,1)S(1)}, u32[]{:S(2)}, u32[]{:S(2)}) collective-permute-start(bf16[256,768]{1,0:T(8,128)(2,1)S(1)} %get-tuple-element.114.refs_3_.refs_1_), channel_id=1, source_target_pairs={{0,4},{1,5},{2,6},{3,7},{4,0},{5,1},{6,2},{7,3},{8,12},{9,13},{10,... | collective-permute-start | bytes 1179656 | tf_op jit(solution)/shard_map/ppermute | solution.py:51
  36.5 19.2 %collective-permute-start.21 = (bf16[4,256,384]{2,1,0:T(8,128)(2,1)S(1)}, bf16[4,256,384]{2,1,0:T(8,128)(2,1)S(1)}, u32[]{:S(2)}, u32[]{:S(2)}) collective-permute-start(bf16[4,256,384]{2,1,0:T(8,128)(2,1)S(1)} %get-tuple-element.180), channel_id=1, source_target_pairs={{0,4},{1,5},{2,6},{3,7},{4,0},{5,1},{6,2},{7,3},{8,12},{9,13},{10,... | collective-permute-start | bytes 2359304 | tf_op jit(solution)/shard_map/ppermute | solution.py:51
  37.1 8.1 %collective-permute-start.8 = (bf16[256,768]{1,0:T(8,128)(2,1)S(1)}, bf16[256,768]{1,0:T(8,128)(2,1)S(1)}, u32[]{:S(2)}, u32[]{:S(2)}) collective-permute-start(bf16[256,768]{1,0:T(8,128)(2,1)S(1)} %get-tuple-element.116.refs_2_), channel_id=1, source_target_pairs={{0,1},{1,0},{2,3},{3,2},{4,5},{5,4},{6,7},{7,6},{8,9},{9,8},{10,11... | collective-permute-start | bytes 1179656 | tf_op jit(solution)/shard_map/ppermute | solution.py:51
  37.1 19.5 %collective-permute-start.20 = (bf16[4,256,384]{2,1,0:T(8,128)(2,1)S(1)}, bf16[4,256,384]{2,1,0:T(8,128)(2,1)S(1)}, u32[]{:S(2)}, u32[]{:S(2)}) collective-permute-start(bf16[4,256,384]{2,1,0:T(8,128)(2,1)S(1)} %get-tuple-element.181.refs_5_), channel_id=1, source_target_pairs={{0,1},{1,0},{2,3},{3,2},{4,5},{5,4},{6,7},{7,6},{8,9},{9,8},{10,11... | collective-permute-start | bytes 2359304 | tf_op jit(solution)/shard_map/ppermute | solution.py:51
  41.6 2.7 %collective-permute-start.10 = (f32[8,128]{1,0:T(8,128)S(1)}, f32[8,128]{1,0:T(8,128)S(1)}, u32[]{:S(2)}, u32[]{:S(2)}) collective-permute-start(f32[8,128]{1,0:T(8,128)S(1)} %step.1), channel_id=1, source_target_pairs={{0,1},{1,0},{2,3},{3,2},{4,5},{5,4},{6,7},{7,6},{8,9},{9,8},{10,11... | collective-permute-start | bytes 12296 | tf_op jit(solution)/shard_map/ppermute | solution.py:51
  44.4 2.0 %collective-permute-start.11 = (bf16[256,768]{1,0:T(8,128)(2,1)S(1)}, bf16[256,768]{1,0:T(8,128)(2,1)S(1)}, u32[]{:S(2)}, u32[]{:S(2)}) collective-permute-start(bf16[256,768]{1,0:T(8,128)(2,1)S(1)} %relay.5), channel_id=1, source_target_pairs={{0,1},{1,0},{2,3},{3,2},{4,5},{5,4},{6,7},{7,6},{8,9},{9,8},{10,11... | collective-permute-start | bytes 1179656 | tf_op jit(solution)/shard_map/ppermute | solution.py:51
  44.6 20.0 %collective-permute-start.17 = (bf16[4,384,256]{2,1,0:T(8,128)(2,1)S(1)}, bf16[4,384,256]{2,1,0:T(8,128)(2,1)S(1)}, u32[]{:S(2)}, u32[]{:S(2)}) collective-permute-start(bf16[4,384,256]{2,1,0:T(8,128)(2,1)S(1)} %get-tuple-element.182), channel_id=1, source_target_pairs={{0,8},{1,9},{2,10},{3,11},{4,12},{5,13},{6,14},{7,15},{8,0},{9,1},... | collective-permute-start | bytes 2359304 | tf_op jit(solution)/shard_map/ppermute | solution.py:51
  45.1 10.8 %collective-permute-start.18 = (bf16[256,768]{1,0:T(8,128)(2,1)S(1)}, bf16[256,768]{1,0:T(8,128)(2,1)S(1)}, u32[]{:S(2)}, u32[]{:S(2)}) collective-permute-start(bf16[256,768]{1,0:T(8,128)(2,1)S(1)} %get-tuple-element.114.refs_3_.refs_1_), channel_id=1, source_target_pairs={{0,1},{1,0},{2,3},{3,2},{4,5},{5,4},{6,7},{7,6},{8,9},{9,8},{10,11... | collective-permute-start | bytes 1179656 | tf_op jit(solution)/shard_map/ppermute | solution.py:51
  46.4 10.1 %collective-permute-start.19 = (bf16[256,768]{1,0:T(8,128)(2,1)S(1)}, bf16[256,768]{1,0:T(8,128)(2,1)S(1)}, u32[]{:S(2)}, u32[]{:S(2)}) collective-permute-start(bf16[256,768]{1,0:T(8,128)(2,1)S(1)} %collective-permute-done.6.refs_10_.refs_3_), channel_id=1, source_target_pairs={{0,1},{1,0},{2,3},{3,2},{4,5},{5,4},{6,7},{7,6},{8,9},{9,8},{10,11... | collective-permute-start | bytes 1179656 | tf_op jit(solution)/shard_map/ppermute | solution.py:51
  55.9 1.5 %collective-permute-start.22 = (bf16[1,256,384]{2,1,0:T(8,128)(2,1)S(1)}, bf16[1,256,384]{2,1,0:T(8,128)(2,1)S(1)}, u32[]{:S(2)}, u32[]{:S(2)}) collective-permute-start(bf16[1,256,384]{2,1,0:T(8,128)(2,1)S(1)} %get-tuple-element.187), channel_id=1, source_target_pairs={{0,1},{1,0},{2,3},{3,2},{4,5},{5,4},{6,7},{7,6},{8,9},{9,8},{10,11... | collective-permute-start | bytes 589832 | tf_op jit(solution)/shard_map/ppermute | solution.py:51
  56.0 11.7 %collective-permute-start.14 = (bf16[2,768,256]{2,1,0:T(8,128)(2,1)S(1)}, bf16[2,768,256]{2,1,0:T(8,128)(2,1)S(1)}, u32[]{:S(2)}, u32[]{:S(2)}) collective-permute-start(bf16[2,768,256]{2,1,0:T(8,128)(2,1)S(1)} %get-tuple-element.120.refs_2_.refs_1_), channel_id=1, source_target_pairs={{0,1},{1,0},{2,3},{3,2},{4,5},{5,4},{6,7},{7,6},{8,9},{9,8},{10,11... | collective-permute-start | bytes 2359304 | tf_op jit(solution)/shard_map/ppermute | solution.py:51
  56.5 2.3 %collective-permute-start.23 = (bf16[1,256,384]{2,1,0:T(8,128)(2,1)S(1)}, bf16[1,256,384]{2,1,0:T(8,128)(2,1)S(1)}, u32[]{:S(2)}, u32[]{:S(2)}) collective-permute-start(bf16[1,256,384]{2,1,0:T(8,128)(2,1)S(1)} %get-tuple-element.186), channel_id=1, source_target_pairs={{0,1},{1,0},{2,3},{3,2},{4,5},{5,4},{6,7},{7,6},{8,9},{9,8},{10,11... | collective-permute-start | bytes 589832 | tf_op jit(solution)/shard_map/ppermute | solution.py:51
  56.6 2.5 %collective-permute-start.24 = (bf16[1,256,384]{2,1,0:T(8,128)(2,1)S(1)}, bf16[1,256,384]{2,1,0:T(8,128)(2,1)S(1)}, u32[]{:S(2)}, u32[]{:S(2)}) collective-permute-start(bf16[1,256,384]{2,1,0:T(8,128)(2,1)S(1)} %get-tuple-element.185), channel_id=1, source_target_pairs={{0,1},{1,0},{2,3},{3,2},{4,5},{5,4},{6,7},{7,6},{8,9},{9,8},{10,11... | collective-permute-start | bytes 589832 | tf_op jit(solution)/shard_map/ppermute | solution.py:51
  57.4 2.0 %collective-permute-start.25 = (bf16[1,256,384]{2,1,0:T(8,128)(2,1)S(1)}, bf16[1,256,384]{2,1,0:T(8,128)(2,1)S(1)}, u32[]{:S(2)}, u32[]{:S(2)}) collective-permute-start(bf16[1,256,384]{2,1,0:T(8,128)(2,1)S(1)} %get-tuple-element.184), channel_id=1, source_target_pairs={{0,1},{1,0},{2,3},{3,2},{4,5},{5,4},{6,7},{7,6},{8,9},{9,8},{10,11... | collective-permute-start | bytes 589832 | tf_op jit(solution)/shard_map/ppermute | solution.py:51
  58.8 13.1 %collective-permute-start.16 = (bf16[4,384,256]{2,1,0:T(8,128)(2,1)S(1)}, bf16[4,384,256]{2,1,0:T(8,128)(2,1)S(1)}, u32[]{:S(2)}, u32[]{:S(2)}) collective-permute-start(bf16[4,384,256]{2,1,0:T(8,128)(2,1)S(1)} %get-tuple-element.183.refs_5_), channel_id=1, source_target_pairs={{0,1},{1,0},{2,3},{3,2},{4,5},{5,4},{6,7},{7,6},{8,9},{9,8},{10,11... | collective-permute-start | bytes 2359304 | tf_op jit(solution)/shard_map/ppermute | solution.py:51
  59.1 12.8 %collective-permute-start.15 = (bf16[2,768,256]{2,1,0:T(8,128)(2,1)S(1)}, bf16[2,768,256]{2,1,0:T(8,128)(2,1)S(1)}, u32[]{:S(2)}, u32[]{:S(2)}) collective-permute-start(bf16[2,768,256]{2,1,0:T(8,128)(2,1)S(1)} %collective-permute-done.9.refs_0_.refs_3_), channel_id=1, source_target_pairs={{0,1},{1,0},{2,3},{3,2},{4,5},{5,4},{6,7},{7,6},{8,9},{9,8},{10,11... | collective-permute-start | bytes 2359304 | tf_op jit(solution)/shard_map/ppermute | solution.py:51
  64.7 7.2 %collective-permute-start.26 = (bf16[4,384,256]{2,1,0:T(8,128)(2,1)S(1)}, bf16[4,384,256]{2,1,0:T(8,128)(2,1)S(1)}, u32[]{:S(2)}, u32[]{:S(2)}) collective-permute-start(bf16[4,384,256]{2,1,0:T(8,128)(2,1)S(1)} %relay.7.refs_7_), channel_id=1, source_target_pairs={{0,1},{1,0},{2,3},{3,2},{4,5},{5,4},{6,7},{7,6},{8,9},{9,8},{10,11... | collective-permute-start | bytes 2359304 | tf_op jit(solution)/shard_map/ppermute | solution.py:51
  64.8 2.4 %collective-permute-start.27 = (f32[8,8,384]{2,1,0:T(8,128)S(1)}, f32[8,8,384]{2,1,0:T(8,128)S(1)}, u32[]{:S(2)}, u32[]{:S(2)}) collective-permute-start(f32[8,8,384]{2,1,0:T(8,128)S(1)} %get-tuple-element.147), channel_id=1, source_target_pairs={{0,1},{1,0},{2,3},{3,2},{4,5},{5,4},{6,7},{7,6},{8,9},{9,8},{10,11... | collective-permute-start | bytes 294920 | tf_op jit(solution)/shard_map/ppermute | solution.py:51
  67.2 4.2 %collective-permute-start.28 = (f32[4,8,384]{2,1,0:T(8,128)S(1)}, f32[4,8,384]{2,1,0:T(8,128)S(1)}, u32[]{:S(2)}, u32[]{:S(2)}) collective-permute-start(f32[4,8,384]{2,1,0:T(8,128)S(1)} %slice.56), channel_id=1, source_target_pairs={{0,8},{1,9},{2,10},{3,11},{4,12},{5,13},{6,14},{7,15},{8,0},{9,1},... | collective-permute-start | bytes 147464 | tf_op jit(solution)/shard_map/ppermute | solution.py:51
  67.7 16.2 %collective-permute-start.30 = (bf16[4,96,768]{2,1,0:T(8,128)(2,1)S(1)}, bf16[4,96,768]{2,1,0:T(8,128)(2,1)S(1)}, u32[]{:S(2)}, u32[]{:S(2)}) collective-permute-start(bf16[4,96,768]{2,1,0:T(8,128)(2,1)S(1)} %get-tuple-element.150), channel_id=1, source_target_pairs={{0,4},{1,5},{2,6},{3,7},{4,0},{5,1},{6,2},{7,3},{8,12},{9,13},{10,... | collective-permute-start | bytes 1769480 | tf_op jit(solution)/shard_map/ppermute | solution.py:55
  71.3 17.7 %collective-permute-start.33 = (bf16[4,192,384]{2,1,0:T(8,128)(2,1)S(1)}, bf16[4,192,384]{2,1,0:T(8,128)(2,1)S(1)}, u32[]{:S(2)}, u32[]{:S(2)}) collective-permute-start(bf16[4,192,384]{2,1,0:T(8,128)(2,1)S(1)} %get-tuple-element.156), channel_id=1, source_target_pairs={{0,2},{1,3},{2,0},{3,1},{4,6},{5,7},{6,4},{7,5},{8,10},{9,11},{10,... | collective-permute-start | bytes 1769480 | tf_op jit(solution)/shard_map/ppermute | solution.py:55
  73.9 15.1 %collective-permute-start.29 = (bf16[2,208,384]{2,1,0:T(8,128)(2,1)S(1)}, bf16[2,208,384]{2,1,0:T(8,128)(2,1)S(1)}, u32[]{:S(2)}, u32[]{:S(2)}) collective-permute-start(bf16[2,208,384]{2,1,0:T(8,128)(2,1)S(1)} %get-tuple-element.149), channel_id=1, source_target_pairs={{0,2},{1,5},{2,0},{3,7},{4,6},{5,1},{6,4},{7,3},{8,10},{9,13},{10,... | collective-permute-start | bytes 958472 | tf_op jit(solution)/shard_map/ppermute | solution.py:55
  77.5 14.9 %collective-permute-start.32 = (bf16[2,208,384]{2,1,0:T(8,128)(2,1)S(1)}, bf16[2,208,384]{2,1,0:T(8,128)(2,1)S(1)}, u32[]{:S(2)}, u32[]{:S(2)}) collective-permute-start(bf16[2,208,384]{2,1,0:T(8,128)(2,1)S(1)} %get-tuple-element.155), channel_id=1, source_target_pairs={{0,2},{1,5},{2,0},{3,7},{4,6},{5,1},{6,4},{7,3},{8,10},{9,13},{10,... | collective-permute-start | bytes 958472 | tf_op jit(solution)/shard_map/ppermute | solution.py:55
  84.1 18.5 %collective-permute-start.35 = (bf16[2,96,768]{2,1,0:T(8,128)(2,1)S(1)}, bf16[2,96,768]{2,1,0:T(8,128)(2,1)S(1)}, u32[]{:S(2)}, u32[]{:S(2)}) collective-permute-start(bf16[2,96,768]{2,1,0:T(8,128)(2,1)S(1)} %get-tuple-element.159), channel_id=1, source_target_pairs={{0,16},{1,17},{2,18},{3,19},{4,20},{5,21},{6,22},{7,23},{8,24},{9,... | collective-permute-start | bytes 884744 | tf_op jit(solution)/shard_map/ppermute | solution.py:55
  89.2 13.9 %collective-permute-start.37 = (bf16[2,192,384]{2,1,0:T(8,128)(2,1)S(1)}, bf16[2,192,384]{2,1,0:T(8,128)(2,1)S(1)}, u32[]{:S(2)}, u32[]{:S(2)}) collective-permute-start(bf16[2,192,384]{2,1,0:T(8,128)(2,1)S(1)} %get-tuple-element.162), channel_id=1, source_target_pairs={{0,8},{1,9},{2,10},{3,11},{4,12},{5,13},{6,14},{7,15},{8,0},{9,1},... | collective-permute-start | bytes 884744 | tf_op jit(solution)/shard_map/ppermute | solution.py:55
  89.8 9.5 %collective-permute-start.12 = (bf16[2,64,768]{2,1,0:T(8,128)(2,1)S(1)}, bf16[2,64,768]{2,1,0:T(8,128)(2,1)S(1)}, u32[]{:S(2)}, u32[]{:S(2)}) collective-permute-start(bf16[2,64,768]{2,1,0:T(8,128)(2,1)S(1)} %get-tuple-element.134), channel_id=1, source_target_pairs={{0,1},{1,0},{2,3},{3,2},{4,5},{5,4},{6,7},{7,6},{8,9},{9,8},{10,11... | collective-permute-start | bytes 589832 | tf_op jit(solution)/shard_map/ppermute | solution.py:51
  89.8 12.2 %collective-permute-start.13 = (bf16[2,64,768]{2,1,0:T(8,128)(2,1)S(1)}, bf16[2,64,768]{2,1,0:T(8,128)(2,1)S(1)}, u32[]{:S(2)}, u32[]{:S(2)}) collective-permute-start(bf16[2,64,768]{2,1,0:T(8,128)(2,1)S(1)} %get-tuple-element.144), channel_id=1, source_target_pairs={{0,1},{1,0},{2,3},{3,2},{4,5},{5,4},{6,7},{7,6},{8,9},{9,8},{10,11... | collective-permute-start | bytes 589832 | tf_op jit(solution)/shard_map/ppermute | solution.py:51
  92.4 5.3 %collective-permute-start.31 = (bf16[1,208,384]{2,1,0:T(8,128)(2,1)S(1)}, bf16[1,208,384]{2,1,0:T(8,128)(2,1)S(1)}, u32[]{:S(2)}, u32[]{:S(2)}) collective-permute-start(bf16[1,208,384]{2,1,0:T(8,128)(2,1)S(1)} %get-tuple-element.154), channel_id=1, source_target_pairs={{0,4},{1,3},{2,6},{3,1},{4,0},{5,7},{6,2},{7,5},{8,12},{9,11},{10,... | collective-permute-start | bytes 479240 | tf_op jit(solution)/shard_map/ppermute | solution.py:55
  97.7 12.2 %collective-permute-start.38 = (bf16[1,208,384]{2,1,0:T(8,128)(2,1)S(1)}, bf16[1,208,384]{2,1,0:T(8,128)(2,1)S(1)}, u32[]{:S(2)}, u32[]{:S(2)}) collective-permute-start(bf16[1,208,384]{2,1,0:T(8,128)(2,1)S(1)} %get-tuple-element.167), channel_id=1, source_target_pairs={{0,4},{1,3},{2,6},{3,1},{4,0},{5,7},{6,2},{7,5},{8,12},{9,11},{10,... | collective-permute-start | bytes 479240 | tf_op jit(solution)/shard_map/ppermute | solution.py:55
  99.3 11.0 %collective-permute-start.39 = (bf16[1,208,384]{2,1,0:T(8,128)(2,1)S(1)}, bf16[1,208,384]{2,1,0:T(8,128)(2,1)S(1)}, u32[]{:S(2)}, u32[]{:S(2)}) collective-permute-start(bf16[1,208,384]{2,1,0:T(8,128)(2,1)S(1)} %add_last.1.refs_4_.refs_2_), channel_id=1, source_target_pairs={{0,16},{1,17},{2,18},{3,19},{4,20},{5,21},{6,22},{7,23},{8,24},{9,... | collective-permute-start | bytes 479240 | tf_op jit(solution)/shard_map/ppermute | solution.py:51
  102.0 12.3 %collective-permute-start.34 = (bf16[4,64,768]{2,1,0:T(8,128)(2,1)S(1)}, bf16[4,64,768]{2,1,0:T(8,128)(2,1)S(1)}, u32[]{:S(2)}, u32[]{:S(2)}) collective-permute-start(bf16[4,64,768]{2,1,0:T(8,128)(2,1)S(1)} %gather.1), channel_id=1, source_target_pairs={{0,2},{1,3},{2,0},{3,1},{4,6},{5,7},{6,4},{7,5},{8,10},{9,11},{10,... | collective-permute-start | bytes 1179656 | tf_op jit(solution)/shard_map/ppermute | solution.py:51
  102.6 6.6 %collective-permute-start.36 = (bf16[1,96,768]{2,1,0:T(8,128)(2,1)S(1)}, bf16[1,96,768]{2,1,0:T(8,128)(2,1)S(1)}, u32[]{:S(2)}, u32[]{:S(2)}) collective-permute-start(bf16[1,96,768]{2,1,0:T(8,128)(2,1)S(1)} %get-tuple-element.161), channel_id=1, source_target_pairs={{0,8},{1,9},{2,10},{3,11},{4,12},{5,13},{6,14},{7,15},{8,0},{9,1},... | collective-permute-start | bytes 442376 | tf_op jit(solution)/shard_map/ppermute | solution.py:55
  103.2 10.3 %collective-permute-start.40 = (bf16[1,192,384]{2,1,0:T(8,128)(2,1)S(1)}, bf16[1,192,384]{2,1,0:T(8,128)(2,1)S(1)}, u32[]{:S(2)}, u32[]{:S(2)}) collective-permute-start(bf16[1,192,384]{2,1,0:T(8,128)(2,1)S(1)} %get-tuple-element.176), channel_id=1, source_target_pairs={{0,16},{1,17},{2,18},{3,19},{4,20},{5,21},{6,22},{7,23},{8,24},{9,... | collective-permute-start | bytes 442376 | tf_op jit(solution)/shard_map/ppermute | solution.py:55

commit v5 on v4

--- a/solution.py
+++ b/solution.py
@@ -843,6 +843,7 @@
         return [item, place.swap(item, 1), beyond, place.swap(beyond, 1)]
 
     cot_far = place.swap(relay(cot, [far_mine]), x_mask)
+    cot_far = relay(cot_far, [lefts])
     cots = [cot, cot_far, place.swap(cot, 1), place.swap(cot_far, 1)]
     lefts_beyond = place.swap(lefts, z_mask)
     left_sets = four_sets(lefts, lefts_beyond)
@@ -907,7 +908,7 @@
         [kept(BF, width, 4 * rows), vector],
         after=[rights],
     )
-    token = step([lefts_beyond])
+    token = step([lefts_beyond, rights])
     act_far_other = place.swap(relay(act_got[1], [token]), 1)
     down_send, down_keep = kernel_call(
         down_terms_kernel,

time: 116 us -> 116 us (level)
    pallas_call x31 -> x32, Pallas kernels: 43.6 us -> 43.6 us  [kernel_call(): pl.pallas_call(run, out_shape=outs, in_specs=[SPECS[kind] for kind in spe...]
where the time goes in v5:
time: 116 us
  Pallas kernels  43.6 us (38%)
  waiting for transfers between devices  35.6 us (31%)
  starting transfers between devices  33.4 us (29%)
  other arithmetic  1.5 us (1%)
    pallas_call x32, Pallas kernels, kernel_call(): pl.pallas_call(run, out_shape=outs, in_specs=[SPECS[kind] for kind in spe...  43.6 us
    ppermute x31, starting transfers between devices, swap(): return lax.ppermute(value, AXES, pairs)  18.5 us
    ppermute x10, waiting for transfers between devices, swap_by_core(): return lax.ppermute(value, AXES, pairs)  18.3 us
    ppermute x31, waiting for transfers between devices, swap(): return lax.ppermute(value, AXES, pairs)  17.3 us
    ppermute x10, starting transfers between devices, swap_by_core(): return lax.ppermute(value, AXES, pairs)  14.9 us
  transfers between devices with their start and end apart: 41, of which 17 were waited for; matrix products, arithmetic and copies ran while one was open for 1% of the time, Pallas kernels for 35%

profile of v5, /device:TPU:0, one launch (start us, length us, event | category | flops | bytes accessed | tf_op | source)
XLA Modules:
  0.0 115.7 jit_solution(17403449792817077908)
XLA Ops:
  0.6 0.7 pad_add_fusion.refs_0_
  1.4 1.6 %token_slice.1 = (bf16[64,768]{1,0:T(8,128)(2,1)S(1)}, bf16[64,768]{1,0:T(8,128)(2,1)S(1)}, bf16[2,64,768]{2,1,0:T(8,128)(2,1)S(1)}) custom-call(s32[6]{0:T(128)S(1)} %pad_add_fusion.refs_0_, bf16[2,2,64,768]{3,2,1,0:T(8,128)(2,1)} %bitcast.15), custom_call_target="tpu_custom_call" | custom-call | flops 1000 | bytes 1000 | tf_op jit(solution)/shard_map/token_slice/pallas_call | solution.py:666
  3.0 3.0 %collective-permute-start = (bf16[2,64,768]{2,1,0:T(8,128)(2,1)S(1)}, bf16[2,64,768]{2,1,0:T(8,128)(2,1)S(1)}, u32[]{:S(2)}, u32[]{:S(2)}) collective-permute-start(bf16[2,64,768]{2,1,0:T(8,128)(2,1)S(1)} %get-tuple-element.101), channel_id=1, source_target_pairs={{0,2},{1,3},{2,0},{3,1},{4,6},{5,7},{6,4},{7,5},{8,10},{9,11},{10,... | collective-permute-start | bytes 589832 | tf_op jit(solution)/shard_map/ppermute | solution.py:51
  6.0 2.5 %load.1 = (bf16[768,2304]{1,0:T(8,128)(2,1)S(1)}, bf16[768,768]{1,0:T(8,128)(2,1)S(1)}, bf16[256,768]{1,0:T(8,128)(2,1)S(1)}, f32[768]{0:T(1024)S(1)}, f32[768]{...) custom-call(bf16[768,2304]{1,0:T(8,128)(2,1)} %refs_1_.5, ...), custom_call_target="tpu_custom_call" | custom-call | flops 1000 | bytes 1000 | tf_op jit(solution)/shard_map/load/pallas_call | solution.py:666
  8.5 2.4 %collective-permute-done.refs_1_ = bf16[2,64,768]{2,1,0:T(8,128)(2,1)S(1)} collective-permute-done((bf16[2,64,768]{2,1,0:T(8,128)(2,1)S(1)}, bf16[2,64,768]{2,1,0:T(8,128)(2,1)S(1)}, u32[]{:S(2)}, u32[]{:S(2)}) %collective-permute-start) | collective-permute-done | bytes 196640 | tf_op jit(solution)/shard_map/ppermute | solution.py:51
  11.5 1.8 %collective-permute-start.3 = (bf16[256,768]{1,0:T(8,128)(2,1)S(1)}, bf16[256,768]{1,0:T(8,128)(2,1)S(1)}, u32[]{:S(2)}, u32[]{:S(2)}) collective-permute-start(bf16[256,768]{1,0:T(8,128)(2,1)S(1)} %relay.5), channel_id=1, source_target_pairs={{0,2},{1,3},{2,0},{3,1},{4,6},{5,7},{6,4},{7,5},{8,10},{9,11},{10,... | collective-permute-start | bytes 1179656 | tf_op jit(solution)/shard_map/ppermute | solution.py:51
  13.8 0.8 collective-permute-done.1.refs_3_
  14.8 5.3 %attention.1 = (bf16[256,768]{1,0:T(8,128)(2,1)S(1)}, bf16[2,768,256]{2,1,0:T(8,128)(2,1)S(1)}, bf16[768,256]{1,0:T(8,128)(2,1)S(1)}, bf16[768,256]{1,0:T(8,128)...) custom-call(s32[6]{0:T(128)S(1)} %pad_add_fusion.refs_0_, ...), custom_call_target="tpu_custom_call" | custom-call | flops 1000 | bytes 1000 | tf_op jit(solution)/shard_map/attention/pallas_call | solution.py:666
  20.1 1.7 %collective-permute-start.9 = (bf16[2,768,256]{2,1,0:T(8,128)(2,1)S(1)}, bf16[2,768,256]{2,1,0:T(8,128)(2,1)S(1)}, u32[]{:S(2)}, u32[]{:S(2)}) collective-permute-start(bf16[2,768,256]{2,1,0:T(8,128)(2,1)S(1)} %get-tuple-element.120.refs_1_.refs_2_), channel_id=1, source_target_pairs={{0,8},{1,9},{2,10},{3,11},{4,12},{5,13},{6,14},{7,15},{8,0},{9,1},... | collective-permute-start | bytes 2359304 | tf_op jit(solution)/shard_map/ppermute | solution.py:51
  21.7 3.0 %hidden_far.1 = (bf16[256,768]{1,0:T(8,128)(2,1)S(1)}, bf16[2,256,768]{2,1,0:T(8,128)(2,1)S(1)}, bf16[2,256,768]{2,1,0:T(8,128)(2,1)S(1)}) custom-call(s32[6]{0:T(128)S(1)} %pad_add_fusion.refs_0_, f32[768]{0:T(1024)S(1)} %get-tuple-element.99.refs_1_.refs_6_, f32[768]{0:T(1024)S(1)} %get-tuple-element.100.refs_2_, ...), custom_call_target="tpu_custom_call" | custom-call | flops 1000 | bytes 1000 | tf_op jit(solution)/shard_map/hidden_far/pallas_call | solution.py:666
  24.7 0.6 collective-permute-start.7
  25.9 1.5 %collective-permute-start.6 = (bf16[256,768]{1,0:T(8,128)(2,1)S(1)}, bf16[256,768]{1,0:T(8,128)(2,1)S(1)}, u32[]{:S(2)}, u32[]{:S(2)}) collective-permute-start(bf16[256,768]{1,0:T(8,128)(2,1)S(1)} %get-tuple-element.114.refs_3_.refs_1_), channel_id=1, source_target_pairs={{0,4},{1,5},{2,6},{3,7},{4,0},{5,1},{6,2},{7,3},{8,12},{9,13},{10,... | collective-permute-start | bytes 1179656 | tf_op jit(solution)/shard_map/ppermute | solution.py:51
  27.5 2.9 %hidden_near.1 = (bf16[256,768]{1,0:T(8,128)(2,1)S(1)}, bf16[256,768]{1,0:T(8,128)(2,1)S(1)}, bf16[2,256,768]{2,1,0:T(8,128)(2,1)S(1)}, bf16[3072,768]{1,0:T(8,128)(2,1)S(1)}) custom-call(s32[6]{0:T(128)S(1)} %pad_add_fusion.refs_0_, bf16[3072,768]{1,0:T(8,128)(2,1)} %refs_1_.4, f32[3072]{0:T(1024)S(1)} %get-tuple-element.98.refs_3_.refs_2_, ...), custom_call_target="tpu_custom_call" | custom-call | flops 1000 | bytes 1000 | tf_op jit(solution)/shard_map/hidden_near/pallas_call | solution.py:666
  30.4 5.8 %hidden_back.1 = (bf16[2,4,256,384]{3,2,1,0:T(8,128)(2,1)S(1)}, f32[256,768]{1,0:T(8,128)S(1)}, bf16[8,96,256]{2,1,0:T(8,128)(2,1)S(1)}, bf16[768,256]{1,0:T(8,1...) custom-call(s32[6]{0:T(128)S(1)} %pad_add_fusion.refs_0_, ...), custom_call_target="tpu_custom_call" | custom-call | flops 1000 | bytes 1000 | tf_op jit(solution)/shard_map/hidden_back/pallas_call | solution.py:666
  36.6 0.6 collective-permute-start.21
  37.7 4.0 %attention_back.1 = (bf16[8,384,256]{2,1,0:T(8,128)(2,1)S(1)}, bf16[768,2304]{1,0:T(8,128)(2,1)S(1)}) custom-call(s32[6]{0:T(128)S(1)} %pad_add_fusion.refs_0_, bf16[768,2304]{1,0:T(8,128)(2,1)} %refs_1_.5, bf16[2,768,256]{2,1,0:T(8,128)(2,1)S(1)} %get-tuple-element.120.refs_1_.refs_2_, bf16[768,256]{1,0:T(8,128)(2,1)S(1)} %get-tuple-element.121.refs_3_, ...), custom_call_target="tpu_custom_call" | custom-call | flops 1000 | bytes 1000 | tf_op jit(solution)/shard_map/attention_back/pallas_call | solution.py:666
  41.8 2.5 %collective-permute-done.7 = bf16[2,256,768]{2,1,0:T(8,128)(2,1)S(1)} collective-permute-done((bf16[2,256,768]{2,1,0:T(8,128)(2,1)S(1)}, bf16[2,256,768]{2,1,0:T(8,128)(2,1)S(1)}, u32[]{:S(2)}, u32[]{:S(2)}) %collective-permute-start.7) | collective-permute-done | bytes 786464 | tf_op jit(solution)/shard_map/ppermute | solution.py:51
  45.3 1.0 out_grad.1
  46.8 2.0 %down_terms.1 = (bf16[4,96,768]{2,1,0:T(8,128)(2,1)S(1)}, bf16[4,96,768]{2,1,0:T(8,128)(2,1)S(1)}) custom-call(s32[6]{0:T(128)S(1)} %pad_add_fusion.refs_0_, bf16[768,1024]{1,0:T(8,128)(2,1)S(1)} %get-tuple-element.131.refs_1_, bf16[256,768]{1,0:T(8,128)(2,1)S(1)} %get-tuple-element.115.refs_2_.refs_1_, bf16[256,768]{1,0:T(8,128)(2,1)S(1)} %get-tuple-element.189.refs_3_, ...), custom_call_target="tpu_custom_call" | custom-call | flops 1000 | bytes 1000 | tf_op jit(solution)/shard_map/down_terms/pallas_call | solution.py:666
  48.8 1.9 %mixed.1 = (bf16[2,64,768]{2,1,0:T(8,128)(2,1)S(1)}, bf16[2,64,768]{2,1,0:T(8,128)(2,1)S(1)}) custom-call(s32[6]{0:T(128)S(1)} %pad_add_fusion.refs_0_, bf16[256,768]{1,0:T(8,128)(2,1)S(1)} %get-tuple-element.115.refs_2_.refs_1_, bf16[256,768]{1,0:T(8,128)(2,1)S(1)} %get-tuple-element.116.refs_2_, bf16[2,256,768]{2,1,0:T(8,128)(2,1)S(1)} %get-tuple-element.117.refs_3_, ...), custom_call_target="tpu_custom_call" | custom-call | flops 1000 | bytes 1000 | tf_op jit(solution)/shard_map/mixed/pallas_call | solution.py:666
  50.7 2.3 %first_back.1 = (bf16[2,64,768]{2,1,0:T(8,128)(2,1)S(1)}, bf16[2,64,768]{2,1,0:T(8,128)(2,1)S(1)}, f32[8,8,384]{2,1,0:T(8,128)S(1)}) custom-call(s32[6]{0:T(128)S(1)} %pad_add_fusion.refs_0_, f32[768]{0:T(1024)S(1)} %get-tuple-element.106.refs_6_.refs_1_, bf16[256,768]{1,0:T(8,128)(2,1)S(1)} %get-tuple-element.135.refs_2_, ...), custom_call_target="tpu_custom_call" | custom-call | flops 1000 | bytes 1000 | tf_op jit(solution)/shard_map/first_back/pallas_call | solution.py:666
  53.0 2.9 %collective-permute-done.21.refs_0_ = bf16[4,256,384]{2,1,0:T(8,128)(2,1)S(1)} collective-permute-done((bf16[4,256,384]{2,1,0:T(8,128)(2,1)S(1)}, bf16[4,256,384]{2,1,0:T(8,128)(2,1)S(1)}, u32[]{:S(2)}, u32[]{:S(2)}) %collective-permute-start.21) | collective-permute-done | bytes 786464 | tf_op jit(solution)/shard_map/ppermute | solution.py:51
  57.7 1.3 %collective-permute-done.23.refs_9_ = bf16[1,256,384]{2,1,0:T(8,128)(2,1)S(1)} collective-permute-done((bf16[1,256,384]{2,1,0:T(8,128)(2,1)S(1)}, bf16[1,256,384]{2,1,0:T(8,128)(2,1)S(1)}, u32[]{:S(2)}, u32[]{:S(2)}) %collective-permute-start.23) | collective-permute-done | bytes 196640 | tf_op jit(solution)/shard_map/ppermute | solution.py:51
  59.5 2.7 %up_terms.1 = (bf16[4,192,384]{2,1,0:T(8,128)(2,1)S(1)}, bf16[4,192,384]{2,1,0:T(8,128)(2,1)S(1)}) custom-call(s32[6]{0:T(128)S(1)} %pad_add_fusion.refs_0_, bf16[256,768]{1,0:T(8,128)(2,1)S(1)} %get-tuple-element.114.refs_3_.refs_1_, bf16[256,768]{1,0:T(8,128)(2,1)S(1)} %collective-permute-done.18.refs_2_, ...), custom_call_target="tpu_custom_call" | custom-call | flops 1000 | bytes 1000 | tf_op jit(solution)/shard_map/up_terms/pallas_call | solution.py:666
  62.2 2.4 %collective-permute-done.17.refs_0_ = bf16[4,384,256]{2,1,0:T(8,128)(2,1)S(1)} collective-permute-done((bf16[4,384,256]{2,1,0:T(8,128)(2,1)S(1)}, bf16[4,384,256]{2,1,0:T(8,128)(2,1)S(1)}, u32[]{:S(2)}, u32[]{:S(2)}) %collective-permute-start.17) | collective-permute-done | bytes 786464 | tf_op jit(solution)/shard_map/ppermute | solution.py:51
  65.2 1.9 %collective-permute-done.27 = f32[8,8,384]{2,1,0:T(8,128)S(1)} collective-permute-done((f32[8,8,384]{2,1,0:T(8,128)S(1)}, f32[8,8,384]{2,1,0:T(8,128)S(1)}, u32[]{:S(2)}, u32[]{:S(2)}) %collective-permute-start.27) | collective-permute-done | bytes 98336 | tf_op jit(solution)/shard_map/ppermute | solution.py:51
  67.7 1.5 %collective-permute-start.30 = (bf16[4,96,768]{2,1,0:T(8,128)(2,1)S(1)}, bf16[4,96,768]{2,1,0:T(8,128)(2,1)S(1)}, u32[]{:S(2)}, u32[]{:S(2)}) collective-permute-start(bf16[4,96,768]{2,1,0:T(8,128)(2,1)S(1)} %get-tuple-element.150), channel_id=1, source_target_pairs={{0,4},{1,5},{2,6},{3,7},{4,0},{5,1},{6,2},{7,3},{8,12},{9,13},{10,... | collective-permute-start | bytes 1769480 | tf_op jit(solution)/shard_map/ppermute | solution.py:55
  69.2 2.1 %collective-permute-done.28 = f32[4,8,384]{2,1,0:T(8,128)S(1)} collective-permute-done((f32[4,8,384]{2,1,0:T(8,128)S(1)}, f32[4,8,384]{2,1,0:T(8,128)S(1)}, u32[]{:S(2)}, u32[]{:S(2)}) %collective-permute-start.28) | collective-permute-done | bytes 49184 | tf_op jit(solution)/shard_map/ppermute | solution.py:51
  71.9 2.0 %mix_terms.2 = (bf16[2,208,384]{2,1,0:T(8,128)(2,1)S(1)}, bf16[2,208,384]{2,1,0:T(8,128)(2,1)S(1)}) custom-call(s32[6]{0:T(128)S(1)} %pad_add_fusion.refs_0_, bf16[2,768,256]{2,1,0:T(8,128)(2,1)S(1)} %get-tuple-element.120.refs_1_.refs_2_, bf16[2,768,256]{2,1,0:T(8,128)(2,1)S(1)} %collective-permute-done.14.refs_2_, ...), custom_call_target="tpu_custom_call" | custom-call | flops 1000 | bytes 1000 | tf_op jit(solution)/shard_map/mix_terms/pallas_call | solution.py:666
  73.9 1.6 %collective-permute-start.29 = (bf16[2,208,384]{2,1,0:T(8,128)(2,1)S(1)}, bf16[2,208,384]{2,1,0:T(8,128)(2,1)S(1)}, u32[]{:S(2)}, u32[]{:S(2)}) collective-permute-start(bf16[2,208,384]{2,1,0:T(8,128)(2,1)S(1)} %get-tuple-element.149), channel_id=1, source_target_pairs={{0,2},{1,5},{2,0},{3,7},{4,6},{5,1},{6,4},{7,3},{8,10},{9,13},{10,... | collective-permute-start | bytes 958472 | tf_op jit(solution)/shard_map/ppermute | solution.py:55
  75.5 2.0 %mix_terms.3 = (bf16[2,208,384]{2,1,0:T(8,128)(2,1)S(1)}, bf16[2,208,384]{2,1,0:T(8,128)(2,1)S(1)}) custom-call(s32[6]{0:T(128)S(1)} %pad_add_fusion.refs_0_, bf16[2,768,256]{2,1,0:T(8,128)(2,1)S(1)} %get-tuple-element.120.refs_1_.refs_2_, bf16[2,768,256]{2,1,0:T(8,128)(2,1)S(1)} %collective-permute-done.14.refs_2_, ...), custom_call_target="tpu_custom_call" | custom-call | flops 1000 | bytes 1000 | tf_op jit(solution)/shard_map/mix_terms/pallas_call | solution.py:666
  77.5 0.6 collective-permute-start.32
  78.0 5.9 %collective-permute-done.30.refs_1_ = bf16[4,96,768]{2,1,0:T(8,128)(2,1)S(1)} collective-permute-done((bf16[4,96,768]{2,1,0:T(8,128)(2,1)S(1)}, bf16[4,96,768]{2,1,0:T(8,128)(2,1)S(1)}, u32[]{:S(2)}, u32[]{:S(2)}) %collective-permute-start.30) | collective-permute-done | bytes 589856 | tf_op jit(solution)/shard_map/ppermute | solution.py:55
  84.0 2.7 %collective-permute-start.35 = (bf16[2,96,768]{2,1,0:T(8,128)(2,1)S(1)}, bf16[2,96,768]{2,1,0:T(8,128)(2,1)S(1)}, u32[]{:S(2)}, u32[]{:S(2)}) collective-permute-start(bf16[2,96,768]{2,1,0:T(8,128)(2,1)S(1)} %get-tuple-element.159), channel_id=1, source_target_pairs={{0,16},{1,17},{2,18},{3,19},{4,20},{5,21},{6,22},{7,23},{8,24},{9,... | collective-permute-start | bytes 884744 | tf_op jit(solution)/shard_map/ppermute | solution.py:55
  86.7 2.3 %collective-permute-done.29.refs_1_ = bf16[2,208,384]{2,1,0:T(8,128)(2,1)S(1)} collective-permute-done((bf16[2,208,384]{2,1,0:T(8,128)(2,1)S(1)}, bf16[2,208,384]{2,1,0:T(8,128)(2,1)S(1)}, u32[]{:S(2)}, u32[]{:S(2)}) %collective-permute-start.29) | collective-permute-done | bytes 319520 | tf_op jit(solution)/shard_map/ppermute | solution.py:55
  90.3 2.1 %collective-permute-done.32.refs_1_ = bf16[2,208,384]{2,1,0:T(8,128)(2,1)S(1)} collective-permute-done((bf16[2,208,384]{2,1,0:T(8,128)(2,1)S(1)}, bf16[2,208,384]{2,1,0:T(8,128)(2,1)S(1)}, u32[]{:S(2)}, u32[]{:S(2)}) %collective-permute-start.32) | collective-permute-done | bytes 319520 | tf_op jit(solution)/shard_map/ppermute | solution.py:55
  92.4 1.5 %collective-permute-start.31 = (bf16[1,208,384]{2,1,0:T(8,128)(2,1)S(1)}, bf16[1,208,384]{2,1,0:T(8,128)(2,1)S(1)}, u32[]{:S(2)}, u32[]{:S(2)}) collective-permute-start(bf16[1,208,384]{2,1,0:T(8,128)(2,1)S(1)} %get-tuple-element.154), channel_id=1, source_target_pairs={{0,4},{1,3},{2,6},{3,1},{4,0},{5,7},{6,2},{7,5},{8,12},{9,11},{10,... | collective-permute-start | bytes 479240 | tf_op jit(solution)/shard_map/ppermute | solution.py:55
  94.0 3.7 %collective-permute-done.31.refs_1_ = bf16[1,208,384]{2,1,0:T(8,128)(2,1)S(1)} collective-permute-done((bf16[1,208,384]{2,1,0:T(8,128)(2,1)S(1)}, bf16[1,208,384]{2,1,0:T(8,128)(2,1)S(1)}, u32[]{:S(2)}, u32[]{:S(2)}) %collective-permute-start.31) | collective-permute-done | bytes 159776 | tf_op jit(solution)/shard_map/ppermute | solution.py:55
  97.7 1.5 %collective-permute-start.38 = (bf16[1,208,384]{2,1,0:T(8,128)(2,1)S(1)}, bf16[1,208,384]{2,1,0:T(8,128)(2,1)S(1)}, u32[]{:S(2)}, u32[]{:S(2)}) collective-permute-start(bf16[1,208,384]{2,1,0:T(8,128)(2,1)S(1)} %get-tuple-element.167), channel_id=1, source_target_pairs={{0,4},{1,3},{2,6},{3,1},{4,0},{5,7},{6,2},{7,5},{8,12},{9,11},{10,... | collective-permute-start | bytes 479240 | tf_op jit(solution)/shard_map/ppermute | solution.py:55
  99.3 2.7 %collective-permute-start.39 = (bf16[1,208,384]{2,1,0:T(8,128)(2,1)S(1)}, bf16[1,208,384]{2,1,0:T(8,128)(2,1)S(1)}, u32[]{:S(2)}, u32[]{:S(2)}) collective-permute-start(bf16[1,208,384]{2,1,0:T(8,128)(2,1)S(1)} %add_last.1.refs_4_.refs_2_), channel_id=1, source_target_pairs={{0,16},{1,17},{2,18},{3,19},{4,20},{5,21},{6,22},{7,23},{8,24},{9,... | collective-permute-start | bytes 479240 | tf_op jit(solution)/shard_map/ppermute | solution.py:51
  101.9 0.6 collective-permute-start.34
  103.2 4.0 %collective-permute-start.40 = (bf16[1,192,384]{2,1,0:T(8,128)(2,1)S(1)}, bf16[1,192,384]{2,1,0:T(8,128)(2,1)S(1)}, u32[]{:S(2)}, u32[]{:S(2)}) collective-permute-start(bf16[1,192,384]{2,1,0:T(8,128)(2,1)S(1)} %get-tuple-element.176), channel_id=1, source_target_pairs={{0,16},{1,17},{2,18},{3,19},{4,20},{5,21},{6,22},{7,23},{8,24},{9,... | collective-permute-start | bytes 442376 | tf_op jit(solution)/shard_map/ppermute | solution.py:55
  107.2 2.0 %collective-permute-done.36.refs_1_ = bf16[1,96,768]{2,1,0:T(8,128)(2,1)S(1)} collective-permute-done((bf16[1,96,768]{2,1,0:T(8,128)(2,1)S(1)}, bf16[1,96,768]{2,1,0:T(8,128)(2,1)S(1)}, u32[]{:S(2)}, u32[]{:S(2)}) %collective-permute-start.36) | collective-permute-done | bytes 147488 | tf_op jit(solution)/shard_map/ppermute | solution.py:55
  109.2 0.7 down_end.1
  110.3 0.8 mix_end.1
  111.1 2.3 %collective-permute-done.40 = bf16[1,192,384]{2,1,0:T(8,128)(2,1)S(1)} collective-permute-done((bf16[1,192,384]{2,1,0:T(8,128)(2,1)S(1)}, bf16[1,192,384]{2,1,0:T(8,128)(2,1)S(1)}, u32[]{:S(2)}, u32[]{:S(2)}) %collective-permute-start.40) | collective-permute-done | bytes 147488 | tf_op jit(solution)/shard_map/ppermute | solution.py:55
  113.5 0.7 add_bitcast_fusion
  114.2 1.5 %place.1 = (bf16[256,768]{1,0:T(8,128)(2,1)}, bf16[256,768]{1,0:T(8,128)(2,1)}) custom-call(s32[6]{0:T(128)S(1)} %pad_add_fusion.refs_0_, bf16[2,64,768]{2,1,0:T(8,128)(2,1)S(1)} %get-tuple-element.133.refs_11_.refs_0_.refs_1_, bf16[2,64,768]{2,1,0:T(8,128)(2,1)S(1)} %collective-permute-done.12.refs_1_.refs_2_, ...), custom_call_target="tpu_custom_call" | custom-call | flops 1000 | bytes 1000 | tf_op jit(solution)/shard_map/place/pallas_call | solution.py:666
  (75 shorter events, 10.8 us)
Async XLA Ops:
  3.0 7.9 %collective-permute-start = (bf16[2,64,768]{2,1,0:T(8,128)(2,1)S(1)}, bf16[2,64,768]{2,1,0:T(8,128)(2,1)S(1)}, u32[]{:S(2)}, u32[]{:S(2)}) collective-permute-start(bf16[2,64,768]{2,1,0:T(8,128)(2,1)S(1)} %get-tuple-element.101), channel_id=1, source_target_pairs={{0,2},{1,3},{2,0},{3,1},{4,6},{5,7},{6,4},{7,5},{8,10},{9,11},{10,... | collective-permute-start | bytes 589832 | tf_op jit(solution)/shard_map/ppermute | solution.py:51
  11.5 13.8 %collective-permute-start.3 = (bf16[256,768]{1,0:T(8,128)(2,1)S(1)}, bf16[256,768]{1,0:T(8,128)(2,1)S(1)}, u32[]{:S(2)}, u32[]{:S(2)}) collective-permute-start(bf16[256,768]{1,0:T(8,128)(2,1)S(1)} %relay.5), channel_id=1, source_target_pairs={{0,2},{1,3},{2,0},{3,1},{4,6},{5,7},{6,4},{7,5},{8,10},{9,11},{10,... | collective-permute-start | bytes 1179656 | tf_op jit(solution)/shard_map/ppermute | solution.py:51
  13.3 1.3 %collective-permute-start.1 = (bf16[64,768]{1,0:T(8,128)(2,1)S(1)}, bf16[64,768]{1,0:T(8,128)(2,1)S(1)}, u32[]{:S(2)}, u32[]{:S(2)}) collective-permute-start(bf16[64,768]{1,0:T(8,128)(2,1)S(1)} %get-tuple-element.104), channel_id=1, source_target_pairs={{0,1},{1,0},{2,3},{3,2},{4,5},{5,4},{6,7},{7,6},{8,9},{9,8},{10,11... | collective-permute-start | bytes 294920 | tf_op jit(solution)/shard_map/ppermute | solution.py:51
  13.3 1.5 %collective-permute-start.2 = (bf16[64,768]{1,0:T(8,128)(2,1)S(1)}, bf16[64,768]{1,0:T(8,128)(2,1)S(1)}, u32[]{:S(2)}, u32[]{:S(2)}) collective-permute-start(bf16[64,768]{1,0:T(8,128)(2,1)S(1)} %get-tuple-element.105), channel_id=1, source_target_pairs={{0,1},{1,0},{2,3},{3,2},{4,5},{5,4},{6,7},{7,6},{8,9},{9,8},{10,11... | collective-permute-start | bytes 294920 | tf_op jit(solution)/shard_map/ppermute | solution.py:51
  20.1 21.6 %collective-permute-start.9 = (bf16[2,768,256]{2,1,0:T(8,128)(2,1)S(1)}, bf16[2,768,256]{2,1,0:T(8,128)(2,1)S(1)}, u32[]{:S(2)}, u32[]{:S(2)}) collective-permute-start(bf16[2,768,256]{2,1,0:T(8,128)(2,1)S(1)} %get-tuple-element.120.refs_1_.refs_2_), channel_id=1, source_target_pairs={{0,8},{1,9},{2,10},{3,11},{4,12},{5,13},{6,14},{7,15},{8,0},{9,1},... | collective-permute-start | bytes 2359304 | tf_op jit(solution)/shard_map/ppermute | solution.py:51
  24.7 19.6 %collective-permute-start.7 = (bf16[2,256,768]{2,1,0:T(8,128)(2,1)S(1)}, bf16[2,256,768]{2,1,0:T(8,128)(2,1)S(1)}, u32[]{:S(2)}, u32[]{:S(2)}) collective-permute-start(bf16[2,256,768]{2,1,0:T(8,128)(2,1)S(1)} %get-tuple-element.117.refs_3_), channel_id=1, source_target_pairs={{0,2},{1,3},{2,0},{3,1},{4,6},{5,7},{6,4},{7,5},{8,10},{9,11},{10,... | collective-permute-start | bytes 2359304 | tf_op jit(solution)/shard_map/ppermute | solution.py:51
  25.3 5.0 %collective-permute-start.4 = (bf16[256,768]{1,0:T(8,128)(2,1)S(1)}, bf16[256,768]{1,0:T(8,128)(2,1)S(1)}, u32[]{:S(2)}, u32[]{:S(2)}) collective-permute-start(bf16[256,768]{1,0:T(8,128)(2,1)S(1)} %get-tuple-element.102.refs_2_.refs_0_.refs_1_), channel_id=1, source_target_pairs={{0,1},{1,0},{2,3},{3,2},{4,5},{5,4},{6,7},{7,6},{8,9},{9,8},{10,11... | collective-permute-start | bytes 1179656 | tf_op jit(solution)/shard_map/ppermute | solution.py:51
  25.4 5.0 %collective-permute-start.5 = (bf16[256,768]{1,0:T(8,128)(2,1)S(1)}, bf16[256,768]{1,0:T(8,128)(2,1)S(1)}, u32[]{:S(2)}, u32[]{:S(2)}) collective-permute-start(bf16[256,768]{1,0:T(8,128)(2,1)S(1)} %relay.6.refs_2_), channel_id=1, source_target_pairs={{0,1},{1,0},{2,3},{3,2},{4,5},{5,4},{6,7},{7,6},{8,9},{9,8},{10,11... | collective-permute-start | bytes 1179656 | tf_op jit(solution)/shard_map/ppermute | solution.py:51
  25.9 11.2 %collective-permute-start.6 = (bf16[256,768]{1,0:T(8,128)(2,1)S(1)}, bf16[256,768]{1,0:T(8,128)(2,1)S(1)}, u32[]{:S(2)}, u32[]{:S(2)}) collective-permute-start(bf16[256,768]{1,0:T(8,128)(2,1)S(1)} %get-tuple-element.114.refs_3_.refs_1_), channel_id=1, source_target_pairs={{0,4},{1,5},{2,6},{3,7},{4,0},{5,1},{6,2},{7,3},{8,12},{9,13},{10,... | collective-permute-start | bytes 1179656 | tf_op jit(solution)/shard_map/ppermute | solution.py:51
  36.6 19.3 %collective-permute-start.21 = (bf16[4,256,384]{2,1,0:T(8,128)(2,1)S(1)}, bf16[4,256,384]{2,1,0:T(8,128)(2,1)S(1)}, u32[]{:S(2)}, u32[]{:S(2)}) collective-permute-start(bf16[4,256,384]{2,1,0:T(8,128)(2,1)S(1)} %get-tuple-element.180), channel_id=1, source_target_pairs={{0,4},{1,5},{2,6},{3,7},{4,0},{5,1},{6,2},{7,3},{8,12},{9,13},{10,... | collective-permute-start | bytes 2359304 | tf_op jit(solution)/shard_map/ppermute | solution.py:51
  37.2 8.0 %collective-permute-start.8 = (bf16[256,768]{1,0:T(8,128)(2,1)S(1)}, bf16[256,768]{1,0:T(8,128)(2,1)S(1)}, u32[]{:S(2)}, u32[]{:S(2)}) collective-permute-start(bf16[256,768]{1,0:T(8,128)(2,1)S(1)} %get-tuple-element.116.refs_2_), channel_id=1, source_target_pairs={{0,1},{1,0},{2,3},{3,2},{4,5},{5,4},{6,7},{7,6},{8,9},{9,8},{10,11... | collective-permute-start | bytes 1179656 | tf_op jit(solution)/shard_map/ppermute | solution.py:51
  37.2 19.6 %collective-permute-start.20 = (bf16[4,256,384]{2,1,0:T(8,128)(2,1)S(1)}, bf16[4,256,384]{2,1,0:T(8,128)(2,1)S(1)}, u32[]{:S(2)}, u32[]{:S(2)}) collective-permute-start(bf16[4,256,384]{2,1,0:T(8,128)(2,1)S(1)} %get-tuple-element.181.refs_5_), channel_id=1, source_target_pairs={{0,1},{1,0},{2,3},{3,2},{4,5},{5,4},{6,7},{7,6},{8,9},{9,8},{10,11... | collective-permute-start | bytes 2359304 | tf_op jit(solution)/shard_map/ppermute | solution.py:51
  41.7 2.6 %collective-permute-start.10 = (f32[8,128]{1,0:T(8,128)S(1)}, f32[8,128]{1,0:T(8,128)S(1)}, u32[]{:S(2)}, u32[]{:S(2)}) collective-permute-start(f32[8,128]{1,0:T(8,128)S(1)} %step.1), channel_id=1, source_target_pairs={{0,1},{1,0},{2,3},{3,2},{4,5},{5,4},{6,7},{7,6},{8,9},{9,8},{10,11... | collective-permute-start | bytes 12296 | tf_op jit(solution)/shard_map/ppermute | solution.py:51
  44.4 2.0 %collective-permute-start.11 = (bf16[256,768]{1,0:T(8,128)(2,1)S(1)}, bf16[256,768]{1,0:T(8,128)(2,1)S(1)}, u32[]{:S(2)}, u32[]{:S(2)}) collective-permute-start(bf16[256,768]{1,0:T(8,128)(2,1)S(1)} %relay.7), channel_id=1, source_target_pairs={{0,1},{1,0},{2,3},{3,2},{4,5},{5,4},{6,7},{7,6},{8,9},{9,8},{10,11... | collective-permute-start | bytes 1179656 | tf_op jit(solution)/shard_map/ppermute | solution.py:51
  44.6 20.0 %collective-permute-start.17 = (bf16[4,384,256]{2,1,0:T(8,128)(2,1)S(1)}, bf16[4,384,256]{2,1,0:T(8,128)(2,1)S(1)}, u32[]{:S(2)}, u32[]{:S(2)}) collective-permute-start(bf16[4,384,256]{2,1,0:T(8,128)(2,1)S(1)} %get-tuple-element.182), channel_id=1, source_target_pairs={{0,8},{1,9},{2,10},{3,11},{4,12},{5,13},{6,14},{7,15},{8,0},{9,1},... | collective-permute-start | bytes 2359304 | tf_op jit(solution)/shard_map/ppermute | solution.py:51
  45.1 11.0 %collective-permute-start.18 = (bf16[256,768]{1,0:T(8,128)(2,1)S(1)}, bf16[256,768]{1,0:T(8,128)(2,1)S(1)}, u32[]{:S(2)}, u32[]{:S(2)}) collective-permute-start(bf16[256,768]{1,0:T(8,128)(2,1)S(1)} %get-tuple-element.114.refs_3_.refs_1_), channel_id=1, source_target_pairs={{0,1},{1,0},{2,3},{3,2},{4,5},{5,4},{6,7},{7,6},{8,9},{9,8},{10,11... | collective-permute-start | bytes 1179656 | tf_op jit(solution)/shard_map/ppermute | solution.py:51
  46.4 10.3 %collective-permute-start.19 = (bf16[256,768]{1,0:T(8,128)(2,1)S(1)}, bf16[256,768]{1,0:T(8,128)(2,1)S(1)}, u32[]{:S(2)}, u32[]{:S(2)}) collective-permute-start(bf16[256,768]{1,0:T(8,128)(2,1)S(1)} %collective-permute-done.6.refs_10_.refs_3_), channel_id=1, source_target_pairs={{0,1},{1,0},{2,3},{3,2},{4,5},{5,4},{6,7},{7,6},{8,9},{9,8},{10,11... | collective-permute-start | bytes 1179656 | tf_op jit(solution)/shard_map/ppermute | solution.py:51
  56.1 1.5 %collective-permute-start.22 = (bf16[1,256,384]{2,1,0:T(8,128)(2,1)S(1)}, bf16[1,256,384]{2,1,0:T(8,128)(2,1)S(1)}, u32[]{:S(2)}, u32[]{:S(2)}) collective-permute-start(bf16[1,256,384]{2,1,0:T(8,128)(2,1)S(1)} %get-tuple-element.187), channel_id=1, source_target_pairs={{0,1},{1,0},{2,3},{3,2},{4,5},{5,4},{6,7},{7,6},{8,9},{9,8},{10,11... | collective-permute-start | bytes 589832 | tf_op jit(solution)/shard_map/ppermute | solution.py:51
  56.2 11.5 %collective-permute-start.14 = (bf16[2,768,256]{2,1,0:T(8,128)(2,1)S(1)}, bf16[2,768,256]{2,1,0:T(8,128)(2,1)S(1)}, u32[]{:S(2)}, u32[]{:S(2)}) collective-permute-start(bf16[2,768,256]{2,1,0:T(8,128)(2,1)S(1)} %get-tuple-element.120.refs_1_.refs_2_), channel_id=1, source_target_pairs={{0,1},{1,0},{2,3},{3,2},{4,5},{5,4},{6,7},{7,6},{8,9},{9,8},{10,11... | collective-permute-start | bytes 2359304 | tf_op jit(solution)/shard_map/ppermute | solution.py:51
  56.6 2.3 %collective-permute-start.23 = (bf16[1,256,384]{2,1,0:T(8,128)(2,1)S(1)}, bf16[1,256,384]{2,1,0:T(8,128)(2,1)S(1)}, u32[]{:S(2)}, u32[]{:S(2)}) collective-permute-start(bf16[1,256,384]{2,1,0:T(8,128)(2,1)S(1)} %get-tuple-element.186), channel_id=1, source_target_pairs={{0,1},{1,0},{2,3},{3,2},{4,5},{5,4},{6,7},{7,6},{8,9},{9,8},{10,11... | collective-permute-start | bytes 589832 | tf_op jit(solution)/shard_map/ppermute | solution.py:51
  56.7 2.5 %collective-permute-start.24 = (bf16[1,256,384]{2,1,0:T(8,128)(2,1)S(1)}, bf16[1,256,384]{2,1,0:T(8,128)(2,1)S(1)}, u32[]{:S(2)}, u32[]{:S(2)}) collective-permute-start(bf16[1,256,384]{2,1,0:T(8,128)(2,1)S(1)} %get-tuple-element.185), channel_id=1, source_target_pairs={{0,1},{1,0},{2,3},{3,2},{4,5},{5,4},{6,7},{7,6},{8,9},{9,8},{10,11... | collective-permute-start | bytes 589832 | tf_op jit(solution)/shard_map/ppermute | solution.py:51
  57.6 2.0 %collective-permute-start.25 = (bf16[1,256,384]{2,1,0:T(8,128)(2,1)S(1)}, bf16[1,256,384]{2,1,0:T(8,128)(2,1)S(1)}, u32[]{:S(2)}, u32[]{:S(2)}) collective-permute-start(bf16[1,256,384]{2,1,0:T(8,128)(2,1)S(1)} %get-tuple-element.184), channel_id=1, source_target_pairs={{0,1},{1,0},{2,3},{3,2},{4,5},{5,4},{6,7},{7,6},{8,9},{9,8},{10,11... | collective-permute-start | bytes 589832 | tf_op jit(solution)/shard_map/ppermute | solution.py:51
  59.0 12.9 %collective-permute-start.16 = (bf16[4,384,256]{2,1,0:T(8,128)(2,1)S(1)}, bf16[4,384,256]{2,1,0:T(8,128)(2,1)S(1)}, u32[]{:S(2)}, u32[]{:S(2)}) collective-permute-start(bf16[4,384,256]{2,1,0:T(8,128)(2,1)S(1)} %get-tuple-element.183.refs_5_), channel_id=1, source_target_pairs={{0,1},{1,0},{2,3},{3,2},{4,5},{5,4},{6,7},{7,6},{8,9},{9,8},{10,11... | collective-permute-start | bytes 2359304 | tf_op jit(solution)/shard_map/ppermute | solution.py:51
  59.3 12.6 %collective-permute-start.15 = (bf16[2,768,256]{2,1,0:T(8,128)(2,1)S(1)}, bf16[2,768,256]{2,1,0:T(8,128)(2,1)S(1)}, u32[]{:S(2)}, u32[]{:S(2)}) collective-permute-start(bf16[2,768,256]{2,1,0:T(8,128)(2,1)S(1)} %collective-permute-done.9.refs_0_.refs_3_), channel_id=1, source_target_pairs={{0,1},{1,0},{2,3},{3,2},{4,5},{5,4},{6,7},{7,6},{8,9},{9,8},{10,11... | collective-permute-start | bytes 2359304 | tf_op jit(solution)/shard_map/ppermute | solution.py:51
  64.7 7.2 %collective-permute-start.26 = (bf16[4,384,256]{2,1,0:T(8,128)(2,1)S(1)}, bf16[4,384,256]{2,1,0:T(8,128)(2,1)S(1)}, u32[]{:S(2)}, u32[]{:S(2)}) collective-permute-start(bf16[4,384,256]{2,1,0:T(8,128)(2,1)S(1)} %relay.9.refs_7_), channel_id=1, source_target_pairs={{0,1},{1,0},{2,3},{3,2},{4,5},{5,4},{6,7},{7,6},{8,9},{9,8},{10,11... | collective-permute-start | bytes 2359304 | tf_op jit(solution)/shard_map/ppermute | solution.py:51
  64.7 2.4 %collective-permute-start.27 = (f32[8,8,384]{2,1,0:T(8,128)S(1)}, f32[8,8,384]{2,1,0:T(8,128)S(1)}, u32[]{:S(2)}, u32[]{:S(2)}) collective-permute-start(f32[8,8,384]{2,1,0:T(8,128)S(1)} %get-tuple-element.147), channel_id=1, source_target_pairs={{0,1},{1,0},{2,3},{3,2},{4,5},{5,4},{6,7},{7,6},{8,9},{9,8},{10,11... | collective-permute-start | bytes 294920 | tf_op jit(solution)/shard_map/ppermute | solution.py:51
  67.2 4.2 %collective-permute-start.28 = (f32[4,8,384]{2,1,0:T(8,128)S(1)}, f32[4,8,384]{2,1,0:T(8,128)S(1)}, u32[]{:S(2)}, u32[]{:S(2)}) collective-permute-start(f32[4,8,384]{2,1,0:T(8,128)S(1)} %slice.56), channel_id=1, source_target_pairs={{0,8},{1,9},{2,10},{3,11},{4,12},{5,13},{6,14},{7,15},{8,0},{9,1},... | collective-permute-start | bytes 147464 | tf_op jit(solution)/shard_map/ppermute | solution.py:51
  67.7 16.2 %collective-permute-start.30 = (bf16[4,96,768]{2,1,0:T(8,128)(2,1)S(1)}, bf16[4,96,768]{2,1,0:T(8,128)(2,1)S(1)}, u32[]{:S(2)}, u32[]{:S(2)}) collective-permute-start(bf16[4,96,768]{2,1,0:T(8,128)(2,1)S(1)} %get-tuple-element.150), channel_id=1, source_target_pairs={{0,4},{1,5},{2,6},{3,7},{4,0},{5,1},{6,2},{7,3},{8,12},{9,13},{10,... | collective-permute-start | bytes 1769480 | tf_op jit(solution)/shard_map/ppermute | solution.py:55
  71.3 17.7 %collective-permute-start.33 = (bf16[4,192,384]{2,1,0:T(8,128)(2,1)S(1)}, bf16[4,192,384]{2,1,0:T(8,128)(2,1)S(1)}, u32[]{:S(2)}, u32[]{:S(2)}) collective-permute-start(bf16[4,192,384]{2,1,0:T(8,128)(2,1)S(1)} %get-tuple-element.156), channel_id=1, source_target_pairs={{0,2},{1,3},{2,0},{3,1},{4,6},{5,7},{6,4},{7,5},{8,10},{9,11},{10,... | collective-permute-start | bytes 1769480 | tf_op jit(solution)/shard_map/ppermute | solution.py:55
  73.9 15.1 %collective-permute-start.29 = (bf16[2,208,384]{2,1,0:T(8,128)(2,1)S(1)}, bf16[2,208,384]{2,1,0:T(8,128)(2,1)S(1)}, u32[]{:S(2)}, u32[]{:S(2)}) collective-permute-start(bf16[2,208,384]{2,1,0:T(8,128)(2,1)S(1)} %get-tuple-element.149), channel_id=1, source_target_pairs={{0,2},{1,5},{2,0},{3,7},{4,6},{5,1},{6,4},{7,3},{8,10},{9,13},{10,... | collective-permute-start | bytes 958472 | tf_op jit(solution)/shard_map/ppermute | solution.py:55
  77.5 14.9 %collective-permute-start.32 = (bf16[2,208,384]{2,1,0:T(8,128)(2,1)S(1)}, bf16[2,208,384]{2,1,0:T(8,128)(2,1)S(1)}, u32[]{:S(2)}, u32[]{:S(2)}) collective-permute-start(bf16[2,208,384]{2,1,0:T(8,128)(2,1)S(1)} %get-tuple-element.155), channel_id=1, source_target_pairs={{0,2},{1,5},{2,0},{3,7},{4,6},{5,1},{6,4},{7,3},{8,10},{9,13},{10,... | collective-permute-start | bytes 958472 | tf_op jit(solution)/shard_map/ppermute | solution.py:55
  84.0 18.5 %collective-permute-start.35 = (bf16[2,96,768]{2,1,0:T(8,128)(2,1)S(1)}, bf16[2,96,768]{2,1,0:T(8,128)(2,1)S(1)}, u32[]{:S(2)}, u32[]{:S(2)}) collective-permute-start(bf16[2,96,768]{2,1,0:T(8,128)(2,1)S(1)} %get-tuple-element.159), channel_id=1, source_target_pairs={{0,16},{1,17},{2,18},{3,19},{4,20},{5,21},{6,22},{7,23},{8,24},{9,... | collective-permute-start | bytes 884744 | tf_op jit(solution)/shard_map/ppermute | solution.py:55
  89.2 13.9 %collective-permute-start.37 = (bf16[2,192,384]{2,1,0:T(8,128)(2,1)S(1)}, bf16[2,192,384]{2,1,0:T(8,128)(2,1)S(1)}, u32[]{:S(2)}, u32[]{:S(2)}) collective-permute-start(bf16[2,192,384]{2,1,0:T(8,128)(2,1)S(1)} %get-tuple-element.162), channel_id=1, source_target_pairs={{0,8},{1,9},{2,10},{3,11},{4,12},{5,13},{6,14},{7,15},{8,0},{9,1},... | collective-permute-start | bytes 884744 | tf_op jit(solution)/shard_map/ppermute | solution.py:55
  89.7 9.5 %collective-permute-start.12 = (bf16[2,64,768]{2,1,0:T(8,128)(2,1)S(1)}, bf16[2,64,768]{2,1,0:T(8,128)(2,1)S(1)}, u32[]{:S(2)}, u32[]{:S(2)}) collective-permute-start(bf16[2,64,768]{2,1,0:T(8,128)(2,1)S(1)} %get-tuple-element.134), channel_id=1, source_target_pairs={{0,1},{1,0},{2,3},{3,2},{4,5},{5,4},{6,7},{7,6},{8,9},{9,8},{10,11... | collective-permute-start | bytes 589832 | tf_op jit(solution)/shard_map/ppermute | solution.py:51
  89.7 12.2 %collective-permute-start.13 = (bf16[2,64,768]{2,1,0:T(8,128)(2,1)S(1)}, bf16[2,64,768]{2,1,0:T(8,128)(2,1)S(1)}, u32[]{:S(2)}, u32[]{:S(2)}) collective-permute-start(bf16[2,64,768]{2,1,0:T(8,128)(2,1)S(1)} %get-tuple-element.144), channel_id=1, source_target_pairs={{0,1},{1,0},{2,3},{3,2},{4,5},{5,4},{6,7},{7,6},{8,9},{9,8},{10,11... | collective-permute-start | bytes 589832 | tf_op jit(solution)/shard_map/ppermute | solution.py:51
  92.4 5.3 %collective-permute-start.31 = (bf16[1,208,384]{2,1,0:T(8,128)(2,1)S(1)}, bf16[1,208,384]{2,1,0:T(8,128)(2,1)S(1)}, u32[]{:S(2)}, u32[]{:S(2)}) collective-permute-start(bf16[1,208,384]{2,1,0:T(8,128)(2,1)S(1)} %get-tuple-element.154), channel_id=1, source_target_pairs={{0,4},{1,3},{2,6},{3,1},{4,0},{5,7},{6,2},{7,5},{8,12},{9,11},{10,... | collective-permute-start | bytes 479240 | tf_op jit(solution)/shard_map/ppermute | solution.py:55
  97.7 12.2 %collective-permute-start.38 = (bf16[1,208,384]{2,1,0:T(8,128)(2,1)S(1)}, bf16[1,208,384]{2,1,0:T(8,128)(2,1)S(1)}, u32[]{:S(2)}, u32[]{:S(2)}) collective-permute-start(bf16[1,208,384]{2,1,0:T(8,128)(2,1)S(1)} %get-tuple-element.167), channel_id=1, source_target_pairs={{0,4},{1,3},{2,6},{3,1},{4,0},{5,7},{6,2},{7,5},{8,12},{9,11},{10,... | collective-permute-start | bytes 479240 | tf_op jit(solution)/shard_map/ppermute | solution.py:55
  99.3 11.0 %collective-permute-start.39 = (bf16[1,208,384]{2,1,0:T(8,128)(2,1)S(1)}, bf16[1,208,384]{2,1,0:T(8,128)(2,1)S(1)}, u32[]{:S(2)}, u32[]{:S(2)}) collective-permute-start(bf16[1,208,384]{2,1,0:T(8,128)(2,1)S(1)} %add_last.1.refs_4_.refs_2_), channel_id=1, source_target_pairs={{0,16},{1,17},{2,18},{3,19},{4,20},{5,21},{6,22},{7,23},{8,24},{9,... | collective-permute-start | bytes 479240 | tf_op jit(solution)/shard_map/ppermute | solution.py:51
  101.9 12.3 %collective-permute-start.34 = (bf16[4,64,768]{2,1,0:T(8,128)(2,1)S(1)}, bf16[4,64,768]{2,1,0:T(8,128)(2,1)S(1)}, u32[]{:S(2)}, u32[]{:S(2)}) collective-permute-start(bf16[4,64,768]{2,1,0:T(8,128)(2,1)S(1)} %gather.1), channel_id=1, source_target_pairs={{0,2},{1,3},{2,0},{3,1},{4,6},{5,7},{6,4},{7,5},{8,10},{9,11},{10,... | collective-permute-start | bytes 1179656 | tf_op jit(solution)/shard_map/ppermute | solution.py:51
  102.6 6.6 %collective-permute-start.36 = (bf16[1,96,768]{2,1,0:T(8,128)(2,1)S(1)}, bf16[1,96,768]{2,1,0:T(8,128)(2,1)S(1)}, u32[]{:S(2)}, u32[]{:S(2)}) collective-permute-start(bf16[1,96,768]{2,1,0:T(8,128)(2,1)S(1)} %get-tuple-element.161), channel_id=1, source_target_pairs={{0,8},{1,9},{2,10},{3,11},{4,12},{5,13},{6,14},{7,15},{8,0},{9,1},... | collective-permute-start | bytes 442376 | tf_op jit(solution)/shard_map/ppermute | solution.py:55
  103.2 10.3 %collective-permute-start.40 = (bf16[1,192,384]{2,1,0:T(8,128)(2,1)S(1)}, bf16[1,192,384]{2,1,0:T(8,128)(2,1)S(1)}, u32[]{:S(2)}, u32[]{:S(2)}) collective-permute-start(bf16[1,192,384]{2,1,0:T(8,128)(2,1)S(1)} %get-tuple-element.176), channel_id=1, source_target_pairs={{0,16},{1,17},{2,18},{3,19},{4,20},{5,21},{6,22},{7,23},{8,24},{9,... | collective-permute-start | bytes 442376 | tf_op jit(solution)/shard_map/ppermute | solution.py:55
